TPU v7x, 32 devices: a whole 2x2x4 slice. The times are simulated.
32 devices in a mesh: groups: 2 (over y), tensor: 4 (over z), dp: 4 (over x, core).
Axes of the slice: x: 2, y: 2, z: 4, core: 2. Of those that a mesh axis runs over, the one named last changes fastest.
Arguments:
- acts: bfloat16 [32, 256, 8192], P(('groups', 'dp'), None, 'tensor'), parts along dimension 0, may hold values from -30 to 30
- grads: bfloat16 [2, 32, 256, 28672], P(None, ('groups', 'dp'), None, 'tensor'), parts along dimension 1, may hold values from -30 to 30
- proj_in: bfloat16 [2, 64, 8192], P(None, None, 'tensor'), may hold values from -0.0625 to 0.0625
- proj_out: bfloat16 [2, 64, 28672], P(None, None, 'tensor'), may hold values from -0.03125 to 0.03125
- queries: bfloat16 [64, 2, 64, 64], P('dp'), may hold values from -1.1953125 to 1.1953125
Outputs:
- scores: float32 [32, 64], P(('groups', 'dp')), parts along dimension 0
There are 2 independent parts, one for each index of `groups`. A program takes and returns all parts, laid end to end along the dimension named above; an argument that names none is the same for every part. Nothing has to cross between parts.
All inputs are finite; a program needn't handle non-finite values.
Results may differ from a plain program's by a relative error of at most 0.003.
The roundings to bfloat16 on the way count: a program that leaves them out, or rounds other values in their place, can miss the bound.
Values may be sent and summed in bfloat16 or wider, within the bound.
No kernel may reach another device: no remote copies, remote signals or barrier semaphores. Data moves between devices by JAX's collectives and lax.ppermute only.
A program may use at most 128 MiB of HBM per device.

v0:
```python
import jax
import jax.numpy as jnp
from jax import lax
from jax.sharding import PartitionSpec as P


def damp(matrix):
    size = matrix.shape[0]
    shift = 0.1 * jnp.trace(matrix) / size
    return matrix + shift * jnp.eye(size, dtype=matrix.dtype)


def chol_apply(factor, rhs):
    lower_sol = lax.linalg.triangular_solve(factor, rhs, left_side=True, lower=True)
    return lax.linalg.triangular_solve(
        factor, lower_sol, left_side=True, lower=True, transpose_a=True
    )


def precondition(query, left, right):
    count, rank = (query.shape[0], query.shape[1])
    left_fac = jnp.linalg.cholesky(left)
    right_fac = jnp.linalg.cholesky(right)
    stacked = jnp.transpose(query, (1, 0, 2)).reshape(rank, count * rank)
    middle = chol_apply(left_fac, stacked).reshape(rank, count, rank)
    turned = jnp.transpose(middle, (2, 1, 0)).reshape(rank, count * rank)
    result = chol_apply(right_fac, turned).reshape(rank, count, rank)
    return jnp.transpose(result, (1, 2, 0))


def diagonal_blocks(whole, rank):
    return jnp.stack([whole[:, 0:rank, 0:rank], whole[:, rank : 2 * rank, rank : 2 * rank]], axis=1)


def local(acts, grads, proj_in, proj_out, queries):
    seq_count, length, width_loc = acts.shape
    rank = proj_in.shape[1]
    hidden_loc = grads.shape[3]
    flat = acts.reshape(-1, width_loc)
    xpart = jnp.einsum(
        "td,rd->tr", flat, proj_in.reshape(2 * rank, width_loc), preferred_element_type=jnp.float32
    )
    gpart = jnp.concatenate(
        [
            jnp.einsum(
                "tf,rf->tr",
                grads[0].reshape(-1, hidden_loc),
                proj_out[0],
                preferred_element_type=jnp.float32,
            ),
            jnp.einsum(
                "tf,rf->tr",
                grads[1].reshape(-1, hidden_loc),
                proj_out[1],
                preferred_element_type=jnp.float32,
            ),
        ],
        axis=1,
    )
    total = seq_count * length * lax.axis_size("dp")
    xin, gout = lax.psum((xpart, gpart), "tensor")
    cov_in = jnp.dot(xin.T, xin, precision=lax.Precision.HIGHEST)
    cov_out = jnp.dot(gout.T, gout, precision=lax.Precision.HIGHEST)
    cov_in, cov_out = lax.psum((cov_in, cov_out), "dp")
    whole = (
        jnp.einsum(
            "sto,sti->soi",
            gout.reshape(seq_count, length, 2 * rank),
            xin.reshape(seq_count, length, 2 * rank),
            precision=lax.Precision.HIGHEST,
        )
        / length
    )
    samples = diagonal_blocks(whole, rank)
    cov_in = cov_in / total
    cov_out = cov_out / total
    precond = []
    for layer in range(2):
        low = layer * rank
        damped_in = damp(cov_in[low : low + rank, low : low + rank])
        damped_out = damp(cov_out[low : low + rank, low : low + rank])
        precond.append(precondition(queries[:, layer].astype(jnp.float32), damped_out, damped_in))
    query_count = queries.shape[0]
    query_b = jnp.stack(precond, axis=1).astype(jnp.bfloat16).reshape(query_count, -1)
    sample_b = samples.astype(jnp.bfloat16).reshape(seq_count, -1)
    return jnp.einsum(
        "sk,qk->sq",
        sample_b,
        lax.all_gather(query_b, "dp", axis=0, tiled=True),
        preferred_element_type=jnp.float32,
    )


def solution(mesh):
    placed = (
        P(("groups", "dp"), None, "tensor"),
        P(None, ("groups", "dp"), None, "tensor"),
        P(None, None, "tensor"),
        P(None, None, "tensor"),
        P("dp", None, None, None),
    )
    return jax.shard_map(
        local, mesh=mesh, in_specs=placed, out_specs=P(("groups", "dp"), None), check_vma=False
    )
```

profile of v0, /device:TPU:0, one launch (start us, length us, event | category | flops | bytes accessed | tf_op | source)
XLA Modules:
  0.0 210.0 jit_solution(16052202837936314791)
XLA Ops:
  6.5 11.5 %fusion.31 = (bf16[1,4,256,7168]{3,2,1,0:T(8,128)(2,1)S(1)}, bf16[1,4,256,7168]{3,2,1,0:T(8,128)(2,1)S(1)}) fusion(bf16[2,4,256,7168]{3,2,1,0:T(8,128)(2,1)} %param.11), kind=kLoop, calls=%fused_computation.70 | loop fusion | bytes 58720256 | tf_op jit(solution)/shard_map/slice | solution.py:47
  18.1 5.9 %fusion.1 = f32[1024,64]{0,1:T(8,128)S(1)} fusion(bf16[1024,7168]{1,0:T(8,128)(2,1)S(1)} %bitcast.118, bf16[2,64,7168]{2,1,0:T(8,128)(2,1)} %param.13), kind=kOutput, calls=%fused_computation.4 | convolution fusion | flops 939524096 | bytes 15859712 | tf_op jit(solution)/shard_map/tf,rf->tr/dot_general | solution.py:51
  24.0 5.8 %fusion.3 = f32[1024,64]{0,1:T(8,128)S(1)} fusion(bf16[1024,7168]{1,0:T(8,128)(2,1)S(1)} %bitcast.117, bf16[2,64,7168]{2,1,0:T(8,128)(2,1)} %param.13), kind=kOutput, calls=%fused_computation.6 | convolution fusion | flops 939524096 | bytes 15859712 | tf_op jit(solution)/shard_map/tf,rf->tr/dot_general | solution.py:45
  29.8 0.9 pad_maximum_fusion
  30.7 2.1 fusion.32
  32.8 55.0 %all-reduce.7.cloned.1.call-done = (f32[1024,128]{1,0:T(8,128)}, f32[1024,128]{0,1:T(8,128)}) async-done(((f32[1024,128]{1,0:T(8,128)}, f32[1024,128]{0,1:T(8,128)}), (f32[1024,128]{1,0:T(8,128)}, f32[1024,128]{0,1:T(8,128)})) %all-reduce.7.cloned.1.call-update) | async-done | bytes 1048592 | tf_op jit(solution)/shard_map/psum | solution.py:61
  87.8 2.9 %fusion.33 = f32[128,128]{0,1:T(8,128)} fusion(f32[1024,128]{1,0:T(8,128)} %get-tuple-element.14), kind=kOutput, calls=%fused_computation.72 | convolution fusion | flops 201326592 | bytes 589824 | tf_op jit(solution)/shard_map/dot_general | solution.py:62
  90.7 2.4 %fusion.34 = f32[128,128]{0,1:T(8,128)} fusion(f32[1024,128]{0,1:T(8,128)} %get-tuple-element.15), kind=kOutput, calls=%fused_computation.73 | convolution fusion | flops 201326592 | bytes 589824 | tf_op jit(solution)/shard_map/dot_general | solution.py:63
  93.2 0.2 all-gather.2.cloned.1.call-start
  93.5 0.3 copy.19
  93.8 0.2 reshape.98
  94.0 0.3 copy.24
  94.5 29.8 %all-reduce.5.cloned.1.call-done = (f32[128,128]{0,1:T(8,128)}, f32[128,128]{0,1:T(8,128)}) async-done(((f32[128,128]{0,1:T(8,128)}, f32[128,128]{0,1:T(8,128)}), (f32[128,128]{0,1:T(8,128)}, f32[128,128]{0,1:T(8,128)})) %all-reduce.5.cloned.1.call-update) | async-done | bytes 131088 | tf_op jit(solution)/shard_map/psum | solution.py:64
  124.2 0.9 broadcast_multiply_fusion
  125.1 0.8 select_reduce_fusion.7
  127.4 5.8 %cholesky.74 = f32[64,64]{1,0:T(8,128)S(1)} custom-call(f32[64,64]{1,0:T(8,128)S(1)} %fusion.30), custom_call_target="Cholesky" | custom-call | tf_op jit(solution)/shard_map/jit(cholesky)/cholesky | solution.py:23
  133.3 0.6 compare_reduce_fusion.3
  133.9 0.7 fusion.9
  134.6 4.9 %custom-call.17 = f32[1,64,64]{1,2,0:T(8,128)S(1)} custom-call(f32[1,64,64]{2,1,0:T(8,128)S(1)} %fusion.9), custom_call_target="InvertDiagBlocksLowerTriangular" | custom-call | tf_op jit(solution)/shard_map/triangular_solve/custom-call.2 | solution.py:15
  139.5 0.8 select_reduce_fusion.6
  141.8 5.8 %cholesky.85 = f32[64,64]{1,0:T(8,128)S(1)} custom-call(f32[64,64]{1,0:T(8,128)S(1)} %fusion.26), custom_call_target="Cholesky" | custom-call | tf_op jit(solution)/shard_map/jit(cholesky)/cholesky | solution.py:22
  147.7 0.6 compare_reduce_fusion.2
  148.3 0.7 fusion.10
  149.0 4.9 %custom-call.15 = f32[1,64,64]{1,2,0:T(8,128)S(1)} custom-call(f32[1,64,64]{2,1,0:T(8,128)S(1)} %fusion.10), custom_call_target="InvertDiagBlocksLowerTriangular" | custom-call | tf_op jit(solution)/shard_map/triangular_solve/custom-call.2 | solution.py:15
  153.9 0.4 fusion.22
  154.3 0.4 fusion.24
  154.8 0.4 copy.20
  155.2 0.2 reshape.78
  155.3 0.4 fusion.27
  155.8 0.4 convolution_convert_fusion.1
  156.4 5.8 %cholesky.96 = f32[64,64]{1,0:T(8,128)S(1)} custom-call(f32[64,64]{1,0:T(8,128)S(1)} %fusion.21), custom_call_target="Cholesky" | custom-call | tf_op jit(solution)/shard_map/jit(cholesky)/cholesky | solution.py:23
  162.3 0.6 compare_reduce_fusion.1
  162.9 0.7 fusion.11
  163.6 4.9 %custom-call.21 = f32[1,64,64]{1,2,0:T(8,128)S(1)} custom-call(f32[1,64,64]{2,1,0:T(8,128)S(1)} %fusion.11), custom_call_target="InvertDiagBlocksLowerTriangular" | custom-call | tf_op jit(solution)/shard_map/triangular_solve/custom-call.2 | solution.py:15
  168.6 5.8 %cholesky.107 = f32[64,64]{1,0:T(8,128)S(1)} custom-call(f32[64,64]{1,0:T(8,128)S(1)} %fusion.17), custom_call_target="Cholesky" | custom-call | tf_op jit(solution)/shard_map/jit(cholesky)/cholesky | solution.py:22
  174.5 0.6 compare_reduce_fusion
  175.1 0.7 fusion.12
  175.8 4.9 %custom-call.19 = f32[1,64,64]{1,2,0:T(8,128)S(1)} custom-call(f32[1,64,64]{2,1,0:T(8,128)S(1)} %fusion.12), custom_call_target="InvertDiagBlocksLowerTriangular" | custom-call | tf_op jit(solution)/shard_map/triangular_solve/custom-call.2 | solution.py:15
  180.7 0.4 fusion.13
  181.1 0.4 fusion.15
  181.6 0.4 copy.25
  182.0 0.2 reshape.83
  182.2 0.4 fusion.18
  182.6 0.4 convolution_convert_fusion
  183.2 1.2 convert_element_type.25
  184.5 0.7 fusion
  185.4 15.9 %all-gather.2.cloned.1.call-done = bf16[64,8192]{1,0:T(8,128)(2,1)} async-done(((bf16[16,8192]{1,0:T(8,128)(2,1)}), bf16[64,8192]{1,0:T(8,128)(2,1)}) %all-gather.2.cloned.1.call-update) | async-done | bytes 1048592 | tf_op jit(solution)/shard_map/all_gather | solution.py:89
  201.3 2.2 %fusion.35 = f32[4,64]{1,0:T(4,128)} fusion(bf16[4,8192]{1,0:T(4,128)(2,1)S(1)} %convert_element_type.22, bf16[64,8192]{1,0:T(8,128)(2,1)} %all-gather.2.cloned.1.call-done), kind=kOutput, calls=%fused_computation.74 | convolution fusion | flops 4194304 | bytes 1115136 | tf_op jit(solution)/shard_map/sk,qk->sq/dot_general | solution.py:86
  (40 shorter events, 2.0 us)
Async XLA Ops:
  6.5 24.2 %copy-start = (bf16[2,64,2048]{2,1,0:T(8,128)(2,1)S(1)}, bf16[2,64,2048]{2,1,0:T(8,128)(2,1)}, u32[]{:S(2)}) copy-start(bf16[2,64,2048]{2,1,0:T(8,128)(2,1)} %param.12) | copy-start | bytes 1572868
  6.5 81.3 %all-reduce.7.cloned.1.call-start = ((), (), s32[]{:S(2)}) async-start(), calls=%async_computation.2 | async-start | bytes 2097152 | tf_op jit(solution)/shard_map/psum | solution.py:61
  18.0 12.7 %copy-start.1 = (bf16[4,256,2048]{2,1,0:T(8,128)(2,1)S(1)}, bf16[4,256,2048]{2,1,0:T(8,128)(2,1)}, u32[]{:S(2)}) copy-start(bf16[4,256,2048]{2,1,0:T(8,128)(2,1)} %param.10) | copy-start | bytes 12582916
  24.0 69.4 %copy-start.4 = (bf16[16,2,64,64]{3,2,1,0:T(8,128)(2,1)S(1)}, bf16[16,2,64,64]{3,2,1,0:T(8,128)(2,1)}, u32[]{:S(2)}) copy-start(bf16[16,2,64,64]{3,2,1,0:T(8,128)(2,1)} %param.14) | copy-start | bytes 786436
  32.8 91.5 %all-reduce.5.cloned.1.call-start = ((), (), s32[]{:S(2)}) async-start(), calls=%async_computation.1 | async-start | bytes 262144 | tf_op jit(solution)/shard_map/psum | solution.py:64
  87.8 96.6 %copy-start.2 = (f32[1024,128]{1,0:T(8,128)S(1)}, f32[1024,128]{1,0:T(8,128)}, u32[]{:S(2)}) copy-start(f32[1024,128]{1,0:T(8,128)} %get-tuple-element.14) | copy-start | bytes 1572868
  87.8 96.6 %copy-start.3 = (f32[1024,128]{0,1:T(8,128)S(1)}, f32[1024,128]{0,1:T(8,128)}, u32[]{:S(2)}) copy-start(f32[1024,128]{0,1:T(8,128)} %get-tuple-element.15) | copy-start | bytes 1572868
  93.2 108.1 %all-gather.2.cloned.1.call-start = ((), (), s32[]{:S(2)}) async-start(), calls=%async_computation | async-start | bytes 1310720 | tf_op jit(solution)/shard_map/all_gather | solution.py:89
Sparse Core Ops, SparseCore 0:
  32.9 54.8 all-reduce.6
  93.3 30.8 all-reduce.4
  184.6 16.7 all-gather.1
where the time goes:
time: 210 us
  waiting for transfers between devices  101 us (48%)
  other arithmetic  52 us (25%)
  matrix products  25.1 us (12%)
  between operations  16.1 us (8%)
  local copies, waits for them, and re-layouts  15.9 us (8%)
    psum x1, waiting for transfers between devices, local(): xin, gout = lax.psum((xpart, gpart), 'tensor')  55 us
    psum x1, waiting for transfers between devices, local(): cov_in, cov_out = lax.psum((cov_in, cov_out), 'dp')  29.8 us
    another operation x8, other arithmetic, chol_apply(): lax.linalg.triangular_solve(factor, lower_sol, left_side=True, lower=True...  22.2 us
    all_gather x1, waiting for transfers between devices, local(): lax.all_gather(query_b, 'dp', axis=0, tiled=True)  15.9 us
    another operation x6, other arithmetic, precondition(): left_fac = jnp.linalg.cholesky(left)  13 us
    another operation x6, other arithmetic, precondition(): right_fac = jnp.linalg.cholesky(right)  13 us
    slice x1, local copies, waits for them, and re-layouts, local(): grads[0].reshape(-1, hidden_loc)  11.5 us
    dot_general x1, matrix products, local(): jnp.einsum('tf,rf->tr', grads[1].reshape(-1, hidden_loc), proj_out[1], pr...  5.93 us
  transfers between devices with their start and end apart: 3, of which 3 were waited for; matrix products, arithmetic and copies ran while one was open for 1% of the time, Pallas kernels for 0%

commit v1 on v0

v1 whole, which is shorter than its diff:
```python
import functools

import jax
import jax.numpy as jnp
from jax import lax
from jax.experimental import pallas as pl
from jax.experimental.pallas import tpu as pltpu
from jax.sharding import PartitionSpec as P

HIGHEST = lax.Precision.HIGHEST
MIB = 1024 * 1024


def nt(a, b, precision=None):
    return lax.dot_general(
        a, b, (((1,), (1,)), ((), ())), precision=precision, preferred_element_type=jnp.float32
    )


def tn(a, b, precision=None):
    return lax.dot_general(
        a, b, (((0,), (0,)), ((), ())), precision=precision, preferred_element_type=jnp.float32
    )


def nn(a, b, precision=None):
    return jnp.dot(a, b, precision=precision, preferred_element_type=jnp.float32)


def vmem():
    return pl.BlockSpec(memory_space=pltpu.VMEM)


def smem():
    return pl.BlockSpec(memory_space=pltpu.SMEM)


def emit(where_ref, outs, acc):
    count = len(outs)
    for k, out in enumerate(outs):
        out[...] = acc[lax.rem(where_ref[0] + k, count)]


def project_in_kernel(where_ref, acts_ref, proj_ref, *rest):
    outs, acc = rest[:-1], rest[-1]
    step = pl.program_id(0)
    seqs, length, width = acts_ref.shape
    both = proj_ref.shape[0] * proj_ref.shape[1]
    part = nt(acts_ref[...].reshape(seqs * length, width), proj_ref[...].reshape(both, width))
    part = part.reshape(seqs, length, both)

    @pl.when(step == 0)
    def _():
        acc[...] = part

    @pl.when(step > 0)
    def _():
        acc[...] += part

    @pl.when(step == pl.num_programs(0) - 1)
    def _():
        emit(where_ref, outs, acc)


def project_out_kernel(where_ref, grads_ref, proj_ref, *rest):
    outs, acc = rest[:-1], rest[-1]
    step = pl.program_id(0)
    _, seqs, length, width = grads_ref.shape
    rank = proj_ref.shape[1]
    none = jnp.zeros((rank, width), proj_ref.dtype)
    first = jnp.concatenate([proj_ref[0], none], axis=0)
    second = jnp.concatenate([none, proj_ref[1]], axis=0)
    part = nt(grads_ref[0].reshape(seqs * length, width), first)
    part = part + nt(grads_ref[1].reshape(seqs * length, width), second)
    part = part.reshape(seqs, length, 2 * rank)

    @pl.when(step == 0)
    def _():
        acc[...] = part

    @pl.when(step > 0)
    def _():
        acc[...] += part

    @pl.when(step == pl.num_programs(0) - 1)
    def _():
        emit(where_ref, outs, acc)


def project_in(where, acts, proj):
    seqs, length, width = acts.shape
    rank = proj.shape[1]
    block = 512
    return pl.pallas_call(
        project_in_kernel,
        grid=(width // block,),
        in_specs=[
            smem(),
            pl.BlockSpec((seqs, length, block), lambda i: (0, 0, i)),
            pl.BlockSpec((2, rank, block), lambda i: (0, 0, i)),
        ],
        out_specs=[pl.BlockSpec((length, 2 * rank), lambda i: (0, 0))] * seqs,
        out_shape=[jax.ShapeDtypeStruct((length, 2 * rank), jnp.float32)] * seqs,
        scratch_shapes=[pltpu.VMEM((seqs, length, 2 * rank), jnp.float32)],
        compiler_params=pltpu.CompilerParams(vmem_limit_bytes=24 * MIB),
        name="project_in",
    )(where, acts, proj)


def project_out(where, grads, proj):
    _, seqs, length, width = grads.shape
    rank = proj.shape[1]
    block = 512
    return pl.pallas_call(
        project_out_kernel,
        grid=(width // block,),
        in_specs=[
            smem(),
            pl.BlockSpec((2, seqs, length, block), lambda i: (0, 0, 0, i)),
            pl.BlockSpec((2, rank, block), lambda i: (0, 0, i)),
        ],
        out_specs=[pl.BlockSpec((length, 2 * rank), lambda i: (0, 0))] * seqs,
        out_shape=[jax.ShapeDtypeStruct((length, 2 * rank), jnp.float32)] * seqs,
        scratch_shapes=[pltpu.VMEM((seqs, length, 2 * rank), jnp.float32)],
        compiler_params=pltpu.CompilerParams(vmem_limit_bytes=24 * MIB),
        name="project_out",
    )(where, grads, proj)


def left_lanes(rows, lanes):
    return lax.broadcasted_iota(jnp.int32, (rows, lanes), 1) < lanes // 2


def side_by_side(whole):
    size = whole.shape[0]
    half = size // 2
    return jnp.where(left_lanes(half, size), whole[:half], whole[half:])


def block_diagonal(pair):
    left = left_lanes(*pair.shape)
    return jnp.concatenate([jnp.where(left, pair, 0.0), jnp.where(left, 0.0, pair)], axis=0)


def total(pieces):
    value = pieces[0][...]
    for piece in pieces[1:]:
        value = value + piece[...]
    return value


def cov_in_kernel(*refs):
    pieces, (x_out, cov_out) = refs[:-2], refs[-2:]
    x = total(pieces)
    x_out[...] = x
    cov_out[...] = side_by_side(tn(x, x, HIGHEST))


def cov_in(pieces):
    length, both = pieces[0].shape
    return pl.pallas_call(
        cov_in_kernel,
        in_specs=[vmem()] * len(pieces),
        out_specs=[vmem()] * 2,
        out_shape=[
            jax.ShapeDtypeStruct((length, both), jnp.float32),
            jax.ShapeDtypeStruct((both // 2, both), jnp.float32),
        ],
        compiler_params=pltpu.CompilerParams(vmem_limit_bytes=8 * MIB),
        name="cov_in",
    )(*pieces)


def cov_out_kernel(length, x_ref, *refs):
    pieces, (cov_out, sample_out) = refs[:-2], refs[-2:]
    x = x_ref[...]
    g = total(pieces)
    cov_out[...] = side_by_side(tn(g, g, HIGHEST))
    sample = tn(x, g, HIGHEST) / length
    sample_out[...] = side_by_side(sample).astype(jnp.bfloat16)


def cov_out(x, pieces):
    length, both = x.shape
    return pl.pallas_call(
        functools.partial(cov_out_kernel, length),
        in_specs=[vmem()] * (1 + len(pieces)),
        out_specs=[vmem()] * 2,
        out_shape=[
            jax.ShapeDtypeStruct((both // 2, both), jnp.float32),
            jax.ShapeDtypeStruct((both // 2, both), jnp.bfloat16),
        ],
        compiler_params=pltpu.CompilerParams(vmem_limit_bytes=8 * MIB),
        name="cov_out",
    )(x, *pieces)


def ordered_sum_kernel(where_ref, *refs):
    pieces, (out, slots) = refs[:-2], refs[-2:]
    count = len(pieces)
    for k, piece in enumerate(pieces):
        slots[lax.rem(where_ref[0] + count - k, count)] = piece[...]
    value = slots[0]
    for k in range(1, count):
        value = value + slots[k]
    out[...] = value


def ordered_sum(where, pieces):
    shape = pieces[0].shape
    return pl.pallas_call(
        ordered_sum_kernel,
        in_specs=[smem()] + [vmem()] * len(pieces),
        out_specs=vmem(),
        out_shape=jax.ShapeDtypeStruct(shape, jnp.float32),
        scratch_shapes=[pltpu.VMEM((len(pieces),) + shape, jnp.float32)],
        compiler_params=pltpu.CompilerParams(vmem_limit_bytes=8 * MIB),
        name="ordered_sum",
    )(where, *pieces)


def scales(steps, spread):
    r = (spread - 1.0) / (spread + 1.0)
    out = []
    for _ in range(steps):
        out.append(2.0 / (2.0 - r * r))
        r = r * r / (2.0 - r * r)
    return out


def damped_inverse(pair, tokens):
    size = pair.shape[0]
    whole = block_diagonal(pair / tokens)
    rows = lax.broadcasted_iota(jnp.int32, whole.shape, 0)
    cols = lax.broadcasted_iota(jnp.int32, whole.shape, 1)
    diagonal = rows == cols
    on_diagonal = jnp.where(diagonal, whole, 0.0)
    first = jnp.sum(on_diagonal[:size]) / size
    second = jnp.sum(on_diagonal[size:]) / size
    unit = jnp.where(rows < size, first, second)
    eye = jnp.where(diagonal, 1.0, 0.0)
    matrix = whole / unit + 0.1 * eye
    low, high = 0.1, size + 0.1
    start = 2.0 / (low + high)
    steps = scales(7, high / low)
    y = matrix * start
    x = (2.0 * start * steps[0]) * eye - (start * steps[0]) * y
    y = steps[0] * (2.0 * y - nn(y, y, HIGHEST))
    for scale in steps[1:-1]:
        both = nn(jnp.concatenate([x, y], axis=0), y, HIGHEST)
        x = scale * (2.0 * x - both[: 2 * size])
        y = scale * (2.0 * y - both[2 * size :])
    x = steps[-1] * (2.0 * x - nn(x, y, HIGHEST))
    x = x + nn(x, eye - nn(matrix, x, HIGHEST), HIGHEST)
    return x / unit


def split(value):
    high = value.astype(jnp.bfloat16)
    rest = value - high.astype(jnp.float32)
    middle = rest.astype(jnp.bfloat16)
    low = (rest - middle.astype(jnp.float32)).astype(jnp.bfloat16)
    return high, middle, low


def right_kernel(tokens, *refs):
    pieces, (queries_ref, out) = refs[:-2], refs[-2:]
    inverse = damped_inverse(total(pieces), tokens)
    size = inverse.shape[0] // 2
    count = queries_ref.shape[0]
    parts = jnp.concatenate(split(inverse), axis=0)
    group = 4
    for layer in range(2):
        low = layer * size
        left = jnp.concatenate(
            [
                parts[2 * size * k + low : 2 * size * k + low + size, low : low + size]
                for k in range(3)
            ],
            axis=0,
        )
        for block in range(count // group):
            first = block * group // 2
            places = [first, first + count // 2, first + 1, first + 1 + count // 2]
            rows = jnp.concatenate([queries_ref[place, layer] for place in places], axis=0)
            result = nt(left, rows)
            result = result[:size] + result[size : 2 * size] + result[2 * size :]
            high, middle, _ = split(result)
            lanes = slice(block * group * size, (block + 1) * group * size)
            out[layer, 0, :, lanes] = high
            out[layer, 1, :, lanes] = middle


def right(pieces, queries, tokens):
    count, layers, rank, _ = queries.shape
    return pl.pallas_call(
        functools.partial(right_kernel, tokens),
        in_specs=[vmem()] * (len(pieces) + 1),
        out_specs=vmem(),
        out_shape=jax.ShapeDtypeStruct((layers, 2, rank, count * rank), jnp.bfloat16),
        compiler_params=pltpu.CompilerParams(vmem_limit_bytes=24 * MIB),
        name="right",
    )(*pieces, queries)


def score_kernel(tokens, seqs, where_ref, half_ref, *refs):
    pieces, samples, (out, slots) = refs[: -2 - seqs], refs[-2 - seqs : -2], refs[-2:]
    inverse = damped_inverse(total(pieces), tokens)
    both = inverse.shape[0]
    size = both // 2
    pairs = half_ref.shape[3] // both
    for k, sample in enumerate(samples):
        slots[lax.rem(where_ref[0] + seqs - k, seqs)] = sample[...].astype(jnp.float32)
    left = left_lanes(size, both)
    sums = [[None] * pairs for _ in range(seqs)]
    for layer in range(2):
        block = inverse[layer * size : (layer + 1) * size]
        other = pltpu.roll(block, size, 1)
        if layer == 0:
            twice = jnp.concatenate([block, other], axis=0)
        else:
            twice = jnp.concatenate([other, block], axis=0)
        high, middle, _ = split(twice)
        once = jnp.concatenate([high, middle], axis=1)
        weights = jnp.concatenate([once, once], axis=0)
        doubled = []
        for s in range(seqs):
            sample = slots[s]
            turned = pltpu.roll(sample, size, 1)
            keep = left if layer == 0 else jnp.logical_not(left)
            doubled.append(jnp.where(keep, sample, turned))
        for pair in range(pairs):
            lanes = slice(pair * both, (pair + 1) * both)
            rows = jnp.concatenate([half_ref[layer, 0, :, lanes], half_ref[layer, 1, :, lanes]], axis=1)
            result = nn(rows, weights)
            result = (result[:, :both] + result[:, both:]).astype(jnp.bfloat16).astype(jnp.float32)
            for s in range(seqs):
                product = jnp.sum((result * doubled[s]).reshape(size // 8, 8, both), axis=0)
                sums[s][pair] = product if layer == 0 else sums[s][pair] + product
    lines = []
    for s in range(seqs):
        for pair in range(pairs):
            lines.append(jnp.sum(sums[s][pair], axis=0, keepdims=True))
    lines = jnp.concatenate(lines, axis=0)
    ends = jnp.where(
        (lax.broadcasted_iota(jnp.int32, (8, both), 1) < size)
        == (lax.broadcasted_iota(jnp.int32, (8, both), 0) == 0),
        1.0,
        0.0,
    )
    result = nt(ends, lines, HIGHEST)
    for s in range(seqs):
        for side in range(2):
            out[s : s + 1, side * pairs : (side + 1) * pairs] = result[
                side : side + 1, s * pairs : (s + 1) * pairs
            ]


def score(where, half, pieces, samples, tokens, queries):
    rank = half.shape[2]
    seqs = len(samples)
    return pl.pallas_call(
        functools.partial(score_kernel, tokens, seqs),
        in_specs=[smem()] + [vmem()] * (1 + len(pieces) + seqs),
        out_specs=vmem(),
        out_shape=jax.ShapeDtypeStruct((seqs, queries), jnp.float32),
        scratch_shapes=[pltpu.VMEM((seqs, rank, 2 * rank), jnp.float32)],
        compiler_params=pltpu.CompilerParams(vmem_limit_bytes=24 * MIB),
        name="score",
    )(where, half, *pieces, *samples)


def shift(value, axis, by):
    size = lax.axis_size(axis)
    return lax.ppermute(value, axis, [(i, (i + by) % size) for i in range(size)])


def everyone(value, axis):
    return [value] + [shift(value, axis, k) for k in range(1, lax.axis_size(axis))]


def scatter(pieces, axis):
    return [pieces[0]] + [shift(piece, axis, k) for k, piece in enumerate(pieces) if k > 0]


def local_owned(acts, grads, proj_in, proj_out, queries):
    seqs, length, _ = acts.shape
    tokens = seqs * length * lax.axis_size("dp")
    where = lax.axis_index("tensor").astype(jnp.int32).reshape(1)
    all_queries = lax.all_gather(queries, "dp", axis=0, tiled=True)
    x_pieces = scatter(project_in(where, acts, proj_in), "tensor")
    g_pieces = scatter(project_out(where, grads, proj_out), "tensor")
    x, in_part = cov_in(x_pieces)
    in_sum = ordered_sum(where, everyone(in_part, "tensor"))
    half = right(everyone(in_sum, "dp"), all_queries, tokens)
    out_part, sample = cov_out(x, g_pieces)
    out_sum = ordered_sum(where, everyone(out_part, "tensor"))
    return score(
        where,
        half,
        everyone(out_sum, "dp"),
        everyone(sample, "tensor"),
        tokens,
        all_queries.shape[0],
    )


def damp(matrix):
    size = matrix.shape[0]
    shift_by = 0.1 * jnp.trace(matrix) / size
    return matrix + shift_by * jnp.eye(size, dtype=matrix.dtype)


def chol_apply(factor, rhs):
    lower_sol = lax.linalg.triangular_solve(factor, rhs, left_side=True, lower=True)
    return lax.linalg.triangular_solve(
        factor, lower_sol, left_side=True, lower=True, transpose_a=True
    )


def precondition(query, left, right_side):
    count, rank = (query.shape[0], query.shape[1])
    left_fac = jnp.linalg.cholesky(left)
    right_fac = jnp.linalg.cholesky(right_side)
    stacked = jnp.transpose(query, (1, 0, 2)).reshape(rank, count * rank)
    middle = chol_apply(left_fac, stacked).reshape(rank, count, rank)
    turned = jnp.transpose(middle, (2, 1, 0)).reshape(rank, count * rank)
    result = chol_apply(right_fac, turned).reshape(rank, count, rank)
    return jnp.transpose(result, (1, 2, 0))


def diagonal_blocks(whole, rank):
    return jnp.stack([whole[:, 0:rank, 0:rank], whole[:, rank : 2 * rank, rank : 2 * rank]], axis=1)


def local_general(acts, grads, proj_in, proj_out, queries):
    seq_count, length, width_loc = acts.shape
    rank = proj_in.shape[1]
    hidden_loc = grads.shape[3]
    flat = acts.reshape(-1, width_loc)
    xpart = nt(flat, proj_in.reshape(2 * rank, width_loc))
    gpart = jnp.concatenate(
        [nt(grads[layer].reshape(-1, hidden_loc), proj_out[layer]) for layer in range(2)], axis=1
    )
    count = seq_count * length * lax.axis_size("dp")
    xin, gout = lax.psum((xpart, gpart), "tensor")
    in_cov, out_cov = lax.psum((tn(xin, xin, HIGHEST), tn(gout, gout, HIGHEST)), "dp")
    whole = (
        jnp.einsum(
            "sto,sti->soi",
            gout.reshape(seq_count, length, 2 * rank),
            xin.reshape(seq_count, length, 2 * rank),
            precision=HIGHEST,
        )
        / length
    )
    samples = diagonal_blocks(whole, rank)
    in_cov = in_cov / count
    out_cov = out_cov / count
    precond = []
    for layer in range(2):
        low = layer * rank
        damped_in = damp(in_cov[low : low + rank, low : low + rank])
        damped_out = damp(out_cov[low : low + rank, low : low + rank])
        precond.append(precondition(queries[:, layer].astype(jnp.float32), damped_out, damped_in))
    query_count = queries.shape[0]
    query_b = jnp.stack(precond, axis=1).astype(jnp.bfloat16).reshape(query_count, -1)
    sample_b = samples.astype(jnp.bfloat16).reshape(seq_count, -1)
    return nt(sample_b, lax.all_gather(query_b, "dp", axis=0, tiled=True))


def local(acts, grads, proj_in, proj_out, queries):
    if acts.shape[0] == lax.axis_size("tensor"):
        return local_owned(acts, grads, proj_in, proj_out, queries)
    return local_general(acts, grads, proj_in, proj_out, queries)


def solution(mesh):
    placed = (
        P(("groups", "dp"), None, "tensor"),
        P(None, ("groups", "dp"), None, "tensor"),
        P(None, None, "tensor"),
        P(None, None, "tensor"),
        P("dp", None, None, None),
    )
    return jax.shard_map(
        local, mesh=mesh, in_specs=placed, out_specs=P(("groups", "dp"), None), check_vma=False
    )
```

time: 210 us -> 87.7 us (0.42)
  waiting for transfers between devices: 101 us -> 9.41 us
  other arithmetic: 52 us -> 0 us
  Pallas kernels: 0 us -> 30.1 us
  starting transfers between devices: 0.27 us -> 28.8 us
  matrix products: 25.1 us -> 0 us
  local copies, waits for them, and re-layouts: 15.9 us -> 4.82 us
  between operations: 16.1 us -> 13.5 us
    psum x2 -> x0, waiting for transfers between devices: 84.8 us -> none  [the longest x1 55 us: local(): xin, gout = lax.psum((xpart, gpart), 'tensor')]
    another operation x22 -> x0, other arithmetic: 48.4 us -> none  [the longest x8 22.2 us: chol_apply(): lax.linalg.triangular_solve(factor, lower_sol, left_side=True, lower=True...]
    pallas_call x0 -> x8, Pallas kernels: none -> 30.1 us  [the longest x1 18.1 us: project_out(): pl.pallas_call(project_out_kernel, grid=(width // block,), in_specs=[smem...]
    ppermute x0 -> x21, starting transfers between devices: none -> 28.8 us  [shift(): lax.ppermute(value, axis, [(i, (i + by) % size) for i in range(size)])]
    dot_general x7 -> x0, matrix products: 22 us -> none  [the longest x1 5.93 us: local(): jnp.einsum('tf,rf->tr', grads[1].reshape(-1, hidden_loc), proj_out[1], pr...]
    all_gather x1, waiting for transfers between devices: 15.9 us -> 0.01 us  [local_owned(): all_queries = lax.all_gather(queries, 'dp', axis=0, tiled=True)]
    slice x1 -> x0, local copies, waits for them, and re-layouts: 11.5 us -> none  [local(): grads[0].reshape(-1, hidden_loc)]
    ppermute x0 -> x21, waiting for transfers between devices: none -> 8.7 us  [shift(): lax.ppermute(value, axis, [(i, (i + by) % size) for i in range(size)])]
  transfers between devices with their start and end apart: 3 -> 22, of which waited for: 3 -> 5; matrix products, arithmetic and copies ran while one was open for 1% -> 0% of each run, Pallas kernels for 0% -> 29%
where the time goes in v1:
time: 87.7 us; the launch traced here: 86.7 us
  Pallas kernels  30.1 us (34%)
  starting transfers between devices  28.8 us (33%)
  between operations  13.5 us (15%)
  waiting for transfers between devices  9.41 us (11%)
  local copies, waits for them, and re-layouts  4.82 us (5%)
    ppermute x21, starting transfers between devices, shift(): lax.ppermute(value, axis, [(i, (i + by) % size) for i in range(size)])  28.8 us
    pallas_call x1, Pallas kernels, project_out(): pl.pallas_call(project_out_kernel, grid=(width // block,), in_specs=[smem...  18.1 us
    ppermute x21, waiting for transfers between devices, shift(): lax.ppermute(value, axis, [(i, (i + by) % size) for i in range(size)])  8.7 us
    pallas_call x1, Pallas kernels, score(): pl.pallas_call(functools.partial(score_kernel, tokens, seqs), in_specs=[s...  5.26 us
    unnamed x8, local copies, waits for them, and re-layouts  4.82 us
    pallas_call x1, Pallas kernels, right(): pl.pallas_call(functools.partial(right_kernel, tokens), in_specs=[vmem()]...  3.58 us
    pallas_call x1, Pallas kernels, project_in(): pl.pallas_call(project_in_kernel, grid=(width // block,), in_specs=[smem(...  2.37 us
  transfers between devices with their start and end apart: 22, of which 5 were waited for; matrix products, arithmetic and copies ran while one was open for 0% of the time, Pallas kernels for 29%

profile of v1, /device:TPU:0, one launch (start us, length us, event | category | flops | bytes accessed | tf_op | source)
XLA Modules:
  0.0 86.7 jit_solution(12441448995541124902)
XLA Ops:
  6.5 0.7 all-gather.2.cloned.1.call-update
  7.3 2.2 %copy-done = bf16[4,256,2048]{2,1,0:T(8,128)(2,1)S(1)} copy-done((bf16[4,256,2048]{2,1,0:T(8,128)(2,1)S(1)}, bf16[4,256,2048]{2,1,0:T(8,128)(2,1)}, u32[]{:S(2)}) %copy-start) | copy-done | bytes 4194328
  9.5 1.0 %copy-done.3 = bf16[2,64,2048]{2,1,0:T(8,128)(2,1)S(1)} copy-done((bf16[2,64,2048]{2,1,0:T(8,128)(2,1)S(1)}, bf16[2,64,2048]{2,1,0:T(8,128)(2,1)}, u32[]{:S(2)}) %copy-start.3) | copy-done | bytes 524312
  10.5 2.4 %project_in.1 = (f32[256,128]{1,0:T(8,128)S(1)}, f32[256,128]{1,0:T(8,128)S(1)}, f32[256,128]{1,0:T(8,128)S(1)}, f32[256,128]{1,0:T(8,128)S(1)}) custom-call(s32[1]{0:T(128)} %bitcast.where_ref, bf16[4,256,2048]{2,1,0:T(8,128)(2,1)S(1)} %copy-done, bf16[2,64,2048]{2,1,0:T(8,128)(2,1)S(1)} %copy-done.3), custom_call_target="tpu_custom_call" | custom-call | tf_op jit(solution)/shard_map/project_in/pallas_call | solution.py:94
  12.9 3.1 %collective-permute-start = (f32[256,128]{1,0:T(8,128)S(1)}, f32[256,128]{1,0:T(8,128)S(1)}, u32[]{:S(2)}, u32[]{:S(2)}) collective-permute-start(f32[256,128]{1,0:T(8,128)S(1)} %get-tuple-element.18), channel_id=1, source_target_pairs={{0,4},{4,8},{8,12},{12,0},{1,5},{5,9},{9,13},{13,1},{2,6},{6,10},{... | collective-permute-start | bytes 393224 | tf_op jit(solution)/shard_map/ppermute | solution.py:375
  15.9 2.6 %collective-permute-start.1 = (f32[256,128]{1,0:T(8,128)S(1)}, f32[256,128]{1,0:T(8,128)S(1)}, u32[]{:S(2)}, u32[]{:S(2)}) collective-permute-start(f32[256,128]{1,0:T(8,128)S(1)} %get-tuple-element.19), channel_id=1, source_target_pairs={{0,8},{4,12},{8,0},{12,4},{1,9},{5,13},{9,1},{13,5},{2,10},{6,14},... | collective-permute-start | bytes 393224 | tf_op jit(solution)/shard_map/ppermute | solution.py:375
  18.5 1.3 %collective-permute-start.2 = (f32[256,128]{1,0:T(8,128)S(1)}, f32[256,128]{1,0:T(8,128)S(1)}, u32[]{:S(2)}, u32[]{:S(2)}) collective-permute-start(f32[256,128]{1,0:T(8,128)S(1)} %get-tuple-element.20), channel_id=1, source_target_pairs={{0,12},{4,0},{8,4},{12,8},{1,13},{5,1},{9,5},{13,9},{2,14},{6,2},{... | collective-permute-start | bytes 393224 | tf_op jit(solution)/shard_map/ppermute | solution.py:375
  19.9 18.1 %project_out.1 = (f32[256,128]{1,0:T(8,128)S(1)}, f32[256,128]{1,0:T(8,128)S(1)}, f32[256,128]{1,0:T(8,128)S(1)}, f32[256,128]{1,0:T(8,128)S(1)}) custom-call(s32[1]{0:T(128)} %bitcast.where_ref, bf16[2,4,256,7168]{3,2,1,0:T(8,128)(2,1)} %grads_ref.1, bf16[2,64,7168]{2,1,0:T(8,128)(2,1)S(1)} %copy-done.2), custom_call_target="tpu_custom_call" | custom-call | tf_op jit(solution)/shard_map/project_out/pallas_call | solution.py:114
  38.0 1.1 %collective-permute-start.9 = (f32[256,128]{1,0:T(8,128)S(1)}, f32[256,128]{1,0:T(8,128)S(1)}, u32[]{:S(2)}, u32[]{:S(2)}) collective-permute-start(f32[256,128]{1,0:T(8,128)S(1)} %get-tuple-element.24), channel_id=1, source_target_pairs={{0,4},{4,8},{8,12},{12,0},{1,5},{5,9},{9,13},{13,1},{2,6},{6,10},{... | collective-permute-start | bytes 393224 | tf_op jit(solution)/shard_map/ppermute | solution.py:375
  39.1 0.2 collective-permute-start.10
  39.3 0.0 collective-permute-done.refs_1_
  39.3 2.6 %collective-permute-start.11 = (f32[256,128]{1,0:T(8,128)S(1)}, f32[256,128]{1,0:T(8,128)S(1)}, u32[]{:S(2)}, u32[]{:S(2)}) collective-permute-start(f32[256,128]{1,0:T(8,128)S(1)} %get-tuple-element.26), channel_id=1, source_target_pairs={{0,12},{4,0},{8,4},{12,8},{1,13},{5,1},{9,5},{13,9},{2,14},{6,2},{... | collective-permute-start | bytes 393224 | tf_op jit(solution)/shard_map/ppermute | solution.py:375
  41.9 0.0 collective-permute-done.1.refs_2_
  41.9 0.0 collective-permute-done.2.refs_3_
  41.9 0.3 cov_in.1
  42.2 1.6 %collective-permute-start.5 = (f32[64,128]{1,0:T(8,128)S(1)}, f32[64,128]{1,0:T(8,128)S(1)}, u32[]{:S(2)}, u32[]{:S(2)}) collective-permute-start(f32[64,128]{1,0:T(8,128)S(1)} %get-tuple-element.21.refs_0_), channel_id=1, source_target_pairs={{0,12},{4,0},{8,4},{12,8},{1,13},{5,1},{9,5},{13,9},{2,14},{6,2},{... | collective-permute-start | bytes 98312 | tf_op jit(solution)/shard_map/ppermute | solution.py:375
  43.9 0.5 collective-permute-start.4
  44.4 2.0 %collective-permute-done.9.refs_1_ = f32[256,128]{1,0:T(8,128)S(1)} collective-permute-done((f32[256,128]{1,0:T(8,128)S(1)}, f32[256,128]{1,0:T(8,128)S(1)}, u32[]{:S(2)}, u32[]{:S(2)}) %collective-permute-start.9) | collective-permute-done | bytes 131104 | tf_op jit(solution)/shard_map/ppermute | solution.py:375
  46.3 0.0 collective-permute-start.3
  46.4 4.7 %collective-permute-done.10.refs_2_ = f32[256,128]{1,0:T(8,128)S(1)} collective-permute-done((f32[256,128]{1,0:T(8,128)S(1)}, f32[256,128]{1,0:T(8,128)S(1)}, u32[]{:S(2)}, u32[]{:S(2)}) %collective-permute-start.10) | collective-permute-done | bytes 131104 | tf_op jit(solution)/shard_map/ppermute | solution.py:375
  51.1 0.0 collective-permute-done.11.refs_3_
  51.1 0.4 cov_out.1
  51.5 3.7 %collective-permute-start.14 = (f32[64,128]{1,0:T(8,128)S(1)}, f32[64,128]{1,0:T(8,128)S(1)}, u32[]{:S(2)}, u32[]{:S(2)}) collective-permute-start(f32[64,128]{1,0:T(8,128)S(1)} %get-tuple-element.27.refs_0_), channel_id=1, source_target_pairs={{0,12},{4,0},{8,4},{12,8},{1,13},{5,1},{9,5},{13,9},{2,14},{6,2},{... | collective-permute-start | bytes 98312 | tf_op jit(solution)/shard_map/ppermute | solution.py:375
  55.3 1.8 %collective-permute-start.13 = (f32[64,128]{1,0:T(8,128)S(1)}, f32[64,128]{1,0:T(8,128)S(1)}, u32[]{:S(2)}, u32[]{:S(2)}) collective-permute-start(f32[64,128]{1,0:T(8,128)S(1)} %get-tuple-element.27.refs_0_), channel_id=1, source_target_pairs={{0,8},{4,12},{8,0},{12,4},{1,9},{5,13},{9,1},{13,5},{2,10},{6,14},... | collective-permute-start | bytes 98312 | tf_op jit(solution)/shard_map/ppermute | solution.py:375
  57.0 0.0 collective-permute-done.5.refs_3_
  57.0 0.0 collective-permute-start.12
  57.0 0.0 collective-permute-done.4.refs_2_
  57.0 0.0 collective-permute-done.3.refs_1_
  57.1 0.1 collective-permute-start.8
  57.2 1.5 %collective-permute-start.7 = (f32[64,128]{1,0:T(8,128)S(1)}, f32[64,128]{1,0:T(8,128)S(1)}, u32[]{:S(2)}, u32[]{:S(2)}) collective-permute-start(f32[64,128]{1,0:T(8,128)S(1)} %ordered_sum.2.refs_0_), channel_id=1, source_target_pairs={{0,2},{1,3},{2,0},{3,1},{4,6},{5,7},{6,4},{7,5},{8,10},{9,11},{10,... | collective-permute-start | bytes 98312 | tf_op jit(solution)/shard_map/ppermute | solution.py:375
  58.7 0.0 collective-permute-done.14.refs_3_
  58.7 0.2 collective-permute-start.6
  58.9 1.7 %collective-permute-done.13.refs_2_ = f32[64,128]{1,0:T(8,128)S(1)} collective-permute-done((f32[64,128]{1,0:T(8,128)S(1)}, f32[64,128]{1,0:T(8,128)S(1)}, u32[]{:S(2)}, u32[]{:S(2)}) %collective-permute-start.13) | collective-permute-done | bytes 32800 | tf_op jit(solution)/shard_map/ppermute | solution.py:375
  60.5 2.1 %collective-permute-start.20 = (bf16[64,128]{1,0:T(8,128)(2,1)S(1)}, bf16[64,128]{1,0:T(8,128)(2,1)S(1)}, u32[]{:S(2)}, u32[]{:S(2)}) collective-permute-start(bf16[64,128]{1,0:T(8,128)(2,1)S(1)} %get-tuple-element.28.refs_4_), channel_id=1, source_target_pairs={{0,12},{4,0},{8,4},{12,8},{1,13},{5,1},{9,5},{13,9},{2,14},{6,2},{... | collective-permute-start | bytes 49160 | tf_op jit(solution)/shard_map/ppermute | solution.py:375
  62.7 0.1 collective-permute-done.12.refs_1_
  62.8 1.3 %collective-permute-start.17 = (f32[64,128]{1,0:T(8,128)S(1)}, f32[64,128]{1,0:T(8,128)S(1)}, u32[]{:S(2)}, u32[]{:S(2)}) collective-permute-start(f32[64,128]{1,0:T(8,128)S(1)} %ordered_sum.3.refs_0_), channel_id=1, source_target_pairs={{0,3},{1,0},{2,1},{3,2},{4,7},{5,4},{6,5},{7,6},{8,11},{9,8},{10,9... | collective-permute-start | bytes 98312 | tf_op jit(solution)/shard_map/ppermute | solution.py:375
  64.1 0.2 collective-permute-done.20.refs_7_
  64.3 1.5 %collective-permute-start.16 = (f32[64,128]{1,0:T(8,128)S(1)}, f32[64,128]{1,0:T(8,128)S(1)}, u32[]{:S(2)}, u32[]{:S(2)}) collective-permute-start(f32[64,128]{1,0:T(8,128)S(1)} %ordered_sum.3.refs_0_), channel_id=1, source_target_pairs={{0,2},{1,3},{2,0},{3,1},{4,6},{5,7},{6,4},{7,5},{8,10},{9,11},{10,... | collective-permute-start | bytes 98312 | tf_op jit(solution)/shard_map/ppermute | solution.py:375
  65.8 0.0 collective-permute-done.8.refs_3_
  65.8 0.0 collective-permute-start.15
  65.8 0.0 collective-permute-done.7.refs_2_
  65.8 1.3 %collective-permute-start.19 = (bf16[64,128]{1,0:T(8,128)(2,1)S(1)}, bf16[64,128]{1,0:T(8,128)(2,1)S(1)}, u32[]{:S(2)}, u32[]{:S(2)}) collective-permute-start(bf16[64,128]{1,0:T(8,128)(2,1)S(1)} %get-tuple-element.28.refs_4_), channel_id=1, source_target_pairs={{0,8},{4,12},{8,0},{12,4},{1,9},{5,13},{9,1},{13,5},{2,10},{6,14},... | collective-permute-start | bytes 49160 | tf_op jit(solution)/shard_map/ppermute | solution.py:375
  67.1 2.3 %collective-permute-start.18 = (bf16[64,128]{1,0:T(8,128)(2,1)S(1)}, bf16[64,128]{1,0:T(8,128)(2,1)S(1)}, u32[]{:S(2)}, u32[]{:S(2)}) collective-permute-start(bf16[64,128]{1,0:T(8,128)(2,1)S(1)} %get-tuple-element.28.refs_4_), channel_id=1, source_target_pairs={{0,4},{4,8},{8,12},{12,0},{1,5},{5,9},{9,13},{13,1},{2,6},{6,10},{... | collective-permute-start | bytes 49160 | tf_op jit(solution)/shard_map/ppermute | solution.py:375
  69.4 1.6 %copy-done.1 = bf16[64,2,64,64]{3,2,1,0:T(8,128)(2,1)S(1)} copy-done((bf16[64,2,64,64]{3,2,1,0:T(8,128)(2,1)S(1)}, bf16[64,2,64,64]{3,2,1,0:T(8,128)(2,1)}, u32[]{:S(2)}) %copy-start.1) | copy-done | bytes 1048600
  71.0 3.6 %right.1.half_ref = bf16[2,2,64,4096]{3,2,1,0:T(8,128)(2,1)S(1)} custom-call(f32[64,128]{1,0:T(8,128)S(1)} %ordered_sum.2.refs_0_, f32[64,128]{1,0:T(8,128)S(1)} %collective-permute-done.6.refs_1_, f32[64,128]{1,0:T(8,128)S(1)} %collective-permute-done.7.refs_2_, f32[64,128]{1,0:T(8,128)S(1)} %collective-permute-done.8.refs_3_, ...), custom_call_target="tpu_custom_call" | custom-call | tf_op jit(solution)/shard_map/right/pallas_call | solution.py:296
  74.6 0.0 collective-permute-done.18.refs_5_
  74.6 0.0 collective-permute-done.17.refs_3_
  74.6 5.3 %score.1 = f32[4,64]{1,0:T(4,128)} custom-call(s32[1]{0:T(128)} %bitcast.where_ref, bf16[2,2,64,4096]{3,2,1,0:T(8,128)(2,1)S(1)} %right.1.half_ref, f32[64,128]{1,0:T(8,128)S(1)} %ordered_sum.3.refs_0_, f32[64,128]{1,0:T(8,128)S(1)} %collective-permute-done.15.refs_1_, f32[64,128]{1,0:T(8,128)S(1)} %collective-permute-done.16.refs_2_, ...), custom_call_target="tpu_custom_call" | custom-call | tf_op jit(solution)/shard_map/score/pallas_call | solution.py:362
  (13 shorter events, 0.1 us)
Async XLA Ops:
  6.5 62.9 %all-gather.2.cloned.1.call-start = ((), (), s32[]{:S(2)}) async-start(), calls=%async_computation | async-start | bytes 2621440 | tf_op jit(solution)/shard_map/all_gather | solution.py:390
  7.3 2.2 %copy-start = (bf16[4,256,2048]{2,1,0:T(8,128)(2,1)S(1)}, bf16[4,256,2048]{2,1,0:T(8,128)(2,1)}, u32[]{:S(2)}) copy-start(bf16[4,256,2048]{2,1,0:T(8,128)(2,1)} %acts_ref.1) | copy-start | bytes 12582916
  9.4 1.0 %copy-start.3 = (bf16[2,64,2048]{2,1,0:T(8,128)(2,1)S(1)}, bf16[2,64,2048]{2,1,0:T(8,128)(2,1)}, u32[]{:S(2)}) copy-start(bf16[2,64,2048]{2,1,0:T(8,128)(2,1)} %proj_ref.2) | copy-start | bytes 1572868
  10.5 9.4 %copy-start.2 = (bf16[2,64,7168]{2,1,0:T(8,128)(2,1)S(1)}, bf16[2,64,7168]{2,1,0:T(8,128)(2,1)}, u32[]{:S(2)}) copy-start(bf16[2,64,7168]{2,1,0:T(8,128)(2,1)} %proj_ref.3) | copy-start | bytes 5505028
  12.9 26.4 %collective-permute-start = (f32[256,128]{1,0:T(8,128)S(1)}, f32[256,128]{1,0:T(8,128)S(1)}, u32[]{:S(2)}, u32[]{:S(2)}) collective-permute-start(f32[256,128]{1,0:T(8,128)S(1)} %get-tuple-element.18), channel_id=1, source_target_pairs={{0,4},{4,8},{8,12},{12,0},{1,5},{5,9},{9,13},{13,1},{2,6},{6,10},{... | collective-permute-start | bytes 393224 | tf_op jit(solution)/shard_map/ppermute | solution.py:375
  15.9 26.0 %collective-permute-start.1 = (f32[256,128]{1,0:T(8,128)S(1)}, f32[256,128]{1,0:T(8,128)S(1)}, u32[]{:S(2)}, u32[]{:S(2)}) collective-permute-start(f32[256,128]{1,0:T(8,128)S(1)} %get-tuple-element.19), channel_id=1, source_target_pairs={{0,8},{4,12},{8,0},{12,4},{1,9},{5,13},{9,1},{13,5},{2,10},{6,14},... | collective-permute-start | bytes 393224 | tf_op jit(solution)/shard_map/ppermute | solution.py:375
  18.5 23.4 %collective-permute-start.2 = (f32[256,128]{1,0:T(8,128)S(1)}, f32[256,128]{1,0:T(8,128)S(1)}, u32[]{:S(2)}, u32[]{:S(2)}) collective-permute-start(f32[256,128]{1,0:T(8,128)S(1)} %get-tuple-element.20), channel_id=1, source_target_pairs={{0,12},{4,0},{8,4},{12,8},{1,13},{5,1},{9,5},{13,9},{2,14},{6,2},{... | collective-permute-start | bytes 393224 | tf_op jit(solution)/shard_map/ppermute | solution.py:375
  38.0 8.3 %collective-permute-start.9 = (f32[256,128]{1,0:T(8,128)S(1)}, f32[256,128]{1,0:T(8,128)S(1)}, u32[]{:S(2)}, u32[]{:S(2)}) collective-permute-start(f32[256,128]{1,0:T(8,128)S(1)} %get-tuple-element.24), channel_id=1, source_target_pairs={{0,4},{4,8},{8,12},{12,0},{1,5},{5,9},{9,13},{13,1},{2,6},{6,10},{... | collective-permute-start | bytes 393224 | tf_op jit(solution)/shard_map/ppermute | solution.py:375
  39.1 12.0 %collective-permute-start.10 = (f32[256,128]{1,0:T(8,128)S(1)}, f32[256,128]{1,0:T(8,128)S(1)}, u32[]{:S(2)}, u32[]{:S(2)}) collective-permute-start(f32[256,128]{1,0:T(8,128)S(1)} %get-tuple-element.25), channel_id=1, source_target_pairs={{0,8},{4,12},{8,0},{12,4},{1,9},{5,13},{9,1},{13,5},{2,10},{6,14},... | collective-permute-start | bytes 393224 | tf_op jit(solution)/shard_map/ppermute | solution.py:375
  39.3 11.8 %collective-permute-start.11 = (f32[256,128]{1,0:T(8,128)S(1)}, f32[256,128]{1,0:T(8,128)S(1)}, u32[]{:S(2)}, u32[]{:S(2)}) collective-permute-start(f32[256,128]{1,0:T(8,128)S(1)} %get-tuple-element.26), channel_id=1, source_target_pairs={{0,12},{4,0},{8,4},{12,8},{1,13},{5,1},{9,5},{13,9},{2,14},{6,2},{... | collective-permute-start | bytes 393224 | tf_op jit(solution)/shard_map/ppermute | solution.py:375
  42.2 14.8 %collective-permute-start.5 = (f32[64,128]{1,0:T(8,128)S(1)}, f32[64,128]{1,0:T(8,128)S(1)}, u32[]{:S(2)}, u32[]{:S(2)}) collective-permute-start(f32[64,128]{1,0:T(8,128)S(1)} %get-tuple-element.21.refs_0_), channel_id=1, source_target_pairs={{0,12},{4,0},{8,4},{12,8},{1,13},{5,1},{9,5},{13,9},{2,14},{6,2},{... | collective-permute-start | bytes 98312 | tf_op jit(solution)/shard_map/ppermute | solution.py:375
  43.9 13.2 %collective-permute-start.4 = (f32[64,128]{1,0:T(8,128)S(1)}, f32[64,128]{1,0:T(8,128)S(1)}, u32[]{:S(2)}, u32[]{:S(2)}) collective-permute-start(f32[64,128]{1,0:T(8,128)S(1)} %get-tuple-element.21.refs_0_), channel_id=1, source_target_pairs={{0,8},{4,12},{8,0},{12,4},{1,9},{5,13},{9,1},{13,5},{2,10},{6,14},... | collective-permute-start | bytes 98312 | tf_op jit(solution)/shard_map/ppermute | solution.py:375
  46.3 10.7 %collective-permute-start.3 = (f32[64,128]{1,0:T(8,128)S(1)}, f32[64,128]{1,0:T(8,128)S(1)}, u32[]{:S(2)}, u32[]{:S(2)}) collective-permute-start(f32[64,128]{1,0:T(8,128)S(1)} %get-tuple-element.21.refs_0_), channel_id=1, source_target_pairs={{0,4},{4,8},{8,12},{12,0},{1,5},{5,9},{9,13},{13,1},{2,6},{6,10},{... | collective-permute-start | bytes 98312 | tf_op jit(solution)/shard_map/ppermute | solution.py:375
  51.5 7.2 %collective-permute-start.14 = (f32[64,128]{1,0:T(8,128)S(1)}, f32[64,128]{1,0:T(8,128)S(1)}, u32[]{:S(2)}, u32[]{:S(2)}) collective-permute-start(f32[64,128]{1,0:T(8,128)S(1)} %get-tuple-element.27.refs_0_), channel_id=1, source_target_pairs={{0,12},{4,0},{8,4},{12,8},{1,13},{5,1},{9,5},{13,9},{2,14},{6,2},{... | collective-permute-start | bytes 98312 | tf_op jit(solution)/shard_map/ppermute | solution.py:375
  55.3 5.3 %collective-permute-start.13 = (f32[64,128]{1,0:T(8,128)S(1)}, f32[64,128]{1,0:T(8,128)S(1)}, u32[]{:S(2)}, u32[]{:S(2)}) collective-permute-start(f32[64,128]{1,0:T(8,128)S(1)} %get-tuple-element.27.refs_0_), channel_id=1, source_target_pairs={{0,8},{4,12},{8,0},{12,4},{1,9},{5,13},{9,1},{13,5},{2,10},{6,14},... | collective-permute-start | bytes 98312 | tf_op jit(solution)/shard_map/ppermute | solution.py:375
  57.0 5.7 %collective-permute-start.12 = (f32[64,128]{1,0:T(8,128)S(1)}, f32[64,128]{1,0:T(8,128)S(1)}, u32[]{:S(2)}, u32[]{:S(2)}) collective-permute-start(f32[64,128]{1,0:T(8,128)S(1)} %get-tuple-element.27.refs_0_), channel_id=1, source_target_pairs={{0,4},{4,8},{8,12},{12,0},{1,5},{5,9},{9,13},{13,1},{2,6},{6,10},{... | collective-permute-start | bytes 98312 | tf_op jit(solution)/shard_map/ppermute | solution.py:375
  57.1 8.7 %collective-permute-start.8 = (f32[64,128]{1,0:T(8,128)S(1)}, f32[64,128]{1,0:T(8,128)S(1)}, u32[]{:S(2)}, u32[]{:S(2)}) collective-permute-start(f32[64,128]{1,0:T(8,128)S(1)} %ordered_sum.2.refs_0_), channel_id=1, source_target_pairs={{0,3},{1,0},{2,1},{3,2},{4,7},{5,4},{6,5},{7,6},{8,11},{9,8},{10,9... | collective-permute-start | bytes 98312 | tf_op jit(solution)/shard_map/ppermute | solution.py:375
  57.2 8.7 %collective-permute-start.7 = (f32[64,128]{1,0:T(8,128)S(1)}, f32[64,128]{1,0:T(8,128)S(1)}, u32[]{:S(2)}, u32[]{:S(2)}) collective-permute-start(f32[64,128]{1,0:T(8,128)S(1)} %ordered_sum.2.refs_0_), channel_id=1, source_target_pairs={{0,2},{1,3},{2,0},{3,1},{4,6},{5,7},{6,4},{7,5},{8,10},{9,11},{10,... | collective-permute-start | bytes 98312 | tf_op jit(solution)/shard_map/ppermute | solution.py:375
  58.7 8.4 %collective-permute-start.6 = (f32[64,128]{1,0:T(8,128)S(1)}, f32[64,128]{1,0:T(8,128)S(1)}, u32[]{:S(2)}, u32[]{:S(2)}) collective-permute-start(f32[64,128]{1,0:T(8,128)S(1)} %ordered_sum.2.refs_0_), channel_id=1, source_target_pairs={{0,1},{1,2},{2,3},{3,0},{4,5},{5,6},{6,7},{7,4},{8,9},{9,10},{10,1... | collective-permute-start | bytes 98312 | tf_op jit(solution)/shard_map/ppermute | solution.py:375
  60.5 3.7 %collective-permute-start.20 = (bf16[64,128]{1,0:T(8,128)(2,1)S(1)}, bf16[64,128]{1,0:T(8,128)(2,1)S(1)}, u32[]{:S(2)}, u32[]{:S(2)}) collective-permute-start(bf16[64,128]{1,0:T(8,128)(2,1)S(1)} %get-tuple-element.28.refs_4_), channel_id=1, source_target_pairs={{0,12},{4,0},{8,4},{12,8},{1,13},{5,1},{9,5},{13,9},{2,14},{6,2},{... | collective-permute-start | bytes 49160 | tf_op jit(solution)/shard_map/ppermute | solution.py:375
  62.8 11.8 %collective-permute-start.17 = (f32[64,128]{1,0:T(8,128)S(1)}, f32[64,128]{1,0:T(8,128)S(1)}, u32[]{:S(2)}, u32[]{:S(2)}) collective-permute-start(f32[64,128]{1,0:T(8,128)S(1)} %ordered_sum.3.refs_0_), channel_id=1, source_target_pairs={{0,3},{1,0},{2,1},{3,2},{4,7},{5,4},{6,5},{7,6},{8,11},{9,8},{10,9... | collective-permute-start | bytes 98312 | tf_op jit(solution)/shard_map/ppermute | solution.py:375
  64.3 10.3 %collective-permute-start.16 = (f32[64,128]{1,0:T(8,128)S(1)}, f32[64,128]{1,0:T(8,128)S(1)}, u32[]{:S(2)}, u32[]{:S(2)}) collective-permute-start(f32[64,128]{1,0:T(8,128)S(1)} %ordered_sum.3.refs_0_), channel_id=1, source_target_pairs={{0,2},{1,3},{2,0},{3,1},{4,6},{5,7},{6,4},{7,5},{8,10},{9,11},{10,... | collective-permute-start | bytes 98312 | tf_op jit(solution)/shard_map/ppermute | solution.py:375
  65.8 8.8 %collective-permute-start.15 = (f32[64,128]{1,0:T(8,128)S(1)}, f32[64,128]{1,0:T(8,128)S(1)}, u32[]{:S(2)}, u32[]{:S(2)}) collective-permute-start(f32[64,128]{1,0:T(8,128)S(1)} %ordered_sum.3.refs_0_), channel_id=1, source_target_pairs={{0,1},{1,2},{2,3},{3,0},{4,5},{5,6},{6,7},{7,4},{8,9},{9,10},{10,1... | collective-permute-start | bytes 98312 | tf_op jit(solution)/shard_map/ppermute | solution.py:375
  65.8 8.8 %collective-permute-start.19 = (bf16[64,128]{1,0:T(8,128)(2,1)S(1)}, bf16[64,128]{1,0:T(8,128)(2,1)S(1)}, u32[]{:S(2)}, u32[]{:S(2)}) collective-permute-start(bf16[64,128]{1,0:T(8,128)(2,1)S(1)} %get-tuple-element.28.refs_4_), channel_id=1, source_target_pairs={{0,8},{4,12},{8,0},{12,4},{1,9},{5,13},{9,1},{13,5},{2,10},{6,14},... | collective-permute-start | bytes 49160 | tf_op jit(solution)/shard_map/ppermute | solution.py:375
  67.1 7.5 %collective-permute-start.18 = (bf16[64,128]{1,0:T(8,128)(2,1)S(1)}, bf16[64,128]{1,0:T(8,128)(2,1)S(1)}, u32[]{:S(2)}, u32[]{:S(2)}) collective-permute-start(bf16[64,128]{1,0:T(8,128)(2,1)S(1)} %get-tuple-element.28.refs_4_), channel_id=1, source_target_pairs={{0,4},{4,8},{8,12},{12,0},{1,5},{5,9},{9,13},{13,1},{2,6},{6,10},{... | collective-permute-start | bytes 49160 | tf_op jit(solution)/shard_map/ppermute | solution.py:375
  69.4 1.6 %copy-start.1 = (bf16[64,2,64,64]{3,2,1,0:T(8,128)(2,1)S(1)}, bf16[64,2,64,64]{3,2,1,0:T(8,128)(2,1)}, u32[]{:S(2)}) copy-start(bf16[64,2,64,64]{3,2,1,0:T(8,128)(2,1)} %all-gather.2.cloned.1.call-done.refs_4_) | copy-start | bytes 3145732
Sparse Core Ops, SparseCore 0:
  8.9 25.2 all-gather.1

commit v2 on v0

v2 whole, which is shorter than its diff:
```python
import functools

import jax
import jax.numpy as jnp
from jax import lax
from jax.experimental import pallas as pl
from jax.experimental.pallas import tpu as pltpu
from jax.sharding import PartitionSpec as P

HIGHEST = lax.Precision.HIGHEST
MIB = 1024 * 1024


def nt(a, b, precision=None):
    return lax.dot_general(
        a, b, (((1,), (1,)), ((), ())), precision=precision, preferred_element_type=jnp.float32
    )


def tn(a, b, precision=None):
    return lax.dot_general(
        a, b, (((0,), (0,)), ((), ())), precision=precision, preferred_element_type=jnp.float32
    )


def nn(a, b, precision=None):
    return jnp.dot(a, b, precision=precision, preferred_element_type=jnp.float32)


def vmem():
    return pl.BlockSpec(memory_space=pltpu.VMEM)


def smem():
    return pl.BlockSpec(memory_space=pltpu.SMEM)


def params(mib):
    return pltpu.CompilerParams(vmem_limit_bytes=mib * MIB)


def project_kernel(one, side_ref, rows_ref, proj_ref, near_ref, far_ref, acc):
    step = pl.program_id(0)
    rank, width = proj_ref.shape[1:]
    tokens = acc.shape[2]
    if one:
        rows = rows_ref[...].reshape(tokens, width)
        part = nt(proj_ref[...].reshape(2 * rank, width), rows).reshape(2, rank, tokens)
        parts = [part[0], part[1]]
    else:
        parts = [nt(proj_ref[k], rows_ref[k].reshape(tokens, width)) for k in range(2)]

    @pl.when(step == 0)
    def _():
        for k in range(2):
            acc[k] = parts[k]

    @pl.when(step > 0)
    def _():
        for k in range(2):
            acc[k] += parts[k]

    @pl.when(step == pl.num_programs(0) - 1)
    def _():
        near_ref[...] = acc[side_ref[0]]
        far_ref[...] = acc[1 - side_ref[0]]


def project(side, rows, proj, block):
    one = rows.ndim == 3
    seqs, length, width = rows.shape[-3:]
    rank = proj.shape[1]
    if one:
        rows_spec = pl.BlockSpec((seqs, length, block), lambda i: (0, 0, i))
    else:
        rows_spec = pl.BlockSpec((2, seqs, length, block), lambda i: (0, 0, 0, i))
    shape = (rank, seqs * length)
    return pl.pallas_call(
        functools.partial(project_kernel, one),
        grid=(width // block,),
        in_specs=[smem(), rows_spec, pl.BlockSpec((2, rank, block), lambda i: (0, 0, i))],
        out_specs=[pl.BlockSpec(shape, lambda i: (0, 0))] * 2,
        out_shape=[jax.ShapeDtypeStruct(shape, jnp.float32)] * 2,
        scratch_shapes=[pltpu.VMEM((2,) + shape, jnp.float32)],
        compiler_params=params(52),
        name="project_in" if one else "project_out",
    )(side, rows, proj)


def to_owner(near, far):
    return [
        near,
        lax.ppermute(near, "tensor", [(0, 1), (3, 2)]),
        lax.ppermute(far, "tensor", [(1, 2), (2, 1)]),
        lax.ppermute(far, "tensor", [(0, 2), (3, 1)]),
    ]


def total(pieces):
    value = pieces[0][...]
    for piece in pieces[1:]:
        value = value + piece[...]
    return value


def fold(square):
    half = square.shape[0] // 2
    return jnp.concatenate([square[:half], square[half:]], axis=1)


def unfold(folded):
    size = folded.shape[1] // 2
    return jnp.concatenate([folded[:, :size], folded[:, size:]], axis=0)


def cov_in_kernel(*refs):
    pieces, (x_out, cov_out) = refs[:-2], refs[-2:]
    x = total(pieces)
    x_out[...] = x
    folded = fold(nt(x, x, HIGHEST))
    for k in range(cov_out.shape[0]):
        cov_out[k] = folded


def cov_in(pieces, copies):
    rank, tokens = pieces[0].shape
    return pl.pallas_call(
        cov_in_kernel,
        in_specs=[vmem()] * len(pieces),
        out_specs=[vmem()] * 2,
        out_shape=[
            jax.ShapeDtypeStruct((rank, tokens), jnp.float32),
            jax.ShapeDtypeStruct((copies, rank // 2, 2 * rank), jnp.float32),
        ],
        compiler_params=params(16),
        name="cov_in",
    )(*pieces)


def cov_out_kernel(x_ref, *refs):
    pieces, (cov_out, sample_out) = refs[:-2], refs[-2:]
    g = total(pieces)
    folded = fold(nt(g, g, HIGHEST))
    for k in range(cov_out.shape[0]):
        cov_out[k] = folded
    seqs = sample_out.shape[0]
    length = x_ref.shape[1] // seqs
    for s in range(seqs):
        tokens = slice(s * length, (s + 1) * length)
        sample = nt(x_ref[:, tokens], g[:, tokens], HIGHEST) / length
        sample = sample.astype(jnp.bfloat16).astype(jnp.float32)
        sample_out[s] = jnp.concatenate([sample, sample], axis=1)


def cov_out(x, pieces, copies, seqs):
    rank = x.shape[0]
    return pl.pallas_call(
        cov_out_kernel,
        in_specs=[vmem()] * (1 + len(pieces)),
        out_specs=[vmem()] * 2,
        out_shape=[
            jax.ShapeDtypeStruct((copies, rank // 2, 2 * rank), jnp.float32),
            jax.ShapeDtypeStruct((seqs, rank, 2 * rank), jnp.float32),
        ],
        compiler_params=params(16),
        name="cov_out",
    )(x, *pieces)


def scales(steps, spread):
    r = (spread - 1.0) / (spread + 1.0)
    out = []
    for _ in range(steps):
        out.append(2.0 / (2.0 - r * r))
        r = r * r / (2.0 - r * r)
    return out


def damped_inverse(folded_ref, tokens):
    folded = folded_ref[0]
    for k in range(1, folded_ref.shape[0]):
        folded = folded + folded_ref[k]
    whole = unfold(folded / tokens)
    size = whole.shape[0]
    rows = lax.broadcasted_iota(jnp.int32, whole.shape, 0)
    cols = lax.broadcasted_iota(jnp.int32, whole.shape, 1)
    diagonal = rows == cols
    unit = jnp.sum(jnp.where(diagonal, whole, 0.0)) / size
    eye = jnp.where(diagonal, 1.0, 0.0)
    matrix = whole / unit + 0.1 * eye
    low, high = 0.1, size + 0.1
    start = 2.0 / (low + high)
    steps = scales(7, high / low)
    y = matrix * start
    x = (2.0 * start * steps[0]) * eye - (start * steps[0]) * y
    y = steps[0] * (2.0 * y - nn(y, y, HIGHEST))
    for scale in steps[1:-1]:
        both = nn(jnp.concatenate([x, y], axis=0), y, HIGHEST)
        x = scale * (2.0 * x - both[:size])
        y = scale * (2.0 * y - both[size:])
    x = steps[-1] * (2.0 * x - nn(x, y, HIGHEST))
    x = x + nn(x, eye - nn(matrix, x, HIGHEST), HIGHEST)
    return x / unit


def split(value):
    high = value.astype(jnp.bfloat16)
    rest = value - high.astype(jnp.float32)
    middle = rest.astype(jnp.bfloat16)
    low = (rest - middle.astype(jnp.float32)).astype(jnp.bfloat16)
    return high, middle, low


def right_kernel(tokens, side_ref, cov_ref, queries_ref, out, held, sem):
    copy = pltpu.make_async_copy(queries_ref.at[:, side_ref[0]], held, sem)
    copy.start()
    inverse = damped_inverse(cov_ref, tokens)
    size = inverse.shape[0]
    count = held.shape[0]
    left = jnp.concatenate(split(inverse), axis=0)
    copy.wait()
    group = 4
    for block in range(count // group):
        first = block * group // 2
        places = [first, first + count // 2, first + 1, first + 1 + count // 2]
        rows = jnp.concatenate([held[place] for place in places], axis=0)
        result = nt(left, rows)
        result = result[:size] + result[size : 2 * size] + result[2 * size :]
        high, middle, _ = split(result)
        lanes = slice(block * group * size, (block + 1) * group * size)
        out[0, :, lanes] = high
        out[1, :, lanes] = middle


def right(side, cov, queries, tokens):
    count, _, rank, _ = queries.shape
    return pl.pallas_call(
        functools.partial(right_kernel, tokens),
        in_specs=[smem(), vmem(), pl.BlockSpec(memory_space=pl.ANY)],
        out_specs=vmem(),
        out_shape=jax.ShapeDtypeStruct((2, rank, count * rank), jnp.bfloat16),
        scratch_shapes=[pltpu.VMEM((count, rank, rank), queries.dtype), pltpu.SemaphoreType.DMA],
        compiler_params=params(48),
        name="right",
    )(side, cov, queries)


def score_kernel(tokens, cov_ref, half_ref, sample_ref, out):
    inverse = damped_inverse(cov_ref, tokens)
    size = inverse.shape[0]
    both = 2 * size
    pairs = half_ref.shape[2] // both
    seqs = sample_ref.shape[0]
    none = jnp.zeros_like(inverse)
    twice = jnp.concatenate(
        [
            jnp.concatenate([inverse, none], axis=1),
            jnp.concatenate([none, inverse], axis=1),
        ],
        axis=0,
    )
    high, middle, _ = split(twice)
    once = jnp.concatenate([high, middle], axis=1)
    weights = jnp.concatenate([once, once], axis=0)
    samples = [sample_ref[s] for s in range(seqs)]
    lines = [[] for _ in range(seqs)]
    for pair in range(pairs):
        lanes = slice(pair * both, (pair + 1) * both)
        rows = jnp.concatenate([half_ref[0, :, lanes], half_ref[1, :, lanes]], axis=1)
        result = nn(rows, weights)
        result = (result[:, :both] + result[:, both:]).astype(jnp.bfloat16).astype(jnp.float32)
        for s in range(seqs):
            lines[s].append(jnp.sum(result * samples[s], axis=0, keepdims=True))
    lines = jnp.concatenate([line for part in lines for line in part], axis=0)
    shape = (8, both)
    ends = jnp.where(
        (lax.broadcasted_iota(jnp.int32, shape, 1) < size)
        == (lax.broadcasted_iota(jnp.int32, shape, 0) == 0),
        1.0,
        0.0,
    )
    result = nt(ends, lines, HIGHEST)
    result = jnp.concatenate(
        [
            jnp.concatenate(
                [result[k : k + 1, s * pairs : (s + 1) * pairs] for k in range(2)], axis=1
            )
            for s in range(seqs)
        ],
        axis=0,
    )
    for k in range(out.shape[0]):
        out[k] = result


def score(cov, half, sample, tokens, queries, copies):
    return pl.pallas_call(
        functools.partial(score_kernel, tokens),
        in_specs=[vmem()] * 3,
        out_specs=vmem(),
        out_shape=jax.ShapeDtypeStruct((copies, sample.shape[0], queries), jnp.float32),
        compiler_params=params(24),
        name="score",
    )(cov, half, sample)


def exchange(copies, axis):
    return lax.all_to_all(copies, axis, 0, 0, tiled=True)


def local_owned(acts, grads, proj_in, proj_out, queries):
    seqs, length, _ = acts.shape
    parts = lax.axis_size("dp")
    tokens = seqs * length * parts
    side = (lax.axis_index("tensor") // 2).astype(jnp.int32).reshape(1)
    all_queries = lax.all_gather(queries, "dp", axis=0, tiled=True)
    x_pieces = to_owner(*project(side, acts, proj_in, 512))
    g_pieces = to_owner(*project(side, grads, proj_out, 512))
    x, in_cov = cov_in(x_pieces, parts)
    half = right(side, exchange(in_cov, "dp"), all_queries, tokens)
    out_cov, sample = cov_out(x, g_pieces, parts, seqs)
    scores = score(
        exchange(out_cov, "dp"), half, sample, tokens, all_queries.shape[0], lax.axis_size("tensor")
    )
    scores = exchange(scores, "tensor")
    return scores[1] + scores[2]


def damp(matrix):
    size = matrix.shape[0]
    shift_by = 0.1 * jnp.trace(matrix) / size
    return matrix + shift_by * jnp.eye(size, dtype=matrix.dtype)


def chol_apply(factor, rhs):
    lower_sol = lax.linalg.triangular_solve(factor, rhs, left_side=True, lower=True)
    return lax.linalg.triangular_solve(
        factor, lower_sol, left_side=True, lower=True, transpose_a=True
    )


def precondition(query, left, right_side):
    count, rank = (query.shape[0], query.shape[1])
    left_fac = jnp.linalg.cholesky(left)
    right_fac = jnp.linalg.cholesky(right_side)
    stacked = jnp.transpose(query, (1, 0, 2)).reshape(rank, count * rank)
    middle = chol_apply(left_fac, stacked).reshape(rank, count, rank)
    turned = jnp.transpose(middle, (2, 1, 0)).reshape(rank, count * rank)
    result = chol_apply(right_fac, turned).reshape(rank, count, rank)
    return jnp.transpose(result, (1, 2, 0))


def diagonal_blocks(whole, rank):
    return jnp.stack([whole[:, 0:rank, 0:rank], whole[:, rank : 2 * rank, rank : 2 * rank]], axis=1)


def local_general(acts, grads, proj_in, proj_out, queries):
    seq_count, length, width_loc = acts.shape
    rank = proj_in.shape[1]
    hidden_loc = grads.shape[3]
    flat = acts.reshape(-1, width_loc)
    xpart = nt(flat, proj_in.reshape(2 * rank, width_loc))
    gpart = jnp.concatenate(
        [nt(grads[layer].reshape(-1, hidden_loc), proj_out[layer]) for layer in range(2)], axis=1
    )
    count = seq_count * length * lax.axis_size("dp")
    xin, gout = lax.psum((xpart, gpart), "tensor")
    in_cov, out_cov = lax.psum((tn(xin, xin, HIGHEST), tn(gout, gout, HIGHEST)), "dp")
    whole = (
        jnp.einsum(
            "sto,sti->soi",
            gout.reshape(seq_count, length, 2 * rank),
            xin.reshape(seq_count, length, 2 * rank),
            precision=HIGHEST,
        )
        / length
    )
    samples = diagonal_blocks(whole, rank)
    in_cov = in_cov / count
    out_cov = out_cov / count
    precond = []
    for layer in range(2):
        low = layer * rank
        damped_in = damp(in_cov[low : low + rank, low : low + rank])
        damped_out = damp(out_cov[low : low + rank, low : low + rank])
        precond.append(precondition(queries[:, layer].astype(jnp.float32), damped_out, damped_in))
    query_count = queries.shape[0]
    query_b = jnp.stack(precond, axis=1).astype(jnp.bfloat16).reshape(query_count, -1)
    sample_b = samples.astype(jnp.bfloat16).reshape(seq_count, -1)
    return nt(sample_b, lax.all_gather(query_b, "dp", axis=0, tiled=True))


def local(acts, grads, proj_in, proj_out, queries):
    if lax.axis_size("tensor") == 4:
        return local_owned(acts, grads, proj_in, proj_out, queries)
    return local_general(acts, grads, proj_in, proj_out, queries)


def solution(mesh):
    placed = (
        P(("groups", "dp"), None, "tensor"),
        P(None, ("groups", "dp"), None, "tensor"),
        P(None, None, "tensor"),
        P(None, None, "tensor"),
        P("dp", None, None, None),
    )
    return jax.shard_map(
        local, mesh=mesh, in_specs=placed, out_specs=P(("groups", "dp"), None), check_vma=False
    )
```

time: 210 us -> 85.4 us (0.41)
  waiting for transfers between devices: 101 us -> 3.55 us
  other arithmetic: 52 us -> 1.25 us
  Pallas kernels: 0 us -> 31.1 us
  matrix products: 25.1 us -> 0 us
  starting transfers between devices: 0.27 us -> 22.3 us
  local copies, waits for them, and re-layouts: 15.9 us -> 3.33 us
  blocking collectives: 0 us -> 9.52 us
  between operations: 16.1 us -> 13.6 us
    psum x2 -> x0, waiting for transfers between devices: 84.8 us -> none  [the longest x1 55 us: local(): xin, gout = lax.psum((xpart, gpart), 'tensor')]
    another operation x22 -> x0, other arithmetic: 48.4 us -> none  [the longest x8 22.2 us: chol_apply(): lax.linalg.triangular_solve(factor, lower_sol, left_side=True, lower=True...]
    pallas_call x0 -> x6, Pallas kernels: none -> 31.1 us  [the longest x2 22.8 us: project(): pl.pallas_call(functools.partial(project_kernel, one), grid=(width // blo...]
    dot_general x7 -> x0, matrix products: 22 us -> none  [the longest x1 5.93 us: local(): jnp.einsum('tf,rf->tr', grads[1].reshape(-1, hidden_loc), proj_out[1], pr...]
    all_gather x1, waiting for transfers between devices: 15.9 us -> 0.02 us  [local_owned(): all_queries = lax.all_gather(queries, 'dp', axis=0, tiled=True)]
    ppermute x0 -> x6, starting transfers between devices: none -> 15.7 us  [the longest x2 7.97 us: to_owner(): lax.ppermute(far, 'tensor', [(0, 2), (3, 1)])]
    slice x1 -> x0, local copies, waits for them, and re-layouts: 11.5 us -> none  [local(): grads[0].reshape(-1, hidden_loc)]
    all_to_all x0 -> x1, blocking collectives: none -> 9.52 us  [exchange(): return lax.all_to_all(copies, axis, 0, 0, tiled=True)]
  transfers between devices with their start and end apart: 3 -> 9, of which waited for: 3 -> 2; matrix products, arithmetic and copies ran while one was open for 1% -> 0% of each run, Pallas kernels for 0% -> 33%
where the time goes in v2:
time: 85.4 us; the launch traced here: 84.6 us
  Pallas kernels  31.1 us (36%)
  starting transfers between devices  22.3 us (26%)
  between operations  13.6 us (16%)
  blocking collectives  9.52 us (11%)
  waiting for transfers between devices  3.55 us (4%)
  local copies, waits for them, and re-layouts  3.33 us (4%)
  other arithmetic  1.25 us (1%)
    pallas_call x2, Pallas kernels, project(): pl.pallas_call(functools.partial(project_kernel, one), grid=(width // blo...  22.8 us
    all_to_all x1, blocking collectives, exchange(): return lax.all_to_all(copies, axis, 0, 0, tiled=True)  9.52 us
    ppermute x2, starting transfers between devices, to_owner(): lax.ppermute(far, 'tensor', [(0, 2), (3, 1)])  7.97 us
    all_to_all x2, starting transfers between devices, exchange(): return lax.all_to_all(copies, axis, 0, 0, tiled=True)  6.56 us
    ppermute x2, starting transfers between devices, to_owner(): lax.ppermute(near, 'tensor', [(0, 1), (3, 2)])  6.36 us
    pallas_call x1, Pallas kernels, score(): pl.pallas_call(functools.partial(score_kernel, tokens), in_specs=[vmem()]...  3.29 us
    unnamed x6, local copies, waits for them, and re-layouts  2.82 us
    pallas_call x1, Pallas kernels, right(): pl.pallas_call(functools.partial(right_kernel, tokens), in_specs=[smem(),...  2.71 us
  transfers between devices with their start and end apart: 9, of which 2 were waited for; matrix products, arithmetic and copies ran while one was open for 0% of the time, Pallas kernels for 33%

profile of v2, /device:TPU:0, one launch (start us, length us, event | category | flops | bytes accessed | tf_op | source)
XLA Modules:
  0.0 84.6 jit_solution(13515316427752127374)
XLA Ops:
  6.5 0.0 all-gather.2.cloned.1.call-start
  6.5 0.7 all-gather.2.cloned.1.call-update
  7.3 0.0 copy-start.1
  7.3 1.0 %copy-done.1 = bf16[2,64,2048]{2,1,0:T(8,128)(2,1)S(1)} copy-done((bf16[2,64,2048]{2,1,0:T(8,128)(2,1)S(1)}, bf16[2,64,2048]{2,1,0:T(8,128)(2,1)}, u32[]{:S(2)}) %copy-start.1) | copy-done | bytes 524312
  8.3 4.2 %project_in.1 = (f32[64,1024]{1,0:T(8,128)S(1)}, f32[64,1024]{1,0:T(8,128)S(1)}) custom-call(s32[1]{0:T(128)} %bitcast.side_ref, bf16[4,256,2048]{2,1,0:T(8,128)(2,1)} %rows_ref.2, bf16[2,64,2048]{2,1,0:T(8,128)(2,1)S(1)} %copy-done.1), custom_call_target="tpu_custom_call" | custom-call | tf_op jit(solution)/shard_map/project_in/pallas_call | solution.py:78
  12.5 4.9 %collective-permute-start = (f32[64,1024]{1,0:T(8,128)S(1)}, f32[64,1024]{1,0:T(8,128)S(1)}, u32[]{:S(2)}, u32[]{:S(2)}) collective-permute-start(f32[64,1024]{1,0:T(8,128)S(1)} %get-tuple-element.13.refs_0_), channel_id=1, source_target_pairs={{0,4},{12,8},{1,5},{13,9},{2,6},{14,10},{3,7},{15,11},{16,20},{28,... | collective-permute-start | bytes 786440 | tf_op jit(solution)/shard_map/ppermute | solution.py:93
  17.4 0.7 collective-permute-start.1
  18.1 4.0 %collective-permute-start.2 = (f32[64,1024]{1,0:T(8,128)S(1)}, f32[64,1024]{1,0:T(8,128)S(1)}, u32[]{:S(2)}, u32[]{:S(2)}) collective-permute-start(f32[64,1024]{1,0:T(8,128)S(1)} %get-tuple-element.14), channel_id=1, source_target_pairs={{0,8},{12,4},{1,9},{13,5},{2,10},{14,6},{3,11},{15,7},{16,24},{28,... | collective-permute-start | bytes 786440 | tf_op jit(solution)/shard_map/ppermute | solution.py:95
  22.1 18.6 %project_out.1 = (f32[64,1024]{1,0:T(8,128)S(1)}, f32[64,1024]{1,0:T(8,128)S(1)}) custom-call(s32[1]{0:T(128)} %bitcast.side_ref, bf16[2,4,256,7168]{3,2,1,0:T(8,128)(2,1)} %rows_ref.3, bf16[2,64,7168]{2,1,0:T(8,128)(2,1)} %proj_ref.3), custom_call_target="tpu_custom_call" | custom-call | tf_op jit(solution)/shard_map/project_out/pallas_call | solution.py:78
  40.7 1.4 %collective-permute-start.3 = (f32[64,1024]{1,0:T(8,128)S(1)}, f32[64,1024]{1,0:T(8,128)S(1)}, u32[]{:S(2)}, u32[]{:S(2)}) collective-permute-start(f32[64,1024]{1,0:T(8,128)S(1)} %get-tuple-element.16.refs_0_), channel_id=1, source_target_pairs={{0,4},{12,8},{1,5},{13,9},{2,6},{14,10},{3,7},{15,11},{16,20},{28,... | collective-permute-start | bytes 786440 | tf_op jit(solution)/shard_map/ppermute | solution.py:93
  42.1 0.7 collective-permute-start.4
  42.8 0.0 collective-permute-done.refs_1_
  42.8 4.0 %collective-permute-start.5 = (f32[64,1024]{1,0:T(8,128)S(1)}, f32[64,1024]{1,0:T(8,128)S(1)}, u32[]{:S(2)}, u32[]{:S(2)}) collective-permute-start(f32[64,1024]{1,0:T(8,128)S(1)} %get-tuple-element.17), channel_id=1, source_target_pairs={{0,8},{12,4},{1,9},{13,5},{2,10},{14,6},{3,11},{15,7},{16,24},{28,... | collective-permute-start | bytes 786440 | tf_op jit(solution)/shard_map/ppermute | solution.py:95
  46.8 0.0 collective-permute-done.1.refs_2_
  46.8 0.0 collective-permute-done.2.refs_3_
  46.9 1.1 %cov_in.1 = (f32[64,1024]{1,0:T(8,128)S(1)}, f32[4,32,128]{2,1,0:T(8,128)}) custom-call(f32[64,1024]{1,0:T(8,128)S(1)} %get-tuple-element.13.refs_0_, f32[64,1024]{1,0:T(8,128)S(1)} %collective-permute-done.refs_1_, f32[64,1024]{1,0:T(8,128)S(1)} %collective-permute-done.1.refs_2_, f32[64,1024]{1,0:T(8,128)S(1)} %collective-permute-done.2.refs_3_), custom_call_target="tpu_custom_call" | custom-call | tf_op jit(solution)/shard_map/cov_in/pallas_call | solution.py:127
  48.0 3.3 %all-to-all-start.1 = ((f32[4,32,128]{2,1,0:T(8,128)}), f32[4,32,128]{2,1,0:T(8,128)S(1)}, u32[]{:S(2)}, u32[]{:S(2)}) async-start(f32[4,32,128]{2,1,0:T(8,128)} %get-tuple-element.19), calls=%async_computation.1 | async-start | bytes 131072 | tf_op jit(solution)/shard_map/all_to_all | solution.py:308
  51.2 0.0 collective-permute-done.3.refs_1_
  51.3 0.0 collective-permute-done.4.refs_2_
  51.3 1.9 %collective-permute-done.5.refs_3_ = f32[64,1024]{1,0:T(8,128)S(1)} collective-permute-done((f32[64,1024]{1,0:T(8,128)S(1)}, f32[64,1024]{1,0:T(8,128)S(1)}, u32[]{:S(2)}, u32[]{:S(2)}) %collective-permute-start.5) | collective-permute-done | bytes 262176 | tf_op jit(solution)/shard_map/ppermute | solution.py:95
  53.2 1.3 %cov_out.1 = (f32[4,32,128]{2,1,0:T(8,128)}, f32[4,64,128]{2,1,0:T(8,128)S(1)}) custom-call(f32[64,1024]{1,0:T(8,128)S(1)} %get-tuple-element.15.x_ref, f32[64,1024]{1,0:T(8,128)S(1)} %get-tuple-element.16.refs_0_, f32[64,1024]{1,0:T(8,128)S(1)} %collective-permute-done.3.refs_1_, f32[64,1024]{1,0:T(8,128)S(1)} %collective-permute-done.4.refs_2_, ...), custom_call_target="tpu_custom_call" | custom-call | tf_op jit(solution)/shard_map/cov_out/pallas_call | solution.py:157
  54.5 0.9 %all-to-all-done.1.cov_ref = f32[4,32,128]{2,1,0:T(8,128)S(1)} async-done(((f32[4,32,128]{2,1,0:T(8,128)}), f32[4,32,128]{2,1,0:T(8,128)S(1)}, u32[]{:S(2)}, u32[]{:S(2)}) %all-to-all-start.1) | async-done | bytes 65568 | tf_op jit(solution)/shard_map/all_to_all | solution.py:308
  55.3 3.3 %all-to-all-start = ((f32[4,32,128]{2,1,0:T(8,128)}), f32[4,32,128]{2,1,0:T(8,128)S(1)}, u32[]{:S(2)}, u32[]{:S(2)}) async-start(f32[4,32,128]{2,1,0:T(8,128)} %get-tuple-element.18), calls=%async_computation | async-start | bytes 131072 | tf_op jit(solution)/shard_map/all_to_all | solution.py:308
  58.6 0.0 all-gather.2.cloned.1.call-done.queries_ref
  58.7 0.0 copy-start
  58.7 1.6 %copy-done = bf16[64,2,64,64]{3,2,1,0:T(8,128)(2,1)S(1)} copy-done((bf16[64,2,64,64]{3,2,1,0:T(8,128)(2,1)S(1)}, bf16[64,2,64,64]{3,2,1,0:T(8,128)(2,1)}, u32[]{:S(2)}) %copy-start) | copy-done | bytes 1048600
  60.2 2.7 %right.1.half_ref = bf16[2,64,4096]{2,1,0:T(8,128)(2,1)S(1)} custom-call(s32[1]{0:T(128)} %bitcast.side_ref, f32[4,32,128]{2,1,0:T(8,128)S(1)} %all-to-all-done.1.cov_ref, bf16[64,2,64,64]{3,2,1,0:T(8,128)(2,1)S(1)} %copy-done), custom_call_target="tpu_custom_call" | custom-call | tf_op jit(solution)/shard_map/right/pallas_call | solution.py:237
  63.0 0.0 all-to-all-done.cov_ref
  63.0 3.3 %score.1 = f32[4,4,64]{2,1,0:T(4,128)S(1)} custom-call(f32[4,32,128]{2,1,0:T(8,128)S(1)} %all-to-all-done.cov_ref, bf16[2,64,4096]{2,1,0:T(8,128)(2,1)S(1)} %right.1.half_ref, f32[4,64,128]{2,1,0:T(8,128)S(1)} %get-tuple-element.20.sample_ref), custom_call_target="tpu_custom_call" | custom-call | tf_op jit(solution)/shard_map/score/pallas_call | solution.py:297
  66.3 0.1 reshape.5
  66.4 9.5 %all_to_all.15 = f32[4,1,256]{2,1,0:T(1,128)S(1)} all-to-all(f32[4,1,256]{2,1,0:T(1,128)S(1)} %reshape.5), channel_id=1, replica_groups=mesh['groups'=2,'tensor'=4,'dp'=4] {'tensor'}, dimensions={0} | all-to-all | bytes 8192 | tf_op jit(solution)/shard_map/all_to_all | solution.py:308
  75.9 0.5 broadcast.1
  76.4 0.7 reduce
  77.1 0.1 reshape.6
  77.2 0.6 fusion
Async XLA Ops:
  6.5 52.1 %all-gather.2.cloned.1.call-start = ((), (), s32[]{:S(2)}) async-start(), calls=%async_computation.3 | async-start | bytes 2621440 | tf_op jit(solution)/shard_map/all_gather | solution.py:316
  7.3 1.0 %copy-start.1 = (bf16[2,64,2048]{2,1,0:T(8,128)(2,1)S(1)}, bf16[2,64,2048]{2,1,0:T(8,128)(2,1)}, u32[]{:S(2)}) copy-start(bf16[2,64,2048]{2,1,0:T(8,128)(2,1)} %proj_ref.2) | copy-start | bytes 1572868
  12.5 30.4 %collective-permute-start = (f32[64,1024]{1,0:T(8,128)S(1)}, f32[64,1024]{1,0:T(8,128)S(1)}, u32[]{:S(2)}, u32[]{:S(2)}) collective-permute-start(f32[64,1024]{1,0:T(8,128)S(1)} %get-tuple-element.13.refs_0_), channel_id=1, source_target_pairs={{0,4},{12,8},{1,5},{13,9},{2,6},{14,10},{3,7},{15,11},{16,20},{28,... | collective-permute-start | bytes 786440 | tf_op jit(solution)/shard_map/ppermute | solution.py:93
  17.4 29.4 %collective-permute-start.1 = (f32[64,1024]{1,0:T(8,128)S(1)}, f32[64,1024]{1,0:T(8,128)S(1)}, u32[]{:S(2)}, u32[]{:S(2)}) collective-permute-start(f32[64,1024]{1,0:T(8,128)S(1)} %get-tuple-element.14), channel_id=1, source_target_pairs={{4,8},{8,4},{5,9},{9,5},{6,10},{10,6},{7,11},{11,7},{20,24},{24,20... | collective-permute-start | bytes 786440 | tf_op jit(solution)/shard_map/ppermute | solution.py:94
  18.1 28.7 %collective-permute-start.2 = (f32[64,1024]{1,0:T(8,128)S(1)}, f32[64,1024]{1,0:T(8,128)S(1)}, u32[]{:S(2)}, u32[]{:S(2)}) collective-permute-start(f32[64,1024]{1,0:T(8,128)S(1)} %get-tuple-element.14), channel_id=1, source_target_pairs={{0,8},{12,4},{1,9},{13,5},{2,10},{14,6},{3,11},{15,7},{16,24},{28,... | collective-permute-start | bytes 786440 | tf_op jit(solution)/shard_map/ppermute | solution.py:95
  40.7 10.5 %collective-permute-start.3 = (f32[64,1024]{1,0:T(8,128)S(1)}, f32[64,1024]{1,0:T(8,128)S(1)}, u32[]{:S(2)}, u32[]{:S(2)}) collective-permute-start(f32[64,1024]{1,0:T(8,128)S(1)} %get-tuple-element.16.refs_0_), channel_id=1, source_target_pairs={{0,4},{12,8},{1,5},{13,9},{2,6},{14,10},{3,7},{15,11},{16,20},{28,... | collective-permute-start | bytes 786440 | tf_op jit(solution)/shard_map/ppermute | solution.py:93
  42.1 9.1 %collective-permute-start.4 = (f32[64,1024]{1,0:T(8,128)S(1)}, f32[64,1024]{1,0:T(8,128)S(1)}, u32[]{:S(2)}, u32[]{:S(2)}) collective-permute-start(f32[64,1024]{1,0:T(8,128)S(1)} %get-tuple-element.17), channel_id=1, source_target_pairs={{4,8},{8,4},{5,9},{9,5},{6,10},{10,6},{7,11},{11,7},{20,24},{24,20... | collective-permute-start | bytes 786440 | tf_op jit(solution)/shard_map/ppermute | solution.py:94
  42.8 10.4 %collective-permute-start.5 = (f32[64,1024]{1,0:T(8,128)S(1)}, f32[64,1024]{1,0:T(8,128)S(1)}, u32[]{:S(2)}, u32[]{:S(2)}) collective-permute-start(f32[64,1024]{1,0:T(8,128)S(1)} %get-tuple-element.17), channel_id=1, source_target_pairs={{0,8},{12,4},{1,9},{13,5},{2,10},{14,6},{3,11},{15,7},{16,24},{28,... | collective-permute-start | bytes 786440 | tf_op jit(solution)/shard_map/ppermute | solution.py:95
  48.0 7.4 %all-to-all-start.1 = ((f32[4,32,128]{2,1,0:T(8,128)}), f32[4,32,128]{2,1,0:T(8,128)S(1)}, u32[]{:S(2)}, u32[]{:S(2)}) async-start(f32[4,32,128]{2,1,0:T(8,128)} %get-tuple-element.19), calls=%async_computation.1 | async-start | bytes 131072 | tf_op jit(solution)/shard_map/all_to_all | solution.py:308
  55.3 7.6 %all-to-all-start = ((f32[4,32,128]{2,1,0:T(8,128)}), f32[4,32,128]{2,1,0:T(8,128)S(1)}, u32[]{:S(2)}, u32[]{:S(2)}) async-start(f32[4,32,128]{2,1,0:T(8,128)} %get-tuple-element.18), calls=%async_computation | async-start | bytes 131072 | tf_op jit(solution)/shard_map/all_to_all | solution.py:308
  58.7 1.6 %copy-start = (bf16[64,2,64,64]{3,2,1,0:T(8,128)(2,1)S(1)}, bf16[64,2,64,64]{3,2,1,0:T(8,128)(2,1)}, u32[]{:S(2)}) copy-start(bf16[64,2,64,64]{3,2,1,0:T(8,128)(2,1)} %all-gather.2.cloned.1.call-done.queries_ref) | copy-start | bytes 3145732
Sparse Core Ops, SparseCore 0:
  8.9 25.2 all-gather.1

commit v3 on v2

v3 whole, which is shorter than its diff:
```python
import functools

import jax
import jax.numpy as jnp
from jax import lax
from jax.experimental import pallas as pl
from jax.experimental.pallas import tpu as pltpu
from jax.sharding import PartitionSpec as P

HIGHEST = lax.Precision.HIGHEST
MIB = 1024 * 1024


def nt(a, b, precision=None):
    return lax.dot_general(
        a, b, (((1,), (1,)), ((), ())), precision=precision, preferred_element_type=jnp.float32
    )


def tn(a, b, precision=None):
    return lax.dot_general(
        a, b, (((0,), (0,)), ((), ())), precision=precision, preferred_element_type=jnp.float32
    )


def nn(a, b, precision=None):
    return jnp.dot(a, b, precision=precision, preferred_element_type=jnp.float32)


def vmem():
    return pl.BlockSpec(memory_space=pltpu.VMEM)


def smem():
    return pl.BlockSpec(memory_space=pltpu.SMEM)


def hbm():
    return pl.BlockSpec(memory_space=pl.ANY)


def in_hbm(value):
    return pltpu.with_memory_space_constraint(value, pltpu.HBM)


def params(mib):
    return pltpu.CompilerParams(vmem_limit_bytes=mib * MIB)


def project_in_kernel(side_ref, rows_hbm, proj_hbm, near_ref, far_ref, rows, proj, acc, sems, proj_sem):
    seqs, length, width = rows.shape
    rank = proj.shape[1]
    proj_copy = pltpu.make_async_copy(proj_hbm, proj, proj_sem)
    proj_copy.start()
    copies = [pltpu.make_async_copy(rows_hbm.at[s], rows.at[s], sems.at[s]) for s in range(seqs)]
    for copy in copies:
        copy.start()
    proj_copy.wait()
    weights = proj[...].reshape(2 * rank, width)
    for s in range(seqs):
        copies[s].wait()
        tokens = slice(s * length, (s + 1) * length)
        part = nt(weights, rows[s])
        acc[0, :, tokens] = part[:rank]
        acc[1, :, tokens] = part[rank:]
    near_ref[...] = acc[side_ref[0]]
    far_ref[...] = acc[1 - side_ref[0]]


def project_out_kernel(side_ref, rows_hbm, proj_hbm, near_ref, far_ref, rows, proj, acc, sems, proj_sem):
    _, seqs, length, width = rows.shape
    half = width // 2
    proj_copy = pltpu.make_async_copy(proj_hbm, proj, proj_sem)
    proj_copy.start()
    copies = {}
    for s in range(seqs):
        for part in range(2):
            lanes = pl.ds(part * half, half)
            for layer in range(2):
                copies[s, part, layer] = pltpu.make_async_copy(
                    rows_hbm.at[layer, s, :, lanes],
                    rows.at[layer, s, :, lanes],
                    sems.at[s, part, layer],
                )
                copies[s, part, layer].start()
    proj_copy.wait()
    for s in range(seqs):
        tokens = slice(s * length, (s + 1) * length)
        for part in range(2):
            lanes = slice(part * half, (part + 1) * half)
            for layer in range(2):
                copies[s, part, layer].wait()
            for layer in range(2):
                value = nt(proj[layer, :, lanes], rows[layer, s, :, lanes])
                if part > 0:
                    value = value + acc[layer, :, tokens]
                acc[layer, :, tokens] = value
    near_ref[...] = acc[side_ref[0]]
    far_ref[...] = acc[1 - side_ref[0]]


def project(side, rows, proj, mib):
    one = rows.ndim == 3
    seqs, length, _ = rows.shape[-3:]
    rank = proj.shape[1]
    shape = (rank, seqs * length)
    return pl.pallas_call(
        project_in_kernel if one else project_out_kernel,
        in_specs=[smem(), hbm(), hbm()],
        out_specs=[vmem()] * 2,
        out_shape=[jax.ShapeDtypeStruct(shape, jnp.float32)] * 2,
        scratch_shapes=[
            pltpu.VMEM(rows.shape, rows.dtype),
            pltpu.VMEM(proj.shape, proj.dtype),
            pltpu.VMEM((2,) + shape, jnp.float32),
            pltpu.SemaphoreType.DMA((seqs,) if one else (seqs, 2, 2)),
            pltpu.SemaphoreType.DMA,
        ],
        compiler_params=params(mib),
        name="project_in" if one else "project_out",
    )(side, in_hbm(rows), in_hbm(proj) if one else proj)


def to_owner(near, far):
    return [
        near,
        lax.ppermute(near, "tensor", [(0, 1), (3, 2)]),
        lax.ppermute(far, "tensor", [(1, 2), (2, 1)]),
        lax.ppermute(far, "tensor", [(0, 2), (3, 1)]),
    ]


def total(pieces):
    value = pieces[0][...]
    for piece in pieces[1:]:
        value = value + piece[...]
    return value


def cov_in_kernel(*refs):
    pieces, (x_out, cov_out) = refs[:-2], refs[-2:]
    x = total(pieces)
    x_out[...] = x
    cov_out[...] = nt(x, jnp.concatenate([x, jnp.zeros_like(x)], axis=0), HIGHEST)


def cov_in(pieces):
    rank, tokens = pieces[0].shape
    return pl.pallas_call(
        cov_in_kernel,
        in_specs=[vmem()] * len(pieces),
        out_specs=[vmem()] * 2,
        out_shape=[
            jax.ShapeDtypeStruct((rank, tokens), jnp.float32),
            jax.ShapeDtypeStruct((rank, 2 * rank), jnp.float32),
        ],
        compiler_params=params(16),
        name="cov_in",
    )(*pieces)


def cov_out_kernel(x_ref, cov_ref, *refs):
    pieces, (cov_out, sample_out) = refs[:-2], refs[-2:]
    g = total(pieces)
    cov_out[...] = cov_ref[...] + nt(g, jnp.concatenate([jnp.zeros_like(g), g], axis=0), HIGHEST)
    seqs = sample_out.shape[0]
    length = x_ref.shape[1] // seqs
    for s in range(seqs):
        tokens = slice(s * length, (s + 1) * length)
        sample = nt(x_ref[:, tokens], g[:, tokens], HIGHEST) / length
        sample = sample.astype(jnp.bfloat16).astype(jnp.float32)
        sample_out[s] = jnp.concatenate([sample, sample], axis=1)


def cov_out(x, cov, pieces, seqs):
    rank = x.shape[0]
    return pl.pallas_call(
        cov_out_kernel,
        in_specs=[vmem()] * (2 + len(pieces)),
        out_specs=[vmem()] * 2,
        out_shape=[
            jax.ShapeDtypeStruct((rank, 2 * rank), jnp.float32),
            jax.ShapeDtypeStruct((seqs, rank, 2 * rank), jnp.float32),
        ],
        compiler_params=params(16),
        name="cov_out",
    )(x, cov, *pieces)


def scales(steps, spread):
    r = (spread - 1.0) / (spread + 1.0)
    out = []
    for _ in range(steps):
        out.append(2.0 / (2.0 - r * r))
        r = r * r / (2.0 - r * r)
    return out


def damped_inverses(pair):
    size, both = pair.shape
    left = lax.broadcasted_iota(jnp.int32, pair.shape, 1) < size
    whole = jnp.concatenate([jnp.where(left, pair, 0.0), jnp.where(left, 0.0, pair)], axis=0)
    rows = lax.broadcasted_iota(jnp.int32, whole.shape, 0)
    cols = lax.broadcasted_iota(jnp.int32, whole.shape, 1)
    diagonal = rows == cols
    on_diagonal = jnp.where(diagonal, whole, 0.0)
    unit = jnp.where(
        rows < size, jnp.sum(on_diagonal[:size]) / size, jnp.sum(on_diagonal[size:]) / size
    )
    eye = jnp.where(diagonal, 1.0, 0.0)
    matrix = whole / unit + 0.1 * eye
    low, high = 0.1, size + 0.1
    start = 2.0 / (low + high)
    steps = scales(7, high / low)
    y = matrix * start
    x = (2.0 * start * steps[0]) * eye - (start * steps[0]) * y
    y = steps[0] * (2.0 * y - nn(y, y, HIGHEST))
    for scale in steps[1:-1]:
        product = nn(jnp.concatenate([x, y], axis=0), y, HIGHEST)
        x = scale * (2.0 * x - product[:both])
        y = scale * (2.0 * y - product[both:])
    x = steps[-1] * (2.0 * x - nn(x, y, HIGHEST))
    x = x + nn(x, eye - nn(matrix, x, HIGHEST), HIGHEST)
    return x / unit


def split(value):
    high = value.astype(jnp.bfloat16)
    rest = value - high.astype(jnp.float32)
    middle = rest.astype(jnp.bfloat16)
    low = (rest - middle.astype(jnp.float32)).astype(jnp.bfloat16)
    return high, middle, low


def score_kernel(tokens, side_ref, own_ref, other_ref, sample_ref, queries_hbm, out, held, half, sem):
    copy = pltpu.make_async_copy(queries_hbm.at[:, side_ref[0]], held, sem)
    copy.start()
    inverses = damped_inverses((own_ref[...] + other_ref[...]) / tokens)
    both = inverses.shape[0]
    size = both // 2
    count = held.shape[0]
    seqs = sample_ref.shape[0]
    pairs = count // 2
    first = jnp.concatenate(split(inverses[:size, :size]), axis=0)
    right = inverses[size:]
    twice = jnp.concatenate([pltpu.roll(right, size, 1), right], axis=0)
    high, middle, _ = split(twice)
    once = jnp.concatenate([high, middle], axis=1)
    second = jnp.concatenate([once, once], axis=0)
    copy.wait()
    group = 4
    for block in range(count // group):
        start = block * group // 2
        places = [start, start + pairs, start + 1, start + 1 + pairs]
        rows = jnp.concatenate([held[place] for place in places], axis=0)
        result = nt(first, rows)
        result = result[:size] + result[size : 2 * size] + result[2 * size :]
        high, middle, _ = split(result)
        lanes = slice(block * group * size, (block + 1) * group * size)
        half[0, :, lanes] = high
        half[1, :, lanes] = middle
    samples = [sample_ref[s] for s in range(seqs)]
    lines = [[] for _ in range(seqs)]
    for pair in range(pairs):
        lanes = slice(pair * both, (pair + 1) * both)
        rows = jnp.concatenate([half[0, :, lanes], half[1, :, lanes]], axis=1)
        result = nn(rows, second)
        result = (result[:, :both] + result[:, both:]).astype(jnp.bfloat16).astype(jnp.float32)
        for s in range(seqs):
            lines[s].append(jnp.sum(result * samples[s], axis=0, keepdims=True))
    lines = jnp.concatenate([line for part in lines for line in part], axis=0)
    shape = (8, both)
    ends = jnp.where(
        (lax.broadcasted_iota(jnp.int32, shape, 1) < size)
        == (lax.broadcasted_iota(jnp.int32, shape, 0) == 0),
        1.0,
        0.0,
    )
    result = nt(ends, lines, HIGHEST)
    for s in range(seqs):
        for k in range(2):
            out[s : s + 1, k * pairs : (k + 1) * pairs] = result[
                k : k + 1, s * pairs : (s + 1) * pairs
            ]


def score(side, own, other, sample, queries, tokens):
    count, _, rank, _ = queries.shape
    return pl.pallas_call(
        functools.partial(score_kernel, tokens),
        in_specs=[smem(), vmem(), vmem(), vmem(), hbm()],
        out_specs=vmem(),
        out_shape=jax.ShapeDtypeStruct((sample.shape[0], count), jnp.float32),
        scratch_shapes=[
            pltpu.VMEM((count, rank, rank), queries.dtype),
            pltpu.VMEM((2, rank, count * rank), jnp.bfloat16),
            pltpu.SemaphoreType.DMA,
        ],
        compiler_params=params(16),
        name="score",
    )(side, own, other, sample, in_hbm(queries))


def swap(value, axis, bit):
    return lax.ppermute(value, axis, [(i, i ^ bit) for i in range(lax.axis_size(axis))])


def local_owned(acts, grads, proj_in, proj_out, queries):
    seqs, length, _ = acts.shape
    parts = lax.axis_size("dp")
    tokens = seqs * length * parts
    place = lax.axis_index("tensor").astype(jnp.int32)
    side = (place >= 2).astype(jnp.int32).reshape(1)
    all_queries = lax.all_gather(queries, "dp", axis=0, tiled=True)
    x_pieces = to_owner(*project(side, acts, proj_in, 16))
    g_pieces = to_owner(*project(side, grads, proj_out, 40))
    x, cov = cov_in(x_pieces)
    cov, sample = cov_out(x, cov, g_pieces, seqs)
    other = jnp.zeros_like(cov)
    bit = 1
    while bit < parts:
        cov = cov if bit == 1 else cov + other
        other = swap(cov, "dp", bit)
        bit *= 2
    scores = score(side, cov, other, sample, all_queries, tokens)
    owner = (place == 1) | (place == 2)
    return (
        jnp.where(owner, scores, 0.0)
        + lax.ppermute(scores, "tensor", [(1, 2), (2, 1)])
        + lax.ppermute(scores, "tensor", [(1, 0), (2, 3)])
        + lax.ppermute(scores, "tensor", [(2, 0), (1, 3)])
    )


def damp(matrix):
    size = matrix.shape[0]
    shift_by = 0.1 * jnp.trace(matrix) / size
    return matrix + shift_by * jnp.eye(size, dtype=matrix.dtype)


def chol_apply(factor, rhs):
    lower_sol = lax.linalg.triangular_solve(factor, rhs, left_side=True, lower=True)
    return lax.linalg.triangular_solve(
        factor, lower_sol, left_side=True, lower=True, transpose_a=True
    )


def precondition(query, left, right_side):
    count, rank = (query.shape[0], query.shape[1])
    left_fac = jnp.linalg.cholesky(left)
    right_fac = jnp.linalg.cholesky(right_side)
    stacked = jnp.transpose(query, (1, 0, 2)).reshape(rank, count * rank)
    middle = chol_apply(left_fac, stacked).reshape(rank, count, rank)
    turned = jnp.transpose(middle, (2, 1, 0)).reshape(rank, count * rank)
    result = chol_apply(right_fac, turned).reshape(rank, count, rank)
    return jnp.transpose(result, (1, 2, 0))


def diagonal_blocks(whole, rank):
    return jnp.stack([whole[:, 0:rank, 0:rank], whole[:, rank : 2 * rank, rank : 2 * rank]], axis=1)


def local_general(acts, grads, proj_in, proj_out, queries):
    seq_count, length, width_loc = acts.shape
    rank = proj_in.shape[1]
    hidden_loc = grads.shape[3]
    flat = acts.reshape(-1, width_loc)
    xpart = nt(flat, proj_in.reshape(2 * rank, width_loc))
    gpart = jnp.concatenate(
        [nt(grads[layer].reshape(-1, hidden_loc), proj_out[layer]) for layer in range(2)], axis=1
    )
    count = seq_count * length * lax.axis_size("dp")
    xin, gout = lax.psum((xpart, gpart), "tensor")
    in_cov, out_cov = lax.psum((tn(xin, xin, HIGHEST), tn(gout, gout, HIGHEST)), "dp")
    whole = (
        jnp.einsum(
            "sto,sti->soi",
            gout.reshape(seq_count, length, 2 * rank),
            xin.reshape(seq_count, length, 2 * rank),
            precision=HIGHEST,
        )
        / length
    )
    samples = diagonal_blocks(whole, rank)
    in_cov = in_cov / count
    out_cov = out_cov / count
    precond = []
    for layer in range(2):
        low = layer * rank
        damped_in = damp(in_cov[low : low + rank, low : low + rank])
        damped_out = damp(out_cov[low : low + rank, low : low + rank])
        precond.append(precondition(queries[:, layer].astype(jnp.float32), damped_out, damped_in))
    query_count = queries.shape[0]
    query_b = jnp.stack(precond, axis=1).astype(jnp.bfloat16).reshape(query_count, -1)
    sample_b = samples.astype(jnp.bfloat16).reshape(seq_count, -1)
    return nt(sample_b, lax.all_gather(query_b, "dp", axis=0, tiled=True))


def local(acts, grads, proj_in, proj_out, queries):
    parts = lax.axis_size("dp")
    if lax.axis_size("tensor") == 4 and parts & (parts - 1) == 0:
        return local_owned(acts, grads, proj_in, proj_out, queries)
    return local_general(acts, grads, proj_in, proj_out, queries)


def solution(mesh):
    placed = (
        P(("groups", "dp"), None, "tensor"),
        P(None, ("groups", "dp"), None, "tensor"),
        P(None, None, "tensor"),
        P(None, None, "tensor"),
        P("dp", None, None, None),
    )
    return jax.shard_map(
        local, mesh=mesh, in_specs=placed, out_specs=P(("groups", "dp"), None), check_vma=False
    )
```

time: 85.4 us -> 75 us (0.88)
  waiting for transfers between devices: 3.55 us -> 17.5 us
  blocking collectives: 9.52 us -> 0 us
  Pallas kernels: 31.1 us -> 22.6 us
  local copies, waits for them, and re-layouts: 3.33 us -> 0.01 us
  starting transfers between devices: 22.3 us -> 20.5 us
    ppermute x0 -> x5, waiting for transfers between devices: none -> 10.7 us  [the longest x1 3.77 us: local_owned(): lax.ppermute(scores, 'tensor', [(1, 0), (2, 3)])]
    all_to_all x1 -> x0, blocking collectives: 9.52 us -> none  [exchange(): return lax.all_to_all(copies, axis, 0, 0, tiled=True)]
    pallas_call x5 -> x4, Pallas kernels: 30 us -> 22.2 us  [the longest x2 16.7 us: project(): pl.pallas_call(project_in_kernel if one else project_out_kernel, in_specs...]
    all_to_all x2 -> x0, starting transfers between devices: 6.56 us -> none  [exchange(): return lax.all_to_all(copies, axis, 0, 0, tiled=True)]
    ppermute x0 -> x5, starting transfers between devices: none -> 4.79 us  [the longest x2 1.54 us: swap(): lax.ppermute(value, axis, [(i, i ^ bit) for i in range(lax.axis_size(axis...]
    unnamed x6 -> x2, local copies, waits for them, and re-layouts: 2.82 us -> 0.01 us
    ppermute x2, waiting for transfers between devices: 1.93 us -> 4.51 us  [to_owner(): lax.ppermute(far, 'tensor', [(0, 2), (3, 1)])]
    ppermute x2, waiting for transfers between devices: 0.01 us -> 1.57 us  [to_owner(): lax.ppermute(near, 'tensor', [(0, 1), (3, 2)])]
  transfers between devices with their start and end apart: 9 -> 12, of which waited for: 2 -> 6; matrix products, arithmetic and copies ran while one was open for 0% -> 0% of each run, Pallas kernels for 33% -> 24%
where the time goes in v3:
time: 75 us; the launch traced here: 74.7 us
  Pallas kernels  22.6 us (30%)
  starting transfers between devices  20.5 us (27%)
  waiting for transfers between devices  17.5 us (23%)
  between operations  13.6 us (18%)
    pallas_call x2, Pallas kernels, project(): pl.pallas_call(project_in_kernel if one else project_out_kernel, in_specs...  16.7 us
    ppermute x2, starting transfers between devices, to_owner(): lax.ppermute(far, 'tensor', [(0, 2), (3, 1)])  7.97 us
    ppermute x2, starting transfers between devices, to_owner(): lax.ppermute(near, 'tensor', [(0, 1), (3, 2)])  6.36 us
    ppermute x2, waiting for transfers between devices, to_owner(): lax.ppermute(far, 'tensor', [(0, 2), (3, 1)])  4.51 us
    pallas_call x1, Pallas kernels, score(): pl.pallas_call(functools.partial(score_kernel, tokens), in_specs=[smem(),...  4.49 us
    ppermute x1, waiting for transfers between devices, local_owned(): lax.ppermute(scores, 'tensor', [(1, 0), (2, 3)])  3.77 us
    ppermute x2, waiting for transfers between devices, swap(): lax.ppermute(value, axis, [(i, i ^ bit) for i in range(lax.axis_size(axis...  3.64 us
    ppermute x1, waiting for transfers between devices, local_owned(): lax.ppermute(scores, 'tensor', [(2, 0), (1, 3)])  3.33 us
  transfers between devices with their start and end apart: 12, of which 6 were waited for; matrix products, arithmetic and copies ran while one was open for 0% of the time, Pallas kernels for 24%

profile of v3, /device:TPU:0, one launch (start us, length us, event | category | flops | bytes accessed | tf_op | source)
XLA Modules:
  0.0 74.7 jit_solution(8127722780470670234)
XLA Ops:
  6.5 0.0 copy-start
  6.5 0.0 all-gather.2.cloned.1.call-start
  6.5 0.7 all-gather.2.cloned.1.call-update
  7.3 4.9 %project_in.1 = (f32[64,1024]{1,0:T(8,128)S(1)}, f32[64,1024]{1,0:T(8,128)S(1)}) custom-call(s32[1]{0:T(128)} %bitcast.side_ref, bf16[4,256,2048]{2,1,0:T(8,128)(2,1)} %rows_hbm.2, bf16[2,64,2048]{2,1,0:T(8,128)(2,1)} %proj_hbm.2), custom_call_target="tpu_custom_call" | custom-call | tf_op jit(solution)/shard_map/project_in/pallas_call | solution.py:107
  12.2 4.9 %collective-permute-start = (f32[64,1024]{1,0:T(8,128)S(1)}, f32[64,1024]{1,0:T(8,128)S(1)}, u32[]{:S(2)}, u32[]{:S(2)}) collective-permute-start(f32[64,1024]{1,0:T(8,128)S(1)} %get-tuple-element.13.refs_0_), channel_id=1, source_target_pairs={{0,4},{12,8},{1,5},{13,9},{2,6},{14,10},{3,7},{15,11},{16,20},{28,... | collective-permute-start | bytes 786440 | tf_op jit(solution)/shard_map/ppermute | solution.py:127
  17.1 0.7 collective-permute-start.1
  17.8 4.0 %collective-permute-start.2 = (f32[64,1024]{1,0:T(8,128)S(1)}, f32[64,1024]{1,0:T(8,128)S(1)}, u32[]{:S(2)}, u32[]{:S(2)}) collective-permute-start(f32[64,1024]{1,0:T(8,128)S(1)} %get-tuple-element.14), channel_id=1, source_target_pairs={{0,8},{12,4},{1,9},{13,5},{2,10},{14,6},{3,11},{15,7},{16,24},{28,... | collective-permute-start | bytes 786440 | tf_op jit(solution)/shard_map/ppermute | solution.py:129
  21.8 0.0 copy-done
  21.8 11.8 %project_out.1 = (f32[64,1024]{1,0:T(8,128)S(1)}, f32[64,1024]{1,0:T(8,128)S(1)}) custom-call(s32[1]{0:T(128)} %bitcast.side_ref, bf16[2,4,256,7168]{3,2,1,0:T(8,128)(2,1)} %rows_hbm.3, bf16[2,64,7168]{2,1,0:T(8,128)(2,1)S(1)} %copy-done), custom_call_target="tpu_custom_call" | custom-call | tf_op jit(solution)/shard_map/project_out/pallas_call | solution.py:107
  33.6 1.4 %collective-permute-start.3 = (f32[64,1024]{1,0:T(8,128)S(1)}, f32[64,1024]{1,0:T(8,128)S(1)}, u32[]{:S(2)}, u32[]{:S(2)}) collective-permute-start(f32[64,1024]{1,0:T(8,128)S(1)} %get-tuple-element.17.refs_0_), channel_id=1, source_target_pairs={{0,4},{12,8},{1,5},{13,9},{2,6},{14,10},{3,7},{15,11},{16,20},{28,... | collective-permute-start | bytes 786440 | tf_op jit(solution)/shard_map/ppermute | solution.py:127
  35.0 0.7 collective-permute-start.4
  35.7 0.0 collective-permute-done.refs_1_
  35.7 4.0 %collective-permute-start.5 = (f32[64,1024]{1,0:T(8,128)S(1)}, f32[64,1024]{1,0:T(8,128)S(1)}, u32[]{:S(2)}, u32[]{:S(2)}) collective-permute-start(f32[64,1024]{1,0:T(8,128)S(1)} %get-tuple-element.18), channel_id=1, source_target_pairs={{0,8},{12,4},{1,9},{13,5},{2,10},{14,6},{3,11},{15,7},{16,24},{28,... | collective-permute-start | bytes 786440 | tf_op jit(solution)/shard_map/ppermute | solution.py:129
  39.7 0.0 collective-permute-done.1.refs_2_
  39.7 0.0 collective-permute-done.2.refs_3_
  39.8 0.4 cov_in.1
  40.2 1.6 %collective-permute-done.3.refs_1_ = f32[64,1024]{1,0:T(8,128)S(1)} collective-permute-done((f32[64,1024]{1,0:T(8,128)S(1)}, f32[64,1024]{1,0:T(8,128)S(1)}, u32[]{:S(2)}, u32[]{:S(2)}) %collective-permute-start.3) | collective-permute-done | bytes 262176 | tf_op jit(solution)/shard_map/ppermute | solution.py:127
  41.7 0.0 collective-permute-done.4.refs_2_
  41.7 4.5 %collective-permute-done.5.refs_3_ = f32[64,1024]{1,0:T(8,128)S(1)} collective-permute-done((f32[64,1024]{1,0:T(8,128)S(1)}, f32[64,1024]{1,0:T(8,128)S(1)}, u32[]{:S(2)}, u32[]{:S(2)}) %collective-permute-start.5) | collective-permute-done | bytes 262176 | tf_op jit(solution)/shard_map/ppermute | solution.py:129
  46.2 1.0 %cov_out.1 = (f32[64,128]{1,0:T(8,128)S(1)}, f32[4,64,128]{2,1,0:T(8,128)S(1)}) custom-call(f32[64,1024]{1,0:T(8,128)S(1)} %get-tuple-element.15.x_ref, f32[64,128]{1,0:T(8,128)S(1)} %get-tuple-element.16.cov_ref, f32[64,1024]{1,0:T(8,128)S(1)} %get-tuple-element.17.refs_0_, f32[64,1024]{1,0:T(8,128)S(1)} %collective-permute-done.3.refs_1_, ...), custom_call_target="tpu_custom_call" | custom-call | tf_op jit(solution)/shard_map/cov_out/pallas_call | solution.py:177
  47.2 0.1 collective-permute-start.6
  47.3 1.2 %collective-permute-done.6 = f32[64,128]{1,0:T(8,128)S(1)} collective-permute-done((f32[64,128]{1,0:T(8,128)S(1)}, f32[64,128]{1,0:T(8,128)S(1)}, u32[]{:S(2)}, u32[]{:S(2)}) %collective-permute-start.6) | collective-permute-done | bytes 32800 | tf_op jit(solution)/shard_map/ppermute | solution.py:305
  48.5 1.5 %collective-permute-start.7 = (f32[64,128]{1,0:T(8,128)S(1)}, f32[64,128]{1,0:T(8,128)S(1)}, u32[]{:S(2)}, u32[]{:S(2)}) collective-permute-start(f32[64,128]{1,0:T(8,128)S(1)} %add.12.own_ref), channel_id=1, source_target_pairs={{0,2},{1,3},{2,0},{3,1},{4,6},{5,7},{6,4},{7,5},{8,10},{9,11},{10,... | collective-permute-start | bytes 98312 | tf_op jit(solution)/shard_map/ppermute | solution.py:305
  50.0 2.4 %collective-permute-done.7.other_ref = f32[64,128]{1,0:T(8,128)S(1)} collective-permute-done((f32[64,128]{1,0:T(8,128)S(1)}, f32[64,128]{1,0:T(8,128)S(1)}, u32[]{:S(2)}, u32[]{:S(2)}) %collective-permute-start.7) | collective-permute-done | bytes 32800 | tf_op jit(solution)/shard_map/ppermute | solution.py:305
  52.4 0.0 all-gather.2.cloned.1.call-done.queries_hbm
  52.4 4.5 %score.1 = f32[4,64]{1,0:T(4,128)S(1)} custom-call(s32[1]{0:T(128)} %bitcast.side_ref, f32[64,128]{1,0:T(8,128)S(1)} %add.12.own_ref, f32[64,128]{1,0:T(8,128)S(1)} %collective-permute-done.7.other_ref, f32[4,64,128]{2,1,0:T(8,128)S(1)} %get-tuple-element.20.sample_ref, bf16[64,2,64,64]{3,2,1,0:T(8,128)(2,1)} %all-gather.2.cloned.1.call-done.queries_hbm), custom_call_target="tpu_custom_call" | custom-call | tf_op jit(solution)/shard_map/score/pallas_call | solution.py:289
  56.9 1.3 %collective-permute-start.10 = (f32[4,64]{1,0:T(4,128)S(1)}, f32[4,64]{1,0:T(4,128)S(1)}, u32[]{:S(2)}, u32[]{:S(2)}) collective-permute-start(f32[4,64]{1,0:T(4,128)S(1)} %score.1), channel_id=1, source_target_pairs={{8,0},{4,12},{9,1},{5,13},{10,2},{6,14},{11,3},{7,15},{24,16},{20,... | collective-permute-start | bytes 3080 | tf_op jit(solution)/shard_map/ppermute | solution.py:331
  58.2 0.7 collective-permute-start.8
  58.9 1.3 %collective-permute-start.9 = (f32[4,64]{1,0:T(4,128)S(1)}, f32[4,64]{1,0:T(4,128)S(1)}, u32[]{:S(2)}, u32[]{:S(2)}) collective-permute-start(f32[4,64]{1,0:T(4,128)S(1)} %score.1), channel_id=1, source_target_pairs={{4,0},{8,12},{5,1},{9,13},{6,2},{10,14},{7,3},{11,15},{20,16},{24,... | collective-permute-start | bytes 3080 | tf_op jit(solution)/shard_map/ppermute | solution.py:330
  60.2 3.3 %collective-permute-done.10 = f32[4,64]{1,0:T(4,128)S(1)} collective-permute-done((f32[4,64]{1,0:T(4,128)S(1)}, f32[4,64]{1,0:T(4,128)S(1)}, u32[]{:S(2)}, u32[]{:S(2)}) %collective-permute-start.10) | collective-permute-done | bytes 1056 | tf_op jit(solution)/shard_map/ppermute | solution.py:331
  63.5 0.0 collective-permute-done.8
  63.5 3.8 %collective-permute-done.9 = f32[4,64]{1,0:T(4,128)S(1)} collective-permute-done((f32[4,64]{1,0:T(4,128)S(1)}, f32[4,64]{1,0:T(4,128)S(1)}, u32[]{:S(2)}, u32[]{:S(2)}) %collective-permute-start.9) | collective-permute-done | bytes 1056 | tf_op jit(solution)/shard_map/ppermute | solution.py:330
  67.3 0.6 add_add_fusion
  (1 shorter events, 0.0 us)
Async XLA Ops:
  6.5 15.3 %copy-start = (bf16[2,64,7168]{2,1,0:T(8,128)(2,1)S(1)}, bf16[2,64,7168]{2,1,0:T(8,128)(2,1)}, u32[]{:S(2)}) copy-start(bf16[2,64,7168]{2,1,0:T(8,128)(2,1)} %proj_hbm.3) | copy-start | bytes 5505028
  6.5 45.9 %all-gather.2.cloned.1.call-start = ((), (), s32[]{:S(2)}) async-start(), calls=%async_computation | async-start | bytes 2621440 | tf_op jit(solution)/shard_map/all_gather | solution.py:314
  12.2 23.5 %collective-permute-start = (f32[64,1024]{1,0:T(8,128)S(1)}, f32[64,1024]{1,0:T(8,128)S(1)}, u32[]{:S(2)}, u32[]{:S(2)}) collective-permute-start(f32[64,1024]{1,0:T(8,128)S(1)} %get-tuple-element.13.refs_0_), channel_id=1, source_target_pairs={{0,4},{12,8},{1,5},{13,9},{2,6},{14,10},{3,7},{15,11},{16,20},{28,... | collective-permute-start | bytes 786440 | tf_op jit(solution)/shard_map/ppermute | solution.py:127
  17.1 22.6 %collective-permute-start.1 = (f32[64,1024]{1,0:T(8,128)S(1)}, f32[64,1024]{1,0:T(8,128)S(1)}, u32[]{:S(2)}, u32[]{:S(2)}) collective-permute-start(f32[64,1024]{1,0:T(8,128)S(1)} %get-tuple-element.14), channel_id=1, source_target_pairs={{4,8},{8,4},{5,9},{9,5},{6,10},{10,6},{7,11},{11,7},{20,24},{24,20... | collective-permute-start | bytes 786440 | tf_op jit(solution)/shard_map/ppermute | solution.py:128
  17.8 21.9 %collective-permute-start.2 = (f32[64,1024]{1,0:T(8,128)S(1)}, f32[64,1024]{1,0:T(8,128)S(1)}, u32[]{:S(2)}, u32[]{:S(2)}) collective-permute-start(f32[64,1024]{1,0:T(8,128)S(1)} %get-tuple-element.14), channel_id=1, source_target_pairs={{0,8},{12,4},{1,9},{13,5},{2,10},{14,6},{3,11},{15,7},{16,24},{28,... | collective-permute-start | bytes 786440 | tf_op jit(solution)/shard_map/ppermute | solution.py:129
  33.6 8.1 %collective-permute-start.3 = (f32[64,1024]{1,0:T(8,128)S(1)}, f32[64,1024]{1,0:T(8,128)S(1)}, u32[]{:S(2)}, u32[]{:S(2)}) collective-permute-start(f32[64,1024]{1,0:T(8,128)S(1)} %get-tuple-element.17.refs_0_), channel_id=1, source_target_pairs={{0,4},{12,8},{1,5},{13,9},{2,6},{14,10},{3,7},{15,11},{16,20},{28,... | collective-permute-start | bytes 786440 | tf_op jit(solution)/shard_map/ppermute | solution.py:127
  35.0 6.7 %collective-permute-start.4 = (f32[64,1024]{1,0:T(8,128)S(1)}, f32[64,1024]{1,0:T(8,128)S(1)}, u32[]{:S(2)}, u32[]{:S(2)}) collective-permute-start(f32[64,1024]{1,0:T(8,128)S(1)} %get-tuple-element.18), channel_id=1, source_target_pairs={{4,8},{8,4},{5,9},{9,5},{6,10},{10,6},{7,11},{11,7},{20,24},{24,20... | collective-permute-start | bytes 786440 | tf_op jit(solution)/shard_map/ppermute | solution.py:128
  35.7 10.5 %collective-permute-start.5 = (f32[64,1024]{1,0:T(8,128)S(1)}, f32[64,1024]{1,0:T(8,128)S(1)}, u32[]{:S(2)}, u32[]{:S(2)}) collective-permute-start(f32[64,1024]{1,0:T(8,128)S(1)} %get-tuple-element.18), channel_id=1, source_target_pairs={{0,8},{12,4},{1,9},{13,5},{2,10},{14,6},{3,11},{15,7},{16,24},{28,... | collective-permute-start | bytes 786440 | tf_op jit(solution)/shard_map/ppermute | solution.py:129
  47.2 1.3 %collective-permute-start.6 = (f32[64,128]{1,0:T(8,128)S(1)}, f32[64,128]{1,0:T(8,128)S(1)}, u32[]{:S(2)}, u32[]{:S(2)}) collective-permute-start(f32[64,128]{1,0:T(8,128)S(1)} %get-tuple-element.19), channel_id=1, source_target_pairs={{0,1},{1,0},{2,3},{3,2},{4,5},{5,4},{6,7},{7,6},{8,9},{9,8},{10,11... | collective-permute-start | bytes 98312 | tf_op jit(solution)/shard_map/ppermute | solution.py:305
  48.5 3.9 %collective-permute-start.7 = (f32[64,128]{1,0:T(8,128)S(1)}, f32[64,128]{1,0:T(8,128)S(1)}, u32[]{:S(2)}, u32[]{:S(2)}) collective-permute-start(f32[64,128]{1,0:T(8,128)S(1)} %add.12.own_ref), channel_id=1, source_target_pairs={{0,2},{1,3},{2,0},{3,1},{4,6},{5,7},{6,4},{7,5},{8,10},{9,11},{10,... | collective-permute-start | bytes 98312 | tf_op jit(solution)/shard_map/ppermute | solution.py:305
  56.9 6.6 %collective-permute-start.10 = (f32[4,64]{1,0:T(4,128)S(1)}, f32[4,64]{1,0:T(4,128)S(1)}, u32[]{:S(2)}, u32[]{:S(2)}) collective-permute-start(f32[4,64]{1,0:T(4,128)S(1)} %score.1), channel_id=1, source_target_pairs={{8,0},{4,12},{9,1},{5,13},{10,2},{6,14},{11,3},{7,15},{24,16},{20,... | collective-permute-start | bytes 3080 | tf_op jit(solution)/shard_map/ppermute | solution.py:331
  58.2 5.3 %collective-permute-start.8 = (f32[4,64]{1,0:T(4,128)S(1)}, f32[4,64]{1,0:T(4,128)S(1)}, u32[]{:S(2)}, u32[]{:S(2)}) collective-permute-start(f32[4,64]{1,0:T(4,128)S(1)} %score.1), channel_id=1, source_target_pairs={{4,8},{8,4},{5,9},{9,5},{6,10},{10,6},{7,11},{11,7},{20,24},{24,20... | collective-permute-start | bytes 3080 | tf_op jit(solution)/shard_map/ppermute | solution.py:329
  58.9 8.4 %collective-permute-start.9 = (f32[4,64]{1,0:T(4,128)S(1)}, f32[4,64]{1,0:T(4,128)S(1)}, u32[]{:S(2)}, u32[]{:S(2)}) collective-permute-start(f32[4,64]{1,0:T(4,128)S(1)} %score.1), channel_id=1, source_target_pairs={{4,0},{8,12},{5,1},{9,13},{6,2},{10,14},{7,3},{11,15},{20,16},{24,... | collective-permute-start | bytes 3080 | tf_op jit(solution)/shard_map/ppermute | solution.py:330
Sparse Core Ops, SparseCore 0:
  8.9 25.2 all-gather.1

commit v4 on v3

--- a/solution.py
+++ b/solution.py
@@ -124,9 +124,9 @@
 def to_owner(near, far):
     return [
         near,
+        lax.ppermute(far, "tensor", [(0, 2), (3, 1)]),
+        lax.ppermute(far, "tensor", [(1, 2), (2, 1)]),
         lax.ppermute(near, "tensor", [(0, 1), (3, 2)]),
-        lax.ppermute(far, "tensor", [(1, 2), (2, 1)]),
-        lax.ppermute(far, "tensor", [(0, 2), (3, 1)]),
     ]
 
 
@@ -137,26 +137,39 @@
     return value
 
 
-def cov_in_kernel(*refs):
-    pieces, (x_out, cov_out) = refs[:-2], refs[-2:]
+def cov_in_kernel(side_ref, queries_hbm, *refs):
+    pieces, (x_out, cov_out, packed_out, held, sem) = refs[:-5], refs[-5:]
+    copy = pltpu.make_async_copy(queries_hbm.at[:, side_ref[0]], held, sem)
+    copy.start()
     x = total(pieces)
     x_out[...] = x
     cov_out[...] = nt(x, jnp.concatenate([x, jnp.zeros_like(x)], axis=0), HIGHEST)
-
-
-def cov_in(pieces):
+    copy.wait()
+    half = held.shape[0] // 2
+    for k in range(half):
+        pair = [held[k].astype(jnp.float32), held[k + half].astype(jnp.float32)]
+        packed_out[k] = jnp.concatenate(pair, axis=1).astype(packed_out.dtype)
+
+
+def cov_in(side, queries, pieces):
     rank, tokens = pieces[0].shape
+    count = queries.shape[0]
     return pl.pallas_call(
         cov_in_kernel,
-        in_specs=[vmem()] * len(pieces),
-        out_specs=[vmem()] * 2,
+        in_specs=[smem(), hbm()] + [vmem()] * len(pieces),
+        out_specs=[vmem()] * 3,
         out_shape=[
             jax.ShapeDtypeStruct((rank, tokens), jnp.float32),
             jax.ShapeDtypeStruct((rank, 2 * rank), jnp.float32),
+            jax.ShapeDtypeStruct((count // 2, rank, 2 * rank), queries.dtype),
+        ],
+        scratch_shapes=[
+            pltpu.VMEM((count, rank, rank), queries.dtype),
+            pltpu.SemaphoreType.DMA,
         ],
         compiler_params=params(16),
         name="cov_in",
-    )(*pieces)
+    )(side, in_hbm(queries), *pieces)
 
 
 def cov_out_kernel(x_ref, cov_ref, *refs):
@@ -232,33 +245,47 @@
     return high, middle, low
 
 
-def score_kernel(tokens, side_ref, own_ref, other_ref, sample_ref, queries_hbm, out, held, half, sem):
-    copy = pltpu.make_async_copy(queries_hbm.at[:, side_ref[0]], held, sem)
-    copy.start()
+def score_kernel(tokens, place_ref, own_ref, other_ref, sample_ref, *refs):
+    pieces, (out, held, half) = refs[:-3], refs[-3:]
+    parts = len(pieces)
+    for k, piece in enumerate(pieces):
+        held[place_ref[0] ^ k] = piece[...]
     inverses = damped_inverses((own_ref[...] + other_ref[...]) / tokens)
     both = inverses.shape[0]
     size = both // 2
-    count = held.shape[0]
     seqs = sample_ref.shape[0]
-    pairs = count // 2
+    blocks = held.shape[1]
+    pairs = parts * blocks
     first = jnp.concatenate(split(inverses[:size, :size]), axis=0)
+    none = jnp.zeros_like(first)
+    first = jnp.concatenate(
+        [jnp.concatenate([first, none], axis=1), jnp.concatenate([none, first], axis=1)], axis=0
+    )
     right = inverses[size:]
     twice = jnp.concatenate([pltpu.roll(right, size, 1), right], axis=0)
     high, middle, _ = split(twice)
     once = jnp.concatenate([high, middle], axis=1)
     second = jnp.concatenate([once, once], axis=0)
-    copy.wait()
-    group = 4
-    for block in range(count // group):
-        start = block * group // 2
-        places = [start, start + pairs, start + 1, start + 1 + pairs]
-        rows = jnp.concatenate([held[place] for place in places], axis=0)
-        result = nt(first, rows)
-        result = result[:size] + result[size : 2 * size] + result[2 * size :]
-        high, middle, _ = split(result)
-        lanes = slice(block * group * size, (block + 1) * group * size)
-        half[0, :, lanes] = high
-        half[1, :, lanes] = middle
+    for part in range(parts // 2):
+        for block in range(0, blocks, 2):
+            rows = jnp.concatenate(
+                [
+                    held[part, block],
+                    held[part + parts // 2, block],
+                    held[part, block + 1],
+                    held[part + parts // 2, block + 1],
+                ],
+                axis=0,
+            )
+            result = nt(first, rows)
+            for k in range(2):
+                three = result[3 * size * k : 3 * size * (k + 1)]
+                value = three[:size] + three[size : 2 * size] + three[2 * size :]
+                high, middle, _ = split(value)
+                pair = (2 * part + k) * blocks + block
+                lanes = slice(pair * both, (pair + 2) * both)
+                half[0, :, lanes] = high
+                half[1, :, lanes] = middle
     samples = [sample_ref[s] for s in range(seqs)]
     lines = [[] for _ in range(seqs)]
     for pair in range(pairs):
@@ -284,21 +311,22 @@
             ]
 
 
-def score(side, own, other, sample, queries, tokens):
-    count, _, rank, _ = queries.shape
+def score(place, own, other, sample, pieces, tokens):
+    blocks, rank, both = pieces[0].shape
+    parts = len(pieces)
+    count = 2 * parts * blocks
     return pl.pallas_call(
         functools.partial(score_kernel, tokens),
-        in_specs=[smem(), vmem(), vmem(), vmem(), hbm()],
+        in_specs=[smem()] + [vmem()] * (3 + parts),
         out_specs=vmem(),
         out_shape=jax.ShapeDtypeStruct((sample.shape[0], count), jnp.float32),
         scratch_shapes=[
-            pltpu.VMEM((count, rank, rank), queries.dtype),
+            pltpu.VMEM((parts, blocks, rank, both), pieces[0].dtype),
             pltpu.VMEM((2, rank, count * rank), jnp.bfloat16),
-            pltpu.SemaphoreType.DMA,
         ],
         compiler_params=params(16),
         name="score",
-    )(side, own, other, sample, in_hbm(queries))
+    )(place, own, other, sample, *pieces)
 
 
 def swap(value, axis, bit):
@@ -309,12 +337,14 @@
     seqs, length, _ = acts.shape
     parts = lax.axis_size("dp")
     tokens = seqs * length * parts
-    place = lax.axis_index("tensor").astype(jnp.int32)
-    side = (place >= 2).astype(jnp.int32).reshape(1)
-    all_queries = lax.all_gather(queries, "dp", axis=0, tiled=True)
+    across = lax.axis_index("tensor").astype(jnp.int32)
+    side = (across >= 2).astype(jnp.int32)
+    side = side.reshape(1)
+    place = lax.axis_index("dp").astype(jnp.int32).reshape(1)
     x_pieces = to_owner(*project(side, acts, proj_in, 16))
     g_pieces = to_owner(*project(side, grads, proj_out, 40))
-    x, cov = cov_in(x_pieces)
+    x, cov, packed = cov_in(side, queries, x_pieces)
+    query_pieces = [packed] + [swap(packed, "dp", bits) for bits in range(1, parts)]
     cov, sample = cov_out(x, cov, g_pieces, seqs)
     other = jnp.zeros_like(cov)
     bit = 1
@@ -322,14 +352,10 @@
         cov = cov if bit == 1 else cov + other
         other = swap(cov, "dp", bit)
         bit *= 2
-    scores = score(side, cov, other, sample, all_queries, tokens)
-    owner = (place == 1) | (place == 2)
-    return (
-        jnp.where(owner, scores, 0.0)
-        + lax.ppermute(scores, "tensor", [(1, 2), (2, 1)])
-        + lax.ppermute(scores, "tensor", [(1, 0), (2, 3)])
-        + lax.ppermute(scores, "tensor", [(2, 0), (1, 3)])
-    )
+    scores = score(place, cov, other, sample, query_pieces, tokens)
+    scores = scores + lax.ppermute(scores, "tensor", [(1, 2), (2, 1)])
+    outer = lax.ppermute(scores, "tensor", [(1, 0), (2, 3)])
+    return jnp.where((across == 1) | (across == 2), scores, outer)
 
 
 def damp(matrix):
@@ -398,7 +424,8 @@
 
 def local(acts, grads, proj_in, proj_out, queries):
     parts = lax.axis_size("dp")
-    if lax.axis_size("tensor") == 4 and parts & (parts - 1) == 0:
+    blocks = queries.shape[0]
+    if lax.axis_size("tensor") == 4 and parts > 1 and parts & (parts - 1) == 0 and blocks % 4 == 0:
         return local_owned(acts, grads, proj_in, proj_out, queries)
     return local_general(acts, grads, proj_in, proj_out, queries)
 

time: 75 us -> 61.9 us (0.83)
  between operations: 13.6 us -> 0.17 us
  waiting for transfers between devices: 17.5 us -> 16.2 us
  starting transfers between devices: 20.5 us -> 21.4 us
    ppermute x2, waiting for transfers between devices: 4.51 us -> 0.22 us  [to_owner(): lax.ppermute(far, 'tensor', [(0, 2), (3, 1)])]
    ppermute x2 -> x5, starting transfers between devices: 1.54 us -> 4.72 us  [swap(): lax.ppermute(value, axis, [(i, i ^ bit) for i in range(lax.axis_size(axis...]
    ppermute x3 -> x2, waiting for transfers between devices: 7.11 us -> 9.63 us  [the longest x1 9.63 us: local_owned(): outer = lax.ppermute(scores, 'tensor', [(1, 0), (2, 3)])]
    ppermute x3 -> x2, starting transfers between devices: 3.25 us -> 1.98 us  [the longest x1 1.29 us: local_owned(): outer = lax.ppermute(scores, 'tensor', [(1, 0), (2, 3)])]
    ppermute x2, waiting for transfers between devices: 1.57 us -> 2.66 us  [to_owner(): lax.ppermute(near, 'tensor', [(0, 1), (3, 2)])]
    ppermute x2 -> x5, waiting for transfers between devices: 3.64 us -> 3.63 us  [swap(): lax.ppermute(value, axis, [(i, i ^ bit) for i in range(lax.axis_size(axis...]
  transfers between devices with their start and end apart: 12 -> 13, of which waited for: 6 -> 5; matrix products, arithmetic and copies ran while one was open for 0% -> 0% of each run, Pallas kernels for 24% -> 23%
where the time goes in v4:
time: 61.9 us; the launch traced here: 61.6 us
  Pallas kernels  23.3 us (38%)
  starting transfers between devices  21.4 us (35%)
  waiting for transfers between devices  16.2 us (26%)
    pallas_call x2, Pallas kernels, project(): pl.pallas_call(project_in_kernel if one else project_out_kernel, in_specs...  16.8 us
    ppermute x1, waiting for transfers between devices, local_owned(): outer = lax.ppermute(scores, 'tensor', [(1, 0), (2, 3)])  9.63 us
    ppermute x2, starting transfers between devices, to_owner(): lax.ppermute(far, 'tensor', [(0, 2), (3, 1)])  7.26 us
    ppermute x2, starting transfers between devices, to_owner(): lax.ppermute(near, 'tensor', [(0, 1), (3, 2)])  6.04 us
    ppermute x5, starting transfers between devices, swap(): lax.ppermute(value, axis, [(i, i ^ bit) for i in range(lax.axis_size(axis...  4.72 us
    pallas_call x1, Pallas kernels, score(): pl.pallas_call(functools.partial(score_kernel, tokens), in_specs=[smem()]...  4.36 us
    ppermute x5, waiting for transfers between devices, swap(): lax.ppermute(value, axis, [(i, i ^ bit) for i in range(lax.axis_size(axis...  3.63 us
    ppermute x2, waiting for transfers between devices, to_owner(): lax.ppermute(near, 'tensor', [(0, 1), (3, 2)])  2.66 us
  transfers between devices with their start and end apart: 13, of which 5 were waited for; matrix products, arithmetic and copies ran while one was open for 0% of the time, Pallas kernels for 23%

profile of v4, /device:TPU:0, one launch (start us, length us, event | category | flops | bytes accessed | tf_op | source)
XLA Modules:
  0.0 61.6 jit_solution(9376419950058152761)
XLA Ops:
  0.0 0.0 copy-start
  0.0 5.1 %project_in.1 = (f32[64,1024]{1,0:T(8,128)S(1)}, f32[64,1024]{1,0:T(8,128)S(1)}) custom-call(s32[1]{0:T(128)} %bitcast.1.side_ref, bf16[4,256,2048]{2,1,0:T(8,128)(2,1)} %rows_hbm.2, bf16[2,64,2048]{2,1,0:T(8,128)(2,1)} %proj_hbm.2), custom_call_target="tpu_custom_call" | custom-call | tf_op jit(solution)/shard_map/project_in/pallas_call | solution.py:107
  5.1 6.0 %collective-permute-start = (f32[64,1024]{1,0:T(8,128)S(1)}, f32[64,1024]{1,0:T(8,128)S(1)}, u32[]{:S(2)}, u32[]{:S(2)}) collective-permute-start(f32[64,1024]{1,0:T(8,128)S(1)} %get-tuple-element.15), channel_id=1, source_target_pairs={{0,8},{12,4},{1,9},{13,5},{2,10},{14,6},{3,11},{15,7},{16,24},{28,... | collective-permute-start | bytes 786440 | tf_op jit(solution)/shard_map/ppermute | solution.py:127
  11.0 0.7 %collective-permute-start.1 = (f32[64,1024]{1,0:T(8,128)S(1)}, f32[64,1024]{1,0:T(8,128)S(1)}, u32[]{:S(2)}, u32[]{:S(2)}) collective-permute-start(f32[64,1024]{1,0:T(8,128)S(1)} %get-tuple-element.15), channel_id=1, source_target_pairs={{4,8},{8,4},{5,9},{9,5},{6,10},{10,6},{7,11},{11,7},{20,24},{24,20... | collective-permute-start | bytes 786440 | tf_op jit(solution)/shard_map/ppermute | solution.py:128
  11.7 3.1 %collective-permute-start.2 = (f32[64,1024]{1,0:T(8,128)S(1)}, f32[64,1024]{1,0:T(8,128)S(1)}, u32[]{:S(2)}, u32[]{:S(2)}) collective-permute-start(f32[64,1024]{1,0:T(8,128)S(1)} %get-tuple-element.14.refs_0_), channel_id=1, source_target_pairs={{0,4},{12,8},{1,5},{13,9},{2,6},{14,10},{3,7},{15,11},{16,20},{28,... | collective-permute-start | bytes 786440 | tf_op jit(solution)/shard_map/ppermute | solution.py:129
  14.8 0.0 copy-done
  14.8 11.8 %project_out.1 = (f32[64,1024]{1,0:T(8,128)S(1)}, f32[64,1024]{1,0:T(8,128)S(1)}) custom-call(s32[1]{0:T(128)} %bitcast.1.side_ref, bf16[2,4,256,7168]{3,2,1,0:T(8,128)(2,1)} %rows_hbm.3, bf16[2,64,7168]{2,1,0:T(8,128)(2,1)S(1)} %copy-done), custom_call_target="tpu_custom_call" | custom-call | tf_op jit(solution)/shard_map/project_out/pallas_call | solution.py:107
  26.6 1.3 %collective-permute-start.3 = (f32[64,1024]{1,0:T(8,128)S(1)}, f32[64,1024]{1,0:T(8,128)S(1)}, u32[]{:S(2)}, u32[]{:S(2)}) collective-permute-start(f32[64,1024]{1,0:T(8,128)S(1)} %get-tuple-element.19), channel_id=1, source_target_pairs={{0,8},{12,4},{1,9},{13,5},{2,10},{14,6},{3,11},{15,7},{16,24},{28,... | collective-permute-start | bytes 786440 | tf_op jit(solution)/shard_map/ppermute | solution.py:127
  27.9 0.7 %collective-permute-start.4 = (f32[64,1024]{1,0:T(8,128)S(1)}, f32[64,1024]{1,0:T(8,128)S(1)}, u32[]{:S(2)}, u32[]{:S(2)}) collective-permute-start(f32[64,1024]{1,0:T(8,128)S(1)} %get-tuple-element.19), channel_id=1, source_target_pairs={{4,8},{8,4},{5,9},{9,5},{6,10},{10,6},{7,11},{11,7},{20,24},{24,20... | collective-permute-start | bytes 786440 | tf_op jit(solution)/shard_map/ppermute | solution.py:128
  28.6 0.0 collective-permute-done.refs_1_
  28.6 3.0 %collective-permute-start.5 = (f32[64,1024]{1,0:T(8,128)S(1)}, f32[64,1024]{1,0:T(8,128)S(1)}, u32[]{:S(2)}, u32[]{:S(2)}) collective-permute-start(f32[64,1024]{1,0:T(8,128)S(1)} %get-tuple-element.18.refs_0_), channel_id=1, source_target_pairs={{0,4},{12,8},{1,5},{13,9},{2,6},{14,10},{3,7},{15,11},{16,20},{28,... | collective-permute-start | bytes 786440 | tf_op jit(solution)/shard_map/ppermute | solution.py:129
  31.6 0.0 collective-permute-done.1.refs_2_
  31.6 0.0 collective-permute-done.2.refs_3_
  31.6 1.2 %cov_in.1 = (f32[64,1024]{1,0:T(8,128)S(1)}, f32[64,128]{1,0:T(8,128)S(1)}, bf16[8,64,128]{2,1,0:T(8,128)(2,1)S(1)}) custom-call(s32[1]{0:T(128)} %bitcast.1.side_ref, bf16[16,2,64,64]{3,2,1,0:T(8,128)(2,1)} %queries_hbm.1, f32[64,1024]{1,0:T(8,128)S(1)} %get-tuple-element.14.refs_0_, f32[64,1024]{1,0:T(8,128)S(1)} %collective-permute-done.refs_1_, ...), custom_call_target="tpu_custom_call" | custom-call | tf_op jit(solution)/shard_map/cov_in/pallas_call | solution.py:157
  32.8 0.2 collective-permute-start.10
  32.9 1.5 %collective-permute-start.8 = (bf16[8,64,128]{2,1,0:T(8,128)(2,1)S(1)}, bf16[8,64,128]{2,1,0:T(8,128)(2,1)S(1)}, u32[]{:S(2)}, u32[]{:S(2)}) collective-permute-start(bf16[8,64,128]{2,1,0:T(8,128)(2,1)S(1)} %get-tuple-element.22.refs_0_), channel_id=1, source_target_pairs={{0,1},{1,0},{2,3},{3,2},{4,5},{5,4},{6,7},{7,6},{8,9},{9,8},{10,11... | collective-permute-start | bytes 393224 | tf_op jit(solution)/shard_map/ppermute | solution.py:333
  34.5 0.2 collective-permute-done.3.refs_1_
  34.7 1.5 %collective-permute-start.9 = (bf16[8,64,128]{2,1,0:T(8,128)(2,1)S(1)}, bf16[8,64,128]{2,1,0:T(8,128)(2,1)S(1)}, u32[]{:S(2)}, u32[]{:S(2)}) collective-permute-start(bf16[8,64,128]{2,1,0:T(8,128)(2,1)S(1)} %get-tuple-element.22.refs_0_), channel_id=1, source_target_pairs={{0,2},{1,3},{2,0},{3,1},{4,6},{5,7},{6,4},{7,5},{8,10},{9,11},{10,... | collective-permute-start | bytes 393224 | tf_op jit(solution)/shard_map/ppermute | solution.py:333
  36.2 0.0 collective-permute-done.4.refs_2_
  36.2 2.7 %collective-permute-done.5.refs_3_ = f32[64,1024]{1,0:T(8,128)S(1)} collective-permute-done((f32[64,1024]{1,0:T(8,128)S(1)}, f32[64,1024]{1,0:T(8,128)S(1)}, u32[]{:S(2)}, u32[]{:S(2)}) %collective-permute-start.5) | collective-permute-done | bytes 262176 | tf_op jit(solution)/shard_map/ppermute | solution.py:129
  38.8 1.0 %cov_out.1 = (f32[64,128]{1,0:T(8,128)S(1)}, f32[4,64,128]{2,1,0:T(8,128)S(1)}) custom-call(f32[64,1024]{1,0:T(8,128)S(1)} %get-tuple-element.16.x_ref, f32[64,128]{1,0:T(8,128)S(1)} %get-tuple-element.17.cov_ref, f32[64,1024]{1,0:T(8,128)S(1)} %get-tuple-element.18.refs_0_, f32[64,1024]{1,0:T(8,128)S(1)} %collective-permute-done.3.refs_1_, ...), custom_call_target="tpu_custom_call" | custom-call | tf_op jit(solution)/shard_map/cov_out/pallas_call | solution.py:190
  39.8 0.1 collective-permute-start.6
  39.9 1.2 %collective-permute-done.6 = f32[64,128]{1,0:T(8,128)S(1)} collective-permute-done((f32[64,128]{1,0:T(8,128)S(1)}, f32[64,128]{1,0:T(8,128)S(1)}, u32[]{:S(2)}, u32[]{:S(2)}) %collective-permute-start.6) | collective-permute-done | bytes 32800 | tf_op jit(solution)/shard_map/ppermute | solution.py:333
  41.1 1.5 %collective-permute-start.7 = (f32[64,128]{1,0:T(8,128)S(1)}, f32[64,128]{1,0:T(8,128)S(1)}, u32[]{:S(2)}, u32[]{:S(2)}) collective-permute-start(f32[64,128]{1,0:T(8,128)S(1)} %add.6.own_ref), channel_id=1, source_target_pairs={{0,2},{1,3},{2,0},{3,1},{4,6},{5,7},{6,4},{7,5},{8,10},{9,11},{10,... | collective-permute-start | bytes 98312 | tf_op jit(solution)/shard_map/ppermute | solution.py:333
  42.6 2.4 %collective-permute-done.7.other_ref = f32[64,128]{1,0:T(8,128)S(1)} collective-permute-done((f32[64,128]{1,0:T(8,128)S(1)}, f32[64,128]{1,0:T(8,128)S(1)}, u32[]{:S(2)}, u32[]{:S(2)}) %collective-permute-start.7) | collective-permute-done | bytes 32800 | tf_op jit(solution)/shard_map/ppermute | solution.py:333
  45.0 0.0 collective-permute-done.10.refs_3_
  45.0 0.0 collective-permute-done.8.refs_1_
  45.0 0.0 collective-permute-done.9.refs_2_
  45.0 4.4 %score.1 = f32[4,64]{1,0:T(4,128)S(1)} custom-call(s32[1]{0:T(128)} %bitcast.place_ref, f32[64,128]{1,0:T(8,128)S(1)} %add.6.own_ref, f32[64,128]{1,0:T(8,128)S(1)} %collective-permute-done.7.other_ref, f32[4,64,128]{2,1,0:T(8,128)S(1)} %get-tuple-element.21.sample_ref, bf16[8,64,128]{2,1,0:T(8,128)(2,1)S(1)} %get-tuple-element.22.refs_0_, ...), custom_call_target="tpu_custom_call" | custom-call | tf_op jit(solution)/shard_map/score/pallas_call | solution.py:318
  49.4 0.7 %collective-permute-start.11 = (f32[4,64]{1,0:T(4,128)S(1)}, f32[4,64]{1,0:T(4,128)S(1)}, u32[]{:S(2)}, u32[]{:S(2)}) collective-permute-start(f32[4,64]{1,0:T(4,128)S(1)} %score.1), channel_id=1, source_target_pairs={{4,8},{8,4},{5,9},{9,5},{6,10},{10,6},{7,11},{11,7},{20,24},{24,20... | collective-permute-start | bytes 3080 | tf_op jit(solution)/shard_map/ppermute | solution.py:356
  50.1 0.0 collective-permute-done.11
  50.1 1.3 %collective-permute-start.12 = (f32[4,64]{1,0:T(4,128)S(1)}, f32[4,64]{1,0:T(4,128)S(1)}, u32[]{:S(2)}, u32[]{:S(2)}) collective-permute-start(f32[4,64]{1,0:T(4,128)S(1)} %add.7), channel_id=1, source_target_pairs={{4,0},{8,12},{5,1},{9,13},{6,2},{10,14},{7,3},{11,15},{20,16},{24,... | collective-permute-start | bytes 3080 | tf_op jit(solution)/shard_map/ppermute | solution.py:357
  51.4 9.6 %collective-permute-done.12 = f32[4,64]{1,0:T(4,128)S(1)} collective-permute-done((f32[4,64]{1,0:T(4,128)S(1)}, f32[4,64]{1,0:T(4,128)S(1)}, u32[]{:S(2)}, u32[]{:S(2)}) %collective-permute-start.12) | collective-permute-done | bytes 1056 | tf_op jit(solution)/shard_map/ppermute | solution.py:357
  61.0 0.6 broadcast_select_fusion
  (2 shorter events, 0.0 us)
Async XLA Ops:
  0.0 14.8 %copy-start = (bf16[2,64,7168]{2,1,0:T(8,128)(2,1)S(1)}, bf16[2,64,7168]{2,1,0:T(8,128)(2,1)}, u32[]{:S(2)}) copy-start(bf16[2,64,7168]{2,1,0:T(8,128)(2,1)} %proj_hbm.3) | copy-start | bytes 5505028
  5.1 23.5 %collective-permute-start = (f32[64,1024]{1,0:T(8,128)S(1)}, f32[64,1024]{1,0:T(8,128)S(1)}, u32[]{:S(2)}, u32[]{:S(2)}) collective-permute-start(f32[64,1024]{1,0:T(8,128)S(1)} %get-tuple-element.15), channel_id=1, source_target_pairs={{0,8},{12,4},{1,9},{13,5},{2,10},{14,6},{3,11},{15,7},{16,24},{28,... | collective-permute-start | bytes 786440 | tf_op jit(solution)/shard_map/ppermute | solution.py:127
  11.0 20.6 %collective-permute-start.1 = (f32[64,1024]{1,0:T(8,128)S(1)}, f32[64,1024]{1,0:T(8,128)S(1)}, u32[]{:S(2)}, u32[]{:S(2)}) collective-permute-start(f32[64,1024]{1,0:T(8,128)S(1)} %get-tuple-element.15), channel_id=1, source_target_pairs={{4,8},{8,4},{5,9},{9,5},{6,10},{10,6},{7,11},{11,7},{20,24},{24,20... | collective-permute-start | bytes 786440 | tf_op jit(solution)/shard_map/ppermute | solution.py:128
  11.7 19.9 %collective-permute-start.2 = (f32[64,1024]{1,0:T(8,128)S(1)}, f32[64,1024]{1,0:T(8,128)S(1)}, u32[]{:S(2)}, u32[]{:S(2)}) collective-permute-start(f32[64,1024]{1,0:T(8,128)S(1)} %get-tuple-element.14.refs_0_), channel_id=1, source_target_pairs={{0,4},{12,8},{1,5},{13,9},{2,6},{14,10},{3,7},{15,11},{16,20},{28,... | collective-permute-start | bytes 786440 | tf_op jit(solution)/shard_map/ppermute | solution.py:129
  26.6 8.1 %collective-permute-start.3 = (f32[64,1024]{1,0:T(8,128)S(1)}, f32[64,1024]{1,0:T(8,128)S(1)}, u32[]{:S(2)}, u32[]{:S(2)}) collective-permute-start(f32[64,1024]{1,0:T(8,128)S(1)} %get-tuple-element.19), channel_id=1, source_target_pairs={{0,8},{12,4},{1,9},{13,5},{2,10},{14,6},{3,11},{15,7},{16,24},{28,... | collective-permute-start | bytes 786440 | tf_op jit(solution)/shard_map/ppermute | solution.py:127
  27.9 8.3 %collective-permute-start.4 = (f32[64,1024]{1,0:T(8,128)S(1)}, f32[64,1024]{1,0:T(8,128)S(1)}, u32[]{:S(2)}, u32[]{:S(2)}) collective-permute-start(f32[64,1024]{1,0:T(8,128)S(1)} %get-tuple-element.19), channel_id=1, source_target_pairs={{4,8},{8,4},{5,9},{9,5},{6,10},{10,6},{7,11},{11,7},{20,24},{24,20... | collective-permute-start | bytes 786440 | tf_op jit(solution)/shard_map/ppermute | solution.py:128
  28.6 10.2 %collective-permute-start.5 = (f32[64,1024]{1,0:T(8,128)S(1)}, f32[64,1024]{1,0:T(8,128)S(1)}, u32[]{:S(2)}, u32[]{:S(2)}) collective-permute-start(f32[64,1024]{1,0:T(8,128)S(1)} %get-tuple-element.18.refs_0_), channel_id=1, source_target_pairs={{0,4},{12,8},{1,5},{13,9},{2,6},{14,10},{3,7},{15,11},{16,20},{28,... | collective-permute-start | bytes 786440 | tf_op jit(solution)/shard_map/ppermute | solution.py:129
  32.8 12.2 %collective-permute-start.10 = (bf16[8,64,128]{2,1,0:T(8,128)(2,1)S(1)}, bf16[8,64,128]{2,1,0:T(8,128)(2,1)S(1)}, u32[]{:S(2)}, u32[]{:S(2)}) collective-permute-start(bf16[8,64,128]{2,1,0:T(8,128)(2,1)S(1)} %get-tuple-element.22.refs_0_), channel_id=1, source_target_pairs={{0,3},{1,2},{2,1},{3,0},{4,7},{5,6},{6,5},{7,4},{8,11},{9,10},{10,... | collective-permute-start | bytes 393224 | tf_op jit(solution)/shard_map/ppermute | solution.py:333
  32.9 12.1 %collective-permute-start.8 = (bf16[8,64,128]{2,1,0:T(8,128)(2,1)S(1)}, bf16[8,64,128]{2,1,0:T(8,128)(2,1)S(1)}, u32[]{:S(2)}, u32[]{:S(2)}) collective-permute-start(bf16[8,64,128]{2,1,0:T(8,128)(2,1)S(1)} %get-tuple-element.22.refs_0_), channel_id=1, source_target_pairs={{0,1},{1,0},{2,3},{3,2},{4,5},{5,4},{6,7},{7,6},{8,9},{9,8},{10,11... | collective-permute-start | bytes 393224 | tf_op jit(solution)/shard_map/ppermute | solution.py:333
  34.7 10.3 %collective-permute-start.9 = (bf16[8,64,128]{2,1,0:T(8,128)(2,1)S(1)}, bf16[8,64,128]{2,1,0:T(8,128)(2,1)S(1)}, u32[]{:S(2)}, u32[]{:S(2)}) collective-permute-start(bf16[8,64,128]{2,1,0:T(8,128)(2,1)S(1)} %get-tuple-element.22.refs_0_), channel_id=1, source_target_pairs={{0,2},{1,3},{2,0},{3,1},{4,6},{5,7},{6,4},{7,5},{8,10},{9,11},{10,... | collective-permute-start | bytes 393224 | tf_op jit(solution)/shard_map/ppermute | solution.py:333
  39.8 1.3 %collective-permute-start.6 = (f32[64,128]{1,0:T(8,128)S(1)}, f32[64,128]{1,0:T(8,128)S(1)}, u32[]{:S(2)}, u32[]{:S(2)}) collective-permute-start(f32[64,128]{1,0:T(8,128)S(1)} %get-tuple-element.20), channel_id=1, source_target_pairs={{0,1},{1,0},{2,3},{3,2},{4,5},{5,4},{6,7},{7,6},{8,9},{9,8},{10,11... | collective-permute-start | bytes 98312 | tf_op jit(solution)/shard_map/ppermute | solution.py:333
  41.1 3.9 %collective-permute-start.7 = (f32[64,128]{1,0:T(8,128)S(1)}, f32[64,128]{1,0:T(8,128)S(1)}, u32[]{:S(2)}, u32[]{:S(2)}) collective-permute-start(f32[64,128]{1,0:T(8,128)S(1)} %add.6.own_ref), channel_id=1, source_target_pairs={{0,2},{1,3},{2,0},{3,1},{4,6},{5,7},{6,4},{7,5},{8,10},{9,11},{10,... | collective-permute-start | bytes 98312 | tf_op jit(solution)/shard_map/ppermute | solution.py:333
  49.4 0.7 %collective-permute-start.11 = (f32[4,64]{1,0:T(4,128)S(1)}, f32[4,64]{1,0:T(4,128)S(1)}, u32[]{:S(2)}, u32[]{:S(2)}) collective-permute-start(f32[4,64]{1,0:T(4,128)S(1)} %score.1), channel_id=1, source_target_pairs={{4,8},{8,4},{5,9},{9,5},{6,10},{10,6},{7,11},{11,7},{20,24},{24,20... | collective-permute-start | bytes 3080 | tf_op jit(solution)/shard_map/ppermute | solution.py:356
  50.1 10.9 %collective-permute-start.12 = (f32[4,64]{1,0:T(4,128)S(1)}, f32[4,64]{1,0:T(4,128)S(1)}, u32[]{:S(2)}, u32[]{:S(2)}) collective-permute-start(f32[4,64]{1,0:T(4,128)S(1)} %add.7), channel_id=1, source_target_pairs={{4,0},{8,12},{5,1},{9,13},{6,2},{10,14},{7,3},{11,15},{20,16},{24,... | collective-permute-start | bytes 3080 | tf_op jit(solution)/shard_map/ppermute | solution.py:357

commit v5 on v4

--- a/solution.py
+++ b/solution.py
@@ -47,157 +47,183 @@
     return pltpu.CompilerParams(vmem_limit_bytes=mib * MIB)
 
 
-def project_in_kernel(side_ref, rows_hbm, proj_hbm, near_ref, far_ref, rows, proj, acc, sems, proj_sem):
+def project_in_kernel(side_ref, rows_hbm, proj_hbm, out, rows, proj, sems, proj_sem):
     seqs, length, width = rows.shape
     rank = proj.shape[1]
     proj_copy = pltpu.make_async_copy(proj_hbm, proj, proj_sem)
     proj_copy.start()
-    copies = [pltpu.make_async_copy(rows_hbm.at[s], rows.at[s], sems.at[s]) for s in range(seqs)]
-    for copy in copies:
-        copy.start()
+
+    def copy(s):
+        return pltpu.make_async_copy(rows_hbm.at[s], rows.at[s], sems.at[s])
+
+    for s in range(seqs):
+        copy(s).start()
     proj_copy.wait()
-    weights = proj[...].reshape(2 * rank, width)
-    for s in range(seqs):
-        copies[s].wait()
-        tokens = slice(s * length, (s + 1) * length)
-        part = nt(weights, rows[s])
-        acc[0, :, tokens] = part[:rank]
-        acc[1, :, tokens] = part[rank:]
-    near_ref[...] = acc[side_ref[0]]
-    far_ref[...] = acc[1 - side_ref[0]]
-
-
-def project_out_kernel(side_ref, rows_hbm, proj_hbm, near_ref, far_ref, rows, proj, acc, sems, proj_sem):
+
+    @pl.loop(0, seqs)
+    def _(s):
+        copy(s).wait()
+        part = nt(proj[...].reshape(2 * rank, width), rows[s])
+        tokens = pl.ds(pl.multiple_of(s * length, length), length)
+        out[side_ref[0], :, tokens] = part[:rank]
+        out[1 - side_ref[0], :, tokens] = part[rank:]
+
+
+def project_in(side, rows, proj):
+    seqs, length, _ = rows.shape
+    rank = proj.shape[1]
+    return pl.pallas_call(
+        project_in_kernel,
+        in_specs=[smem(), hbm(), hbm()],
+        out_specs=vmem(),
+        out_shape=jax.ShapeDtypeStruct((2, rank, seqs * length), jnp.float32),
+        scratch_shapes=[
+            pltpu.VMEM(rows.shape, rows.dtype),
+            pltpu.VMEM(proj.shape, proj.dtype),
+            pltpu.SemaphoreType.DMA((seqs,)),
+            pltpu.SemaphoreType.DMA,
+        ],
+        compiler_params=params(16),
+        name="project_in",
+    )(side, in_hbm(rows), in_hbm(proj))
+
+
+def project_out_kernel(first, side_ref, rows_hbm, proj_ref, after, out, rows, sems):
+    del after
     _, seqs, length, width = rows.shape
     half = width // 2
-    proj_copy = pltpu.make_async_copy(proj_hbm, proj, proj_sem)
-    proj_copy.start()
-    copies = {}
+
+    def copy(layer, s, part):
+        lanes = pl.ds(part * half, half)
+        return pltpu.make_async_copy(
+            rows_hbm.at[layer, first + s, :, lanes],
+            rows.at[layer, s, :, lanes],
+            sems.at[layer, s, part],
+        )
+
     for s in range(seqs):
         for part in range(2):
-            lanes = pl.ds(part * half, half)
             for layer in range(2):
-                copies[s, part, layer] = pltpu.make_async_copy(
-                    rows_hbm.at[layer, s, :, lanes],
-                    rows.at[layer, s, :, lanes],
-                    sems.at[s, part, layer],
-                )
-                copies[s, part, layer].start()
-    proj_copy.wait()
-    for s in range(seqs):
-        tokens = slice(s * length, (s + 1) * length)
+                copy(layer, s, part).start()
+
+    @pl.loop(0, seqs)
+    def _(s):
+        values = [None, None]
         for part in range(2):
             lanes = slice(part * half, (part + 1) * half)
             for layer in range(2):
-                copies[s, part, layer].wait()
+                copy(layer, s, part).wait()
             for layer in range(2):
-                value = nt(proj[layer, :, lanes], rows[layer, s, :, lanes])
-                if part > 0:
-                    value = value + acc[layer, :, tokens]
-                acc[layer, :, tokens] = value
-    near_ref[...] = acc[side_ref[0]]
-    far_ref[...] = acc[1 - side_ref[0]]
-
-
-def project(side, rows, proj, mib):
-    one = rows.ndim == 3
-    seqs, length, _ = rows.shape[-3:]
+                value = nt(proj_ref[layer, :, lanes], rows[layer, s, :, lanes])
+                values[layer] = value if part == 0 else values[layer] + value
+        tokens = pl.ds(pl.multiple_of(s * length, length), length)
+        out[side_ref[0], :, tokens] = values[0]
+        out[1 - side_ref[0], :, tokens] = values[1]
+
+
+def project_out(side, rows, proj, first, seqs, after):
+    _, _, length, width = rows.shape
     rank = proj.shape[1]
-    shape = (rank, seqs * length)
-    return pl.pallas_call(
-        project_in_kernel if one else project_out_kernel,
-        in_specs=[smem(), hbm(), hbm()],
+    return pl.pallas_call(
+        functools.partial(project_out_kernel, first),
+        in_specs=[smem(), hbm(), vmem(), hbm()],
+        out_specs=vmem(),
+        out_shape=jax.ShapeDtypeStruct((2, rank, seqs * length), jnp.float32),
+        scratch_shapes=[
+            pltpu.VMEM((2, seqs, length, width), rows.dtype),
+            pltpu.SemaphoreType.DMA((2, seqs, 2)),
+        ],
+        compiler_params=params(20),
+        name="project_out",
+    )(side, in_hbm(rows), proj, after)
+
+
+def inwards(value):
+    return lax.ppermute(value, "tensor", [(0, 1), (3, 2)])
+
+
+def across(value):
+    return lax.ppermute(value, "tensor", [(1, 2), (2, 1)])
+
+
+def gathered(own_ref, outer_ref, other_ref):
+    return own_ref[0] + outer_ref[0] + other_ref[...]
+
+
+def cov_in_kernel(own_ref, outer_ref, other_ref, after, x_out, cov_out):
+    del after
+    x = gathered(own_ref, outer_ref, other_ref)
+    x_out[...] = x
+    cov_out[...] = nt(x, jnp.concatenate([x, jnp.zeros_like(x)], axis=0), HIGHEST)
+
+
+def cov_in(own, outer, other, after):
+    rank, tokens = other.shape
+    return pl.pallas_call(
+        cov_in_kernel,
+        in_specs=[vmem()] * 3 + [hbm()],
         out_specs=[vmem()] * 2,
-        out_shape=[jax.ShapeDtypeStruct(shape, jnp.float32)] * 2,
-        scratch_shapes=[
-            pltpu.VMEM(rows.shape, rows.dtype),
-            pltpu.VMEM(proj.shape, proj.dtype),
-            pltpu.VMEM((2,) + shape, jnp.float32),
-            pltpu.SemaphoreType.DMA((seqs,) if one else (seqs, 2, 2)),
-            pltpu.SemaphoreType.DMA,
-        ],
-        compiler_params=params(mib),
-        name="project_in" if one else "project_out",
-    )(side, in_hbm(rows), in_hbm(proj) if one else proj)
-
-
-def to_owner(near, far):
-    return [
-        near,
-        lax.ppermute(far, "tensor", [(0, 2), (3, 1)]),
-        lax.ppermute(far, "tensor", [(1, 2), (2, 1)]),
-        lax.ppermute(near, "tensor", [(0, 1), (3, 2)]),
-    ]
-
-
-def total(pieces):
-    value = pieces[0][...]
-    for piece in pieces[1:]:
-        value = value + piece[...]
-    return value
-
-
-def cov_in_kernel(side_ref, queries_hbm, *refs):
-    pieces, (x_out, cov_out, packed_out, held, sem) = refs[:-5], refs[-5:]
+        out_shape=[
+            jax.ShapeDtypeStruct((rank, tokens), jnp.float32),
+            jax.ShapeDtypeStruct((rank, 2 * rank), jnp.float32),
+        ],
+        compiler_params=params(16),
+        name="cov_in",
+    )(own, outer, other, after)
+
+
+def cov_out_kernel(first, x_ref, cov_ref, own_ref, outer_ref, other_ref, cov_out, sample_out):
+    g = gathered(own_ref, outer_ref, other_ref)
+    cov_out[...] = cov_ref[...] + nt(g, jnp.concatenate([jnp.zeros_like(g), g], axis=0), HIGHEST)
+    seqs = sample_out.shape[0]
+    length = g.shape[1] // seqs
+    for s in range(seqs):
+        x = x_ref[:, (first + s) * length : (first + s + 1) * length]
+        sample = nt(x, g[:, s * length : (s + 1) * length], HIGHEST) / length
+        sample = sample.astype(jnp.bfloat16).astype(jnp.float32)
+        sample_out[s] = jnp.concatenate([sample, sample], axis=1)
+
+
+def cov_out(x, cov, own, outer, other, first, seqs):
+    rank = x.shape[0]
+    return pl.pallas_call(
+        functools.partial(cov_out_kernel, first),
+        in_specs=[vmem()] * 5,
+        out_specs=[vmem()] * 2,
+        out_shape=[
+            jax.ShapeDtypeStruct((rank, 2 * rank), jnp.float32),
+            jax.ShapeDtypeStruct((seqs, rank, 2 * rank), jnp.float32),
+        ],
+        compiler_params=params(16),
+        name="cov_out",
+    )(x, cov, own, outer, other)
+
+
+def pack_kernel(side_ref, queries_hbm, after, out, held, sem):
+    del after
     copy = pltpu.make_async_copy(queries_hbm.at[:, side_ref[0]], held, sem)
     copy.start()
-    x = total(pieces)
-    x_out[...] = x
-    cov_out[...] = nt(x, jnp.concatenate([x, jnp.zeros_like(x)], axis=0), HIGHEST)
     copy.wait()
     half = held.shape[0] // 2
     for k in range(half):
         pair = [held[k].astype(jnp.float32), held[k + half].astype(jnp.float32)]
-        packed_out[k] = jnp.concatenate(pair, axis=1).astype(packed_out.dtype)
-
-
-def cov_in(side, queries, pieces):
-    rank, tokens = pieces[0].shape
-    count = queries.shape[0]
-    return pl.pallas_call(
-        cov_in_kernel,
-        in_specs=[smem(), hbm()] + [vmem()] * len(pieces),
-        out_specs=[vmem()] * 3,
-        out_shape=[
-            jax.ShapeDtypeStruct((rank, tokens), jnp.float32),
-            jax.ShapeDtypeStruct((rank, 2 * rank), jnp.float32),
-            jax.ShapeDtypeStruct((count // 2, rank, 2 * rank), queries.dtype),
-        ],
+        out[k] = jnp.concatenate(pair, axis=1).astype(out.dtype)
+
+
+def pack(side, queries, after):
+    count, _, rank, _ = queries.shape
+    return pl.pallas_call(
+        pack_kernel,
+        in_specs=[smem(), hbm(), hbm()],
+        out_specs=vmem(),
+        out_shape=jax.ShapeDtypeStruct((count // 2, rank, 2 * rank), queries.dtype),
         scratch_shapes=[
             pltpu.VMEM((count, rank, rank), queries.dtype),
             pltpu.SemaphoreType.DMA,
         ],
         compiler_params=params(16),
-        name="cov_in",
-    )(side, in_hbm(queries), *pieces)
-
-
-def cov_out_kernel(x_ref, cov_ref, *refs):
-    pieces, (cov_out, sample_out) = refs[:-2], refs[-2:]
-    g = total(pieces)
-    cov_out[...] = cov_ref[...] + nt(g, jnp.concatenate([jnp.zeros_like(g), g], axis=0), HIGHEST)
-    seqs = sample_out.shape[0]
-    length = x_ref.shape[1] // seqs
-    for s in range(seqs):
-        tokens = slice(s * length, (s + 1) * length)
-        sample = nt(x_ref[:, tokens], g[:, tokens], HIGHEST) / length
-        sample = sample.astype(jnp.bfloat16).astype(jnp.float32)
-        sample_out[s] = jnp.concatenate([sample, sample], axis=1)
-
-
-def cov_out(x, cov, pieces, seqs):
-    rank = x.shape[0]
-    return pl.pallas_call(
-        cov_out_kernel,
-        in_specs=[vmem()] * (2 + len(pieces)),
-        out_specs=[vmem()] * 2,
-        out_shape=[
-            jax.ShapeDtypeStruct((rank, 2 * rank), jnp.float32),
-            jax.ShapeDtypeStruct((seqs, rank, 2 * rank), jnp.float32),
-        ],
-        compiler_params=params(16),
-        name="cov_out",
-    )(x, cov, *pieces)
+        name="pack",
+    )(side, in_hbm(queries), after)
 
 
 def scales(steps, spread):
@@ -245,7 +271,7 @@
     return high, middle, low
 
 
-def score_kernel(tokens, place_ref, own_ref, other_ref, sample_ref, *refs):
+def score_kernel(tokens, place_ref, own_ref, other_ref, first_ref, second_ref, *refs):
     pieces, (out, held, half) = refs[:-3], refs[-3:]
     parts = len(pieces)
     for k, piece in enumerate(pieces):
@@ -253,7 +279,8 @@
     inverses = damped_inverses((own_ref[...] + other_ref[...]) / tokens)
     both = inverses.shape[0]
     size = both // 2
-    seqs = sample_ref.shape[0]
+    samples = [ref[s] for ref in (first_ref, second_ref) for s in range(ref.shape[0])]
+    seqs = len(samples)
     blocks = held.shape[1]
     pairs = parts * blocks
     first = jnp.concatenate(split(inverses[:size, :size]), axis=0)
@@ -286,7 +313,6 @@
                 lanes = slice(pair * both, (pair + 2) * both)
                 half[0, :, lanes] = high
                 half[1, :, lanes] = middle
-    samples = [sample_ref[s] for s in range(seqs)]
     lines = [[] for _ in range(seqs)]
     for pair in range(pairs):
         lanes = slice(pair * both, (pair + 1) * both)
@@ -311,51 +337,68 @@
             ]
 
 
-def score(place, own, other, sample, pieces, tokens):
+def score(place, own, other, samples, pieces, tokens):
     blocks, rank, both = pieces[0].shape
     parts = len(pieces)
     count = 2 * parts * blocks
+    seqs = sum(sample.shape[0] for sample in samples)
     return pl.pallas_call(
         functools.partial(score_kernel, tokens),
-        in_specs=[smem()] + [vmem()] * (3 + parts),
+        in_specs=[smem()] + [vmem()] * (4 + parts),
         out_specs=vmem(),
-        out_shape=jax.ShapeDtypeStruct((sample.shape[0], count), jnp.float32),
+        out_shape=jax.ShapeDtypeStruct((seqs, count), jnp.float32),
         scratch_shapes=[
             pltpu.VMEM((parts, blocks, rank, both), pieces[0].dtype),
             pltpu.VMEM((2, rank, count * rank), jnp.bfloat16),
         ],
         compiler_params=params(16),
         name="score",
-    )(place, own, other, sample, *pieces)
+    )(place, own, other, *samples, *pieces)
 
 
 def swap(value, axis, bit):
     return lax.ppermute(value, axis, [(i, i ^ bit) for i in range(lax.axis_size(axis))])
+
+
+def after(value, earlier):
+    return lax.optimization_barrier((value, earlier))[0]
 
 
 def local_owned(acts, grads, proj_in, proj_out, queries):
     seqs, length, _ = acts.shape
     parts = lax.axis_size("dp")
     tokens = seqs * length * parts
-    across = lax.axis_index("tensor").astype(jnp.int32)
-    side = (across >= 2).astype(jnp.int32)
-    side = side.reshape(1)
+    column = lax.axis_index("tensor").astype(jnp.int32)
+    side = (column >= 2).astype(jnp.int32).reshape(1)
     place = lax.axis_index("dp").astype(jnp.int32).reshape(1)
-    x_pieces = to_owner(*project(side, acts, proj_in, 16))
-    g_pieces = to_owner(*project(side, grads, proj_out, 40))
-    x, cov, packed = cov_in(side, queries, x_pieces)
+    half = seqs // 2
+    x = project_in(side, acts, proj_in)
+    x_outer = inwards(x)
+    g = project_out(side, grads, proj_out, 0, half, x)
+    g_outer = inwards(g)
+    h = project_out(side, grads, proj_out, half, seqs - half, g)
+    h_outer = inwards(h)
+    x_far = x[1] + after(x_outer, h)[1]
+    x_other = across(x_far)
+    g_far = g[1] + after(g_outer, x_far)[1]
+    g_other = across(g_far)
+    packed = pack(side, queries, g_far)
     query_pieces = [packed] + [swap(packed, "dp", bits) for bits in range(1, parts)]
-    cov, sample = cov_out(x, cov, g_pieces, seqs)
+    h_far = h[1] + after(h_outer, packed)[1]
+    h_other = across(h_far)
+    x_sum, cov = cov_in(x, x_outer, x_other, h_far)
+    cov, sample = cov_out(x_sum, cov, g, g_outer, g_other, 0, half)
+    cov, last = cov_out(x_sum, cov, h, h_outer, h_other, half, seqs - half)
     other = jnp.zeros_like(cov)
     bit = 1
     while bit < parts:
         cov = cov if bit == 1 else cov + other
         other = swap(cov, "dp", bit)
         bit *= 2
-    scores = score(place, cov, other, sample, query_pieces, tokens)
-    scores = scores + lax.ppermute(scores, "tensor", [(1, 2), (2, 1)])
+    scores = score(place, cov, other, [sample, last], query_pieces, tokens)
+    scores = scores + across(scores)
     outer = lax.ppermute(scores, "tensor", [(1, 0), (2, 3)])
-    return jnp.where((across == 1) | (across == 2), scores, outer)
+    return jnp.where((column == 1) | (column == 2), scores, outer)
 
 
 def damp(matrix):
@@ -424,8 +467,8 @@
 
 def local(acts, grads, proj_in, proj_out, queries):
     parts = lax.axis_size("dp")
-    blocks = queries.shape[0]
-    if lax.axis_size("tensor") == 4 and parts > 1 and parts & (parts - 1) == 0 and blocks % 4 == 0:
+    even = parts > 1 and parts & (parts - 1) == 0
+    if lax.axis_size("tensor") == 4 and even and acts.shape[0] > 1 and queries.shape[0] % 4 == 0:
         return local_owned(acts, grads, proj_in, proj_out, queries)
     return local_general(acts, grads, proj_in, proj_out, queries)
 

time: 61.9 us -> 62.6 us (1.011)
  starting transfers between devices: 21.4 us -> 15.3 us
  Pallas kernels: 23.3 us -> 27.5 us
  waiting for transfers between devices: 16.2 us -> 18.6 us
    ppermute x7, starting transfers between devices: 15.3 us -> 10.3 us  [the longest x3 7.57 us: inwards(): return lax.ppermute(value, 'tensor', [(0, 1), (3, 2)])]
    pallas_call x4 -> x7, Pallas kernels: 19 us -> 23.1 us  [the longest x2 16.4 us: project_out(): pl.pallas_call(functools.partial(project_out_kernel, first), in_specs=[sm...]
    ppermute x1, waiting for transfers between devices: 9.63 us -> 11.6 us  [local_owned(): outer = lax.ppermute(scores, 'tensor', [(1, 0), (2, 3)])]
    ppermute x5, starting transfers between devices: 4.72 us -> 3.77 us  [swap(): lax.ppermute(value, axis, [(i, i ^ bit) for i in range(lax.axis_size(axis...]
  transfers between devices with their start and end apart: 13 -> 13, of which waited for: 5 -> 5; matrix products, arithmetic and copies ran while one was open for 0% -> 0% of each run, Pallas kernels for 23% -> 31%
where the time goes in v5:
time: 62.6 us; the launch traced here: 62.3 us
  Pallas kernels  27.5 us (44%)
  waiting for transfers between devices  18.6 us (30%)
  starting transfers between devices  15.3 us (24%)
  other arithmetic  0.66 us (1%)
    pallas_call x2, Pallas kernels, project_out(): pl.pallas_call(functools.partial(project_out_kernel, first), in_specs=[sm...  16.4 us
    ppermute x1, waiting for transfers between devices, local_owned(): outer = lax.ppermute(scores, 'tensor', [(1, 0), (2, 3)])  11.6 us
    ppermute x3, starting transfers between devices, inwards(): return lax.ppermute(value, 'tensor', [(0, 1), (3, 2)])  7.57 us
    pallas_call x1, Pallas kernels, score(): pl.pallas_call(functools.partial(score_kernel, tokens), in_specs=[smem()]...  4.35 us
    pallas_call x1, Pallas kernels, project_in(): pl.pallas_call(project_in_kernel, in_specs=[smem(), hbm(), hbm()], out_sp...  4.09 us
    ppermute x5, waiting for transfers between devices, swap(): lax.ppermute(value, axis, [(i, i ^ bit) for i in range(lax.axis_size(axis...  3.97 us
    ppermute x5, starting transfers between devices, swap(): lax.ppermute(value, axis, [(i, i ^ bit) for i in range(lax.axis_size(axis...  3.77 us
    ppermute x3, waiting for transfers between devices, inwards(): return lax.ppermute(value, 'tensor', [(0, 1), (3, 2)])  3.01 us
  transfers between devices with their start and end apart: 13, of which 5 were waited for; matrix products, arithmetic and copies ran while one was open for 0% of the time, Pallas kernels for 31%

profile of v5, /device:TPU:0, one launch (start us, length us, event | category | flops | bytes accessed | tf_op | source)
XLA Modules:
  0.0 62.3 jit_solution(7252131953442102738)
XLA Ops:
  0.0 0.0 copy-start
  0.0 4.1 %project_in.1.after.own_ref = f32[2,64,1024]{2,1,0:T(8,128)S(1)} custom-call(s32[1]{0:T(128)} %bitcast.1.side_ref, bf16[4,256,2048]{2,1,0:T(8,128)(2,1)} %rows_hbm.3, bf16[2,64,2048]{2,1,0:T(8,128)(2,1)} %proj_hbm.1), custom_call_target="tpu_custom_call" | custom-call | tf_op jit(solution)/shard_map/project_in/pallas_call | solution.py:75
  4.1 5.0 %collective-permute-start = (f32[2,64,1024]{2,1,0:T(8,128)S(1)}, f32[2,64,1024]{2,1,0:T(8,128)S(1)}, u32[]{:S(2)}, u32[]{:S(2)}) collective-permute-start(f32[2,64,1024]{2,1,0:T(8,128)S(1)} %project_in.1.after.own_ref), channel_id=1, source_target_pairs={{0,4},{12,8},{1,5},{13,9},{2,6},{14,10},{3,7},{15,11},{16,20},{28,... | collective-permute-start | bytes 1572872 | tf_op jit(solution)/shard_map/ppermute | solution.py:142
  9.1 0.0 copy-done
  9.1 8.2 %project_out.2.after.own_ref = f32[2,64,512]{2,1,0:T(8,128)S(1)} custom-call(s32[1]{0:T(128)} %bitcast.1.side_ref, bf16[2,4,256,7168]{3,2,1,0:T(8,128)(2,1)} %rows_hbm.5, bf16[2,64,7168]{2,1,0:T(8,128)(2,1)S(1)} %copy-done, f32[2,64,1024]{2,1,0:T(8,128)S(1)} %project_in.1.after.own_ref), custom_call_target="tpu_custom_call" | custom-call | tf_op jit(solution)/shard_map/project_out/pallas_call | solution.py:127
  17.3 1.3 %collective-permute-start.3 = (f32[2,64,512]{2,1,0:T(8,128)S(1)}, f32[2,64,512]{2,1,0:T(8,128)S(1)}, u32[]{:S(2)}, u32[]{:S(2)}) collective-permute-start(f32[2,64,512]{2,1,0:T(8,128)S(1)} %project_out.2.after.own_ref), channel_id=1, source_target_pairs={{0,4},{12,8},{1,5},{13,9},{2,6},{14,10},{3,7},{15,11},{16,20},{28,... | collective-permute-start | bytes 786440 | tf_op jit(solution)/shard_map/ppermute | solution.py:142
  18.6 8.2 %project_out.3.own_ref = f32[2,64,512]{2,1,0:T(8,128)S(1)} custom-call(s32[1]{0:T(128)} %bitcast.1.side_ref, bf16[2,4,256,7168]{3,2,1,0:T(8,128)(2,1)} %rows_hbm.5, bf16[2,64,7168]{2,1,0:T(8,128)(2,1)S(1)} %copy-done, f32[2,64,512]{2,1,0:T(8,128)S(1)} %project_out.2.after.own_ref), custom_call_target="tpu_custom_call" | custom-call | tf_op jit(solution)/shard_map/project_out/pallas_call | solution.py:127
  26.8 1.3 %collective-permute-start.2 = (f32[2,64,512]{2,1,0:T(8,128)S(1)}, f32[2,64,512]{2,1,0:T(8,128)S(1)}, u32[]{:S(2)}, u32[]{:S(2)}) collective-permute-start(f32[2,64,512]{2,1,0:T(8,128)S(1)} %project_out.3.own_ref), channel_id=1, source_target_pairs={{0,4},{12,8},{1,5},{13,9},{2,6},{14,10},{3,7},{15,11},{16,20},{28,... | collective-permute-start | bytes 786440 | tf_op jit(solution)/shard_map/ppermute | solution.py:142
  28.1 0.0 collective-permute-done.outer_ref
  28.2 0.7 %collective-permute-start.1 = (f32[64,1024]{1,0:T(8,128)S(1)}, f32[64,1024]{1,0:T(8,128)S(1)}, u32[]{:S(2)}, u32[]{:S(2)}) collective-permute-start(f32[64,1024]{1,0:T(8,128)S(1)} %fusion), channel_id=1, source_target_pairs={{4,8},{8,4},{5,9},{9,5},{6,10},{10,6},{7,11},{11,7},{20,24},{24,20... | collective-permute-start | bytes 786440 | tf_op jit(solution)/shard_map/ppermute | solution.py:146
  28.8 0.0 collective-permute-done.3.outer_ref
  28.9 0.7 %collective-permute-start.4 = (f32[64,512]{1,0:T(8,128)S(1)}, f32[64,512]{1,0:T(8,128)S(1)}, u32[]{:S(2)}, u32[]{:S(2)}) collective-permute-start(f32[64,512]{1,0:T(8,128)S(1)} %fusion.1.after), channel_id=1, source_target_pairs={{4,8},{8,4},{5,9},{9,5},{6,10},{10,6},{7,11},{11,7},{20,24},{24,20... | collective-permute-start | bytes 393224 | tf_op jit(solution)/shard_map/ppermute | solution.py:146
  29.6 1.1 %pack.1.refs_0_ = bf16[8,64,128]{2,1,0:T(8,128)(2,1)S(1)} custom-call(s32[1]{0:T(128)} %bitcast.1.side_ref, bf16[16,2,64,64]{3,2,1,0:T(8,128)(2,1)} %queries_hbm.1, f32[64,512]{1,0:T(8,128)S(1)} %fusion.1.after), custom_call_target="tpu_custom_call" | custom-call | tf_op jit(solution)/shard_map/pack/pallas_call | solution.py:215
  30.6 3.0 %collective-permute-done.2.outer_ref = f32[2,64,512]{2,1,0:T(8,128)S(1)} collective-permute-done((f32[2,64,512]{2,1,0:T(8,128)S(1)}, f32[2,64,512]{2,1,0:T(8,128)S(1)}, u32[]{:S(2)}, u32[]{:S(2)}) %collective-permute-start.2) | collective-permute-done | bytes 262176 | tf_op jit(solution)/shard_map/ppermute | solution.py:142
  33.7 0.7 %collective-permute-start.5 = (f32[64,512]{1,0:T(8,128)S(1)}, f32[64,512]{1,0:T(8,128)S(1)}, u32[]{:S(2)}, u32[]{:S(2)}) collective-permute-start(f32[64,512]{1,0:T(8,128)S(1)} %fusion.2.after), channel_id=1, source_target_pairs={{4,8},{8,4},{5,9},{9,5},{6,10},{10,6},{7,11},{11,7},{20,24},{24,20... | collective-permute-start | bytes 393224 | tf_op jit(solution)/shard_map/ppermute | solution.py:146
  34.3 0.1 collective-permute-start.10
  34.5 1.5 %collective-permute-start.8 = (bf16[8,64,128]{2,1,0:T(8,128)(2,1)S(1)}, bf16[8,64,128]{2,1,0:T(8,128)(2,1)S(1)}, u32[]{:S(2)}, u32[]{:S(2)}) collective-permute-start(bf16[8,64,128]{2,1,0:T(8,128)(2,1)S(1)} %pack.1.refs_0_), channel_id=1, source_target_pairs={{0,1},{1,0},{2,3},{3,2},{4,5},{5,4},{6,7},{7,6},{8,9},{9,8},{10,11... | collective-permute-start | bytes 393224 | tf_op jit(solution)/shard_map/ppermute | solution.py:360
  36.0 0.0 collective-permute-done.1.other_ref
  36.0 0.5 collective-permute-start.9
  36.6 0.4 cov_in.1
  36.9 0.0 collective-permute-done.4.other_ref
  37.0 0.6 cov_out.2
  37.6 0.0 collective-permute-done.5.other_ref
  37.6 0.6 cov_out.3
  38.2 0.1 collective-permute-start.6
  38.2 1.2 %collective-permute-done.6 = f32[64,128]{1,0:T(8,128)S(1)} collective-permute-done((f32[64,128]{1,0:T(8,128)S(1)}, f32[64,128]{1,0:T(8,128)S(1)}, u32[]{:S(2)}, u32[]{:S(2)}) %collective-permute-start.6) | collective-permute-done | bytes 32800 | tf_op jit(solution)/shard_map/ppermute | solution.py:360
  39.4 1.5 %collective-permute-start.7 = (f32[64,128]{1,0:T(8,128)S(1)}, f32[64,128]{1,0:T(8,128)S(1)}, u32[]{:S(2)}, u32[]{:S(2)}) collective-permute-start(f32[64,128]{1,0:T(8,128)S(1)} %add.28.own_ref), channel_id=1, source_target_pairs={{0,2},{1,3},{2,0},{3,1},{4,6},{5,7},{6,4},{7,5},{8,10},{9,11},{10,... | collective-permute-start | bytes 98312 | tf_op jit(solution)/shard_map/ppermute | solution.py:360
  40.9 0.0 collective-permute-done.10.refs_3_
  40.9 0.0 collective-permute-done.8.refs_1_
  40.9 2.1 %collective-permute-done.9.refs_2_ = bf16[8,64,128]{2,1,0:T(8,128)(2,1)S(1)} collective-permute-done((bf16[8,64,128]{2,1,0:T(8,128)(2,1)S(1)}, bf16[8,64,128]{2,1,0:T(8,128)(2,1)S(1)}, u32[]{:S(2)}, u32[]{:S(2)}) %collective-permute-start.9) | collective-permute-done | bytes 131104 | tf_op jit(solution)/shard_map/ppermute | solution.py:360
  43.1 0.7 %collective-permute-done.7.other_ref = f32[64,128]{1,0:T(8,128)S(1)} collective-permute-done((f32[64,128]{1,0:T(8,128)S(1)}, f32[64,128]{1,0:T(8,128)S(1)}, u32[]{:S(2)}, u32[]{:S(2)}) %collective-permute-start.7) | collective-permute-done | bytes 32800 | tf_op jit(solution)/shard_map/ppermute | solution.py:360
  43.7 4.3 %score.1 = f32[4,64]{1,0:T(4,128)S(1)} custom-call(s32[1]{0:T(128)} %bitcast.place_ref, f32[64,128]{1,0:T(8,128)S(1)} %add.28.own_ref, f32[64,128]{1,0:T(8,128)S(1)} %collective-permute-done.7.other_ref, f32[2,64,128]{2,1,0:T(8,128)S(1)} %get-tuple-element.21.first_ref, f32[2,64,128]{2,1,0:T(8,128)S(1)} %get-tuple-element.22.second_ref, ...), custom_call_target="tpu_custom_call" | custom-call | tf_op jit(solution)/shard_map/score/pallas_call | solution.py:345
  48.1 0.7 %collective-permute-start.11 = (f32[4,64]{1,0:T(4,128)S(1)}, f32[4,64]{1,0:T(4,128)S(1)}, u32[]{:S(2)}, u32[]{:S(2)}) collective-permute-start(f32[4,64]{1,0:T(4,128)S(1)} %score.1), channel_id=1, source_target_pairs={{4,8},{8,4},{5,9},{9,5},{6,10},{10,6},{7,11},{11,7},{20,24},{24,20... | collective-permute-start | bytes 3080 | tf_op jit(solution)/shard_map/ppermute | solution.py:146
  48.8 0.0 collective-permute-done.11
  48.8 1.3 %collective-permute-start.12 = (f32[4,64]{1,0:T(4,128)S(1)}, f32[4,64]{1,0:T(4,128)S(1)}, u32[]{:S(2)}, u32[]{:S(2)}) collective-permute-start(f32[4,64]{1,0:T(4,128)S(1)} %add.29), channel_id=1, source_target_pairs={{4,0},{8,12},{5,1},{9,13},{6,2},{10,14},{7,3},{11,15},{20,16},{24,... | collective-permute-start | bytes 3080 | tf_op jit(solution)/shard_map/ppermute | solution.py:400
  50.1 11.6 %collective-permute-done.12 = f32[4,64]{1,0:T(4,128)S(1)} collective-permute-done((f32[4,64]{1,0:T(4,128)S(1)}, f32[4,64]{1,0:T(4,128)S(1)}, u32[]{:S(2)}, u32[]{:S(2)}) %collective-permute-start.12) | collective-permute-done | bytes 1056 | tf_op jit(solution)/shard_map/ppermute | solution.py:400
  61.7 0.6 broadcast_select_fusion
  (5 shorter events, 0.1 us)
Async XLA Ops:
  0.0 9.1 %copy-start = (bf16[2,64,7168]{2,1,0:T(8,128)(2,1)S(1)}, bf16[2,64,7168]{2,1,0:T(8,128)(2,1)}, u32[]{:S(2)}) copy-start(bf16[2,64,7168]{2,1,0:T(8,128)(2,1)} %proj_ref.3) | copy-start | bytes 5505028
  4.1 24.0 %collective-permute-start = (f32[2,64,1024]{2,1,0:T(8,128)S(1)}, f32[2,64,1024]{2,1,0:T(8,128)S(1)}, u32[]{:S(2)}, u32[]{:S(2)}) collective-permute-start(f32[2,64,1024]{2,1,0:T(8,128)S(1)} %project_in.1.after.own_ref), channel_id=1, source_target_pairs={{0,4},{12,8},{1,5},{13,9},{2,6},{14,10},{3,7},{15,11},{16,20},{28,... | collective-permute-start | bytes 1572872 | tf_op jit(solution)/shard_map/ppermute | solution.py:142
  17.3 11.6 %collective-permute-start.3 = (f32[2,64,512]{2,1,0:T(8,128)S(1)}, f32[2,64,512]{2,1,0:T(8,128)S(1)}, u32[]{:S(2)}, u32[]{:S(2)}) collective-permute-start(f32[2,64,512]{2,1,0:T(8,128)S(1)} %project_out.2.after.own_ref), channel_id=1, source_target_pairs={{0,4},{12,8},{1,5},{13,9},{2,6},{14,10},{3,7},{15,11},{16,20},{28,... | collective-permute-start | bytes 786440 | tf_op jit(solution)/shard_map/ppermute | solution.py:142
  26.8 6.8 %collective-permute-start.2 = (f32[2,64,512]{2,1,0:T(8,128)S(1)}, f32[2,64,512]{2,1,0:T(8,128)S(1)}, u32[]{:S(2)}, u32[]{:S(2)}) collective-permute-start(f32[2,64,512]{2,1,0:T(8,128)S(1)} %project_out.3.own_ref), channel_id=1, source_target_pairs={{0,4},{12,8},{1,5},{13,9},{2,6},{14,10},{3,7},{15,11},{16,20},{28,... | collective-permute-start | bytes 786440 | tf_op jit(solution)/shard_map/ppermute | solution.py:142
  28.2 7.9 %collective-permute-start.1 = (f32[64,1024]{1,0:T(8,128)S(1)}, f32[64,1024]{1,0:T(8,128)S(1)}, u32[]{:S(2)}, u32[]{:S(2)}) collective-permute-start(f32[64,1024]{1,0:T(8,128)S(1)} %fusion), channel_id=1, source_target_pairs={{4,8},{8,4},{5,9},{9,5},{6,10},{10,6},{7,11},{11,7},{20,24},{24,20... | collective-permute-start | bytes 786440 | tf_op jit(solution)/shard_map/ppermute | solution.py:146
  28.9 8.1 %collective-permute-start.4 = (f32[64,512]{1,0:T(8,128)S(1)}, f32[64,512]{1,0:T(8,128)S(1)}, u32[]{:S(2)}, u32[]{:S(2)}) collective-permute-start(f32[64,512]{1,0:T(8,128)S(1)} %fusion.1.after), channel_id=1, source_target_pairs={{4,8},{8,4},{5,9},{9,5},{6,10},{10,6},{7,11},{11,7},{20,24},{24,20... | collective-permute-start | bytes 393224 | tf_op jit(solution)/shard_map/ppermute | solution.py:146
  33.7 3.9 %collective-permute-start.5 = (f32[64,512]{1,0:T(8,128)S(1)}, f32[64,512]{1,0:T(8,128)S(1)}, u32[]{:S(2)}, u32[]{:S(2)}) collective-permute-start(f32[64,512]{1,0:T(8,128)S(1)} %fusion.2.after), channel_id=1, source_target_pairs={{4,8},{8,4},{5,9},{9,5},{6,10},{10,6},{7,11},{11,7},{20,24},{24,20... | collective-permute-start | bytes 393224 | tf_op jit(solution)/shard_map/ppermute | solution.py:146
  34.3 6.6 %collective-permute-start.10 = (bf16[8,64,128]{2,1,0:T(8,128)(2,1)S(1)}, bf16[8,64,128]{2,1,0:T(8,128)(2,1)S(1)}, u32[]{:S(2)}, u32[]{:S(2)}) collective-permute-start(bf16[8,64,128]{2,1,0:T(8,128)(2,1)S(1)} %pack.1.refs_0_), channel_id=1, source_target_pairs={{0,3},{1,2},{2,1},{3,0},{4,7},{5,6},{6,5},{7,4},{8,11},{9,10},{10,... | collective-permute-start | bytes 393224 | tf_op jit(solution)/shard_map/ppermute | solution.py:360
  34.5 6.5 %collective-permute-start.8 = (bf16[8,64,128]{2,1,0:T(8,128)(2,1)S(1)}, bf16[8,64,128]{2,1,0:T(8,128)(2,1)S(1)}, u32[]{:S(2)}, u32[]{:S(2)}) collective-permute-start(bf16[8,64,128]{2,1,0:T(8,128)(2,1)S(1)} %pack.1.refs_0_), channel_id=1, source_target_pairs={{0,1},{1,0},{2,3},{3,2},{4,5},{5,4},{6,7},{7,6},{8,9},{9,8},{10,11... | collective-permute-start | bytes 393224 | tf_op jit(solution)/shard_map/ppermute | solution.py:360
  36.0 7.0 %collective-permute-start.9 = (bf16[8,64,128]{2,1,0:T(8,128)(2,1)S(1)}, bf16[8,64,128]{2,1,0:T(8,128)(2,1)S(1)}, u32[]{:S(2)}, u32[]{:S(2)}) collective-permute-start(bf16[8,64,128]{2,1,0:T(8,128)(2,1)S(1)} %pack.1.refs_0_), channel_id=1, source_target_pairs={{0,2},{1,3},{2,0},{3,1},{4,6},{5,7},{6,4},{7,5},{8,10},{9,11},{10,... | collective-permute-start | bytes 393224 | tf_op jit(solution)/shard_map/ppermute | solution.py:360
  38.2 1.3 %collective-permute-start.6 = (f32[64,128]{1,0:T(8,128)S(1)}, f32[64,128]{1,0:T(8,128)S(1)}, u32[]{:S(2)}, u32[]{:S(2)}) collective-permute-start(f32[64,128]{1,0:T(8,128)S(1)} %get-tuple-element.20), channel_id=1, source_target_pairs={{0,1},{1,0},{2,3},{3,2},{4,5},{5,4},{6,7},{7,6},{8,9},{9,8},{10,11... | collective-permute-start | bytes 98312 | tf_op jit(solution)/shard_map/ppermute | solution.py:360
  39.4 4.3 %collective-permute-start.7 = (f32[64,128]{1,0:T(8,128)S(1)}, f32[64,128]{1,0:T(8,128)S(1)}, u32[]{:S(2)}, u32[]{:S(2)}) collective-permute-start(f32[64,128]{1,0:T(8,128)S(1)} %add.28.own_ref), channel_id=1, source_target_pairs={{0,2},{1,3},{2,0},{3,1},{4,6},{5,7},{6,4},{7,5},{8,10},{9,11},{10,... | collective-permute-start | bytes 98312 | tf_op jit(solution)/shard_map/ppermute | solution.py:360
  48.1 0.7 %collective-permute-start.11 = (f32[4,64]{1,0:T(4,128)S(1)}, f32[4,64]{1,0:T(4,128)S(1)}, u32[]{:S(2)}, u32[]{:S(2)}) collective-permute-start(f32[4,64]{1,0:T(4,128)S(1)} %score.1), channel_id=1, source_target_pairs={{4,8},{8,4},{5,9},{9,5},{6,10},{10,6},{7,11},{11,7},{20,24},{24,20... | collective-permute-start | bytes 3080 | tf_op jit(solution)/shard_map/ppermute | solution.py:146
  48.8 12.9 %collective-permute-start.12 = (f32[4,64]{1,0:T(4,128)S(1)}, f32[4,64]{1,0:T(4,128)S(1)}, u32[]{:S(2)}, u32[]{:S(2)}) collective-permute-start(f32[4,64]{1,0:T(4,128)S(1)} %add.29), channel_id=1, source_target_pairs={{4,0},{8,12},{5,1},{9,13},{6,2},{10,14},{7,3},{11,15},{20,16},{24,... | collective-permute-start | bytes 3080 | tf_op jit(solution)/shard_map/ppermute | solution.py:400

commit v6 on v5

--- a/solution.py
+++ b/solution.py
@@ -88,54 +88,65 @@
     )(side, in_hbm(rows), in_hbm(proj))
 
 
-def project_out_kernel(first, side_ref, rows_hbm, proj_ref, after, out, rows, sems):
+def project_out_kernel(first, side_ref, rows_hbm, proj_ref, queries_hbm, after, out, *refs):
     del after
+    packed, (rows, held, sems, sem) = refs[:-4], refs[-4:]
     _, seqs, length, width = rows.shape
     half = width // 2
-
-    def copy(layer, s, part):
-        lanes = pl.ds(part * half, half)
-        return pltpu.make_async_copy(
-            rows_hbm.at[layer, first + s, :, lanes],
-            rows.at[layer, s, :, lanes],
-            sems.at[layer, s, part],
-        )
-
+    copies = {}
     for s in range(seqs):
         for part in range(2):
+            lanes = pl.ds(part * half, half)
             for layer in range(2):
-                copy(layer, s, part).start()
-
-    @pl.loop(0, seqs)
-    def _(s):
+                copies[s, part, layer] = pltpu.make_async_copy(
+                    rows_hbm.at[layer, first + s, :, lanes],
+                    rows.at[layer, s, :, lanes],
+                    sems.at[layer, s, part],
+                )
+                copies[s, part, layer].start()
+    if packed:
+        copy = pltpu.make_async_copy(queries_hbm.at[:, side_ref[0]], held, sem)
+        copy.start()
+    for s in range(seqs):
         values = [None, None]
         for part in range(2):
             lanes = slice(part * half, (part + 1) * half)
             for layer in range(2):
-                copy(layer, s, part).wait()
-            for layer in range(2):
+                copies[s, part, layer].wait()
                 value = nt(proj_ref[layer, :, lanes], rows[layer, s, :, lanes])
                 values[layer] = value if part == 0 else values[layer] + value
-        tokens = pl.ds(pl.multiple_of(s * length, length), length)
+        tokens = slice(s * length, (s + 1) * length)
         out[side_ref[0], :, tokens] = values[0]
         out[1 - side_ref[0], :, tokens] = values[1]
-
-
-def project_out(side, rows, proj, first, seqs, after):
+    if packed:
+        copy.wait()
+        blocks = held.shape[0] // 2
+        for k in range(blocks):
+            pair = [held[k].astype(jnp.float32), held[k + blocks].astype(jnp.float32)]
+            packed[0][k] = jnp.concatenate(pair, axis=1).astype(held.dtype)
+
+
+def project_out(side, rows, proj, queries, first, seqs, after, packs):
     _, _, length, width = rows.shape
     rank = proj.shape[1]
+    count = queries.shape[0]
+    out_shape = [jax.ShapeDtypeStruct((2, rank, seqs * length), jnp.float32)]
+    if packs:
+        out_shape.append(jax.ShapeDtypeStruct((count // 2, rank, 2 * rank), queries.dtype))
     return pl.pallas_call(
         functools.partial(project_out_kernel, first),
-        in_specs=[smem(), hbm(), vmem(), hbm()],
-        out_specs=vmem(),
-        out_shape=jax.ShapeDtypeStruct((2, rank, seqs * length), jnp.float32),
+        in_specs=[smem(), hbm(), vmem(), hbm(), hbm()],
+        out_specs=[vmem()] * len(out_shape),
+        out_shape=out_shape,
         scratch_shapes=[
             pltpu.VMEM((2, seqs, length, width), rows.dtype),
+            pltpu.VMEM((count, rank, rank), queries.dtype),
             pltpu.SemaphoreType.DMA((2, seqs, 2)),
+            pltpu.SemaphoreType.DMA,
         ],
-        compiler_params=params(20),
+        compiler_params=params(24),
         name="project_out",
-    )(side, in_hbm(rows), proj, after)
+    )(side, in_hbm(rows), proj, in_hbm(queries), after)
 
 
 def inwards(value):
@@ -146,48 +157,60 @@
     return lax.ppermute(value, "tensor", [(1, 2), (2, 1)])
 
 
-def gathered(own_ref, outer_ref, other_ref):
-    return own_ref[0] + outer_ref[0] + other_ref[...]
-
-
-def cov_in_kernel(own_ref, outer_ref, other_ref, after, x_out, cov_out):
-    del after
-    x = gathered(own_ref, outer_ref, other_ref)
-    x_out[...] = x
-    cov_out[...] = nt(x, jnp.concatenate([x, jnp.zeros_like(x)], axis=0), HIGHEST)
-
-
-def cov_in(own, outer, other, after):
-    rank, tokens = other.shape
-    return pl.pallas_call(
-        cov_in_kernel,
-        in_specs=[vmem()] * 3 + [hbm()],
-        out_specs=[vmem()] * 2,
-        out_shape=[
-            jax.ShapeDtypeStruct((rank, tokens), jnp.float32),
-            jax.ShapeDtypeStruct((rank, 2 * rank), jnp.float32),
-        ],
-        compiler_params=params(16),
-        name="cov_in",
-    )(own, outer, other, after)
-
-
-def cov_out_kernel(first, x_ref, cov_ref, own_ref, outer_ref, other_ref, cov_out, sample_out):
-    g = gathered(own_ref, outer_ref, other_ref)
-    cov_out[...] = cov_ref[...] + nt(g, jnp.concatenate([jnp.zeros_like(g), g], axis=0), HIGHEST)
+def covariance(value, right):
+    none = jnp.zeros_like(value)
+    both = [none, value] if right else [value, none]
+    return nt(value, jnp.concatenate(both, axis=0), HIGHEST)
+
+
+def samples_of(x, g, sample_out):
     seqs = sample_out.shape[0]
     length = g.shape[1] // seqs
     for s in range(seqs):
-        x = x_ref[:, (first + s) * length : (first + s + 1) * length]
-        sample = nt(x, g[:, s * length : (s + 1) * length], HIGHEST) / length
+        tokens = slice(s * length, (s + 1) * length)
+        sample = nt(x[:, tokens], g[:, tokens], HIGHEST) / length
         sample = sample.astype(jnp.bfloat16).astype(jnp.float32)
         sample_out[s] = jnp.concatenate([sample, sample], axis=1)
 
 
-def cov_out(x, cov, own, outer, other, first, seqs):
+def first_kernel(x_ref, x_outer, g_ref, g_outer, other, after, x_out, cov_out, sample_out):
+    del after
+    tokens = x_ref.shape[2]
+    here = g_ref.shape[2]
+    x = x_ref[0] + x_outer[0] + other[:, :tokens]
+    x_out[...] = x[:, here:]
+    g = g_ref[0] + g_outer[0] + other[:, tokens:]
+    cov_out[...] = covariance(x, False) + covariance(g, True)
+    samples_of(x[:, :here], g, sample_out)
+
+
+def second_kernel(x_ref, cov_ref, h_ref, h_outer, other, cov_out, sample_out):
+    h = h_ref[0] + h_outer[0] + other[...]
+    cov_out[...] = cov_ref[...] + covariance(h, True)
+    samples_of(x_ref[...], h, sample_out)
+
+
+def first_half(x, x_outer, g, g_outer, other, after, seqs):
+    _, rank, tokens = x.shape
+    here = g.shape[2]
+    return pl.pallas_call(
+        first_kernel,
+        in_specs=[vmem()] * 5 + [hbm()],
+        out_specs=[vmem()] * 3,
+        out_shape=[
+            jax.ShapeDtypeStruct((rank, tokens - here), jnp.float32),
+            jax.ShapeDtypeStruct((rank, 2 * rank), jnp.float32),
+            jax.ShapeDtypeStruct((seqs, rank, 2 * rank), jnp.float32),
+        ],
+        compiler_params=params(16),
+        name="first_half",
+    )(x, x_outer, g, g_outer, other, after)
+
+
+def second_half(x, cov, h, h_outer, other, seqs):
     rank = x.shape[0]
     return pl.pallas_call(
-        functools.partial(cov_out_kernel, first),
+        second_kernel,
         in_specs=[vmem()] * 5,
         out_specs=[vmem()] * 2,
         out_shape=[
@@ -195,35 +218,8 @@
             jax.ShapeDtypeStruct((seqs, rank, 2 * rank), jnp.float32),
         ],
         compiler_params=params(16),
-        name="cov_out",
-    )(x, cov, own, outer, other)
-
-
-def pack_kernel(side_ref, queries_hbm, after, out, held, sem):
-    del after
-    copy = pltpu.make_async_copy(queries_hbm.at[:, side_ref[0]], held, sem)
-    copy.start()
-    copy.wait()
-    half = held.shape[0] // 2
-    for k in range(half):
-        pair = [held[k].astype(jnp.float32), held[k + half].astype(jnp.float32)]
-        out[k] = jnp.concatenate(pair, axis=1).astype(out.dtype)
-
-
-def pack(side, queries, after):
-    count, _, rank, _ = queries.shape
-    return pl.pallas_call(
-        pack_kernel,
-        in_specs=[smem(), hbm(), hbm()],
-        out_specs=vmem(),
-        out_shape=jax.ShapeDtypeStruct((count // 2, rank, 2 * rank), queries.dtype),
-        scratch_shapes=[
-            pltpu.VMEM((count, rank, rank), queries.dtype),
-            pltpu.SemaphoreType.DMA,
-        ],
-        compiler_params=params(16),
-        name="pack",
-    )(side, in_hbm(queries), after)
+        name="second_half",
+    )(x, cov, h, h_outer, other)
 
 
 def scales(steps, spread):
@@ -254,10 +250,16 @@
     y = matrix * start
     x = (2.0 * start * steps[0]) * eye - (start * steps[0]) * y
     y = steps[0] * (2.0 * y - nn(y, y, HIGHEST))
-    for scale in steps[1:-1]:
+
+    def step(k, pair):
+        x, y = pair
+        scale = jnp.float32(steps[1])
+        for place in range(2, len(steps) - 1):
+            scale = jnp.where(k == place, jnp.float32(steps[place]), scale)
         product = nn(jnp.concatenate([x, y], axis=0), y, HIGHEST)
-        x = scale * (2.0 * x - product[:both])
-        y = scale * (2.0 * y - product[both:])
+        return scale * (2.0 * x - product[:both]), scale * (2.0 * y - product[both:])
+
+    x, y = lax.fori_loop(1, len(steps) - 1, step, (x, y))
     x = steps[-1] * (2.0 * x - nn(x, y, HIGHEST))
     x = x + nn(x, eye - nn(matrix, x, HIGHEST), HIGHEST)
     return x / unit
@@ -272,10 +274,13 @@
 
 
 def score_kernel(tokens, place_ref, own_ref, other_ref, first_ref, second_ref, *refs):
-    pieces, (out, held, half) = refs[:-3], refs[-3:]
-    parts = len(pieces)
-    for k, piece in enumerate(pieces):
-        held[place_ref[0] ^ k] = piece[...]
+    pieces, (out, held, half, lines) = refs[:-4], refs[-4:]
+    parts = held.shape[0]
+    k = 0
+    for piece in pieces:
+        for place in range(piece.shape[0]):
+            held[place_ref[0] ^ k] = piece[place]
+            k += 1
     inverses = damped_inverses((own_ref[...] + other_ref[...]) / tokens)
     both = inverses.shape[0]
     size = both // 2
@@ -293,35 +298,39 @@
     high, middle, _ = split(twice)
     once = jnp.concatenate([high, middle], axis=1)
     second = jnp.concatenate([once, once], axis=0)
-    for part in range(parts // 2):
-        for block in range(0, blocks, 2):
-            rows = jnp.concatenate(
-                [
-                    held[part, block],
-                    held[part + parts // 2, block],
-                    held[part, block + 1],
-                    held[part + parts // 2, block + 1],
-                ],
-                axis=0,
-            )
-            result = nt(first, rows)
+
+    @pl.loop(0, parts // 2)
+    def _(part):
+        @pl.loop(0, blocks // 2)
+        def _(step):
+            block = 2 * step
+            rows = [
+                held[part + place, block + offset]
+                for offset in range(2)
+                for place in (0, parts // 2)
+            ]
+            result = nt(first, jnp.concatenate(rows, axis=0))
             for k in range(2):
                 three = result[3 * size * k : 3 * size * (k + 1)]
                 value = three[:size] + three[size : 2 * size] + three[2 * size :]
                 high, middle, _ = split(value)
                 pair = (2 * part + k) * blocks + block
-                lanes = slice(pair * both, (pair + 2) * both)
-                half[0, :, lanes] = high
-                half[1, :, lanes] = middle
-    lines = [[] for _ in range(seqs)]
-    for pair in range(pairs):
-        lanes = slice(pair * both, (pair + 1) * both)
-        rows = jnp.concatenate([half[0, :, lanes], half[1, :, lanes]], axis=1)
+                for offset in range(2):
+                    lanes = slice(offset * both, (offset + 1) * both)
+                    half[pair + offset] = jnp.concatenate([high[:, lanes], middle[:, lanes]], axis=1)
+
+    group = 8
+
+    @pl.loop(0, pairs // group)
+    def _(step):
+        start = pl.multiple_of(step * group, group)
+        rows = half[pl.ds(start, group)].reshape(group * size, 2 * both)
         result = nn(rows, second)
         result = (result[:, :both] + result[:, both:]).astype(jnp.bfloat16).astype(jnp.float32)
+        result = result.reshape(group, size, both)
         for s in range(seqs):
-            lines[s].append(jnp.sum(result * samples[s], axis=0, keepdims=True))
-    lines = jnp.concatenate([line for part in lines for line in part], axis=0)
+            lines[s, pl.ds(start, group)] = jnp.sum(result * samples[s][None], axis=1)
+
     shape = (8, both)
     ends = jnp.where(
         (lax.broadcasted_iota(jnp.int32, shape, 1) < size)
@@ -329,7 +338,7 @@
         1.0,
         0.0,
     )
-    result = nt(ends, lines, HIGHEST)
+    result = nt(ends, lines[...].reshape(seqs * pairs, both), HIGHEST)
     for s in range(seqs):
         for k in range(2):
             out[s : s + 1, k * pairs : (k + 1) * pairs] = result[
@@ -338,18 +347,19 @@
 
 
 def score(place, own, other, samples, pieces, tokens):
-    blocks, rank, both = pieces[0].shape
-    parts = len(pieces)
-    count = 2 * parts * blocks
+    _, blocks, rank, both = pieces[0].shape
+    parts = sum(piece.shape[0] for piece in pieces)
+    pairs = parts * blocks
     seqs = sum(sample.shape[0] for sample in samples)
     return pl.pallas_call(
         functools.partial(score_kernel, tokens),
-        in_specs=[smem()] + [vmem()] * (4 + parts),
+        in_specs=[smem()] + [vmem()] * (4 + len(pieces)),
         out_specs=vmem(),
-        out_shape=jax.ShapeDtypeStruct((seqs, count), jnp.float32),
+        out_shape=jax.ShapeDtypeStruct((seqs, 2 * pairs), jnp.float32),
         scratch_shapes=[
             pltpu.VMEM((parts, blocks, rank, both), pieces[0].dtype),
-            pltpu.VMEM((2, rank, count * rank), jnp.bfloat16),
+            pltpu.VMEM((pairs, rank, 2 * both), jnp.bfloat16),
+            pltpu.VMEM((seqs, pairs, both), jnp.float32),
         ],
         compiler_params=params(16),
         name="score",
@@ -374,28 +384,29 @@
     half = seqs // 2
     x = project_in(side, acts, proj_in)
     x_outer = inwards(x)
-    g = project_out(side, grads, proj_out, 0, half, x)
+    (g,) = project_out(side, grads, proj_out, queries, 0, half, x, False)
     g_outer = inwards(g)
-    h = project_out(side, grads, proj_out, half, seqs - half, g)
+    h, packed = project_out(side, grads, proj_out, queries, half, seqs - half, g, True)
     h_outer = inwards(h)
-    x_far = x[1] + after(x_outer, h)[1]
-    x_other = across(x_far)
-    g_far = g[1] + after(g_outer, x_far)[1]
-    g_other = across(g_far)
-    packed = pack(side, queries, g_far)
-    query_pieces = [packed] + [swap(packed, "dp", bits) for bits in range(1, parts)]
-    h_far = h[1] + after(h_outer, packed)[1]
+    far = jnp.concatenate([x[1] + after(x_outer, h)[1], g[1] + after(g_outer, h)[1]], axis=1)
+    other = across(far)
+    pieces = [after(packed, far)[None]]
+    bit = 1
+    while bit < parts:
+        mine = pieces[0] if bit == 1 else jnp.concatenate(pieces, axis=0)
+        pieces = [mine, swap(mine, "dp", bit)]
+        bit *= 2
+    h_far = h[1] + after(h_outer, pieces[0])[1]
     h_other = across(h_far)
-    x_sum, cov = cov_in(x, x_outer, x_other, h_far)
-    cov, sample = cov_out(x_sum, cov, g, g_outer, g_other, 0, half)
-    cov, last = cov_out(x_sum, cov, h, h_outer, h_other, half, seqs - half)
+    x_rest, cov, sample = first_half(x, x_outer, g, g_outer, other, h_far, half)
+    cov, last = second_half(x_rest, cov, h, h_outer, h_other, seqs - half)
     other = jnp.zeros_like(cov)
     bit = 1
     while bit < parts:
         cov = cov if bit == 1 else cov + other
         other = swap(cov, "dp", bit)
         bit *= 2
-    scores = score(place, cov, other, [sample, last], query_pieces, tokens)
+    scores = score(place, cov, other, [sample, last], pieces, tokens)
     scores = scores + across(scores)
     outer = lax.ppermute(scores, "tensor", [(1, 0), (2, 3)])
     return jnp.where((column == 1) | (column == 2), scores, outer)
@@ -468,7 +479,7 @@
 def local(acts, grads, proj_in, proj_out, queries):
     parts = lax.axis_size("dp")
     even = parts > 1 and parts & (parts - 1) == 0
-    if lax.axis_size("tensor") == 4 and even and acts.shape[0] > 1 and queries.shape[0] % 4 == 0:
+    if lax.axis_size("tensor") == 4 and even and acts.shape[0] > 1 and queries.shape[0] % 8 == 0:
         return local_owned(acts, grads, proj_in, proj_out, queries)
     return local_general(acts, grads, proj_in, proj_out, queries)
 

time: 62.6 us -> 70.2 us (1.12)
  Pallas kernels: 27.5 us -> 33.2 us
  waiting for transfers between devices: 18.6 us -> 21.7 us
  starting transfers between devices: 15.3 us -> 14.1 us
    pallas_call x2, Pallas kernels: 16.4 us -> 22.2 us  [project_out(): pl.pallas_call(functools.partial(project_out_kernel, first), in_specs=[sm...]
    ppermute x1, waiting for transfers between devices: 11.6 us -> 15 us  [local_owned(): outer = lax.ppermute(scores, 'tensor', [(1, 0), (2, 3)])]
    pallas_call x4 -> x2, Pallas kernels: 2.64 us -> 1.37 us  [the longest x1 0.77 us: first_half(): pl.pallas_call(first_kernel, in_specs=[vmem()] * 5 + [hbm()], out_specs=[...]
    pallas_call x1, Pallas kernels: 4.35 us -> 5.52 us  [score(): pl.pallas_call(functools.partial(score_kernel, tokens), in_specs=[smem()]...]
    ppermute x4 -> x3, starting transfers between devices: 2.7 us -> 2.04 us  [across(): return lax.ppermute(value, 'tensor', [(1, 2), (2, 1)])]
    ppermute x5 -> x4, starting transfers between devices: 3.77 us -> 3.19 us  [swap(): lax.ppermute(value, axis, [(i, i ^ bit) for i in range(lax.axis_size(axis...]
    ppermute x5 -> x4, waiting for transfers between devices: 3.97 us -> 4.26 us  [swap(): lax.ppermute(value, axis, [(i, i ^ bit) for i in range(lax.axis_size(axis...]
  transfers between devices with their start and end apart: 13 -> 11, of which waited for: 5 -> 5; matrix products, arithmetic and copies ran while one was open for 0% -> 0% of each run, Pallas kernels for 31% -> 34%
where the time goes in v6:
time: 70.2 us; the launch traced here: 69.9 us
  Pallas kernels  33.2 us (47%)
  waiting for transfers between devices  21.7 us (31%)
  starting transfers between devices  14.1 us (20%)
  other arithmetic  0.72 us (1%)
    pallas_call x2, Pallas kernels, project_out(): pl.pallas_call(functools.partial(project_out_kernel, first), in_specs=[sm...  22.2 us
    ppermute x1, waiting for transfers between devices, local_owned(): outer = lax.ppermute(scores, 'tensor', [(1, 0), (2, 3)])  15 us
    ppermute x3, starting transfers between devices, inwards(): return lax.ppermute(value, 'tensor', [(0, 1), (3, 2)])  7.57 us
    pallas_call x1, Pallas kernels, score(): pl.pallas_call(functools.partial(score_kernel, tokens), in_specs=[smem()]...  5.52 us
    ppermute x4, waiting for transfers between devices, swap(): lax.ppermute(value, axis, [(i, i ^ bit) for i in range(lax.axis_size(axis...  4.26 us
    pallas_call x1, Pallas kernels, project_in(): pl.pallas_call(project_in_kernel, in_specs=[smem(), hbm(), hbm()], out_sp...  4.09 us
    ppermute x4, starting transfers between devices, swap(): lax.ppermute(value, axis, [(i, i ^ bit) for i in range(lax.axis_size(axis...  3.19 us
    ppermute x3, waiting for transfers between devices, inwards(): return lax.ppermute(value, 'tensor', [(0, 1), (3, 2)])  2.41 us
  transfers between devices with their start and end apart: 11, of which 5 were waited for; matrix products, arithmetic and copies ran while one was open for 0% of the time, Pallas kernels for 34%

profile of v6, /device:TPU:0, one launch (start us, length us, event | category | flops | bytes accessed | tf_op | source)
XLA Modules:
  0.0 69.9 jit_solution(17754397864802793270)
XLA Ops:
  0.0 0.0 copy-start
  0.0 4.1 %project_in.1.after.x_ref = f32[2,64,1024]{2,1,0:T(8,128)S(1)} custom-call(s32[1]{0:T(128)} %bitcast.1.side_ref, bf16[4,256,2048]{2,1,0:T(8,128)(2,1)} %rows_hbm.3, bf16[2,64,2048]{2,1,0:T(8,128)(2,1)} %proj_hbm.1), custom_call_target="tpu_custom_call" | custom-call | tf_op jit(solution)/shard_map/project_in/pallas_call | solution.py:75
  4.1 5.0 %collective-permute-start = (f32[2,64,1024]{2,1,0:T(8,128)S(1)}, f32[2,64,1024]{2,1,0:T(8,128)S(1)}, u32[]{:S(2)}, u32[]{:S(2)}) collective-permute-start(f32[2,64,1024]{2,1,0:T(8,128)S(1)} %project_in.1.after.x_ref), channel_id=1, source_target_pairs={{0,4},{12,8},{1,5},{13,9},{2,6},{14,10},{3,7},{15,11},{16,20},{28,... | collective-permute-start | bytes 1572872 | tf_op jit(solution)/shard_map/ppermute | solution.py:153
  9.1 0.0 copy-done
  9.1 11.1 %project_out.2.after.g_ref = f32[2,64,512]{2,1,0:T(8,128)S(1)} custom-call(s32[1]{0:T(128)} %bitcast.1.side_ref, bf16[2,4,256,7168]{3,2,1,0:T(8,128)(2,1)} %rows_hbm.5, bf16[2,64,7168]{2,1,0:T(8,128)(2,1)S(1)} %copy-done, bf16[16,2,64,64]{3,2,1,0:T(8,128)(2,1)} %queries_hbm.3, f32[2,64,1024]{2,1,0:T(8,128)S(1)} %project_in.1.after.x_ref), custom_call_target="tpu_custom_call" | custom-call | tf_op jit(solution)/shard_map/project_out/pallas_call | solution.py:136
  20.2 1.3 %collective-permute-start.1 = (f32[2,64,512]{2,1,0:T(8,128)S(1)}, f32[2,64,512]{2,1,0:T(8,128)S(1)}, u32[]{:S(2)}, u32[]{:S(2)}) collective-permute-start(f32[2,64,512]{2,1,0:T(8,128)S(1)} %project_out.2.after.g_ref), channel_id=1, source_target_pairs={{0,4},{12,8},{1,5},{13,9},{2,6},{14,10},{3,7},{15,11},{16,20},{28,... | collective-permute-start | bytes 786440 | tf_op jit(solution)/shard_map/ppermute | solution.py:153
  21.5 11.2 %project_out.3 = (f32[2,64,512]{2,1,0:T(8,128)S(1)}, bf16[8,64,128]{2,1,0:T(8,128)(2,1)S(1)}) custom-call(s32[1]{0:T(128)} %bitcast.1.side_ref, bf16[2,4,256,7168]{3,2,1,0:T(8,128)(2,1)} %rows_hbm.5, bf16[2,64,7168]{2,1,0:T(8,128)(2,1)S(1)} %copy-done, bf16[16,2,64,64]{3,2,1,0:T(8,128)(2,1)} %queries_hbm.3, f32[2,64,512]{2,1,0:T(8,128)S(1)} %project_out.2.after.g_ref), custom_call_target="tpu_custom_call" | custom-call | tf_op jit(solution)/shard_map/project_out/pallas_call | solution.py:136
  32.6 1.3 %collective-permute-start.3 = (f32[2,64,512]{2,1,0:T(8,128)S(1)}, f32[2,64,512]{2,1,0:T(8,128)S(1)}, u32[]{:S(2)}, u32[]{:S(2)}) collective-permute-start(f32[2,64,512]{2,1,0:T(8,128)S(1)} %get-tuple-element.16.h_ref), channel_id=1, source_target_pairs={{0,4},{12,8},{1,5},{13,9},{2,6},{14,10},{3,7},{15,11},{16,20},{28,... | collective-permute-start | bytes 786440 | tf_op jit(solution)/shard_map/ppermute | solution.py:153
  34.0 0.0 collective-permute-done.1.g_outer
  34.0 0.0 collective-permute-done.x_outer
  34.1 0.1 collective-permute-start.4
  34.2 0.7 collective-permute-start.2
  34.9 0.6 collective-permute-done.4
  35.5 1.6 %collective-permute-start.8 = (bf16[2,8,64,128]{3,2,1,0:T(8,128)(2,1)S(1)}, bf16[2,8,64,128]{3,2,1,0:T(8,128)(2,1)S(1)}, u32[]{:S(2)}, u32[]{:S(2)}) collective-permute-start(bf16[2,8,64,128]{3,2,1,0:T(8,128)(2,1)S(1)} %pad_maximum_fusion.1.refs_0_), channel_id=1, source_target_pairs={{0,2},{1,3},{2,0},{3,1},{4,6},{5,7},{6,4},{7,5},{8,10},{9,11},{10,... | collective-permute-start | bytes 786440 | tf_op jit(solution)/shard_map/ppermute | solution.py:370
  37.1 2.4 %collective-permute-done.3.h_outer = f32[2,64,512]{2,1,0:T(8,128)S(1)} collective-permute-done((f32[2,64,512]{2,1,0:T(8,128)S(1)}, f32[2,64,512]{2,1,0:T(8,128)S(1)}, u32[]{:S(2)}, u32[]{:S(2)}) %collective-permute-start.3) | collective-permute-done | bytes 262176 | tf_op jit(solution)/shard_map/ppermute | solution.py:153
  39.5 0.7 collective-permute-start.5
  40.2 0.0 collective-permute-done.2.other
  40.2 0.8 %first_half.1 = (f32[64,512]{1,0:T(8,128)S(1)}, f32[64,128]{1,0:T(8,128)S(1)}, f32[2,64,128]{2,1,0:T(8,128)S(1)}) custom-call(f32[2,64,1024]{2,1,0:T(8,128)S(1)} %project_in.1.after.x_ref, f32[2,64,1024]{2,1,0:T(8,128)S(1)} %collective-permute-done.x_outer, f32[2,64,512]{2,1,0:T(8,128)S(1)} %project_out.2.after.g_ref, ...), custom_call_target="tpu_custom_call" | custom-call | tf_op jit(solution)/shard_map/first_half/pallas_call | solution.py:196
  41.0 0.0 collective-permute-done.5.other
  41.0 0.6 second_half.1
  41.6 0.1 collective-permute-start.6
  41.7 1.2 %collective-permute-done.6 = f32[64,128]{1,0:T(8,128)S(1)} collective-permute-done((f32[64,128]{1,0:T(8,128)S(1)}, f32[64,128]{1,0:T(8,128)S(1)}, u32[]{:S(2)}, u32[]{:S(2)}) %collective-permute-start.6) | collective-permute-done | bytes 32800 | tf_op jit(solution)/shard_map/ppermute | solution.py:370
  42.9 1.5 %collective-permute-start.7 = (f32[64,128]{1,0:T(8,128)S(1)}, f32[64,128]{1,0:T(8,128)S(1)}, u32[]{:S(2)}, u32[]{:S(2)}) collective-permute-start(f32[64,128]{1,0:T(8,128)S(1)} %add.29.own_ref), channel_id=1, source_target_pairs={{0,2},{1,3},{2,0},{3,1},{4,6},{5,7},{6,4},{7,5},{8,10},{9,11},{10,... | collective-permute-start | bytes 98312 | tf_op jit(solution)/shard_map/ppermute | solution.py:370
  44.3 0.0 collective-permute-done.8.refs_1_
  44.3 2.4 %collective-permute-done.7.other_ref = f32[64,128]{1,0:T(8,128)S(1)} collective-permute-done((f32[64,128]{1,0:T(8,128)S(1)}, f32[64,128]{1,0:T(8,128)S(1)}, u32[]{:S(2)}, u32[]{:S(2)}) %collective-permute-start.7) | collective-permute-done | bytes 32800 | tf_op jit(solution)/shard_map/ppermute | solution.py:370
  46.8 5.5 %score.1 = f32[4,64]{1,0:T(4,128)S(1)} custom-call(s32[1]{0:T(128)} %bitcast.place_ref, f32[64,128]{1,0:T(8,128)S(1)} %add.29.own_ref, f32[64,128]{1,0:T(8,128)S(1)} %collective-permute-done.7.other_ref, f32[2,64,128]{2,1,0:T(8,128)S(1)} %get-tuple-element.25.first_ref, f32[2,64,128]{2,1,0:T(8,128)S(1)} %get-tuple-element.26.second_ref, ...), custom_call_target="tpu_custom_call" | custom-call | tf_op jit(solution)/shard_map/score/pallas_call | solution.py:354
  52.3 0.7 collective-permute-start.9
  53.0 0.0 collective-permute-done.9
  53.0 1.3 %collective-permute-start.10 = (f32[4,64]{1,0:T(4,128)S(1)}, f32[4,64]{1,0:T(4,128)S(1)}, u32[]{:S(2)}, u32[]{:S(2)}) collective-permute-start(f32[4,64]{1,0:T(4,128)S(1)} %add.30), channel_id=1, source_target_pairs={{4,0},{8,12},{5,1},{9,13},{6,2},{10,14},{7,3},{11,15},{20,16},{24,... | collective-permute-start | bytes 3080 | tf_op jit(solution)/shard_map/ppermute | solution.py:411
  54.3 15.0 %collective-permute-done.10 = f32[4,64]{1,0:T(4,128)S(1)} collective-permute-done((f32[4,64]{1,0:T(4,128)S(1)}, f32[4,64]{1,0:T(4,128)S(1)}, u32[]{:S(2)}, u32[]{:S(2)}) %collective-permute-start.10) | collective-permute-done | bytes 1056 | tf_op jit(solution)/shard_map/ppermute | solution.py:411
  69.3 0.6 broadcast_select_fusion
  (7 shorter events, 0.1 us)
Async XLA Ops:
  0.0 9.1 %copy-start = (bf16[2,64,7168]{2,1,0:T(8,128)(2,1)S(1)}, bf16[2,64,7168]{2,1,0:T(8,128)(2,1)}, u32[]{:S(2)}) copy-start(bf16[2,64,7168]{2,1,0:T(8,128)(2,1)} %proj_ref.3) | copy-start | bytes 5505028
  4.1 29.9 %collective-permute-start = (f32[2,64,1024]{2,1,0:T(8,128)S(1)}, f32[2,64,1024]{2,1,0:T(8,128)S(1)}, u32[]{:S(2)}, u32[]{:S(2)}) collective-permute-start(f32[2,64,1024]{2,1,0:T(8,128)S(1)} %project_in.1.after.x_ref), channel_id=1, source_target_pairs={{0,4},{12,8},{1,5},{13,9},{2,6},{14,10},{3,7},{15,11},{16,20},{28,... | collective-permute-start | bytes 1572872 | tf_op jit(solution)/shard_map/ppermute | solution.py:153
  20.2 13.8 %collective-permute-start.1 = (f32[2,64,512]{2,1,0:T(8,128)S(1)}, f32[2,64,512]{2,1,0:T(8,128)S(1)}, u32[]{:S(2)}, u32[]{:S(2)}) collective-permute-start(f32[2,64,512]{2,1,0:T(8,128)S(1)} %project_out.2.after.g_ref), channel_id=1, source_target_pairs={{0,4},{12,8},{1,5},{13,9},{2,6},{14,10},{3,7},{15,11},{16,20},{28,... | collective-permute-start | bytes 786440 | tf_op jit(solution)/shard_map/ppermute | solution.py:153
  32.6 6.8 %collective-permute-start.3 = (f32[2,64,512]{2,1,0:T(8,128)S(1)}, f32[2,64,512]{2,1,0:T(8,128)S(1)}, u32[]{:S(2)}, u32[]{:S(2)}) collective-permute-start(f32[2,64,512]{2,1,0:T(8,128)S(1)} %get-tuple-element.16.h_ref), channel_id=1, source_target_pairs={{0,4},{12,8},{1,5},{13,9},{2,6},{14,10},{3,7},{15,11},{16,20},{28,... | collective-permute-start | bytes 786440 | tf_op jit(solution)/shard_map/ppermute | solution.py:153
  34.1 1.4 %collective-permute-start.4 = (bf16[1,8,64,128]{3,2,1,0:T(8,128)(2,1)S(1)}, bf16[1,8,64,128]{3,2,1,0:T(8,128)(2,1)S(1)}, u32[]{:S(2)}, u32[]{:S(2)}) collective-permute-start(bf16[1,8,64,128]{3,2,1,0:T(8,128)(2,1)S(1)} %bitcast.9), channel_id=1, source_target_pairs={{0,1},{1,0},{2,3},{3,2},{4,5},{5,4},{6,7},{7,6},{8,9},{9,8},{10,11... | collective-permute-start | bytes 393224 | tf_op jit(solution)/shard_map/ppermute | solution.py:370
  34.2 6.0 %collective-permute-start.2 = (f32[64,1536]{1,0:T(8,128)S(1)}, f32[64,1536]{1,0:T(8,128)S(1)}, u32[]{:S(2)}, u32[]{:S(2)}) collective-permute-start(f32[64,1536]{1,0:T(8,128)S(1)} %pad_maximum_fusion), channel_id=1, source_target_pairs={{4,8},{8,4},{5,9},{9,5},{6,10},{10,6},{7,11},{11,7},{20,24},{24,20... | collective-permute-start | bytes 1179656 | tf_op jit(solution)/shard_map/ppermute | solution.py:157
  35.5 8.8 %collective-permute-start.8 = (bf16[2,8,64,128]{3,2,1,0:T(8,128)(2,1)S(1)}, bf16[2,8,64,128]{3,2,1,0:T(8,128)(2,1)S(1)}, u32[]{:S(2)}, u32[]{:S(2)}) collective-permute-start(bf16[2,8,64,128]{3,2,1,0:T(8,128)(2,1)S(1)} %pad_maximum_fusion.1.refs_0_), channel_id=1, source_target_pairs={{0,2},{1,3},{2,0},{3,1},{4,6},{5,7},{6,4},{7,5},{8,10},{9,11},{10,... | collective-permute-start | bytes 786440 | tf_op jit(solution)/shard_map/ppermute | solution.py:370
  39.5 1.5 %collective-permute-start.5 = (f32[64,512]{1,0:T(8,128)S(1)}, f32[64,512]{1,0:T(8,128)S(1)}, u32[]{:S(2)}, u32[]{:S(2)}) collective-permute-start(f32[64,512]{1,0:T(8,128)S(1)} %add_bitcast_fusion.after), channel_id=1, source_target_pairs={{4,8},{8,4},{5,9},{9,5},{6,10},{10,6},{7,11},{11,7},{20,24},{24,20... | collective-permute-start | bytes 393224 | tf_op jit(solution)/shard_map/ppermute | solution.py:157
  41.6 1.3 %collective-permute-start.6 = (f32[64,128]{1,0:T(8,128)S(1)}, f32[64,128]{1,0:T(8,128)S(1)}, u32[]{:S(2)}, u32[]{:S(2)}) collective-permute-start(f32[64,128]{1,0:T(8,128)S(1)} %get-tuple-element.24), channel_id=1, source_target_pairs={{0,1},{1,0},{2,3},{3,2},{4,5},{5,4},{6,7},{7,6},{8,9},{9,8},{10,11... | collective-permute-start | bytes 98312 | tf_op jit(solution)/shard_map/ppermute | solution.py:370
  42.9 3.9 %collective-permute-start.7 = (f32[64,128]{1,0:T(8,128)S(1)}, f32[64,128]{1,0:T(8,128)S(1)}, u32[]{:S(2)}, u32[]{:S(2)}) collective-permute-start(f32[64,128]{1,0:T(8,128)S(1)} %add.29.own_ref), channel_id=1, source_target_pairs={{0,2},{1,3},{2,0},{3,1},{4,6},{5,7},{6,4},{7,5},{8,10},{9,11},{10,... | collective-permute-start | bytes 98312 | tf_op jit(solution)/shard_map/ppermute | solution.py:370
  52.3 0.7 collective-permute-start.9
  53.0 16.3 %collective-permute-start.10 = (f32[4,64]{1,0:T(4,128)S(1)}, f32[4,64]{1,0:T(4,128)S(1)}, u32[]{:S(2)}, u32[]{:S(2)}) collective-permute-start(f32[4,64]{1,0:T(4,128)S(1)} %add.30), channel_id=1, source_target_pairs={{4,0},{8,12},{5,1},{9,13},{6,2},{10,14},{7,3},{11,15},{20,16},{24,... | collective-permute-start | bytes 3080 | tf_op jit(solution)/shard_map/ppermute | solution.py:411

commit v7 on v6

--- a/solution.py
+++ b/solution.py
@@ -63,7 +63,7 @@
     @pl.loop(0, seqs)
     def _(s):
         copy(s).wait()
-        part = nt(proj[...].reshape(2 * rank, width), rows[s])
+        part = nt(rows[s], proj[...].reshape(2 * rank, width)).T
         tokens = pl.ds(pl.multiple_of(s * length, length), length)
         out[side_ref[0], :, tokens] = part[:rank]
         out[1 - side_ref[0], :, tokens] = part[rank:]
@@ -93,31 +93,39 @@
     packed, (rows, held, sems, sem) = refs[:-4], refs[-4:]
     _, seqs, length, width = rows.shape
     half = width // 2
-    copies = {}
+
+    def chunk(layer, s, part):
+        lanes = pl.ds(part * half, half)
+        return pltpu.make_async_copy(
+            rows_hbm.at[layer, first + s, :, lanes],
+            rows.at[layer, s, :, lanes],
+            sems.at[layer, s, part],
+        )
+
     for s in range(seqs):
         for part in range(2):
-            lanes = pl.ds(part * half, half)
             for layer in range(2):
-                copies[s, part, layer] = pltpu.make_async_copy(
-                    rows_hbm.at[layer, first + s, :, lanes],
-                    rows.at[layer, s, :, lanes],
-                    sems.at[layer, s, part],
-                )
-                copies[s, part, layer].start()
+                chunk(layer, s, part).start()
     if packed:
         copy = pltpu.make_async_copy(queries_hbm.at[:, side_ref[0]], held, sem)
         copy.start()
-    for s in range(seqs):
+
+    @pl.loop(0, seqs)
+    def _(s):
         values = [None, None]
         for part in range(2):
             lanes = slice(part * half, (part + 1) * half)
             for layer in range(2):
-                copies[s, part, layer].wait()
-                value = nt(proj_ref[layer, :, lanes], rows[layer, s, :, lanes])
+                chunk(layer, s, part).wait()
+            for layer in range(2):
+                value = nt(rows[layer, s, :, lanes], proj_ref[layer, :, lanes])
                 values[layer] = value if part == 0 else values[layer] + value
-        tokens = slice(s * length, (s + 1) * length)
-        out[side_ref[0], :, tokens] = values[0]
-        out[1 - side_ref[0], :, tokens] = values[1]
+        tokens = pl.ds(pl.multiple_of(s * length, length), length)
+        turned = jnp.concatenate(values, axis=1).T
+        rank = turned.shape[0] // 2
+        out[side_ref[0], :, tokens] = turned[:rank]
+        out[1 - side_ref[0], :, tokens] = turned[rank:]
+
     if packed:
         copy.wait()
         blocks = held.shape[0] // 2
@@ -251,15 +259,10 @@
     x = (2.0 * start * steps[0]) * eye - (start * steps[0]) * y
     y = steps[0] * (2.0 * y - nn(y, y, HIGHEST))
 
-    def step(k, pair):
-        x, y = pair
-        scale = jnp.float32(steps[1])
-        for place in range(2, len(steps) - 1):
-            scale = jnp.where(k == place, jnp.float32(steps[place]), scale)
+    for scale in steps[1:-1]:
         product = nn(jnp.concatenate([x, y], axis=0), y, HIGHEST)
-        return scale * (2.0 * x - product[:both]), scale * (2.0 * y - product[both:])
-
-    x, y = lax.fori_loop(1, len(steps) - 1, step, (x, y))
+        x = scale * (2.0 * x - product[:both])
+        y = scale * (2.0 * y - product[both:])
     x = steps[-1] * (2.0 * x - nn(x, y, HIGHEST))
     x = x + nn(x, eye - nn(matrix, x, HIGHEST), HIGHEST)
     return x / unit
@@ -274,7 +277,7 @@
 
 
 def score_kernel(tokens, place_ref, own_ref, other_ref, first_ref, second_ref, *refs):
-    pieces, (out, held, half, lines) = refs[:-4], refs[-4:]
+    pieces, (out, held, half) = refs[:-3], refs[-3:]
     parts = held.shape[0]
     k = 0
     for piece in pieces:
@@ -299,38 +302,35 @@
     once = jnp.concatenate([high, middle], axis=1)
     second = jnp.concatenate([once, once], axis=0)
 
-    @pl.loop(0, parts // 2)
-    def _(part):
-        @pl.loop(0, blocks // 2)
-        def _(step):
-            block = 2 * step
-            rows = [
-                held[part + place, block + offset]
-                for offset in range(2)
-                for place in (0, parts // 2)
-            ]
-            result = nt(first, jnp.concatenate(rows, axis=0))
+    for part in range(parts // 2):
+        for block in range(0, blocks, 2):
+            rows = jnp.concatenate(
+                [
+                    held[part, block],
+                    held[part + parts // 2, block],
+                    held[part, block + 1],
+                    held[part + parts // 2, block + 1],
+                ],
+                axis=0,
+            )
+            result = nt(first, rows)
             for k in range(2):
                 three = result[3 * size * k : 3 * size * (k + 1)]
                 value = three[:size] + three[size : 2 * size] + three[2 * size :]
                 high, middle, _ = split(value)
                 pair = (2 * part + k) * blocks + block
-                for offset in range(2):
-                    lanes = slice(offset * both, (offset + 1) * both)
-                    half[pair + offset] = jnp.concatenate([high[:, lanes], middle[:, lanes]], axis=1)
-
-    group = 8
-
-    @pl.loop(0, pairs // group)
-    def _(step):
-        start = pl.multiple_of(step * group, group)
-        rows = half[pl.ds(start, group)].reshape(group * size, 2 * both)
+                lanes = slice(pair * both, (pair + 2) * both)
+                half[0, :, lanes] = high
+                half[1, :, lanes] = middle
+    lines = [[] for _ in range(seqs)]
+    for pair in range(pairs):
+        lanes = slice(pair * both, (pair + 1) * both)
+        rows = jnp.concatenate([half[0, :, lanes], half[1, :, lanes]], axis=1)
         result = nn(rows, second)
         result = (result[:, :both] + result[:, both:]).astype(jnp.bfloat16).astype(jnp.float32)
-        result = result.reshape(group, size, both)
         for s in range(seqs):
-            lines[s, pl.ds(start, group)] = jnp.sum(result * samples[s][None], axis=1)
-
+            lines[s].append(jnp.sum(result * samples[s], axis=0, keepdims=True))
+    lines = jnp.concatenate([line for part in lines for line in part], axis=0)
     shape = (8, both)
     ends = jnp.where(
         (lax.broadcasted_iota(jnp.int32, shape, 1) < size)
@@ -338,7 +338,7 @@
         1.0,
         0.0,
     )
-    result = nt(ends, lines[...].reshape(seqs * pairs, both), HIGHEST)
+    result = nt(ends, lines, HIGHEST)
     for s in range(seqs):
         for k in range(2):
             out[s : s + 1, k * pairs : (k + 1) * pairs] = result[
@@ -358,8 +358,7 @@
         out_shape=jax.ShapeDtypeStruct((seqs, 2 * pairs), jnp.float32),
         scratch_shapes=[
             pltpu.VMEM((parts, blocks, rank, both), pieces[0].dtype),
-            pltpu.VMEM((pairs, rank, 2 * both), jnp.bfloat16),
-            pltpu.VMEM((seqs, pairs, both), jnp.float32),
+            pltpu.VMEM((2, rank, pairs * both), jnp.bfloat16),
         ],
         compiler_params=params(16),
         name="score",

time: 70.2 us -> 64.1 us (0.913)
  Pallas kernels: 33.2 us -> 25.8 us
  waiting for transfers between devices: 21.7 us -> 23.1 us
    pallas_call x2, Pallas kernels: 22.2 us -> 15.9 us  [project_out(): pl.pallas_call(functools.partial(project_out_kernel, first), in_specs=[sm...]
    ppermute x1, waiting for transfers between devices: 15 us -> 16.4 us  [local_owned(): outer = lax.ppermute(scores, 'tensor', [(1, 0), (2, 3)])]
    pallas_call x1, Pallas kernels: 5.52 us -> 4.35 us  [score(): pl.pallas_call(functools.partial(score_kernel, tokens), in_specs=[smem()]...]
  transfers between devices with their start and end apart: 11 -> 11, of which waited for: 5 -> 5; matrix products, arithmetic and copies ran while one was open for 0% -> 0% of each run, Pallas kernels for 34% -> 27%
where the time goes in v7:
time: 64.1 us; the launch traced here: 63.8 us
  Pallas kernels  25.8 us (40%)
  waiting for transfers between devices  23.1 us (36%)
  starting transfers between devices  14.1 us (22%)
  other arithmetic  0.72 us (1%)
    ppermute x1, waiting for transfers between devices, local_owned(): outer = lax.ppermute(scores, 'tensor', [(1, 0), (2, 3)])  16.4 us
    pallas_call x2, Pallas kernels, project_out(): pl.pallas_call(functools.partial(project_out_kernel, first), in_specs=[sm...  15.9 us
    ppermute x3, starting transfers between devices, inwards(): return lax.ppermute(value, 'tensor', [(0, 1), (3, 2)])  7.57 us
    pallas_call x1, Pallas kernels, score(): pl.pallas_call(functools.partial(score_kernel, tokens), in_specs=[smem()]...  4.35 us
    ppermute x4, waiting for transfers between devices, swap(): lax.ppermute(value, axis, [(i, i ^ bit) for i in range(lax.axis_size(axis...  4.26 us
    pallas_call x1, Pallas kernels, project_in(): pl.pallas_call(project_in_kernel, in_specs=[smem(), hbm(), hbm()], out_sp...  4.18 us
    ppermute x4, starting transfers between devices, swap(): lax.ppermute(value, axis, [(i, i ^ bit) for i in range(lax.axis_size(axis...  3.19 us
    ppermute x3, waiting for transfers between devices, inwards(): return lax.ppermute(value, 'tensor', [(0, 1), (3, 2)])  2.42 us
  transfers between devices with their start and end apart: 11, of which 5 were waited for; matrix products, arithmetic and copies ran while one was open for 0% of the time, Pallas kernels for 27%

profile of v7, /device:TPU:0, one launch (start us, length us, event | category | flops | bytes accessed | tf_op | source)
XLA Modules:
  0.0 63.8 jit_solution(10727071856832123542)
XLA Ops:
  0.0 0.0 copy-start
  0.0 4.2 %project_in.1.after.x_ref = f32[2,64,1024]{2,1,0:T(8,128)S(1)} custom-call(s32[1]{0:T(128)} %bitcast.1.side_ref, bf16[4,256,2048]{2,1,0:T(8,128)(2,1)} %rows_hbm.3, bf16[2,64,2048]{2,1,0:T(8,128)(2,1)} %proj_hbm.1), custom_call_target="tpu_custom_call" | custom-call | tf_op jit(solution)/shard_map/project_in/pallas_call | solution.py:75
  4.2 5.0 %collective-permute-start = (f32[2,64,1024]{2,1,0:T(8,128)S(1)}, f32[2,64,1024]{2,1,0:T(8,128)S(1)}, u32[]{:S(2)}, u32[]{:S(2)}) collective-permute-start(f32[2,64,1024]{2,1,0:T(8,128)S(1)} %project_in.1.after.x_ref), channel_id=1, source_target_pairs={{0,4},{12,8},{1,5},{13,9},{2,6},{14,10},{3,7},{15,11},{16,20},{28,... | collective-permute-start | bytes 1572872 | tf_op jit(solution)/shard_map/ppermute | solution.py:161
  9.2 0.0 copy-done
  9.2 7.9 %project_out.2.after.g_ref = f32[2,64,512]{2,1,0:T(8,128)S(1)} custom-call(s32[1]{0:T(128)} %bitcast.1.side_ref, bf16[2,4,256,7168]{3,2,1,0:T(8,128)(2,1)} %rows_hbm.5, bf16[2,64,7168]{2,1,0:T(8,128)(2,1)S(1)} %copy-done, bf16[16,2,64,64]{3,2,1,0:T(8,128)(2,1)} %queries_hbm.3, f32[2,64,1024]{2,1,0:T(8,128)S(1)} %project_in.1.after.x_ref), custom_call_target="tpu_custom_call" | custom-call | tf_op jit(solution)/shard_map/project_out/pallas_call | solution.py:144
  17.1 1.3 %collective-permute-start.1 = (f32[2,64,512]{2,1,0:T(8,128)S(1)}, f32[2,64,512]{2,1,0:T(8,128)S(1)}, u32[]{:S(2)}, u32[]{:S(2)}) collective-permute-start(f32[2,64,512]{2,1,0:T(8,128)S(1)} %project_out.2.after.g_ref), channel_id=1, source_target_pairs={{0,4},{12,8},{1,5},{13,9},{2,6},{14,10},{3,7},{15,11},{16,20},{28,... | collective-permute-start | bytes 786440 | tf_op jit(solution)/shard_map/ppermute | solution.py:161
  18.4 8.0 %project_out.3 = (f32[2,64,512]{2,1,0:T(8,128)S(1)}, bf16[8,64,128]{2,1,0:T(8,128)(2,1)S(1)}) custom-call(s32[1]{0:T(128)} %bitcast.1.side_ref, bf16[2,4,256,7168]{3,2,1,0:T(8,128)(2,1)} %rows_hbm.5, bf16[2,64,7168]{2,1,0:T(8,128)(2,1)S(1)} %copy-done, bf16[16,2,64,64]{3,2,1,0:T(8,128)(2,1)} %queries_hbm.3, f32[2,64,512]{2,1,0:T(8,128)S(1)} %project_out.2.after.g_ref), custom_call_target="tpu_custom_call" | custom-call | tf_op jit(solution)/shard_map/project_out/pallas_call | solution.py:144
  26.4 1.3 %collective-permute-start.3 = (f32[2,64,512]{2,1,0:T(8,128)S(1)}, f32[2,64,512]{2,1,0:T(8,128)S(1)}, u32[]{:S(2)}, u32[]{:S(2)}) collective-permute-start(f32[2,64,512]{2,1,0:T(8,128)S(1)} %get-tuple-element.16.h_ref), channel_id=1, source_target_pairs={{0,4},{12,8},{1,5},{13,9},{2,6},{14,10},{3,7},{15,11},{16,20},{28,... | collective-permute-start | bytes 786440 | tf_op jit(solution)/shard_map/ppermute | solution.py:161
  27.7 0.0 collective-permute-done.1.g_outer
  27.7 0.0 collective-permute-done.x_outer
  27.8 0.1 collective-permute-start.4
  27.9 0.7 %collective-permute-start.2 = (f32[64,1536]{1,0:T(8,128)S(1)}, f32[64,1536]{1,0:T(8,128)S(1)}, u32[]{:S(2)}, u32[]{:S(2)}) collective-permute-start(f32[64,1536]{1,0:T(8,128)S(1)} %pad_maximum_fusion), channel_id=1, source_target_pairs={{4,8},{8,4},{5,9},{9,5},{6,10},{10,6},{7,11},{11,7},{20,24},{24,20... | collective-permute-start | bytes 1179656 | tf_op jit(solution)/shard_map/ppermute | solution.py:165
  28.6 0.6 %collective-permute-done.4 = bf16[1,8,64,128]{3,2,1,0:T(8,128)(2,1)S(1)} collective-permute-done((bf16[1,8,64,128]{3,2,1,0:T(8,128)(2,1)S(1)}, bf16[1,8,64,128]{3,2,1,0:T(8,128)(2,1)S(1)}, u32[]{:S(2)}, u32[]{:S(2)}) %collective-permute-start.4) | collective-permute-done | bytes 131104 | tf_op jit(solution)/shard_map/ppermute | solution.py:369
  29.3 1.6 %collective-permute-start.8 = (bf16[2,8,64,128]{3,2,1,0:T(8,128)(2,1)S(1)}, bf16[2,8,64,128]{3,2,1,0:T(8,128)(2,1)S(1)}, u32[]{:S(2)}, u32[]{:S(2)}) collective-permute-start(bf16[2,8,64,128]{3,2,1,0:T(8,128)(2,1)S(1)} %pad_maximum_fusion.1.refs_0_), channel_id=1, source_target_pairs={{0,2},{1,3},{2,0},{3,1},{4,6},{5,7},{6,4},{7,5},{8,10},{9,11},{10,... | collective-permute-start | bytes 786440 | tf_op jit(solution)/shard_map/ppermute | solution.py:369
  30.8 2.4 %collective-permute-done.3.h_outer = f32[2,64,512]{2,1,0:T(8,128)S(1)} collective-permute-done((f32[2,64,512]{2,1,0:T(8,128)S(1)}, f32[2,64,512]{2,1,0:T(8,128)S(1)}, u32[]{:S(2)}, u32[]{:S(2)}) %collective-permute-start.3) | collective-permute-done | bytes 262176 | tf_op jit(solution)/shard_map/ppermute | solution.py:161
  33.2 0.7 %collective-permute-start.5 = (f32[64,512]{1,0:T(8,128)S(1)}, f32[64,512]{1,0:T(8,128)S(1)}, u32[]{:S(2)}, u32[]{:S(2)}) collective-permute-start(f32[64,512]{1,0:T(8,128)S(1)} %add_bitcast_fusion.after), channel_id=1, source_target_pairs={{4,8},{8,4},{5,9},{9,5},{6,10},{10,6},{7,11},{11,7},{20,24},{24,20... | collective-permute-start | bytes 393224 | tf_op jit(solution)/shard_map/ppermute | solution.py:165
  33.9 0.0 collective-permute-done.2.other
  33.9 0.8 %first_half.1 = (f32[64,512]{1,0:T(8,128)S(1)}, f32[64,128]{1,0:T(8,128)S(1)}, f32[2,64,128]{2,1,0:T(8,128)S(1)}) custom-call(f32[2,64,1024]{2,1,0:T(8,128)S(1)} %project_in.1.after.x_ref, f32[2,64,1024]{2,1,0:T(8,128)S(1)} %collective-permute-done.x_outer, f32[2,64,512]{2,1,0:T(8,128)S(1)} %project_out.2.after.g_ref, ...), custom_call_target="tpu_custom_call" | custom-call | tf_op jit(solution)/shard_map/first_half/pallas_call | solution.py:204
  34.7 0.0 collective-permute-done.5.other
  34.7 0.6 second_half.1
  35.3 0.1 collective-permute-start.6
  35.4 1.2 %collective-permute-done.6 = f32[64,128]{1,0:T(8,128)S(1)} collective-permute-done((f32[64,128]{1,0:T(8,128)S(1)}, f32[64,128]{1,0:T(8,128)S(1)}, u32[]{:S(2)}, u32[]{:S(2)}) %collective-permute-start.6) | collective-permute-done | bytes 32800 | tf_op jit(solution)/shard_map/ppermute | solution.py:369
  36.6 1.5 %collective-permute-start.7 = (f32[64,128]{1,0:T(8,128)S(1)}, f32[64,128]{1,0:T(8,128)S(1)}, u32[]{:S(2)}, u32[]{:S(2)}) collective-permute-start(f32[64,128]{1,0:T(8,128)S(1)} %add.29.own_ref), channel_id=1, source_target_pairs={{0,2},{1,3},{2,0},{3,1},{4,6},{5,7},{6,4},{7,5},{8,10},{9,11},{10,... | collective-permute-start | bytes 98312 | tf_op jit(solution)/shard_map/ppermute | solution.py:369
  38.1 0.0 collective-permute-done.8.refs_1_
  38.1 2.4 %collective-permute-done.7.other_ref = f32[64,128]{1,0:T(8,128)S(1)} collective-permute-done((f32[64,128]{1,0:T(8,128)S(1)}, f32[64,128]{1,0:T(8,128)S(1)}, u32[]{:S(2)}, u32[]{:S(2)}) %collective-permute-start.7) | collective-permute-done | bytes 32800 | tf_op jit(solution)/shard_map/ppermute | solution.py:369
  40.5 4.4 %score.1 = f32[4,64]{1,0:T(4,128)S(1)} custom-call(s32[1]{0:T(128)} %bitcast.place_ref, f32[64,128]{1,0:T(8,128)S(1)} %add.29.own_ref, f32[64,128]{1,0:T(8,128)S(1)} %collective-permute-done.7.other_ref, f32[2,64,128]{2,1,0:T(8,128)S(1)} %get-tuple-element.25.first_ref, f32[2,64,128]{2,1,0:T(8,128)S(1)} %get-tuple-element.26.second_ref, ...), custom_call_target="tpu_custom_call" | custom-call | tf_op jit(solution)/shard_map/score/pallas_call | solution.py:354
  44.9 0.7 %collective-permute-start.9 = (f32[4,64]{1,0:T(4,128)S(1)}, f32[4,64]{1,0:T(4,128)S(1)}, u32[]{:S(2)}, u32[]{:S(2)}) collective-permute-start(f32[4,64]{1,0:T(4,128)S(1)} %score.1), channel_id=1, source_target_pairs={{4,8},{8,4},{5,9},{9,5},{6,10},{10,6},{7,11},{11,7},{20,24},{24,20... | collective-permute-start | bytes 3080 | tf_op jit(solution)/shard_map/ppermute | solution.py:165
  45.6 0.0 collective-permute-done.9
  45.6 1.3 %collective-permute-start.10 = (f32[4,64]{1,0:T(4,128)S(1)}, f32[4,64]{1,0:T(4,128)S(1)}, u32[]{:S(2)}, u32[]{:S(2)}) collective-permute-start(f32[4,64]{1,0:T(4,128)S(1)} %add.30), channel_id=1, source_target_pairs={{4,0},{8,12},{5,1},{9,13},{6,2},{10,14},{7,3},{11,15},{20,16},{24,... | collective-permute-start | bytes 3080 | tf_op jit(solution)/shard_map/ppermute | solution.py:410
  46.9 16.4 %collective-permute-done.10 = f32[4,64]{1,0:T(4,128)S(1)} collective-permute-done((f32[4,64]{1,0:T(4,128)S(1)}, f32[4,64]{1,0:T(4,128)S(1)}, u32[]{:S(2)}, u32[]{:S(2)}) %collective-permute-start.10) | collective-permute-done | bytes 1056 | tf_op jit(solution)/shard_map/ppermute | solution.py:410
  63.3 0.6 broadcast_select_fusion
  (7 shorter events, 0.1 us)
Async XLA Ops:
  0.0 9.2 %copy-start = (bf16[2,64,7168]{2,1,0:T(8,128)(2,1)S(1)}, bf16[2,64,7168]{2,1,0:T(8,128)(2,1)}, u32[]{:S(2)}) copy-start(bf16[2,64,7168]{2,1,0:T(8,128)(2,1)} %proj_ref.3) | copy-start | bytes 5505028
  4.2 23.5 %collective-permute-start = (f32[2,64,1024]{2,1,0:T(8,128)S(1)}, f32[2,64,1024]{2,1,0:T(8,128)S(1)}, u32[]{:S(2)}, u32[]{:S(2)}) collective-permute-start(f32[2,64,1024]{2,1,0:T(8,128)S(1)} %project_in.1.after.x_ref), channel_id=1, source_target_pairs={{0,4},{12,8},{1,5},{13,9},{2,6},{14,10},{3,7},{15,11},{16,20},{28,... | collective-permute-start | bytes 1572872 | tf_op jit(solution)/shard_map/ppermute | solution.py:161
  17.1 10.6 %collective-permute-start.1 = (f32[2,64,512]{2,1,0:T(8,128)S(1)}, f32[2,64,512]{2,1,0:T(8,128)S(1)}, u32[]{:S(2)}, u32[]{:S(2)}) collective-permute-start(f32[2,64,512]{2,1,0:T(8,128)S(1)} %project_out.2.after.g_ref), channel_id=1, source_target_pairs={{0,4},{12,8},{1,5},{13,9},{2,6},{14,10},{3,7},{15,11},{16,20},{28,... | collective-permute-start | bytes 786440 | tf_op jit(solution)/shard_map/ppermute | solution.py:161
  26.4 6.8 %collective-permute-start.3 = (f32[2,64,512]{2,1,0:T(8,128)S(1)}, f32[2,64,512]{2,1,0:T(8,128)S(1)}, u32[]{:S(2)}, u32[]{:S(2)}) collective-permute-start(f32[2,64,512]{2,1,0:T(8,128)S(1)} %get-tuple-element.16.h_ref), channel_id=1, source_target_pairs={{0,4},{12,8},{1,5},{13,9},{2,6},{14,10},{3,7},{15,11},{16,20},{28,... | collective-permute-start | bytes 786440 | tf_op jit(solution)/shard_map/ppermute | solution.py:161
  27.8 1.4 %collective-permute-start.4 = (bf16[1,8,64,128]{3,2,1,0:T(8,128)(2,1)S(1)}, bf16[1,8,64,128]{3,2,1,0:T(8,128)(2,1)S(1)}, u32[]{:S(2)}, u32[]{:S(2)}) collective-permute-start(bf16[1,8,64,128]{3,2,1,0:T(8,128)(2,1)S(1)} %bitcast.9), channel_id=1, source_target_pairs={{0,1},{1,0},{2,3},{3,2},{4,5},{5,4},{6,7},{7,6},{8,9},{9,8},{10,11... | collective-permute-start | bytes 393224 | tf_op jit(solution)/shard_map/ppermute | solution.py:369
  27.9 6.0 %collective-permute-start.2 = (f32[64,1536]{1,0:T(8,128)S(1)}, f32[64,1536]{1,0:T(8,128)S(1)}, u32[]{:S(2)}, u32[]{:S(2)}) collective-permute-start(f32[64,1536]{1,0:T(8,128)S(1)} %pad_maximum_fusion), channel_id=1, source_target_pairs={{4,8},{8,4},{5,9},{9,5},{6,10},{10,6},{7,11},{11,7},{20,24},{24,20... | collective-permute-start | bytes 1179656 | tf_op jit(solution)/shard_map/ppermute | solution.py:165
  29.3 8.8 %collective-permute-start.8 = (bf16[2,8,64,128]{3,2,1,0:T(8,128)(2,1)S(1)}, bf16[2,8,64,128]{3,2,1,0:T(8,128)(2,1)S(1)}, u32[]{:S(2)}, u32[]{:S(2)}) collective-permute-start(bf16[2,8,64,128]{3,2,1,0:T(8,128)(2,1)S(1)} %pad_maximum_fusion.1.refs_0_), channel_id=1, source_target_pairs={{0,2},{1,3},{2,0},{3,1},{4,6},{5,7},{6,4},{7,5},{8,10},{9,11},{10,... | collective-permute-start | bytes 786440 | tf_op jit(solution)/shard_map/ppermute | solution.py:369
  33.2 1.5 %collective-permute-start.5 = (f32[64,512]{1,0:T(8,128)S(1)}, f32[64,512]{1,0:T(8,128)S(1)}, u32[]{:S(2)}, u32[]{:S(2)}) collective-permute-start(f32[64,512]{1,0:T(8,128)S(1)} %add_bitcast_fusion.after), channel_id=1, source_target_pairs={{4,8},{8,4},{5,9},{9,5},{6,10},{10,6},{7,11},{11,7},{20,24},{24,20... | collective-permute-start | bytes 393224 | tf_op jit(solution)/shard_map/ppermute | solution.py:165
  35.3 1.3 %collective-permute-start.6 = (f32[64,128]{1,0:T(8,128)S(1)}, f32[64,128]{1,0:T(8,128)S(1)}, u32[]{:S(2)}, u32[]{:S(2)}) collective-permute-start(f32[64,128]{1,0:T(8,128)S(1)} %get-tuple-element.24), channel_id=1, source_target_pairs={{0,1},{1,0},{2,3},{3,2},{4,5},{5,4},{6,7},{7,6},{8,9},{9,8},{10,11... | collective-permute-start | bytes 98312 | tf_op jit(solution)/shard_map/ppermute | solution.py:369
  36.6 3.9 %collective-permute-start.7 = (f32[64,128]{1,0:T(8,128)S(1)}, f32[64,128]{1,0:T(8,128)S(1)}, u32[]{:S(2)}, u32[]{:S(2)}) collective-permute-start(f32[64,128]{1,0:T(8,128)S(1)} %add.29.own_ref), channel_id=1, source_target_pairs={{0,2},{1,3},{2,0},{3,1},{4,6},{5,7},{6,4},{7,5},{8,10},{9,11},{10,... | collective-permute-start | bytes 98312 | tf_op jit(solution)/shard_map/ppermute | solution.py:369
  44.9 0.7 %collective-permute-start.9 = (f32[4,64]{1,0:T(4,128)S(1)}, f32[4,64]{1,0:T(4,128)S(1)}, u32[]{:S(2)}, u32[]{:S(2)}) collective-permute-start(f32[4,64]{1,0:T(4,128)S(1)} %score.1), channel_id=1, source_target_pairs={{4,8},{8,4},{5,9},{9,5},{6,10},{10,6},{7,11},{11,7},{20,24},{24,20... | collective-permute-start | bytes 3080 | tf_op jit(solution)/shard_map/ppermute | solution.py:165
  45.6 17.7 %collective-permute-start.10 = (f32[4,64]{1,0:T(4,128)S(1)}, f32[4,64]{1,0:T(4,128)S(1)}, u32[]{:S(2)}, u32[]{:S(2)}) collective-permute-start(f32[4,64]{1,0:T(4,128)S(1)} %add.30), channel_id=1, source_target_pairs={{4,0},{8,12},{5,1},{9,13},{6,2},{10,14},{7,3},{11,15},{20,16},{24,... | collective-permute-start | bytes 3080 | tf_op jit(solution)/shard_map/ppermute | solution.py:410

commit v8 on v7

--- a/solution.py
+++ b/solution.py
@@ -60,13 +60,18 @@
         copy(s).start()
     proj_copy.wait()
 
-    @pl.loop(0, seqs)
-    def _(s):
-        copy(s).wait()
-        part = nt(rows[s], proj[...].reshape(2 * rank, width)).T
-        tokens = pl.ds(pl.multiple_of(s * length, length), length)
-        out[side_ref[0], :, tokens] = part[:rank]
-        out[1 - side_ref[0], :, tokens] = part[rank:]
+    group = 2 - seqs % 2
+
+    @pl.loop(0, seqs // group)
+    def _(step):
+        for k in range(group):
+            copy(step * group + k).wait()
+        for k in range(group):
+            s = step * group + k
+            part = nt(proj[...].reshape(2 * rank, width), rows[s])
+            tokens = pl.ds(pl.multiple_of(s * length, length), length)
+            out[side_ref[0], :, tokens] = part[:rank]
+            out[1 - side_ref[0], :, tokens] = part[rank:]
 
 
 def project_in(side, rows, proj):
@@ -88,71 +93,67 @@
     )(side, in_hbm(rows), in_hbm(proj))
 
 
-def project_out_kernel(first, side_ref, rows_hbm, proj_ref, queries_hbm, after, out, *refs):
+def project_out_kernel(side_ref, rows_hbm, proj_ref, queries_hbm, after, *refs):
     del after
-    packed, (rows, held, sems, sem) = refs[:-4], refs[-4:]
+    (near, far, packed), (rows, held, acc, sems, sem) = refs[:3], refs[3:]
     _, seqs, length, width = rows.shape
-    half = width // 2
-
-    def chunk(layer, s, part):
-        lanes = pl.ds(part * half, half)
-        return pltpu.make_async_copy(
-            rows_hbm.at[layer, first + s, :, lanes],
-            rows.at[layer, s, :, lanes],
-            sems.at[layer, s, part],
-        )
-
+    parts = sems.shape[2]
+    piece = width // parts
+    copies = {}
     for s in range(seqs):
-        for part in range(2):
+        for part in range(parts):
+            lanes = pl.ds(part * piece, piece)
             for layer in range(2):
-                chunk(layer, s, part).start()
-    if packed:
-        copy = pltpu.make_async_copy(queries_hbm.at[:, side_ref[0]], held, sem)
-        copy.start()
-
-    @pl.loop(0, seqs)
-    def _(s):
-        values = [None, None]
-        for part in range(2):
-            lanes = slice(part * half, (part + 1) * half)
+                copies[s, part, layer] = pltpu.make_async_copy(
+                    rows_hbm.at[layer, s, :, lanes],
+                    rows.at[layer, s, :, lanes],
+                    sems.at[layer, s, part],
+                )
+                copies[s, part, layer].start()
+    copy = pltpu.make_async_copy(queries_hbm.at[:, side_ref[0]], held, sem)
+    copy.start()
+    for s in range(seqs):
+        tokens = slice(s * length, (s + 1) * length)
+        for part in range(parts):
+            lanes = slice(part * piece, (part + 1) * piece)
             for layer in range(2):
-                chunk(layer, s, part).wait()
+                copies[s, part, layer].wait()
             for layer in range(2):
-                value = nt(rows[layer, s, :, lanes], proj_ref[layer, :, lanes])
-                values[layer] = value if part == 0 else values[layer] + value
-        tokens = pl.ds(pl.multiple_of(s * length, length), length)
-        turned = jnp.concatenate(values, axis=1).T
-        rank = turned.shape[0] // 2
-        out[side_ref[0], :, tokens] = turned[:rank]
-        out[1 - side_ref[0], :, tokens] = turned[rank:]
-
-    if packed:
-        copy.wait()
-        blocks = held.shape[0] // 2
-        for k in range(blocks):
-            pair = [held[k].astype(jnp.float32), held[k + blocks].astype(jnp.float32)]
-            packed[0][k] = jnp.concatenate(pair, axis=1).astype(held.dtype)
-
-
-def project_out(side, rows, proj, queries, first, seqs, after, packs):
-    _, _, length, width = rows.shape
+                value = nt(proj_ref[layer, :, lanes], rows[layer, s, :, lanes])
+                if part > 0:
+                    value = value + acc[layer, :, tokens]
+                acc[layer, :, tokens] = value
+    far[...] = acc[1 - side_ref[0]]
+    near[...] = acc[side_ref[0]]
+    copy.wait()
+    blocks = held.shape[0] // 2
+    for k in range(blocks):
+        pair = [held[k].astype(jnp.float32), held[k + blocks].astype(jnp.float32)]
+        packed[k] = jnp.concatenate(pair, axis=1).astype(held.dtype)
+
+
+def project_out(side, rows, proj, queries, after):
+    _, seqs, length, width = rows.shape
     rank = proj.shape[1]
     count = queries.shape[0]
-    out_shape = [jax.ShapeDtypeStruct((2, rank, seqs * length), jnp.float32)]
-    if packs:
-        out_shape.append(jax.ShapeDtypeStruct((count // 2, rank, 2 * rank), queries.dtype))
+    parts = 4 if width % 512 == 0 else 1
     return pl.pallas_call(
-        functools.partial(project_out_kernel, first),
+        project_out_kernel,
         in_specs=[smem(), hbm(), vmem(), hbm(), hbm()],
-        out_specs=[vmem()] * len(out_shape),
-        out_shape=out_shape,
+        out_specs=[vmem()] * 3,
+        out_shape=[
+            jax.ShapeDtypeStruct((rank, seqs * length), jnp.float32),
+            jax.ShapeDtypeStruct((rank, seqs * length), jnp.float32),
+            jax.ShapeDtypeStruct((count // 2, rank, 2 * rank), queries.dtype),
+        ],
         scratch_shapes=[
-            pltpu.VMEM((2, seqs, length, width), rows.dtype),
+            pltpu.VMEM(rows.shape, rows.dtype),
             pltpu.VMEM((count, rank, rank), queries.dtype),
-            pltpu.SemaphoreType.DMA((2, seqs, 2)),
+            pltpu.VMEM((2, rank, seqs * length), jnp.float32),
+            pltpu.SemaphoreType.DMA((2, seqs, parts)),
             pltpu.SemaphoreType.DMA,
         ],
-        compiler_params=params(24),
+        compiler_params=params(40),
         name="project_out",
     )(side, in_hbm(rows), proj, in_hbm(queries), after)
 
@@ -181,53 +182,27 @@
         sample_out[s] = jnp.concatenate([sample, sample], axis=1)
 
 
-def first_kernel(x_ref, x_outer, g_ref, g_outer, other, after, x_out, cov_out, sample_out):
-    del after
-    tokens = x_ref.shape[2]
-    here = g_ref.shape[2]
+def covariances_kernel(x_ref, x_outer, near, near_outer, far_outer, other, cov_out, sample_out):
+    tokens = near.shape[1]
     x = x_ref[0] + x_outer[0] + other[:, :tokens]
-    x_out[...] = x[:, here:]
-    g = g_ref[0] + g_outer[0] + other[:, tokens:]
+    g = (near[...] + near_outer[...]) + (far_outer[...] + other[:, tokens:])
     cov_out[...] = covariance(x, False) + covariance(g, True)
-    samples_of(x[:, :here], g, sample_out)
-
-
-def second_kernel(x_ref, cov_ref, h_ref, h_outer, other, cov_out, sample_out):
-    h = h_ref[0] + h_outer[0] + other[...]
-    cov_out[...] = cov_ref[...] + covariance(h, True)
-    samples_of(x_ref[...], h, sample_out)
-
-
-def first_half(x, x_outer, g, g_outer, other, after, seqs):
-    _, rank, tokens = x.shape
-    here = g.shape[2]
+    samples_of(x, g, sample_out)
+
+
+def covariances(x, x_outer, near, near_outer, far_outer, other, seqs):
+    rank = near.shape[0]
     return pl.pallas_call(
-        first_kernel,
-        in_specs=[vmem()] * 5 + [hbm()],
-        out_specs=[vmem()] * 3,
-        out_shape=[
-            jax.ShapeDtypeStruct((rank, tokens - here), jnp.float32),
-            jax.ShapeDtypeStruct((rank, 2 * rank), jnp.float32),
-            jax.ShapeDtypeStruct((seqs, rank, 2 * rank), jnp.float32),
-        ],
-        compiler_params=params(16),
-        name="first_half",
-    )(x, x_outer, g, g_outer, other, after)
-
-
-def second_half(x, cov, h, h_outer, other, seqs):
-    rank = x.shape[0]
-    return pl.pallas_call(
-        second_kernel,
-        in_specs=[vmem()] * 5,
+        covariances_kernel,
+        in_specs=[vmem()] * 6,
         out_specs=[vmem()] * 2,
         out_shape=[
             jax.ShapeDtypeStruct((rank, 2 * rank), jnp.float32),
             jax.ShapeDtypeStruct((seqs, rank, 2 * rank), jnp.float32),
         ],
         compiler_params=params(16),
-        name="second_half",
-    )(x, cov, h, h_outer, other)
+        name="covariances",
+    )(x, x_outer, near, near_outer, far_outer, other)
 
 
 def scales(steps, spread):
@@ -276,7 +251,7 @@
     return high, middle, low
 
 
-def score_kernel(tokens, place_ref, own_ref, other_ref, first_ref, second_ref, *refs):
+def score_kernel(tokens, place_ref, own_ref, other_ref, sample_ref, *refs):
     pieces, (out, held, half) = refs[:-3], refs[-3:]
     parts = held.shape[0]
     k = 0
@@ -287,7 +262,7 @@
     inverses = damped_inverses((own_ref[...] + other_ref[...]) / tokens)
     both = inverses.shape[0]
     size = both // 2
-    samples = [ref[s] for ref in (first_ref, second_ref) for s in range(ref.shape[0])]
+    samples = [sample_ref[s] for s in range(sample_ref.shape[0])]
     seqs = len(samples)
     blocks = held.shape[1]
     pairs = parts * blocks
@@ -346,14 +321,14 @@
             ]
 
 
-def score(place, own, other, samples, pieces, tokens):
+def score(place, own, other, sample, pieces, tokens):
     _, blocks, rank, both = pieces[0].shape
     parts = sum(piece.shape[0] for piece in pieces)
     pairs = parts * blocks
-    seqs = sum(sample.shape[0] for sample in samples)
+    seqs = sample.shape[0]
     return pl.pallas_call(
         functools.partial(score_kernel, tokens),
-        in_specs=[smem()] + [vmem()] * (4 + len(pieces)),
+        in_specs=[smem()] + [vmem()] * (3 + len(pieces)),
         out_specs=vmem(),
         out_shape=jax.ShapeDtypeStruct((seqs, 2 * pairs), jnp.float32),
         scratch_shapes=[
@@ -362,7 +337,7 @@
         ],
         compiler_params=params(16),
         name="score",
-    )(place, own, other, *samples, *pieces)
+    )(place, own, other, sample, *pieces)
 
 
 def swap(value, axis, bit):
@@ -380,35 +355,34 @@
     column = lax.axis_index("tensor").astype(jnp.int32)
     side = (column >= 2).astype(jnp.int32).reshape(1)
     place = lax.axis_index("dp").astype(jnp.int32).reshape(1)
-    half = seqs // 2
     x = project_in(side, acts, proj_in)
     x_outer = inwards(x)
-    (g,) = project_out(side, grads, proj_out, queries, 0, half, x, False)
-    g_outer = inwards(g)
-    h, packed = project_out(side, grads, proj_out, queries, half, seqs - half, g, True)
-    h_outer = inwards(h)
-    far = jnp.concatenate([x[1] + after(x_outer, h)[1], g[1] + after(g_outer, h)[1]], axis=1)
-    other = across(far)
-    pieces = [after(packed, far)[None]]
+    near, far, packed = project_out(side, grads, proj_out, queries, x)
+    far_outer = lax.ppermute(far, "tensor", [(0, 2), (3, 1)])
+    crossing = jnp.concatenate([x[1] + after(x_outer, far)[1], far], axis=1)
+    other = across(crossing)
+    near_outer = inwards(near)
+    pieces = [after(packed, crossing)[None]]
     bit = 1
     while bit < parts:
         mine = pieces[0] if bit == 1 else jnp.concatenate(pieces, axis=0)
         pieces = [mine, swap(mine, "dp", bit)]
         bit *= 2
-    h_far = h[1] + after(h_outer, pieces[0])[1]
-    h_other = across(h_far)
-    x_rest, cov, sample = first_half(x, x_outer, g, g_outer, other, h_far, half)
-    cov, last = second_half(x_rest, cov, h, h_outer, h_other, seqs - half)
+    cov, sample = covariances(x, x_outer, near, near_outer, far_outer, other, seqs)
     other = jnp.zeros_like(cov)
     bit = 1
     while bit < parts:
         cov = cov if bit == 1 else cov + other
         other = swap(cov, "dp", bit)
         bit *= 2
-    scores = score(place, cov, other, [sample, last], pieces, tokens)
-    scores = scores + across(scores)
-    outer = lax.ppermute(scores, "tensor", [(1, 0), (2, 3)])
-    return jnp.where((column == 1) | (column == 2), scores, outer)
+    scores = score(place, cov, other, sample, pieces, tokens)
+    owner = (column == 1) | (column == 2)
+    return (
+        jnp.where(owner, scores, 0.0)
+        + lax.ppermute(scores, "tensor", [(1, 0), (2, 3)])
+        + lax.ppermute(scores, "tensor", [(2, 0), (1, 3)])
+        + across(scores)
+    )
 
 
 def damp(matrix):
@@ -478,7 +452,7 @@
 def local(acts, grads, proj_in, proj_out, queries):
     parts = lax.axis_size("dp")
     even = parts > 1 and parts & (parts - 1) == 0
-    if lax.axis_size("tensor") == 4 and even and acts.shape[0] > 1 and queries.shape[0] % 8 == 0:
+    if lax.axis_size("tensor") == 4 and even and queries.shape[0] % 4 == 0:
         return local_owned(acts, grads, proj_in, proj_out, queries)
     return local_general(acts, grads, proj_in, proj_out, queries)
 

time: 64.1 us -> 61.9 us (0.966)
  starting transfers between devices: 14.1 us -> 20.2 us
  Pallas kernels: 25.8 us -> 20.8 us
  waiting for transfers between devices: 23.1 us -> 19.8 us
    ppermute x1 -> x3, starting transfers between devices: 1.29 us -> 9.29 us  [the longest x1 6.71 us: local_owned(): far_outer = lax.ppermute(far, 'tensor', [(0, 2), (3, 1)])]
    ppermute x1 -> x3, waiting for transfers between devices: 16.4 us -> 10.9 us  [the longest x1 6.11 us: local_owned(): lax.ppermute(scores, 'tensor', [(1, 0), (2, 3)])]
    pallas_call x4 -> x2, Pallas kernels: 17.3 us -> 12.7 us  [the longest x1 11.5 us: project_out(): pl.pallas_call(project_out_kernel, in_specs=[smem(), hbm(), vmem(), hbm()...]
    ppermute x3 -> x2, waiting for transfers between devices: 2.42 us -> 5.21 us  [inwards(): return lax.ppermute(value, 'tensor', [(0, 1), (3, 2)])]
    ppermute x3 -> x2, starting transfers between devices: 7.57 us -> 6.36 us  [inwards(): return lax.ppermute(value, 'tensor', [(0, 1), (3, 2)])]
    ppermute x3 -> x2, starting transfers between devices: 2.04 us -> 1.38 us  [across(): return lax.ppermute(value, 'tensor', [(1, 2), (2, 1)])]
  transfers between devices with their start and end apart: 11 -> 11, of which waited for: 5 -> 6; matrix products, arithmetic and copies ran while one was open for 0% -> 0% of each run, Pallas kernels for 27% -> 21%
where the time goes in v8:
time: 61.9 us; the launch traced here: 61.6 us
  Pallas kernels  20.8 us (34%)
  starting transfers between devices  20.2 us (33%)
  waiting for transfers between devices  19.8 us (32%)
  other arithmetic  0.68 us (1%)
    pallas_call x1, Pallas kernels, project_out(): pl.pallas_call(project_out_kernel, in_specs=[smem(), hbm(), vmem(), hbm()...  11.5 us
    ppermute x1, starting transfers between devices, local_owned(): far_outer = lax.ppermute(far, 'tensor', [(0, 2), (3, 1)])  6.71 us
    ppermute x2, starting transfers between devices, inwards(): return lax.ppermute(value, 'tensor', [(0, 1), (3, 2)])  6.36 us
    ppermute x1, waiting for transfers between devices, local_owned(): lax.ppermute(scores, 'tensor', [(1, 0), (2, 3)])  6.11 us
    ppermute x2, waiting for transfers between devices, inwards(): return lax.ppermute(value, 'tensor', [(0, 1), (3, 2)])  5.21 us
    pallas_call x1, Pallas kernels, score(): pl.pallas_call(functools.partial(score_kernel, tokens), in_specs=[smem()]...  4.35 us
    pallas_call x1, Pallas kernels, project_in(): pl.pallas_call(project_in_kernel, in_specs=[smem(), hbm(), hbm()], out_sp...  3.85 us
    ppermute x4, waiting for transfers between devices, swap(): lax.ppermute(value, axis, [(i, i ^ bit) for i in range(lax.axis_size(axis...  3.62 us
  transfers between devices with their start and end apart: 11, of which 6 were waited for; matrix products, arithmetic and copies ran while one was open for 0% of the time, Pallas kernels for 21%

profile of v8, /device:TPU:0, one launch (start us, length us, event | category | flops | bytes accessed | tf_op | source)
XLA Modules:
  0.0 61.6 jit_solution(12920818940771950757)
XLA Ops:
  0.0 0.0 copy-start
  0.0 3.8 %project_in.1.after.x_ref = f32[2,64,1024]{2,1,0:T(8,128)S(1)} custom-call(s32[1]{0:T(128)} %bitcast.1.side_ref, bf16[4,256,2048]{2,1,0:T(8,128)(2,1)} %rows_hbm.2, bf16[2,64,2048]{2,1,0:T(8,128)(2,1)} %proj_hbm.1), custom_call_target="tpu_custom_call" | custom-call | tf_op jit(solution)/shard_map/project_in/pallas_call | solution.py:80
  3.9 5.0 %collective-permute-start = (f32[2,64,1024]{2,1,0:T(8,128)S(1)}, f32[2,64,1024]{2,1,0:T(8,128)S(1)}, u32[]{:S(2)}, u32[]{:S(2)}) collective-permute-start(f32[2,64,1024]{2,1,0:T(8,128)S(1)} %project_in.1.after.x_ref), channel_id=1, source_target_pairs={{0,4},{12,8},{1,5},{13,9},{2,6},{14,10},{3,7},{15,11},{16,20},{28,... | collective-permute-start | bytes 1572872 | tf_op jit(solution)/shard_map/ppermute | solution.py:162
  8.8 0.0 copy-done
  8.8 11.5 %project_out.1 = (f32[64,1024]{1,0:T(8,128)S(1)}, f32[64,1024]{1,0:T(8,128)S(1)}, bf16[8,64,128]{2,1,0:T(8,128)(2,1)S(1)}) custom-call(s32[1]{0:T(128)} %bitcast.1.side_ref, bf16[2,4,256,7168]{3,2,1,0:T(8,128)(2,1)} %rows_hbm.3, bf16[2,64,7168]{2,1,0:T(8,128)(2,1)S(1)} %copy-done, bf16[16,2,64,64]{3,2,1,0:T(8,128)(2,1)} %queries_hbm.1, ...), custom_call_target="tpu_custom_call" | custom-call | tf_op jit(solution)/shard_map/project_out/pallas_call | solution.py:140
  20.3 0.0 collective-permute-done.x_outer
  20.4 0.7 %collective-permute-start.3 = (f32[64,2048]{1,0:T(8,128)S(1)}, f32[64,2048]{1,0:T(8,128)S(1)}, u32[]{:S(2)}, u32[]{:S(2)}) collective-permute-start(f32[64,2048]{1,0:T(8,128)S(1)} %pad_maximum_fusion), channel_id=1, source_target_pairs={{4,8},{8,4},{5,9},{9,5},{6,10},{10,6},{7,11},{11,7},{20,24},{24,20... | collective-permute-start | bytes 1572872 | tf_op jit(solution)/shard_map/ppermute | solution.py:166
  21.1 0.1 collective-permute-start.6
  21.2 6.7 %collective-permute-start.2 = (f32[64,1024]{1,0:T(8,128)S(1)}, f32[64,1024]{1,0:T(8,128)S(1)}, u32[]{:S(2)}, u32[]{:S(2)}) collective-permute-start(f32[64,1024]{1,0:T(8,128)S(1)} %get-tuple-element.13), channel_id=1, source_target_pairs={{0,8},{12,4},{1,9},{13,5},{2,10},{14,6},{3,11},{15,7},{16,24},{28,... | collective-permute-start | bytes 786440 | tf_op jit(solution)/shard_map/ppermute | solution.py:361
  27.9 1.4 %collective-permute-start.1 = (f32[64,1024]{1,0:T(8,128)S(1)}, f32[64,1024]{1,0:T(8,128)S(1)}, u32[]{:S(2)}, u32[]{:S(2)}) collective-permute-start(f32[64,1024]{1,0:T(8,128)S(1)} %get-tuple-element.12.near), channel_id=1, source_target_pairs={{0,4},{12,8},{1,5},{13,9},{2,6},{14,10},{3,7},{15,11},{16,20},{28,... | collective-permute-start | bytes 786440 | tf_op jit(solution)/shard_map/ppermute | solution.py:162
  29.3 0.0 collective-permute-done.6
  29.4 1.6 %collective-permute-start.7 = (bf16[2,8,64,128]{3,2,1,0:T(8,128)(2,1)S(1)}, bf16[2,8,64,128]{3,2,1,0:T(8,128)(2,1)S(1)}, u32[]{:S(2)}, u32[]{:S(2)}) collective-permute-start(bf16[2,8,64,128]{3,2,1,0:T(8,128)(2,1)S(1)} %pad_maximum_fusion.1.refs_0_), channel_id=1, source_target_pairs={{0,2},{1,3},{2,0},{3,1},{4,6},{5,7},{6,4},{7,5},{8,10},{9,11},{10,... | collective-permute-start | bytes 786440 | tf_op jit(solution)/shard_map/ppermute | solution.py:344
  30.9 3.6 %collective-permute-done.2.far_outer = f32[64,1024]{1,0:T(8,128)S(1)} collective-permute-done((f32[64,1024]{1,0:T(8,128)S(1)}, f32[64,1024]{1,0:T(8,128)S(1)}, u32[]{:S(2)}, u32[]{:S(2)}) %collective-permute-start.2) | collective-permute-done | bytes 262176 | tf_op jit(solution)/shard_map/ppermute | solution.py:361
  34.5 5.2 %collective-permute-done.1.near_outer = f32[64,1024]{1,0:T(8,128)S(1)} collective-permute-done((f32[64,1024]{1,0:T(8,128)S(1)}, f32[64,1024]{1,0:T(8,128)S(1)}, u32[]{:S(2)}, u32[]{:S(2)}) %collective-permute-start.1) | collective-permute-done | bytes 262176 | tf_op jit(solution)/shard_map/ppermute | solution.py:162
  39.7 0.0 collective-permute-done.3.other
  39.7 1.2 %covariances.1 = (f32[64,128]{1,0:T(8,128)S(1)}, f32[4,64,128]{2,1,0:T(8,128)S(1)}) custom-call(f32[2,64,1024]{2,1,0:T(8,128)S(1)} %project_in.1.after.x_ref, f32[2,64,1024]{2,1,0:T(8,128)S(1)} %collective-permute-done.x_outer, f32[64,1024]{1,0:T(8,128)S(1)} %get-tuple-element.12.near, f32[64,1024]{1,0:T(8,128)S(1)} %collective-permute-done.1.near_outer, ...), custom_call_target="tpu_custom_call" | custom-call | tf_op jit(solution)/shard_map/covariances/pallas_call | solution.py:195
  40.9 0.0 collective-permute-start.4
  41.0 1.2 %collective-permute-done.4 = f32[64,128]{1,0:T(8,128)S(1)} collective-permute-done((f32[64,128]{1,0:T(8,128)S(1)}, f32[64,128]{1,0:T(8,128)S(1)}, u32[]{:S(2)}, u32[]{:S(2)}) %collective-permute-start.4) | collective-permute-done | bytes 32800 | tf_op jit(solution)/shard_map/ppermute | solution.py:344
  42.2 1.5 %collective-permute-start.5 = (f32[64,128]{1,0:T(8,128)S(1)}, f32[64,128]{1,0:T(8,128)S(1)}, u32[]{:S(2)}, u32[]{:S(2)}) collective-permute-start(f32[64,128]{1,0:T(8,128)S(1)} %add.20.own_ref), channel_id=1, source_target_pairs={{0,2},{1,3},{2,0},{3,1},{4,6},{5,7},{6,4},{7,5},{8,10},{9,11},{10,... | collective-permute-start | bytes 98312 | tf_op jit(solution)/shard_map/ppermute | solution.py:344
  43.7 0.0 collective-permute-done.7.refs_1_
  43.7 2.4 %collective-permute-done.5.other_ref = f32[64,128]{1,0:T(8,128)S(1)} collective-permute-done((f32[64,128]{1,0:T(8,128)S(1)}, f32[64,128]{1,0:T(8,128)S(1)}, u32[]{:S(2)}, u32[]{:S(2)}) %collective-permute-start.5) | collective-permute-done | bytes 32800 | tf_op jit(solution)/shard_map/ppermute | solution.py:344
  46.1 4.3 %score.1 = f32[4,64]{1,0:T(4,128)S(1)} custom-call(s32[1]{0:T(128)} %bitcast.place_ref, f32[64,128]{1,0:T(8,128)S(1)} %add.20.own_ref, f32[64,128]{1,0:T(8,128)S(1)} %collective-permute-done.5.other_ref, f32[4,64,128]{2,1,0:T(8,128)S(1)} %get-tuple-element.16.sample_ref, bf16[2,8,64,128]{3,2,1,0:T(8,128)(2,1)S(1)} %pad_maximum_fusion.1.refs_0_, ...), custom_call_target="tpu_custom_call" | custom-call | tf_op jit(solution)/shard_map/score/pallas_call | solution.py:329
  50.4 0.7 %collective-permute-start.10 = (f32[4,64]{1,0:T(4,128)S(1)}, f32[4,64]{1,0:T(4,128)S(1)}, u32[]{:S(2)}, u32[]{:S(2)}) collective-permute-start(f32[4,64]{1,0:T(4,128)S(1)} %score.1), channel_id=1, source_target_pairs={{4,8},{8,4},{5,9},{9,5},{6,10},{10,6},{7,11},{11,7},{20,24},{24,20... | collective-permute-start | bytes 3080 | tf_op jit(solution)/shard_map/ppermute | solution.py:166
  51.1 1.3 %collective-permute-start.8 = (f32[4,64]{1,0:T(4,128)S(1)}, f32[4,64]{1,0:T(4,128)S(1)}, u32[]{:S(2)}, u32[]{:S(2)}) collective-permute-start(f32[4,64]{1,0:T(4,128)S(1)} %score.1), channel_id=1, source_target_pairs={{4,0},{8,12},{5,1},{9,13},{6,2},{10,14},{7,3},{11,15},{20,16},{24,... | collective-permute-start | bytes 3080 | tf_op jit(solution)/shard_map/ppermute | solution.py:382
  52.4 1.3 %collective-permute-start.9 = (f32[4,64]{1,0:T(4,128)S(1)}, f32[4,64]{1,0:T(4,128)S(1)}, u32[]{:S(2)}, u32[]{:S(2)}) collective-permute-start(f32[4,64]{1,0:T(4,128)S(1)} %score.1), channel_id=1, source_target_pairs={{8,0},{4,12},{9,1},{5,13},{10,2},{6,14},{11,3},{7,15},{24,16},{20,... | collective-permute-start | bytes 3080 | tf_op jit(solution)/shard_map/ppermute | solution.py:383
  53.7 0.0 collective-permute-done.10
  53.8 6.1 %collective-permute-done.8 = f32[4,64]{1,0:T(4,128)S(1)} collective-permute-done((f32[4,64]{1,0:T(4,128)S(1)}, f32[4,64]{1,0:T(4,128)S(1)}, u32[]{:S(2)}, u32[]{:S(2)}) %collective-permute-start.8) | collective-permute-done | bytes 1056 | tf_op jit(solution)/shard_map/ppermute | solution.py:382
  59.9 1.2 %collective-permute-done.9 = f32[4,64]{1,0:T(4,128)S(1)} collective-permute-done((f32[4,64]{1,0:T(4,128)S(1)}, f32[4,64]{1,0:T(4,128)S(1)}, u32[]{:S(2)}, u32[]{:S(2)}) %collective-permute-start.9) | collective-permute-done | bytes 1056 | tf_op jit(solution)/shard_map/ppermute | solution.py:383
  61.1 0.6 add_add_fusion
  (4 shorter events, 0.1 us)
Async XLA Ops:
  0.0 8.8 %copy-start = (bf16[2,64,7168]{2,1,0:T(8,128)(2,1)S(1)}, bf16[2,64,7168]{2,1,0:T(8,128)(2,1)}, u32[]{:S(2)}) copy-start(bf16[2,64,7168]{2,1,0:T(8,128)(2,1)} %proj_ref.1) | copy-start | bytes 5505028
  3.9 16.5 %collective-permute-start = (f32[2,64,1024]{2,1,0:T(8,128)S(1)}, f32[2,64,1024]{2,1,0:T(8,128)S(1)}, u32[]{:S(2)}, u32[]{:S(2)}) collective-permute-start(f32[2,64,1024]{2,1,0:T(8,128)S(1)} %project_in.1.after.x_ref), channel_id=1, source_target_pairs={{0,4},{12,8},{1,5},{13,9},{2,6},{14,10},{3,7},{15,11},{16,20},{28,... | collective-permute-start | bytes 1572872 | tf_op jit(solution)/shard_map/ppermute | solution.py:162
  20.4 19.3 %collective-permute-start.3 = (f32[64,2048]{1,0:T(8,128)S(1)}, f32[64,2048]{1,0:T(8,128)S(1)}, u32[]{:S(2)}, u32[]{:S(2)}) collective-permute-start(f32[64,2048]{1,0:T(8,128)S(1)} %pad_maximum_fusion), channel_id=1, source_target_pairs={{4,8},{8,4},{5,9},{9,5},{6,10},{10,6},{7,11},{11,7},{20,24},{24,20... | collective-permute-start | bytes 1572872 | tf_op jit(solution)/shard_map/ppermute | solution.py:166
  21.1 8.2 %collective-permute-start.6 = (bf16[1,8,64,128]{3,2,1,0:T(8,128)(2,1)S(1)}, bf16[1,8,64,128]{3,2,1,0:T(8,128)(2,1)S(1)}, u32[]{:S(2)}, u32[]{:S(2)}) collective-permute-start(bf16[1,8,64,128]{3,2,1,0:T(8,128)(2,1)S(1)} %bitcast.5), channel_id=1, source_target_pairs={{0,1},{1,0},{2,3},{3,2},{4,5},{5,4},{6,7},{7,6},{8,9},{9,8},{10,11... | collective-permute-start | bytes 393224 | tf_op jit(solution)/shard_map/ppermute | solution.py:344
  21.2 13.3 %collective-permute-start.2 = (f32[64,1024]{1,0:T(8,128)S(1)}, f32[64,1024]{1,0:T(8,128)S(1)}, u32[]{:S(2)}, u32[]{:S(2)}) collective-permute-start(f32[64,1024]{1,0:T(8,128)S(1)} %get-tuple-element.13), channel_id=1, source_target_pairs={{0,8},{12,4},{1,9},{13,5},{2,10},{14,6},{3,11},{15,7},{16,24},{28,... | collective-permute-start | bytes 786440 | tf_op jit(solution)/shard_map/ppermute | solution.py:361
  27.9 11.8 %collective-permute-start.1 = (f32[64,1024]{1,0:T(8,128)S(1)}, f32[64,1024]{1,0:T(8,128)S(1)}, u32[]{:S(2)}, u32[]{:S(2)}) collective-permute-start(f32[64,1024]{1,0:T(8,128)S(1)} %get-tuple-element.12.near), channel_id=1, source_target_pairs={{0,4},{12,8},{1,5},{13,9},{2,6},{14,10},{3,7},{15,11},{16,20},{28,... | collective-permute-start | bytes 786440 | tf_op jit(solution)/shard_map/ppermute | solution.py:162
  29.4 14.3 %collective-permute-start.7 = (bf16[2,8,64,128]{3,2,1,0:T(8,128)(2,1)S(1)}, bf16[2,8,64,128]{3,2,1,0:T(8,128)(2,1)S(1)}, u32[]{:S(2)}, u32[]{:S(2)}) collective-permute-start(bf16[2,8,64,128]{3,2,1,0:T(8,128)(2,1)S(1)} %pad_maximum_fusion.1.refs_0_), channel_id=1, source_target_pairs={{0,2},{1,3},{2,0},{3,1},{4,6},{5,7},{6,4},{7,5},{8,10},{9,11},{10,... | collective-permute-start | bytes 786440 | tf_op jit(solution)/shard_map/ppermute | solution.py:344
  40.9 1.2 %collective-permute-start.4 = (f32[64,128]{1,0:T(8,128)S(1)}, f32[64,128]{1,0:T(8,128)S(1)}, u32[]{:S(2)}, u32[]{:S(2)}) collective-permute-start(f32[64,128]{1,0:T(8,128)S(1)} %get-tuple-element.15), channel_id=1, source_target_pairs={{0,1},{1,0},{2,3},{3,2},{4,5},{5,4},{6,7},{7,6},{8,9},{9,8},{10,11... | collective-permute-start | bytes 98312 | tf_op jit(solution)/shard_map/ppermute | solution.py:344
  42.2 3.9 %collective-permute-start.5 = (f32[64,128]{1,0:T(8,128)S(1)}, f32[64,128]{1,0:T(8,128)S(1)}, u32[]{:S(2)}, u32[]{:S(2)}) collective-permute-start(f32[64,128]{1,0:T(8,128)S(1)} %add.20.own_ref), channel_id=1, source_target_pairs={{0,2},{1,3},{2,0},{3,1},{4,6},{5,7},{6,4},{7,5},{8,10},{9,11},{10,... | collective-permute-start | bytes 98312 | tf_op jit(solution)/shard_map/ppermute | solution.py:344
  50.4 3.3 %collective-permute-start.10 = (f32[4,64]{1,0:T(4,128)S(1)}, f32[4,64]{1,0:T(4,128)S(1)}, u32[]{:S(2)}, u32[]{:S(2)}) collective-permute-start(f32[4,64]{1,0:T(4,128)S(1)} %score.1), channel_id=1, source_target_pairs={{4,8},{8,4},{5,9},{9,5},{6,10},{10,6},{7,11},{11,7},{20,24},{24,20... | collective-permute-start | bytes 3080 | tf_op jit(solution)/shard_map/ppermute | solution.py:166
  51.1 8.7 %collective-permute-start.8 = (f32[4,64]{1,0:T(4,128)S(1)}, f32[4,64]{1,0:T(4,128)S(1)}, u32[]{:S(2)}, u32[]{:S(2)}) collective-permute-start(f32[4,64]{1,0:T(4,128)S(1)} %score.1), channel_id=1, source_target_pairs={{4,0},{8,12},{5,1},{9,13},{6,2},{10,14},{7,3},{11,15},{20,16},{24,... | collective-permute-start | bytes 3080 | tf_op jit(solution)/shard_map/ppermute | solution.py:382
  52.4 8.6 %collective-permute-start.9 = (f32[4,64]{1,0:T(4,128)S(1)}, f32[4,64]{1,0:T(4,128)S(1)}, u32[]{:S(2)}, u32[]{:S(2)}) collective-permute-start(f32[4,64]{1,0:T(4,128)S(1)} %score.1), channel_id=1, source_target_pairs={{8,0},{4,12},{9,1},{5,13},{10,2},{6,14},{11,3},{7,15},{24,16},{20,... | collective-permute-start | bytes 3080 | tf_op jit(solution)/shard_map/ppermute | solution.py:383

commit v9 on v8

--- a/solution.py
+++ b/solution.py
@@ -47,7 +47,7 @@
     return pltpu.CompilerParams(vmem_limit_bytes=mib * MIB)
 
 
-def project_in_kernel(side_ref, rows_hbm, proj_hbm, out, rows, proj, sems, proj_sem):
+def project_in_kernel(side_ref, rows_hbm, proj_hbm, near, far, rows, proj, acc, sems, proj_sem):
     seqs, length, width = rows.shape
     rank = proj.shape[1]
     proj_copy = pltpu.make_async_copy(proj_hbm, proj, proj_sem)
@@ -70,8 +70,11 @@
             s = step * group + k
             part = nt(proj[...].reshape(2 * rank, width), rows[s])
             tokens = pl.ds(pl.multiple_of(s * length, length), length)
-            out[side_ref[0], :, tokens] = part[:rank]
-            out[1 - side_ref[0], :, tokens] = part[rank:]
+            acc[0, :, tokens] = part[:rank]
+            acc[1, :, tokens] = part[rank:]
+
+    far[...] = acc[1 - side_ref[0]]
+    near[...] = acc[side_ref[0]]
 
 
 def project_in(side, rows, proj):
@@ -80,11 +83,12 @@
     return pl.pallas_call(
         project_in_kernel,
         in_specs=[smem(), hbm(), hbm()],
-        out_specs=vmem(),
-        out_shape=jax.ShapeDtypeStruct((2, rank, seqs * length), jnp.float32),
+        out_specs=[vmem()] * 2,
+        out_shape=[jax.ShapeDtypeStruct((rank, seqs * length), jnp.float32)] * 2,
         scratch_shapes=[
             pltpu.VMEM(rows.shape, rows.dtype),
             pltpu.VMEM(proj.shape, proj.dtype),
+            pltpu.VMEM((2, rank, seqs * length), jnp.float32),
             pltpu.SemaphoreType.DMA((seqs,)),
             pltpu.SemaphoreType.DMA,
         ],
@@ -158,12 +162,24 @@
     )(side, in_hbm(rows), proj, in_hbm(queries), after)
 
 
-def inwards(value):
-    return lax.ppermute(value, "tensor", [(0, 1), (3, 2)])
-
-
 def across(value):
-    return lax.ppermute(value, "tensor", [(1, 2), (2, 1)])
+    return lax.ppermute(value, "tensor", [(1, 2), (2, 1), (0, 0), (3, 3)])
+
+
+def to_owner(near, far):
+    return [
+        near,
+        lax.ppermute(far, "tensor", [(0, 2), (3, 1)]),
+        across(far),
+        lax.ppermute(near, "tensor", [(0, 1), (3, 2)]),
+    ]
+
+
+def total(pieces):
+    value = pieces[0][...]
+    for piece in pieces[1:]:
+        value = value + piece[...]
+    return value
 
 
 def covariance(value, right):
@@ -182,27 +198,48 @@
         sample_out[s] = jnp.concatenate([sample, sample], axis=1)
 
 
-def covariances_kernel(x_ref, x_outer, near, near_outer, far_outer, other, cov_out, sample_out):
-    tokens = near.shape[1]
-    x = x_ref[0] + x_outer[0] + other[:, :tokens]
-    g = (near[...] + near_outer[...]) + (far_outer[...] + other[:, tokens:])
-    cov_out[...] = covariance(x, False) + covariance(g, True)
-    samples_of(x, g, sample_out)
-
-
-def covariances(x, x_outer, near, near_outer, far_outer, other, seqs):
-    rank = near.shape[0]
+def cov_in_kernel(*refs):
+    pieces, (x_out, cov_out) = refs[:-2], refs[-2:]
+    x = total(pieces)
+    x_out[...] = x
+    cov_out[...] = covariance(x, False)
+
+
+def cov_in(pieces):
+    rank, tokens = pieces[0].shape
     return pl.pallas_call(
-        covariances_kernel,
-        in_specs=[vmem()] * 6,
+        cov_in_kernel,
+        in_specs=[vmem()] * len(pieces),
+        out_specs=[vmem()] * 2,
+        out_shape=[
+            jax.ShapeDtypeStruct((rank, tokens), jnp.float32),
+            jax.ShapeDtypeStruct((rank, 2 * rank), jnp.float32),
+        ],
+        compiler_params=params(16),
+        name="cov_in",
+    )(*pieces)
+
+
+def cov_out_kernel(x_ref, cov_ref, *refs):
+    pieces, (cov_out, sample_out) = refs[:-2], refs[-2:]
+    g = total(pieces)
+    cov_out[...] = cov_ref[...] + covariance(g, True)
+    samples_of(x_ref[...], g, sample_out)
+
+
+def cov_out(x, cov, pieces, seqs):
+    rank = x.shape[0]
+    return pl.pallas_call(
+        cov_out_kernel,
+        in_specs=[vmem()] * (2 + len(pieces)),
         out_specs=[vmem()] * 2,
         out_shape=[
             jax.ShapeDtypeStruct((rank, 2 * rank), jnp.float32),
             jax.ShapeDtypeStruct((seqs, rank, 2 * rank), jnp.float32),
         ],
         compiler_params=params(16),
-        name="covariances",
-    )(x, x_outer, near, near_outer, far_outer, other)
+        name="cov_out",
+    )(x, cov, *pieces)
 
 
 def scales(steps, spread):
@@ -355,33 +392,31 @@
     column = lax.axis_index("tensor").astype(jnp.int32)
     side = (column >= 2).astype(jnp.int32).reshape(1)
     place = lax.axis_index("dp").astype(jnp.int32).reshape(1)
-    x = project_in(side, acts, proj_in)
-    x_outer = inwards(x)
-    near, far, packed = project_out(side, grads, proj_out, queries, x)
-    far_outer = lax.ppermute(far, "tensor", [(0, 2), (3, 1)])
-    crossing = jnp.concatenate([x[1] + after(x_outer, far)[1], far], axis=1)
-    other = across(crossing)
-    near_outer = inwards(near)
-    pieces = [after(packed, crossing)[None]]
+    x_near, x_far = project_in(side, acts, proj_in)
+    x_pieces = to_owner(x_near, x_far)
+    near, far, packed = project_out(side, grads, proj_out, queries, x_near)
+    pieces = to_owner(near, far)
+    x, cov = cov_in(x_pieces[:3] + [after(x_pieces[3], pieces[1])])
+    query_pieces = [after(packed, cov)[None]]
     bit = 1
     while bit < parts:
-        mine = pieces[0] if bit == 1 else jnp.concatenate(pieces, axis=0)
-        pieces = [mine, swap(mine, "dp", bit)]
+        mine = query_pieces[0] if bit == 1 else jnp.concatenate(query_pieces, axis=0)
+        query_pieces = [mine, swap(mine, "dp", bit)]
         bit *= 2
-    cov, sample = covariances(x, x_outer, near, near_outer, far_outer, other, seqs)
+    cov, sample = cov_out(x, cov, pieces, seqs)
     other = jnp.zeros_like(cov)
     bit = 1
     while bit < parts:
         cov = cov if bit == 1 else cov + other
         other = swap(cov, "dp", bit)
         bit *= 2
-    scores = score(place, cov, other, sample, pieces, tokens)
+    scores = score(place, cov, other, sample, query_pieces, tokens)
     owner = (column == 1) | (column == 2)
     return (
         jnp.where(owner, scores, 0.0)
         + lax.ppermute(scores, "tensor", [(1, 0), (2, 3)])
         + lax.ppermute(scores, "tensor", [(2, 0), (1, 3)])
-        + across(scores)
+        + jnp.where(owner, across(scores), 0.0)
     )
 
 

time: 61.9 us -> 74.1 us (1.20)
  starting transfers between devices: 20.2 us -> 30.7 us
  waiting for transfers between devices: 19.8 us -> 21.3 us
    ppermute x5 -> x7, starting transfers between devices: 14.4 us -> 24.9 us  [the longest x2 17.6 us: to_owner(): lax.ppermute(near, 'tensor', [(0, 1), (3, 2)])]
    ppermute x1, waiting for transfers between devices: 6.11 us -> 0.41 us  [local_owned(): lax.ppermute(scores, 'tensor', [(1, 0), (2, 3)])]
    ppermute x1, waiting for transfers between devices: 1.19 us -> 5.41 us  [local_owned(): lax.ppermute(scores, 'tensor', [(2, 0), (1, 3)])]
    ppermute x5 -> x7, waiting for transfers between devices: 8.83 us -> 11.8 us  [the longest x2 7.51 us: to_owner(): lax.ppermute(far, 'tensor', [(0, 2), (3, 1)])]
  transfers between devices with their start and end apart: 11 -> 13, of which waited for: 6 -> 7; matrix products, arithmetic and copies ran while one was open for 0% -> 0% of each run, Pallas kernels for 21% -> 17%
where the time goes in v9:
time: 74.1 us; the launch traced here: 73.8 us
  starting transfers between devices  30.7 us (41%)
  waiting for transfers between devices  21.3 us (29%)
  Pallas kernels  21.1 us (28%)
    ppermute x2, starting transfers between devices, to_owner(): lax.ppermute(near, 'tensor', [(0, 1), (3, 2)])  17.6 us
    pallas_call x1, Pallas kernels, project_out(): pl.pallas_call(project_out_kernel, in_specs=[smem(), hbm(), vmem(), hbm()...  11.5 us
    ppermute x2, waiting for transfers between devices, to_owner(): lax.ppermute(far, 'tensor', [(0, 2), (3, 1)])  7.51 us
    ppermute x1, waiting for transfers between devices, local_owned(): lax.ppermute(scores, 'tensor', [(2, 0), (1, 3)])  5.41 us
    ppermute x2, starting transfers between devices, to_owner(): lax.ppermute(far, 'tensor', [(0, 2), (3, 1)])  5.28 us
    pallas_call x1, Pallas kernels, score(): pl.pallas_call(functools.partial(score_kernel, tokens), in_specs=[smem()]...  4.35 us
    ppermute x2, waiting for transfers between devices, to_owner(): lax.ppermute(near, 'tensor', [(0, 1), (3, 2)])  4.3 us
    pallas_call x1, Pallas kernels, project_in(): pl.pallas_call(project_in_kernel, in_specs=[smem(), hbm(), hbm()], out_sp...  3.88 us
  transfers between devices with their start and end apart: 13, of which 7 were waited for; matrix products, arithmetic and copies ran while one was open for 0% of the time, Pallas kernels for 17%

profile of v9, /device:TPU:0, one launch (start us, length us, event | category | flops | bytes accessed | tf_op | source)
XLA Modules:
  0.0 73.8 jit_solution(8914864271093169545)
XLA Ops:
  0.0 0.0 copy-start
  0.0 3.9 %project_in.1 = (f32[64,1024]{1,0:T(8,128)S(1)}, f32[64,1024]{1,0:T(8,128)S(1)}) custom-call(s32[1]{0:T(128)} %bitcast.1.side_ref, bf16[4,256,2048]{2,1,0:T(8,128)(2,1)} %rows_hbm.2, bf16[2,64,2048]{2,1,0:T(8,128)(2,1)} %proj_hbm.1), custom_call_target="tpu_custom_call" | custom-call | tf_op jit(solution)/shard_map/project_in/pallas_call | solution.py:83
  3.9 4.9 %collective-permute-start.2 = (f32[64,1024]{1,0:T(8,128)S(1)}, f32[64,1024]{1,0:T(8,128)S(1)}, u32[]{:S(2)}, u32[]{:S(2)}) collective-permute-start(f32[64,1024]{1,0:T(8,128)S(1)} %get-tuple-element.16.after.refs_0_), channel_id=1, source_target_pairs={{0,4},{12,8},{1,5},{13,9},{2,6},{14,10},{3,7},{15,11},{16,20},{28,... | collective-permute-start | bytes 786440 | tf_op jit(solution)/shard_map/ppermute | solution.py:174
  8.8 0.0 copy-done
  8.9 11.5 %project_out.1 = (f32[64,1024]{1,0:T(8,128)S(1)}, f32[64,1024]{1,0:T(8,128)S(1)}, bf16[8,64,128]{2,1,0:T(8,128)(2,1)S(1)}) custom-call(s32[1]{0:T(128)} %bitcast.1.side_ref, bf16[2,4,256,7168]{3,2,1,0:T(8,128)(2,1)} %rows_hbm.3, bf16[2,64,7168]{2,1,0:T(8,128)(2,1)S(1)} %copy-done, bf16[16,2,64,64]{3,2,1,0:T(8,128)(2,1)} %queries_hbm.1, ...), custom_call_target="tpu_custom_call" | custom-call | tf_op jit(solution)/shard_map/project_out/pallas_call | solution.py:144
  20.3 2.3 %collective-permute-start.3 = (f32[64,1024]{1,0:T(8,128)S(1)}, f32[64,1024]{1,0:T(8,128)S(1)}, u32[]{:S(2)}, u32[]{:S(2)}) collective-permute-start(f32[64,1024]{1,0:T(8,128)S(1)} %get-tuple-element.18), channel_id=1, source_target_pairs={{0,8},{12,4},{1,9},{13,5},{2,10},{14,6},{3,11},{15,7},{16,24},{28,... | collective-permute-start | bytes 786440 | tf_op jit(solution)/shard_map/ppermute | solution.py:172
  22.6 0.7 collective-permute-start.1
  23.3 3.0 %collective-permute-start = (f32[64,1024]{1,0:T(8,128)S(1)}, f32[64,1024]{1,0:T(8,128)S(1)}, u32[]{:S(2)}, u32[]{:S(2)}) collective-permute-start(f32[64,1024]{1,0:T(8,128)S(1)} %get-tuple-element.17), channel_id=1, source_target_pairs={{0,8},{12,4},{1,9},{13,5},{2,10},{14,6},{3,11},{15,7},{16,24},{28,... | collective-permute-start | bytes 786440 | tf_op jit(solution)/shard_map/ppermute | solution.py:172
  26.3 0.0 collective-permute-done.2.refs_3_
  26.3 3.0 %collective-permute-done.3.refs_1_ = f32[64,1024]{1,0:T(8,128)S(1)} collective-permute-done((f32[64,1024]{1,0:T(8,128)S(1)}, f32[64,1024]{1,0:T(8,128)S(1)}, u32[]{:S(2)}, u32[]{:S(2)}) %collective-permute-start.3) | collective-permute-done | bytes 262176 | tf_op jit(solution)/shard_map/ppermute | solution.py:172
  29.4 0.0 collective-permute-done.1.refs_2_
  29.4 4.5 %collective-permute-done.refs_1_ = f32[64,1024]{1,0:T(8,128)S(1)} collective-permute-done((f32[64,1024]{1,0:T(8,128)S(1)}, f32[64,1024]{1,0:T(8,128)S(1)}, u32[]{:S(2)}, u32[]{:S(2)}) %collective-permute-start) | collective-permute-done | bytes 262176 | tf_op jit(solution)/shard_map/ppermute | solution.py:172
  33.8 0.4 cov_in.1
  34.2 0.1 collective-permute-start.8
  34.3 0.7 collective-permute-start.4
  35.0 12.7 %collective-permute-start.5 = (f32[64,1024]{1,0:T(8,128)S(1)}, f32[64,1024]{1,0:T(8,128)S(1)}, u32[]{:S(2)}, u32[]{:S(2)}) collective-permute-start(f32[64,1024]{1,0:T(8,128)S(1)} %get-tuple-element.22.refs_0_), channel_id=1, source_target_pairs={{0,4},{12,8},{1,5},{13,9},{2,6},{14,10},{3,7},{15,11},{16,20},{28,... | collective-permute-start | bytes 786440 | tf_op jit(solution)/shard_map/ppermute | solution.py:174
  47.7 0.0 collective-permute-done.8
  47.7 1.6 %collective-permute-start.9 = (bf16[2,8,64,128]{3,2,1,0:T(8,128)(2,1)S(1)}, bf16[2,8,64,128]{3,2,1,0:T(8,128)(2,1)S(1)}, u32[]{:S(2)}, u32[]{:S(2)}) collective-permute-start(bf16[2,8,64,128]{3,2,1,0:T(8,128)(2,1)S(1)} %pad_maximum_fusion.refs_0_), channel_id=1, source_target_pairs={{0,2},{1,3},{2,0},{3,1},{4,6},{5,7},{6,4},{7,5},{8,10},{9,11},{10,... | collective-permute-start | bytes 786440 | tf_op jit(solution)/shard_map/ppermute | solution.py:381
  49.3 0.0 collective-permute-done.4.refs_2_
  49.3 4.3 %collective-permute-done.5.refs_3_ = f32[64,1024]{1,0:T(8,128)S(1)} collective-permute-done((f32[64,1024]{1,0:T(8,128)S(1)}, f32[64,1024]{1,0:T(8,128)S(1)}, u32[]{:S(2)}, u32[]{:S(2)}) %collective-permute-start.5) | collective-permute-done | bytes 262176 | tf_op jit(solution)/shard_map/ppermute | solution.py:174
  53.6 1.0 %cov_out.1 = (f32[64,128]{1,0:T(8,128)S(1)}, f32[4,64,128]{2,1,0:T(8,128)S(1)}) custom-call(f32[64,1024]{1,0:T(8,128)S(1)} %get-tuple-element.20.x_ref, f32[64,128]{1,0:T(8,128)S(1)} %get-tuple-element.21.cov_ref, f32[64,1024]{1,0:T(8,128)S(1)} %get-tuple-element.22.refs_0_, f32[64,1024]{1,0:T(8,128)S(1)} %collective-permute-done.3.refs_1_, ...), custom_call_target="tpu_custom_call" | custom-call | tf_op jit(solution)/shard_map/cov_out/pallas_call | solution.py:232
  54.6 0.1 collective-permute-start.6
  54.6 1.2 %collective-permute-done.6 = f32[64,128]{1,0:T(8,128)S(1)} collective-permute-done((f32[64,128]{1,0:T(8,128)S(1)}, f32[64,128]{1,0:T(8,128)S(1)}, u32[]{:S(2)}, u32[]{:S(2)}) %collective-permute-start.6) | collective-permute-done | bytes 32800 | tf_op jit(solution)/shard_map/ppermute | solution.py:381
  55.8 1.5 %collective-permute-start.7 = (f32[64,128]{1,0:T(8,128)S(1)}, f32[64,128]{1,0:T(8,128)S(1)}, u32[]{:S(2)}, u32[]{:S(2)}) collective-permute-start(f32[64,128]{1,0:T(8,128)S(1)} %add.12.own_ref), channel_id=1, source_target_pairs={{0,2},{1,3},{2,0},{3,1},{4,6},{5,7},{6,4},{7,5},{8,10},{9,11},{10,... | collective-permute-start | bytes 98312 | tf_op jit(solution)/shard_map/ppermute | solution.py:381
  57.3 2.4 %collective-permute-done.7.other_ref = f32[64,128]{1,0:T(8,128)S(1)} collective-permute-done((f32[64,128]{1,0:T(8,128)S(1)}, f32[64,128]{1,0:T(8,128)S(1)}, u32[]{:S(2)}, u32[]{:S(2)}) %collective-permute-start.7) | collective-permute-done | bytes 32800 | tf_op jit(solution)/shard_map/ppermute | solution.py:381
  59.8 0.0 collective-permute-done.9.refs_1_
  59.8 4.3 %score.1 = f32[4,64]{1,0:T(4,128)S(1)} custom-call(s32[1]{0:T(128)} %bitcast.place_ref, f32[64,128]{1,0:T(8,128)S(1)} %add.12.own_ref, f32[64,128]{1,0:T(8,128)S(1)} %collective-permute-done.7.other_ref, f32[4,64,128]{2,1,0:T(8,128)S(1)} %get-tuple-element.24.sample_ref, bf16[2,8,64,128]{3,2,1,0:T(8,128)(2,1)S(1)} %pad_maximum_fusion.refs_0_, ...), custom_call_target="tpu_custom_call" | custom-call | tf_op jit(solution)/shard_map/score/pallas_call | solution.py:366
  64.1 0.7 collective-permute-start.12
  64.8 1.3 %collective-permute-start.11 = (f32[4,64]{1,0:T(4,128)S(1)}, f32[4,64]{1,0:T(4,128)S(1)}, u32[]{:S(2)}, u32[]{:S(2)}) collective-permute-start(f32[4,64]{1,0:T(4,128)S(1)} %score.1), channel_id=1, source_target_pairs={{8,0},{4,12},{9,1},{5,13},{10,2},{6,14},{11,3},{7,15},{24,16},{20,... | collective-permute-start | bytes 3080 | tf_op jit(solution)/shard_map/ppermute | solution.py:418
  66.1 1.3 %collective-permute-start.10 = (f32[4,64]{1,0:T(4,128)S(1)}, f32[4,64]{1,0:T(4,128)S(1)}, u32[]{:S(2)}, u32[]{:S(2)}) collective-permute-start(f32[4,64]{1,0:T(4,128)S(1)} %score.1), channel_id=1, source_target_pairs={{4,0},{8,12},{5,1},{9,13},{6,2},{10,14},{7,3},{11,15},{20,16},{24,... | collective-permute-start | bytes 3080 | tf_op jit(solution)/shard_map/ppermute | solution.py:417
  67.4 0.0 collective-permute-done.12
  67.4 5.4 %collective-permute-done.11 = f32[4,64]{1,0:T(4,128)S(1)} collective-permute-done((f32[4,64]{1,0:T(4,128)S(1)}, f32[4,64]{1,0:T(4,128)S(1)}, u32[]{:S(2)}, u32[]{:S(2)}) %collective-permute-start.11) | collective-permute-done | bytes 1056 | tf_op jit(solution)/shard_map/ppermute | solution.py:418
  72.8 0.4 collective-permute-done.10
  73.2 0.6 select_add_fusion
  (2 shorter events, 0.0 us)
Async XLA Ops:
  0.0 8.8 %copy-start = (bf16[2,64,7168]{2,1,0:T(8,128)(2,1)S(1)}, bf16[2,64,7168]{2,1,0:T(8,128)(2,1)}, u32[]{:S(2)}) copy-start(bf16[2,64,7168]{2,1,0:T(8,128)(2,1)} %proj_ref.1) | copy-start | bytes 5505028
  3.9 22.4 %collective-permute-start.2 = (f32[64,1024]{1,0:T(8,128)S(1)}, f32[64,1024]{1,0:T(8,128)S(1)}, u32[]{:S(2)}, u32[]{:S(2)}) collective-permute-start(f32[64,1024]{1,0:T(8,128)S(1)} %get-tuple-element.16.after.refs_0_), channel_id=1, source_target_pairs={{0,4},{12,8},{1,5},{13,9},{2,6},{14,10},{3,7},{15,11},{16,20},{28,... | collective-permute-start | bytes 786440 | tf_op jit(solution)/shard_map/ppermute | solution.py:174
  20.3 9.0 %collective-permute-start.3 = (f32[64,1024]{1,0:T(8,128)S(1)}, f32[64,1024]{1,0:T(8,128)S(1)}, u32[]{:S(2)}, u32[]{:S(2)}) collective-permute-start(f32[64,1024]{1,0:T(8,128)S(1)} %get-tuple-element.18), channel_id=1, source_target_pairs={{0,8},{12,4},{1,9},{13,5},{2,10},{14,6},{3,11},{15,7},{16,24},{28,... | collective-permute-start | bytes 786440 | tf_op jit(solution)/shard_map/ppermute | solution.py:172
  22.6 6.7 %collective-permute-start.1 = (f32[64,1024]{1,0:T(8,128)S(1)}, f32[64,1024]{1,0:T(8,128)S(1)}, u32[]{:S(2)}, u32[]{:S(2)}) collective-permute-start(f32[64,1024]{1,0:T(8,128)S(1)} %get-tuple-element.17), channel_id=1, source_target_pairs={{4,8},{8,4},{0,0},{12,12},{5,9},{9,5},{1,1},{13,13},{6,10},{10,6},... | collective-permute-start | bytes 786440 | tf_op jit(solution)/shard_map/ppermute | solution.py:166
  23.3 10.5 %collective-permute-start = (f32[64,1024]{1,0:T(8,128)S(1)}, f32[64,1024]{1,0:T(8,128)S(1)}, u32[]{:S(2)}, u32[]{:S(2)}) collective-permute-start(f32[64,1024]{1,0:T(8,128)S(1)} %get-tuple-element.17), channel_id=1, source_target_pairs={{0,8},{12,4},{1,9},{13,5},{2,10},{14,6},{3,11},{15,7},{16,24},{28,... | collective-permute-start | bytes 786440 | tf_op jit(solution)/shard_map/ppermute | solution.py:172
  34.2 13.4 %collective-permute-start.8 = (bf16[1,8,64,128]{3,2,1,0:T(8,128)(2,1)S(1)}, bf16[1,8,64,128]{3,2,1,0:T(8,128)(2,1)S(1)}, u32[]{:S(2)}, u32[]{:S(2)}) collective-permute-start(bf16[1,8,64,128]{3,2,1,0:T(8,128)(2,1)S(1)} %bitcast.3), channel_id=1, source_target_pairs={{0,1},{1,0},{2,3},{3,2},{4,5},{5,4},{6,7},{7,6},{8,9},{9,8},{10,11... | collective-permute-start | bytes 393224 | tf_op jit(solution)/shard_map/ppermute | solution.py:381
  34.3 15.0 %collective-permute-start.4 = (f32[64,1024]{1,0:T(8,128)S(1)}, f32[64,1024]{1,0:T(8,128)S(1)}, u32[]{:S(2)}, u32[]{:S(2)}) collective-permute-start(f32[64,1024]{1,0:T(8,128)S(1)} %get-tuple-element.18), channel_id=1, source_target_pairs={{4,8},{8,4},{0,0},{12,12},{5,9},{9,5},{1,1},{13,13},{6,10},{10,6},... | collective-permute-start | bytes 786440 | tf_op jit(solution)/shard_map/ppermute | solution.py:166
  35.0 18.6 %collective-permute-start.5 = (f32[64,1024]{1,0:T(8,128)S(1)}, f32[64,1024]{1,0:T(8,128)S(1)}, u32[]{:S(2)}, u32[]{:S(2)}) collective-permute-start(f32[64,1024]{1,0:T(8,128)S(1)} %get-tuple-element.22.refs_0_), channel_id=1, source_target_pairs={{0,4},{12,8},{1,5},{13,9},{2,6},{14,10},{3,7},{15,11},{16,20},{28,... | collective-permute-start | bytes 786440 | tf_op jit(solution)/shard_map/ppermute | solution.py:174
  47.7 12.0 %collective-permute-start.9 = (bf16[2,8,64,128]{3,2,1,0:T(8,128)(2,1)S(1)}, bf16[2,8,64,128]{3,2,1,0:T(8,128)(2,1)S(1)}, u32[]{:S(2)}, u32[]{:S(2)}) collective-permute-start(bf16[2,8,64,128]{3,2,1,0:T(8,128)(2,1)S(1)} %pad_maximum_fusion.refs_0_), channel_id=1, source_target_pairs={{0,2},{1,3},{2,0},{3,1},{4,6},{5,7},{6,4},{7,5},{8,10},{9,11},{10,... | collective-permute-start | bytes 786440 | tf_op jit(solution)/shard_map/ppermute | solution.py:381
  54.6 1.3 %collective-permute-start.6 = (f32[64,128]{1,0:T(8,128)S(1)}, f32[64,128]{1,0:T(8,128)S(1)}, u32[]{:S(2)}, u32[]{:S(2)}) collective-permute-start(f32[64,128]{1,0:T(8,128)S(1)} %get-tuple-element.23), channel_id=1, source_target_pairs={{0,1},{1,0},{2,3},{3,2},{4,5},{5,4},{6,7},{7,6},{8,9},{9,8},{10,11... | collective-permute-start | bytes 98312 | tf_op jit(solution)/shard_map/ppermute | solution.py:381
  55.8 3.9 %collective-permute-start.7 = (f32[64,128]{1,0:T(8,128)S(1)}, f32[64,128]{1,0:T(8,128)S(1)}, u32[]{:S(2)}, u32[]{:S(2)}) collective-permute-start(f32[64,128]{1,0:T(8,128)S(1)} %add.12.own_ref), channel_id=1, source_target_pairs={{0,2},{1,3},{2,0},{3,1},{4,6},{5,7},{6,4},{7,5},{8,10},{9,11},{10,... | collective-permute-start | bytes 98312 | tf_op jit(solution)/shard_map/ppermute | solution.py:381
  64.1 3.3 %collective-permute-start.12 = (f32[4,64]{1,0:T(4,128)S(1)}, f32[4,64]{1,0:T(4,128)S(1)}, u32[]{:S(2)}, u32[]{:S(2)}) collective-permute-start(f32[4,64]{1,0:T(4,128)S(1)} %score.1), channel_id=1, source_target_pairs={{4,8},{8,4},{0,0},{12,12},{5,9},{9,5},{1,1},{13,13},{6,10},{10,6},... | collective-permute-start | bytes 3080 | tf_op jit(solution)/shard_map/ppermute | solution.py:166
  64.8 8.0 %collective-permute-start.11 = (f32[4,64]{1,0:T(4,128)S(1)}, f32[4,64]{1,0:T(4,128)S(1)}, u32[]{:S(2)}, u32[]{:S(2)}) collective-permute-start(f32[4,64]{1,0:T(4,128)S(1)} %score.1), channel_id=1, source_target_pairs={{8,0},{4,12},{9,1},{5,13},{10,2},{6,14},{11,3},{7,15},{24,16},{20,... | collective-permute-start | bytes 3080 | tf_op jit(solution)/shard_map/ppermute | solution.py:418
  66.1 7.1 %collective-permute-start.10 = (f32[4,64]{1,0:T(4,128)S(1)}, f32[4,64]{1,0:T(4,128)S(1)}, u32[]{:S(2)}, u32[]{:S(2)}) collective-permute-start(f32[4,64]{1,0:T(4,128)S(1)} %score.1), channel_id=1, source_target_pairs={{4,0},{8,12},{5,1},{9,13},{6,2},{10,14},{7,3},{11,15},{20,16},{24,... | collective-permute-start | bytes 3080 | tf_op jit(solution)/shard_map/ppermute | solution.py:417

commit v10 on v9

--- a/solution.py
+++ b/solution.py
@@ -163,7 +163,7 @@
 
 
 def across(value):
-    return lax.ppermute(value, "tensor", [(1, 2), (2, 1), (0, 0), (3, 3)])
+    return lax.ppermute(value, "tensor", [(1, 2), (2, 1)])
 
 
 def to_owner(near, far):
@@ -198,26 +198,28 @@
         sample_out[s] = jnp.concatenate([sample, sample], axis=1)
 
 
-def cov_in_kernel(*refs):
-    pieces, (x_out, cov_out) = refs[:-2], refs[-2:]
+def cov_in_kernel(packed_ref, *refs):
+    pieces, (packed, x_out, cov_out) = refs[:-3], refs[-3:]
+    packed[...] = packed_ref[...]
     x = total(pieces)
     x_out[...] = x
     cov_out[...] = covariance(x, False)
 
 
-def cov_in(pieces):
+def cov_in(packed, pieces):
     rank, tokens = pieces[0].shape
     return pl.pallas_call(
         cov_in_kernel,
-        in_specs=[vmem()] * len(pieces),
-        out_specs=[vmem()] * 2,
+        in_specs=[vmem()] * (1 + len(pieces)),
+        out_specs=[vmem()] * 3,
         out_shape=[
+            jax.ShapeDtypeStruct(packed.shape, packed.dtype),
             jax.ShapeDtypeStruct((rank, tokens), jnp.float32),
             jax.ShapeDtypeStruct((rank, 2 * rank), jnp.float32),
         ],
         compiler_params=params(16),
         name="cov_in",
-    )(*pieces)
+    )(packed, *pieces)
 
 
 def cov_out_kernel(x_ref, cov_ref, *refs):
@@ -291,11 +293,8 @@
 def score_kernel(tokens, place_ref, own_ref, other_ref, sample_ref, *refs):
     pieces, (out, held, half) = refs[:-3], refs[-3:]
     parts = held.shape[0]
-    k = 0
-    for piece in pieces:
-        for place in range(piece.shape[0]):
-            held[place_ref[0] ^ k] = piece[place]
-            k += 1
+    for k, piece in enumerate(pieces):
+        held[place_ref[0] ^ k] = piece[...]
     inverses = damped_inverses((own_ref[...] + other_ref[...]) / tokens)
     both = inverses.shape[0]
     size = both // 2
@@ -359,8 +358,8 @@
 
 
 def score(place, own, other, sample, pieces, tokens):
-    _, blocks, rank, both = pieces[0].shape
-    parts = sum(piece.shape[0] for piece in pieces)
+    blocks, rank, both = pieces[0].shape
+    parts = len(pieces)
     pairs = parts * blocks
     seqs = sample.shape[0]
     return pl.pallas_call(
@@ -379,10 +378,6 @@
 
 def swap(value, axis, bit):
     return lax.ppermute(value, axis, [(i, i ^ bit) for i in range(lax.axis_size(axis))])
-
-
-def after(value, earlier):
-    return lax.optimization_barrier((value, earlier))[0]
 
 
 def local_owned(acts, grads, proj_in, proj_out, queries):
@@ -396,13 +391,8 @@
     x_pieces = to_owner(x_near, x_far)
     near, far, packed = project_out(side, grads, proj_out, queries, x_near)
     pieces = to_owner(near, far)
-    x, cov = cov_in(x_pieces[:3] + [after(x_pieces[3], pieces[1])])
-    query_pieces = [after(packed, cov)[None]]
-    bit = 1
-    while bit < parts:
-        mine = query_pieces[0] if bit == 1 else jnp.concatenate(query_pieces, axis=0)
-        query_pieces = [mine, swap(mine, "dp", bit)]
-        bit *= 2
+    packed, x, cov = cov_in(packed, x_pieces)
+    query_pieces = [packed] + [swap(packed, "dp", bits) for bits in range(1, parts)]
     cov, sample = cov_out(x, cov, pieces, seqs)
     other = jnp.zeros_like(cov)
     bit = 1
@@ -412,12 +402,12 @@
         bit *= 2
     scores = score(place, cov, other, sample, query_pieces, tokens)
     owner = (column == 1) | (column == 2)
-    return (
-        jnp.where(owner, scores, 0.0)
-        + lax.ppermute(scores, "tensor", [(1, 0), (2, 3)])
-        + lax.ppermute(scores, "tensor", [(2, 0), (1, 3)])
-        + jnp.where(owner, across(scores), 0.0)
-    )
+    pieces = [
+        lax.ppermute(scores, "tensor", [(2, 0), (1, 3)]),
+        lax.ppermute(scores, "tensor", [(1, 0), (2, 3)]),
+        across(scores),
+    ]
+    return jnp.where(owner, scores, 0.0) + pieces[0] + pieces[1] + pieces[2]
 
 
 def damp(matrix):

time: 74.1 us -> 57.3 us (0.77)
  the two profiles are of different devices: /device:TPU:0 before, /device:TPU:8 now
where the time goes in v10:
time: 57.3 us; the launch traced here: 57.1 us
  Pallas kernels  21.1 us (37%)
  starting transfers between devices  21 us (37%)
  waiting for transfers between devices  14.2 us (25%)
  other arithmetic  0.59 us (1%)
    pallas_call x1, Pallas kernels, project_out(): pl.pallas_call(project_out_kernel, in_specs=[smem(), hbm(), vmem(), hbm()...  11.5 us
    ppermute x3, starting transfers between devices, across(): return lax.ppermute(value, 'tensor', [(1, 2), (2, 1)])  8.32 us
    ppermute x3, waiting for transfers between devices, across(): return lax.ppermute(value, 'tensor', [(1, 2), (2, 1)])  5.58 us
    ppermute x2, waiting for transfers between devices, to_owner(): lax.ppermute(far, 'tensor', [(0, 2), (3, 1)])  4.98 us
    ppermute x5, starting transfers between devices, swap(): lax.ppermute(value, axis, [(i, i ^ bit) for i in range(lax.axis_size(axis...  4.75 us
    pallas_call x1, Pallas kernels, score(): pl.pallas_call(functools.partial(score_kernel, tokens), in_specs=[smem()]...  4.36 us
    pallas_call x1, Pallas kernels, project_in(): pl.pallas_call(project_in_kernel, in_specs=[smem(), hbm(), hbm()], out_sp...  3.88 us
    ppermute x5, waiting for transfers between devices, swap(): lax.ppermute(value, axis, [(i, i ^ bit) for i in range(lax.axis_size(axis...  3.62 us
  transfers between devices with their start and end apart: 14, of which 5 were waited for; matrix products, arithmetic and copies ran while one was open for 0% of the time, Pallas kernels for 23%

profile of v10, /device:TPU:8, one launch (start us, length us, event | category | flops | bytes accessed | tf_op | source)
XLA Modules:
  0.0 57.1 jit_solution(12325467864456173814)
XLA Ops:
  0.0 0.0 copy-start
  0.0 3.9 %project_in.1 = (f32[64,1024]{1,0:T(8,128)S(1)}, f32[64,1024]{1,0:T(8,128)S(1)}) custom-call(s32[1]{0:T(128)} %bitcast.1.side_ref, bf16[4,256,2048]{2,1,0:T(8,128)(2,1)} %rows_hbm.2, bf16[2,64,2048]{2,1,0:T(8,128)(2,1)} %proj_hbm.1), custom_call_target="tpu_custom_call" | custom-call | tf_op jit(solution)/shard_map/project_in/pallas_call | solution.py:83
  3.9 1.3 %collective-permute-start.2 = (f32[64,1024]{1,0:T(8,128)S(1)}, f32[64,1024]{1,0:T(8,128)S(1)}, u32[]{:S(2)}, u32[]{:S(2)}) collective-permute-start(f32[64,1024]{1,0:T(8,128)S(1)} %get-tuple-element.15.after.refs_0_), channel_id=1, source_target_pairs={{0,4},{12,8},{1,5},{13,9},{2,6},{14,10},{3,7},{15,11},{16,20},{28,... | collective-permute-start | bytes 786440 | tf_op jit(solution)/shard_map/ppermute | solution.py:174
  5.2 1.3 %collective-permute-start = (f32[64,1024]{1,0:T(8,128)S(1)}, f32[64,1024]{1,0:T(8,128)S(1)}, u32[]{:S(2)}, u32[]{:S(2)}) collective-permute-start(f32[64,1024]{1,0:T(8,128)S(1)} %get-tuple-element.17), channel_id=1, source_target_pairs={{0,8},{12,4},{1,9},{13,5},{2,10},{14,6},{3,11},{15,7},{16,24},{28,... | collective-permute-start | bytes 786440 | tf_op jit(solution)/shard_map/ppermute | solution.py:172
  6.5 3.5 %collective-permute-start.1 = (f32[64,1024]{1,0:T(8,128)S(1)}, f32[64,1024]{1,0:T(8,128)S(1)}, u32[]{:S(2)}, u32[]{:S(2)}) collective-permute-start(f32[64,1024]{1,0:T(8,128)S(1)} %get-tuple-element.17), channel_id=1, source_target_pairs={{4,8},{8,4},{5,9},{9,5},{6,10},{10,6},{7,11},{11,7},{20,24},{24,20... | collective-permute-start | bytes 786440 | tf_op jit(solution)/shard_map/ppermute | solution.py:166
  10.0 0.0 copy-done
  10.0 11.5 %project_out.1 = (f32[64,1024]{1,0:T(8,128)S(1)}, f32[64,1024]{1,0:T(8,128)S(1)}, bf16[8,64,128]{2,1,0:T(8,128)(2,1)S(1)}) custom-call(s32[1]{0:T(128)} %bitcast.1.side_ref, bf16[2,4,256,7168]{3,2,1,0:T(8,128)(2,1)} %rows_hbm.3, bf16[2,64,7168]{2,1,0:T(8,128)(2,1)S(1)} %copy-done, bf16[16,2,64,64]{3,2,1,0:T(8,128)(2,1)} %queries_hbm.1, ...), custom_call_target="tpu_custom_call" | custom-call | tf_op jit(solution)/shard_map/project_out/pallas_call | solution.py:144
  21.5 1.3 %collective-permute-start.3 = (f32[64,1024]{1,0:T(8,128)S(1)}, f32[64,1024]{1,0:T(8,128)S(1)}, u32[]{:S(2)}, u32[]{:S(2)}) collective-permute-start(f32[64,1024]{1,0:T(8,128)S(1)} %get-tuple-element.21), channel_id=1, source_target_pairs={{0,8},{12,4},{1,9},{13,5},{2,10},{14,6},{3,11},{15,7},{16,24},{28,... | collective-permute-start | bytes 786440 | tf_op jit(solution)/shard_map/ppermute | solution.py:172
  22.8 2.4 %collective-permute-start.4 = (f32[64,1024]{1,0:T(8,128)S(1)}, f32[64,1024]{1,0:T(8,128)S(1)}, u32[]{:S(2)}, u32[]{:S(2)}) collective-permute-start(f32[64,1024]{1,0:T(8,128)S(1)} %get-tuple-element.21), channel_id=1, source_target_pairs={{4,8},{8,4},{5,9},{9,5},{6,10},{10,6},{7,11},{11,7},{20,24},{24,20... | collective-permute-start | bytes 786440 | tf_op jit(solution)/shard_map/ppermute | solution.py:166
  25.1 0.0 collective-permute-done.2.refs_3_
  25.1 1.3 %collective-permute-start.5 = (f32[64,1024]{1,0:T(8,128)S(1)}, f32[64,1024]{1,0:T(8,128)S(1)}, u32[]{:S(2)}, u32[]{:S(2)}) collective-permute-start(f32[64,1024]{1,0:T(8,128)S(1)} %get-tuple-element.20.refs_0_), channel_id=1, source_target_pairs={{0,4},{12,8},{1,5},{13,9},{2,6},{14,10},{3,7},{15,11},{16,20},{28,... | collective-permute-start | bytes 786440 | tf_op jit(solution)/shard_map/ppermute | solution.py:174
  26.4 0.0 collective-permute-done.refs_1_
  26.5 0.0 collective-permute-done.1.refs_2_
  26.5 0.4 cov_in.1
  26.9 0.4 collective-permute-start.10
  27.3 1.2 %collective-permute-start.8 = (bf16[8,64,128]{2,1,0:T(8,128)(2,1)S(1)}, bf16[8,64,128]{2,1,0:T(8,128)(2,1)S(1)}, u32[]{:S(2)}, u32[]{:S(2)}) collective-permute-start(bf16[8,64,128]{2,1,0:T(8,128)(2,1)S(1)} %get-tuple-element.24.refs_0_), channel_id=1, source_target_pairs={{0,1},{1,0},{2,3},{3,2},{4,5},{5,4},{6,7},{7,6},{8,9},{9,8},{10,11... | collective-permute-start | bytes 393224 | tf_op jit(solution)/shard_map/ppermute | solution.py:380
  28.6 5.0 %collective-permute-done.3.refs_1_ = f32[64,1024]{1,0:T(8,128)S(1)} collective-permute-done((f32[64,1024]{1,0:T(8,128)S(1)}, f32[64,1024]{1,0:T(8,128)S(1)}, u32[]{:S(2)}, u32[]{:S(2)}) %collective-permute-start.3) | collective-permute-done | bytes 262176 | tf_op jit(solution)/shard_map/ppermute | solution.py:172
  33.5 1.5 %collective-permute-start.9 = (bf16[8,64,128]{2,1,0:T(8,128)(2,1)S(1)}, bf16[8,64,128]{2,1,0:T(8,128)(2,1)S(1)}, u32[]{:S(2)}, u32[]{:S(2)}) collective-permute-start(bf16[8,64,128]{2,1,0:T(8,128)(2,1)S(1)} %get-tuple-element.24.refs_0_), channel_id=1, source_target_pairs={{0,2},{1,3},{2,0},{3,1},{4,6},{5,7},{6,4},{7,5},{8,10},{9,11},{10,... | collective-permute-start | bytes 393224 | tf_op jit(solution)/shard_map/ppermute | solution.py:380
  35.0 2.6 %collective-permute-done.4.refs_2_ = f32[64,1024]{1,0:T(8,128)S(1)} collective-permute-done((f32[64,1024]{1,0:T(8,128)S(1)}, f32[64,1024]{1,0:T(8,128)S(1)}, u32[]{:S(2)}, u32[]{:S(2)}) %collective-permute-start.4) | collective-permute-done | bytes 262176 | tf_op jit(solution)/shard_map/ppermute | solution.py:166
  37.6 0.0 collective-permute-done.5.refs_3_
  37.6 1.0 %cov_out.1 = (f32[64,128]{1,0:T(8,128)S(1)}, f32[4,64,128]{2,1,0:T(8,128)S(1)}) custom-call(f32[64,1024]{1,0:T(8,128)S(1)} %get-tuple-element.18.x_ref, f32[64,128]{1,0:T(8,128)S(1)} %get-tuple-element.19.cov_ref, f32[64,1024]{1,0:T(8,128)S(1)} %get-tuple-element.20.refs_0_, f32[64,1024]{1,0:T(8,128)S(1)} %collective-permute-done.3.refs_1_, ...), custom_call_target="tpu_custom_call" | custom-call | tf_op jit(solution)/shard_map/cov_out/pallas_call | solution.py:234
  38.6 0.1 collective-permute-start.6
  38.7 1.2 %collective-permute-done.6 = f32[64,128]{1,0:T(8,128)S(1)} collective-permute-done((f32[64,128]{1,0:T(8,128)S(1)}, f32[64,128]{1,0:T(8,128)S(1)}, u32[]{:S(2)}, u32[]{:S(2)}) %collective-permute-start.6) | collective-permute-done | bytes 32800 | tf_op jit(solution)/shard_map/ppermute | solution.py:380
  39.9 1.5 %collective-permute-start.7 = (f32[64,128]{1,0:T(8,128)S(1)}, f32[64,128]{1,0:T(8,128)S(1)}, u32[]{:S(2)}, u32[]{:S(2)}) collective-permute-start(f32[64,128]{1,0:T(8,128)S(1)} %add.12.own_ref), channel_id=1, source_target_pairs={{0,2},{1,3},{2,0},{3,1},{4,6},{5,7},{6,4},{7,5},{8,10},{9,11},{10,... | collective-permute-start | bytes 98312 | tf_op jit(solution)/shard_map/ppermute | solution.py:380
  41.4 2.4 %collective-permute-done.7.other_ref = f32[64,128]{1,0:T(8,128)S(1)} collective-permute-done((f32[64,128]{1,0:T(8,128)S(1)}, f32[64,128]{1,0:T(8,128)S(1)}, u32[]{:S(2)}, u32[]{:S(2)}) %collective-permute-start.7) | collective-permute-done | bytes 32800 | tf_op jit(solution)/shard_map/ppermute | solution.py:380
  43.8 0.0 collective-permute-done.10.refs_3_
  43.8 0.0 collective-permute-done.8.refs_1_
  43.8 0.0 collective-permute-done.9.refs_2_
  43.8 4.4 %score.1 = f32[4,64]{1,0:T(4,128)S(1)} custom-call(s32[1]{0:T(128)} %bitcast.place_ref, f32[64,128]{1,0:T(8,128)S(1)} %add.12.own_ref, f32[64,128]{1,0:T(8,128)S(1)} %collective-permute-done.7.other_ref, f32[4,64,128]{2,1,0:T(8,128)S(1)} %get-tuple-element.23.sample_ref, bf16[8,64,128]{2,1,0:T(8,128)(2,1)S(1)} %get-tuple-element.24.refs_0_, ...), custom_call_target="tpu_custom_call" | custom-call | tf_op jit(solution)/shard_map/score/pallas_call | solution.py:365
  48.2 1.5 %collective-permute-start.11 = (f32[4,64]{1,0:T(4,128)S(1)}, f32[4,64]{1,0:T(4,128)S(1)}, u32[]{:S(2)}, u32[]{:S(2)}) collective-permute-start(f32[4,64]{1,0:T(4,128)S(1)} %score.1), channel_id=1, source_target_pairs={{8,0},{4,12},{9,1},{5,13},{10,2},{6,14},{11,3},{7,15},{24,16},{20,... | collective-permute-start | bytes 3080 | tf_op jit(solution)/shard_map/ppermute | solution.py:406
  49.7 1.3 %collective-permute-start.12 = (f32[4,64]{1,0:T(4,128)S(1)}, f32[4,64]{1,0:T(4,128)S(1)}, u32[]{:S(2)}, u32[]{:S(2)}) collective-permute-start(f32[4,64]{1,0:T(4,128)S(1)} %score.1), channel_id=1, source_target_pairs={{4,0},{8,12},{5,1},{9,13},{6,2},{10,14},{7,3},{11,15},{20,16},{24,... | collective-permute-start | bytes 3080 | tf_op jit(solution)/shard_map/ppermute | solution.py:407
  51.0 2.5 %collective-permute-start.13 = (f32[4,64]{1,0:T(4,128)S(1)}, f32[4,64]{1,0:T(4,128)S(1)}, u32[]{:S(2)}, u32[]{:S(2)}) collective-permute-start(f32[4,64]{1,0:T(4,128)S(1)} %score.1), channel_id=1, source_target_pairs={{4,8},{8,4},{5,9},{9,5},{6,10},{10,6},{7,11},{11,7},{20,24},{24,20... | collective-permute-start | bytes 3080 | tf_op jit(solution)/shard_map/ppermute | solution.py:166
  53.5 0.0 collective-permute-done.11
  53.5 0.0 collective-permute-done.12
  53.5 3.0 %collective-permute-done.13 = f32[4,64]{1,0:T(4,128)S(1)} collective-permute-done((f32[4,64]{1,0:T(4,128)S(1)}, f32[4,64]{1,0:T(4,128)S(1)}, u32[]{:S(2)}, u32[]{:S(2)}) %collective-permute-start.13) | collective-permute-done | bytes 1056 | tf_op jit(solution)/shard_map/ppermute | solution.py:166
  56.5 0.6 %add_add_fusion = f32[4,64]{1,0:T(4,128)} fusion(f32[4,64]{1,0:T(4,128)S(1)} %collective-permute-done.13, f32[4,64]{1,0:T(4,128)S(1)} %collective-permute-done.12, f32[4,64]{1,0:T(4,128)S(1)} %collective-permute-done.11, f32[4,64]{1,0:T(4,128)S(1)} %score.1, pred[]{:T(512)S(6)} %or.3), kind=kLoop, calls=%fused_computation | loop fusion | flops 1024 | bytes 5121 | tf_op jit(solution)/shard_map/add | solution.py:410
  (1 shorter events, 0.0 us)
Async XLA Ops:
  0.0 10.0 %copy-start = (bf16[2,64,7168]{2,1,0:T(8,128)(2,1)S(1)}, bf16[2,64,7168]{2,1,0:T(8,128)(2,1)}, u32[]{:S(2)}) copy-start(bf16[2,64,7168]{2,1,0:T(8,128)(2,1)} %proj_ref.1) | copy-start | bytes 5505028
  3.9 21.2 %collective-permute-start.2 = (f32[64,1024]{1,0:T(8,128)S(1)}, f32[64,1024]{1,0:T(8,128)S(1)}, u32[]{:S(2)}, u32[]{:S(2)}) collective-permute-start(f32[64,1024]{1,0:T(8,128)S(1)} %get-tuple-element.15.after.refs_0_), channel_id=1, source_target_pairs={{0,4},{12,8},{1,5},{13,9},{2,6},{14,10},{3,7},{15,11},{16,20},{28,... | collective-permute-start | bytes 786440 | tf_op jit(solution)/shard_map/ppermute | solution.py:174
  5.2 21.3 %collective-permute-start = (f32[64,1024]{1,0:T(8,128)S(1)}, f32[64,1024]{1,0:T(8,128)S(1)}, u32[]{:S(2)}, u32[]{:S(2)}) collective-permute-start(f32[64,1024]{1,0:T(8,128)S(1)} %get-tuple-element.17), channel_id=1, source_target_pairs={{0,8},{12,4},{1,9},{13,5},{2,10},{14,6},{3,11},{15,7},{16,24},{28,... | collective-permute-start | bytes 786440 | tf_op jit(solution)/shard_map/ppermute | solution.py:172
  6.5 20.0 %collective-permute-start.1 = (f32[64,1024]{1,0:T(8,128)S(1)}, f32[64,1024]{1,0:T(8,128)S(1)}, u32[]{:S(2)}, u32[]{:S(2)}) collective-permute-start(f32[64,1024]{1,0:T(8,128)S(1)} %get-tuple-element.17), channel_id=1, source_target_pairs={{4,8},{8,4},{5,9},{9,5},{6,10},{10,6},{7,11},{11,7},{20,24},{24,20... | collective-permute-start | bytes 786440 | tf_op jit(solution)/shard_map/ppermute | solution.py:166
  21.5 12.1 %collective-permute-start.3 = (f32[64,1024]{1,0:T(8,128)S(1)}, f32[64,1024]{1,0:T(8,128)S(1)}, u32[]{:S(2)}, u32[]{:S(2)}) collective-permute-start(f32[64,1024]{1,0:T(8,128)S(1)} %get-tuple-element.21), channel_id=1, source_target_pairs={{0,8},{12,4},{1,9},{13,5},{2,10},{14,6},{3,11},{15,7},{16,24},{28,... | collective-permute-start | bytes 786440 | tf_op jit(solution)/shard_map/ppermute | solution.py:172
  22.8 14.9 %collective-permute-start.4 = (f32[64,1024]{1,0:T(8,128)S(1)}, f32[64,1024]{1,0:T(8,128)S(1)}, u32[]{:S(2)}, u32[]{:S(2)}) collective-permute-start(f32[64,1024]{1,0:T(8,128)S(1)} %get-tuple-element.21), channel_id=1, source_target_pairs={{4,8},{8,4},{5,9},{9,5},{6,10},{10,6},{7,11},{11,7},{20,24},{24,20... | collective-permute-start | bytes 786440 | tf_op jit(solution)/shard_map/ppermute | solution.py:166
  25.1 12.5 %collective-permute-start.5 = (f32[64,1024]{1,0:T(8,128)S(1)}, f32[64,1024]{1,0:T(8,128)S(1)}, u32[]{:S(2)}, u32[]{:S(2)}) collective-permute-start(f32[64,1024]{1,0:T(8,128)S(1)} %get-tuple-element.20.refs_0_), channel_id=1, source_target_pairs={{0,4},{12,8},{1,5},{13,9},{2,6},{14,10},{3,7},{15,11},{16,20},{28,... | collective-permute-start | bytes 786440 | tf_op jit(solution)/shard_map/ppermute | solution.py:174
  26.9 17.0 %collective-permute-start.10 = (bf16[8,64,128]{2,1,0:T(8,128)(2,1)S(1)}, bf16[8,64,128]{2,1,0:T(8,128)(2,1)S(1)}, u32[]{:S(2)}, u32[]{:S(2)}) collective-permute-start(bf16[8,64,128]{2,1,0:T(8,128)(2,1)S(1)} %get-tuple-element.24.refs_0_), channel_id=1, source_target_pairs={{0,3},{1,2},{2,1},{3,0},{4,7},{5,6},{6,5},{7,4},{8,11},{9,10},{10,... | collective-permute-start | bytes 393224 | tf_op jit(solution)/shard_map/ppermute | solution.py:380
  27.3 16.5 %collective-permute-start.8 = (bf16[8,64,128]{2,1,0:T(8,128)(2,1)S(1)}, bf16[8,64,128]{2,1,0:T(8,128)(2,1)S(1)}, u32[]{:S(2)}, u32[]{:S(2)}) collective-permute-start(bf16[8,64,128]{2,1,0:T(8,128)(2,1)S(1)} %get-tuple-element.24.refs_0_), channel_id=1, source_target_pairs={{0,1},{1,0},{2,3},{3,2},{4,5},{5,4},{6,7},{7,6},{8,9},{9,8},{10,11... | collective-permute-start | bytes 393224 | tf_op jit(solution)/shard_map/ppermute | solution.py:380
  33.5 10.3 %collective-permute-start.9 = (bf16[8,64,128]{2,1,0:T(8,128)(2,1)S(1)}, bf16[8,64,128]{2,1,0:T(8,128)(2,1)S(1)}, u32[]{:S(2)}, u32[]{:S(2)}) collective-permute-start(bf16[8,64,128]{2,1,0:T(8,128)(2,1)S(1)} %get-tuple-element.24.refs_0_), channel_id=1, source_target_pairs={{0,2},{1,3},{2,0},{3,1},{4,6},{5,7},{6,4},{7,5},{8,10},{9,11},{10,... | collective-permute-start | bytes 393224 | tf_op jit(solution)/shard_map/ppermute | solution.py:380
  38.6 1.3 %collective-permute-start.6 = (f32[64,128]{1,0:T(8,128)S(1)}, f32[64,128]{1,0:T(8,128)S(1)}, u32[]{:S(2)}, u32[]{:S(2)}) collective-permute-start(f32[64,128]{1,0:T(8,128)S(1)} %get-tuple-element.22), channel_id=1, source_target_pairs={{0,1},{1,0},{2,3},{3,2},{4,5},{5,4},{6,7},{7,6},{8,9},{9,8},{10,11... | collective-permute-start | bytes 98312 | tf_op jit(solution)/shard_map/ppermute | solution.py:380
  39.9 3.9 %collective-permute-start.7 = (f32[64,128]{1,0:T(8,128)S(1)}, f32[64,128]{1,0:T(8,128)S(1)}, u32[]{:S(2)}, u32[]{:S(2)}) collective-permute-start(f32[64,128]{1,0:T(8,128)S(1)} %add.12.own_ref), channel_id=1, source_target_pairs={{0,2},{1,3},{2,0},{3,1},{4,6},{5,7},{6,4},{7,5},{8,10},{9,11},{10,... | collective-permute-start | bytes 98312 | tf_op jit(solution)/shard_map/ppermute | solution.py:380
  48.2 5.3 %collective-permute-start.11 = (f32[4,64]{1,0:T(4,128)S(1)}, f32[4,64]{1,0:T(4,128)S(1)}, u32[]{:S(2)}, u32[]{:S(2)}) collective-permute-start(f32[4,64]{1,0:T(4,128)S(1)} %score.1), channel_id=1, source_target_pairs={{8,0},{4,12},{9,1},{5,13},{10,2},{6,14},{11,3},{7,15},{24,16},{20,... | collective-permute-start | bytes 3080 | tf_op jit(solution)/shard_map/ppermute | solution.py:406
  49.7 3.8 %collective-permute-start.12 = (f32[4,64]{1,0:T(4,128)S(1)}, f32[4,64]{1,0:T(4,128)S(1)}, u32[]{:S(2)}, u32[]{:S(2)}) collective-permute-start(f32[4,64]{1,0:T(4,128)S(1)} %score.1), channel_id=1, source_target_pairs={{4,0},{8,12},{5,1},{9,13},{6,2},{10,14},{7,3},{11,15},{20,16},{24,... | collective-permute-start | bytes 3080 | tf_op jit(solution)/shard_map/ppermute | solution.py:407
  51.0 5.5 %collective-permute-start.13 = (f32[4,64]{1,0:T(4,128)S(1)}, f32[4,64]{1,0:T(4,128)S(1)}, u32[]{:S(2)}, u32[]{:S(2)}) collective-permute-start(f32[4,64]{1,0:T(4,128)S(1)} %score.1), channel_id=1, source_target_pairs={{4,8},{8,4},{5,9},{9,5},{6,10},{10,6},{7,11},{11,7},{20,24},{24,20... | collective-permute-start | bytes 3080 | tf_op jit(solution)/shard_map/ppermute | solution.py:166

commit v11 on v10

--- a/solution.py
+++ b/solution.py
@@ -47,7 +47,9 @@
     return pltpu.CompilerParams(vmem_limit_bytes=mib * MIB)
 
 
-def project_in_kernel(side_ref, rows_hbm, proj_hbm, near, far, rows, proj, acc, sems, proj_sem):
+def project_in_kernel(
+    side_ref, rows_hbm, proj_hbm, grads_hbm, near, far, early, rows, proj, acc, sems, proj_sem, early_sem
+):
     seqs, length, width = rows.shape
     rank = proj.shape[1]
     proj_copy = pltpu.make_async_copy(proj_hbm, proj, proj_sem)
@@ -58,6 +60,10 @@
 
     for s in range(seqs):
         copy(s).start()
+    early_copy = pltpu.make_async_copy(
+        grads_hbm.at[:, 0, :, pl.ds(0, early.shape[2])], early, early_sem
+    )
+    early_copy.start()
     proj_copy.wait()
 
     group = 2 - seqs % 2
@@ -75,30 +81,36 @@
 
     far[...] = acc[1 - side_ref[0]]
     near[...] = acc[side_ref[0]]
-
-
-def project_in(side, rows, proj):
+    early_copy.wait()
+
+
+def project_in(side, rows, proj, grads):
     seqs, length, _ = rows.shape
+    early = (2, length, grads.shape[3] // 2)
     rank = proj.shape[1]
     return pl.pallas_call(
         project_in_kernel,
-        in_specs=[smem(), hbm(), hbm()],
-        out_specs=[vmem()] * 2,
-        out_shape=[jax.ShapeDtypeStruct((rank, seqs * length), jnp.float32)] * 2,
+        in_specs=[smem(), hbm(), hbm(), hbm()],
+        out_specs=[vmem()] * 3,
+        out_shape=[
+            jax.ShapeDtypeStruct((rank, seqs * length), jnp.float32),
+            jax.ShapeDtypeStruct((rank, seqs * length), jnp.float32),
+            jax.ShapeDtypeStruct(early, grads.dtype),
+        ],
         scratch_shapes=[
             pltpu.VMEM(rows.shape, rows.dtype),
             pltpu.VMEM(proj.shape, proj.dtype),
             pltpu.VMEM((2, rank, seqs * length), jnp.float32),
             pltpu.SemaphoreType.DMA((seqs,)),
             pltpu.SemaphoreType.DMA,
+            pltpu.SemaphoreType.DMA,
         ],
         compiler_params=params(16),
         name="project_in",
-    )(side, in_hbm(rows), in_hbm(proj))
-
-
-def project_out_kernel(side_ref, rows_hbm, proj_ref, queries_hbm, after, *refs):
-    del after
+    )(side, in_hbm(rows), in_hbm(proj), in_hbm(grads))
+
+
+def project_out_kernel(side_ref, rows_hbm, proj_ref, queries_hbm, early, *refs):
     (near, far, packed), (rows, held, acc, sems, sem) = refs[:3], refs[3:]
     _, seqs, length, width = rows.shape
     parts = sems.shape[2]
@@ -106,6 +118,8 @@
     copies = {}
     for s in range(seqs):
         for part in range(parts):
+            if s == 0 and part < parts // 2:
+                continue
             lanes = pl.ds(part * piece, piece)
             for layer in range(2):
                 copies[s, part, layer] = pltpu.make_async_copy(
@@ -120,10 +134,13 @@
         tokens = slice(s * length, (s + 1) * length)
         for part in range(parts):
             lanes = slice(part * piece, (part + 1) * piece)
+            ready = s == 0 and part < parts // 2
             for layer in range(2):
-                copies[s, part, layer].wait()
+                if not ready:
+                    copies[s, part, layer].wait()
             for layer in range(2):
-                value = nt(proj_ref[layer, :, lanes], rows[layer, s, :, lanes])
+                block = early[layer, :, lanes] if ready else rows[layer, s, :, lanes]
+                value = nt(proj_ref[layer, :, lanes], block)
                 if part > 0:
                     value = value + acc[layer, :, tokens]
                 acc[layer, :, tokens] = value
@@ -136,14 +153,14 @@
         packed[k] = jnp.concatenate(pair, axis=1).astype(held.dtype)
 
 
-def project_out(side, rows, proj, queries, after):
+def project_out(side, rows, proj, queries, early):
     _, seqs, length, width = rows.shape
     rank = proj.shape[1]
     count = queries.shape[0]
-    parts = 4 if width % 512 == 0 else 1
+    parts = 4 if width % 512 == 0 else 2
     return pl.pallas_call(
         project_out_kernel,
-        in_specs=[smem(), hbm(), vmem(), hbm(), hbm()],
+        in_specs=[smem(), hbm(), vmem(), hbm(), vmem()],
         out_specs=[vmem()] * 3,
         out_shape=[
             jax.ShapeDtypeStruct((rank, seqs * length), jnp.float32),
@@ -159,7 +176,7 @@
         ],
         compiler_params=params(40),
         name="project_out",
-    )(side, in_hbm(rows), proj, in_hbm(queries), after)
+    )(side, in_hbm(rows), proj, in_hbm(queries), early)
 
 
 def across(value):
@@ -169,9 +186,9 @@
 def to_owner(near, far):
     return [
         near,
+        lax.ppermute(near, "tensor", [(0, 1), (3, 2)]),
+        across(far),
         lax.ppermute(far, "tensor", [(0, 2), (3, 1)]),
-        across(far),
-        lax.ppermute(near, "tensor", [(0, 1), (3, 2)]),
     ]
 
 
@@ -253,33 +270,28 @@
     return out
 
 
-def damped_inverses(pair):
-    size, both = pair.shape
-    left = lax.broadcasted_iota(jnp.int32, pair.shape, 1) < size
-    whole = jnp.concatenate([jnp.where(left, pair, 0.0), jnp.where(left, 0.0, pair)], axis=0)
-    rows = lax.broadcasted_iota(jnp.int32, whole.shape, 0)
-    cols = lax.broadcasted_iota(jnp.int32, whole.shape, 1)
+def damped_inverses(matrices):
+    size = matrices[0].shape[0]
+    rows = lax.broadcasted_iota(jnp.int32, (size, size), 0)
+    cols = lax.broadcasted_iota(jnp.int32, (size, size), 1)
     diagonal = rows == cols
-    on_diagonal = jnp.where(diagonal, whole, 0.0)
-    unit = jnp.where(
-        rows < size, jnp.sum(on_diagonal[:size]) / size, jnp.sum(on_diagonal[size:]) / size
-    )
     eye = jnp.where(diagonal, 1.0, 0.0)
-    matrix = whole / unit + 0.1 * eye
+    units = [jnp.sum(jnp.where(diagonal, matrix, 0.0)) / size for matrix in matrices]
+    damped = [matrix / unit + 0.1 * eye for matrix, unit in zip(matrices, units)]
     low, high = 0.1, size + 0.1
     start = 2.0 / (low + high)
     steps = scales(7, high / low)
-    y = matrix * start
-    x = (2.0 * start * steps[0]) * eye - (start * steps[0]) * y
-    y = steps[0] * (2.0 * y - nn(y, y, HIGHEST))
-
+    y = [matrix * start for matrix in damped]
+    x = [(2.0 * start * steps[0]) * eye - (start * steps[0]) * v for v in y]
+    y = [steps[0] * (2.0 * v - nn(v, v, HIGHEST)) for v in y]
     for scale in steps[1:-1]:
-        product = nn(jnp.concatenate([x, y], axis=0), y, HIGHEST)
-        x = scale * (2.0 * x - product[:both])
-        y = scale * (2.0 * y - product[both:])
-    x = steps[-1] * (2.0 * x - nn(x, y, HIGHEST))
-    x = x + nn(x, eye - nn(matrix, x, HIGHEST), HIGHEST)
-    return x / unit
+        both = [nn(jnp.concatenate(pair, axis=0), pair[1], HIGHEST) for pair in zip(x, y)]
+        x = [scale * (2.0 * u - product[:size]) for u, product in zip(x, both)]
+        y = [scale * (2.0 * v - product[size:]) for v, product in zip(y, both)]
+    x = [steps[-1] * (2.0 * u - nn(u, v, HIGHEST)) for u, v in zip(x, y)]
+    rest = [eye - nn(matrix, u, HIGHEST) for matrix, u in zip(damped, x)]
+    x = [u + nn(u, r, HIGHEST) for u, r in zip(x, rest)]
+    return [u / unit for u, unit in zip(x, units)]
 
 
 def split(value):
@@ -295,20 +307,22 @@
     parts = held.shape[0]
     for k, piece in enumerate(pieces):
         held[place_ref[0] ^ k] = piece[...]
-    inverses = damped_inverses((own_ref[...] + other_ref[...]) / tokens)
-    both = inverses.shape[0]
-    size = both // 2
+    pair = (own_ref[...] + other_ref[...]) / tokens
+    size, both = pair.shape
+    left, right = damped_inverses([pair[:, :size], pair[:, size:]])
     samples = [sample_ref[s] for s in range(sample_ref.shape[0])]
     seqs = len(samples)
     blocks = held.shape[1]
     pairs = parts * blocks
-    first = jnp.concatenate(split(inverses[:size, :size]), axis=0)
+    first = jnp.concatenate(split(left), axis=0)
     none = jnp.zeros_like(first)
     first = jnp.concatenate(
         [jnp.concatenate([first, none], axis=1), jnp.concatenate([none, first], axis=1)], axis=0
     )
-    right = inverses[size:]
-    twice = jnp.concatenate([pltpu.roll(right, size, 1), right], axis=0)
+    none = jnp.zeros_like(right)
+    twice = jnp.concatenate(
+        [jnp.concatenate([right, none], axis=1), jnp.concatenate([none, right], axis=1)], axis=0
+    )
     high, middle, _ = split(twice)
     once = jnp.concatenate([high, middle], axis=1)
     second = jnp.concatenate([once, once], axis=0)
@@ -387,9 +401,9 @@
     column = lax.axis_index("tensor").astype(jnp.int32)
     side = (column >= 2).astype(jnp.int32).reshape(1)
     place = lax.axis_index("dp").astype(jnp.int32).reshape(1)
-    x_near, x_far = project_in(side, acts, proj_in)
+    x_near, x_far, early = project_in(side, acts, proj_in, grads)
     x_pieces = to_owner(x_near, x_far)
-    near, far, packed = project_out(side, grads, proj_out, queries, x_near)
+    near, far, packed = project_out(side, grads, proj_out, queries, early)
     pieces = to_owner(near, far)
     packed, x, cov = cov_in(packed, x_pieces)
     query_pieces = [packed] + [swap(packed, "dp", bits) for bits in range(1, parts)]
@@ -401,13 +415,10 @@
         other = swap(cov, "dp", bit)
         bit *= 2
     scores = score(place, cov, other, sample, query_pieces, tokens)
-    owner = (column == 1) | (column == 2)
-    pieces = [
-        lax.ppermute(scores, "tensor", [(2, 0), (1, 3)]),
-        lax.ppermute(scores, "tensor", [(1, 0), (2, 3)]),
-        across(scores),
-    ]
-    return jnp.where(owner, scores, 0.0) + pieces[0] + pieces[1] + pieces[2]
+    outer = lax.ppermute(scores, "tensor", [(1, 0), (2, 3)])
+    outer = outer + lax.ppermute(scores, "tensor", [(2, 0), (1, 3)])
+    back = lax.ppermute(outer, "tensor", [(0, 1), (3, 2)])
+    return jnp.where((column == 1) | (column == 2), back, outer)
 
 
 def damp(matrix):

time: 57.3 us -> 59.9 us (1.045)
  the two profiles are of different devices: /device:TPU:8 before, /device:TPU:0 now
where the time goes in v11:
time: 59.9 us; the launch traced here: 59.6 us
  starting transfers between devices  20.5 us (34%)
  Pallas kernels  20.1 us (34%)
  waiting for transfers between devices  18.3 us (31%)
    pallas_call x1, Pallas kernels, project_out(): pl.pallas_call(project_out_kernel, in_specs=[smem(), hbm(), vmem(), hbm()...  10.4 us
    ppermute x2, starting transfers between devices, to_owner(): lax.ppermute(near, 'tensor', [(0, 1), (3, 2)])  8.02 us
    ppermute x1, waiting for transfers between devices, local_owned(): outer = outer + lax.ppermute(scores, 'tensor', [(2, 0), (1, 3)])  5.18 us
    pallas_call x1, Pallas kernels, score(): pl.pallas_call(functools.partial(score_kernel, tokens), in_specs=[smem()]...  4.44 us
    ppermute x2, waiting for transfers between devices, to_owner(): lax.ppermute(far, 'tensor', [(0, 2), (3, 1)])  4.19 us
    pallas_call x1, Pallas kernels, project_in(): pl.pallas_call(project_in_kernel, in_specs=[smem(), hbm(), hbm(), hbm()],...  3.89 us
    ppermute x5, waiting for transfers between devices, swap(): lax.ppermute(value, axis, [(i, i ^ bit) for i in range(lax.axis_size(axis...  3.62 us
    ppermute x2, starting transfers between devices, to_owner(): lax.ppermute(far, 'tensor', [(0, 2), (3, 1)])  3.61 us
  transfers between devices with their start and end apart: 14, of which 7 were waited for; matrix products, arithmetic and copies ran while one was open for 0% of the time, Pallas kernels for 20%

profile of v11, /device:TPU:0, one launch (start us, length us, event | category | flops | bytes accessed | tf_op | source)
XLA Modules:
  0.0 59.6 jit_solution(3065796209207007837)
XLA Ops:
  0.0 0.0 copy-start
  0.0 3.9 %project_in.1 = (f32[64,1024]{1,0:T(8,128)S(1)}, f32[64,1024]{1,0:T(8,128)S(1)}, bf16[2,256,3584]{2,1,0:T(8,128)(2,1)S(1)}) custom-call(s32[1]{0:T(128)} %bitcast.1.side_ref, bf16[4,256,2048]{2,1,0:T(8,128)(2,1)} %rows_hbm.2, bf16[2,64,2048]{2,1,0:T(8,128)(2,1)} %proj_hbm.1, bf16[2,4,256,7168]{3,2,1,0:T(8,128)(2,1)} %rows_hbm.3), custom_call_target="tpu_custom_call" | custom-call | tf_op jit(solution)/shard_map/project_in/pallas_call | solution.py:91
  3.9 4.9 %collective-permute-start = (f32[64,1024]{1,0:T(8,128)S(1)}, f32[64,1024]{1,0:T(8,128)S(1)}, u32[]{:S(2)}, u32[]{:S(2)}) collective-permute-start(f32[64,1024]{1,0:T(8,128)S(1)} %get-tuple-element.18.refs_0_), channel_id=1, source_target_pairs={{0,4},{12,8},{1,5},{13,9},{2,6},{14,10},{3,7},{15,11},{16,20},{28,... | collective-permute-start | bytes 786440 | tf_op jit(solution)/shard_map/ppermute | solution.py:189
  8.9 2.3 %collective-permute-start.2 = (f32[64,1024]{1,0:T(8,128)S(1)}, f32[64,1024]{1,0:T(8,128)S(1)}, u32[]{:S(2)}, u32[]{:S(2)}) collective-permute-start(f32[64,1024]{1,0:T(8,128)S(1)} %get-tuple-element.19), channel_id=1, source_target_pairs={{0,8},{12,4},{1,9},{13,5},{2,10},{14,6},{3,11},{15,7},{16,24},{28,... | collective-permute-start | bytes 786440 | tf_op jit(solution)/shard_map/ppermute | solution.py:191
  11.2 0.7 %collective-permute-start.1 = (f32[64,1024]{1,0:T(8,128)S(1)}, f32[64,1024]{1,0:T(8,128)S(1)}, u32[]{:S(2)}, u32[]{:S(2)}) collective-permute-start(f32[64,1024]{1,0:T(8,128)S(1)} %get-tuple-element.19), channel_id=1, source_target_pairs={{4,8},{8,4},{5,9},{9,5},{6,10},{10,6},{7,11},{11,7},{20,24},{24,20... | collective-permute-start | bytes 786440 | tf_op jit(solution)/shard_map/ppermute | solution.py:183
  11.8 0.0 copy-done
  11.9 10.4 %project_out.1 = (f32[64,1024]{1,0:T(8,128)S(1)}, f32[64,1024]{1,0:T(8,128)S(1)}, bf16[8,64,128]{2,1,0:T(8,128)(2,1)S(1)}) custom-call(s32[1]{0:T(128)} %bitcast.1.side_ref, bf16[2,4,256,7168]{3,2,1,0:T(8,128)(2,1)} %rows_hbm.3, bf16[2,64,7168]{2,1,0:T(8,128)(2,1)S(1)} %copy-done, bf16[16,2,64,64]{3,2,1,0:T(8,128)(2,1)} %queries_hbm.1, ...), custom_call_target="tpu_custom_call" | custom-call | tf_op jit(solution)/shard_map/project_out/pallas_call | solution.py:161
  22.3 3.1 %collective-permute-start.3 = (f32[64,1024]{1,0:T(8,128)S(1)}, f32[64,1024]{1,0:T(8,128)S(1)}, u32[]{:S(2)}, u32[]{:S(2)}) collective-permute-start(f32[64,1024]{1,0:T(8,128)S(1)} %get-tuple-element.22.refs_0_), channel_id=1, source_target_pairs={{0,4},{12,8},{1,5},{13,9},{2,6},{14,10},{3,7},{15,11},{16,20},{28,... | collective-permute-start | bytes 786440 | tf_op jit(solution)/shard_map/ppermute | solution.py:189
  25.4 1.3 %collective-permute-start.5 = (f32[64,1024]{1,0:T(8,128)S(1)}, f32[64,1024]{1,0:T(8,128)S(1)}, u32[]{:S(2)}, u32[]{:S(2)}) collective-permute-start(f32[64,1024]{1,0:T(8,128)S(1)} %get-tuple-element.23), channel_id=1, source_target_pairs={{0,8},{12,4},{1,9},{13,5},{2,10},{14,6},{3,11},{15,7},{16,24},{28,... | collective-permute-start | bytes 786440 | tf_op jit(solution)/shard_map/ppermute | solution.py:191
  26.7 0.0 collective-permute-done.refs_1_
  26.7 0.7 %collective-permute-start.4 = (f32[64,1024]{1,0:T(8,128)S(1)}, f32[64,1024]{1,0:T(8,128)S(1)}, u32[]{:S(2)}, u32[]{:S(2)}) collective-permute-start(f32[64,1024]{1,0:T(8,128)S(1)} %get-tuple-element.23), channel_id=1, source_target_pairs={{4,8},{8,4},{5,9},{9,5},{6,10},{10,6},{7,11},{11,7},{20,24},{24,20... | collective-permute-start | bytes 786440 | tf_op jit(solution)/shard_map/ppermute | solution.py:183
  27.4 0.0 collective-permute-done.2.refs_3_
  27.4 0.0 collective-permute-done.1.refs_2_
  27.4 0.4 cov_in.1
  27.8 0.4 collective-permute-start.10
  28.2 1.2 %collective-permute-start.9 = (bf16[8,64,128]{2,1,0:T(8,128)(2,1)S(1)}, bf16[8,64,128]{2,1,0:T(8,128)(2,1)S(1)}, u32[]{:S(2)}, u32[]{:S(2)}) collective-permute-start(bf16[8,64,128]{2,1,0:T(8,128)(2,1)S(1)} %get-tuple-element.26.refs_0_), channel_id=1, source_target_pairs={{0,2},{1,3},{2,0},{3,1},{4,6},{5,7},{6,4},{7,5},{8,10},{9,11},{10,... | collective-permute-start | bytes 393224 | tf_op jit(solution)/shard_map/ppermute | solution.py:394
  29.4 2.6 %collective-permute-done.3.refs_1_ = f32[64,1024]{1,0:T(8,128)S(1)} collective-permute-done((f32[64,1024]{1,0:T(8,128)S(1)}, f32[64,1024]{1,0:T(8,128)S(1)}, u32[]{:S(2)}, u32[]{:S(2)}) %collective-permute-start.3) | collective-permute-done | bytes 262176 | tf_op jit(solution)/shard_map/ppermute | solution.py:189
  32.1 0.0 collective-permute-start.8
  32.1 4.2 %collective-permute-done.5.refs_3_ = f32[64,1024]{1,0:T(8,128)S(1)} collective-permute-done((f32[64,1024]{1,0:T(8,128)S(1)}, f32[64,1024]{1,0:T(8,128)S(1)}, u32[]{:S(2)}, u32[]{:S(2)}) %collective-permute-start.5) | collective-permute-done | bytes 262176 | tf_op jit(solution)/shard_map/ppermute | solution.py:191
  36.3 0.0 collective-permute-done.4.refs_2_
  36.3 1.0 %cov_out.1 = (f32[64,128]{1,0:T(8,128)S(1)}, f32[4,64,128]{2,1,0:T(8,128)S(1)}) custom-call(f32[64,1024]{1,0:T(8,128)S(1)} %get-tuple-element.20.x_ref, f32[64,128]{1,0:T(8,128)S(1)} %get-tuple-element.21.cov_ref, f32[64,1024]{1,0:T(8,128)S(1)} %get-tuple-element.22.refs_0_, f32[64,1024]{1,0:T(8,128)S(1)} %collective-permute-done.3.refs_1_, ...), custom_call_target="tpu_custom_call" | custom-call | tf_op jit(solution)/shard_map/cov_out/pallas_call | solution.py:251
  37.2 0.1 collective-permute-start.6
  37.3 1.2 %collective-permute-done.6 = f32[64,128]{1,0:T(8,128)S(1)} collective-permute-done((f32[64,128]{1,0:T(8,128)S(1)}, f32[64,128]{1,0:T(8,128)S(1)}, u32[]{:S(2)}, u32[]{:S(2)}) %collective-permute-start.6) | collective-permute-done | bytes 32800 | tf_op jit(solution)/shard_map/ppermute | solution.py:394
  38.5 1.5 %collective-permute-start.7 = (f32[64,128]{1,0:T(8,128)S(1)}, f32[64,128]{1,0:T(8,128)S(1)}, u32[]{:S(2)}, u32[]{:S(2)}) collective-permute-start(f32[64,128]{1,0:T(8,128)S(1)} %add.6.own_ref), channel_id=1, source_target_pairs={{0,2},{1,3},{2,0},{3,1},{4,6},{5,7},{6,4},{7,5},{8,10},{9,11},{10,... | collective-permute-start | bytes 98312 | tf_op jit(solution)/shard_map/ppermute | solution.py:394
  40.0 2.4 %collective-permute-done.7.other_ref = f32[64,128]{1,0:T(8,128)S(1)} collective-permute-done((f32[64,128]{1,0:T(8,128)S(1)}, f32[64,128]{1,0:T(8,128)S(1)}, u32[]{:S(2)}, u32[]{:S(2)}) %collective-permute-start.7) | collective-permute-done | bytes 32800 | tf_op jit(solution)/shard_map/ppermute | solution.py:394
  42.4 0.0 collective-permute-done.10.refs_3_
  42.4 0.0 collective-permute-done.9.refs_2_
  42.4 0.0 collective-permute-done.8.refs_1_
  42.4 4.4 %score.1 = f32[4,64]{1,0:T(4,128)S(1)} custom-call(s32[1]{0:T(128)} %bitcast.place_ref, f32[64,128]{1,0:T(8,128)S(1)} %add.6.own_ref, f32[64,128]{1,0:T(8,128)S(1)} %collective-permute-done.7.other_ref, f32[4,64,128]{2,1,0:T(8,128)S(1)} %get-tuple-element.25.sample_ref, bf16[8,64,128]{2,1,0:T(8,128)(2,1)S(1)} %get-tuple-element.26.refs_0_, ...), custom_call_target="tpu_custom_call" | custom-call | tf_op jit(solution)/shard_map/score/pallas_call | solution.py:379
  46.9 1.3 %collective-permute-start.12 = (f32[4,64]{1,0:T(4,128)S(1)}, f32[4,64]{1,0:T(4,128)S(1)}, u32[]{:S(2)}, u32[]{:S(2)}) collective-permute-start(f32[4,64]{1,0:T(4,128)S(1)} %score.1), channel_id=1, source_target_pairs={{8,0},{4,12},{9,1},{5,13},{10,2},{6,14},{11,3},{7,15},{24,16},{20,... | collective-permute-start | bytes 3080 | tf_op jit(solution)/shard_map/ppermute | solution.py:419
  48.2 1.3 %collective-permute-start.11 = (f32[4,64]{1,0:T(4,128)S(1)}, f32[4,64]{1,0:T(4,128)S(1)}, u32[]{:S(2)}, u32[]{:S(2)}) collective-permute-start(f32[4,64]{1,0:T(4,128)S(1)} %score.1), channel_id=1, source_target_pairs={{4,0},{8,12},{5,1},{9,13},{6,2},{10,14},{7,3},{11,15},{20,16},{24,... | collective-permute-start | bytes 3080 | tf_op jit(solution)/shard_map/ppermute | solution.py:418
  49.5 5.2 %collective-permute-done.12 = f32[4,64]{1,0:T(4,128)S(1)} collective-permute-done((f32[4,64]{1,0:T(4,128)S(1)}, f32[4,64]{1,0:T(4,128)S(1)}, u32[]{:S(2)}, u32[]{:S(2)}) %collective-permute-start.12) | collective-permute-done | bytes 1056 | tf_op jit(solution)/shard_map/ppermute | solution.py:419
  54.7 1.4 %collective-permute-done.11 = f32[4,64]{1,0:T(4,128)S(1)} collective-permute-done((f32[4,64]{1,0:T(4,128)S(1)}, f32[4,64]{1,0:T(4,128)S(1)}, u32[]{:S(2)}, u32[]{:S(2)}) %collective-permute-start.11) | collective-permute-done | bytes 1056 | tf_op jit(solution)/shard_map/ppermute | solution.py:418
  56.1 1.6 %collective-permute-start.13 = (f32[4,64]{1,0:T(4,128)S(1)}, f32[4,64]{1,0:T(4,128)S(1)}, u32[]{:S(2)}, u32[]{:S(2)}) collective-permute-start(f32[4,64]{1,0:T(4,128)S(1)} %add.7), channel_id=1, source_target_pairs={{0,4},{12,8},{1,5},{13,9},{2,6},{14,10},{3,7},{15,11},{16,20},{28,... | collective-permute-start | bytes 3080 | tf_op jit(solution)/shard_map/ppermute | solution.py:420
  57.8 1.3 %collective-permute-done.13 = f32[4,64]{1,0:T(4,128)S(1)} collective-permute-done((f32[4,64]{1,0:T(4,128)S(1)}, f32[4,64]{1,0:T(4,128)S(1)}, u32[]{:S(2)}, u32[]{:S(2)}) %collective-permute-start.13) | collective-permute-done | bytes 1056 | tf_op jit(solution)/shard_map/ppermute | solution.py:420
  59.0 0.6 broadcast_select_fusion
  (2 shorter events, 0.0 us)
Async XLA Ops:
  0.0 11.9 %copy-start = (bf16[2,64,7168]{2,1,0:T(8,128)(2,1)S(1)}, bf16[2,64,7168]{2,1,0:T(8,128)(2,1)}, u32[]{:S(2)}) copy-start(bf16[2,64,7168]{2,1,0:T(8,128)(2,1)} %proj_ref.1) | copy-start | bytes 5505028
  3.9 22.8 %collective-permute-start = (f32[64,1024]{1,0:T(8,128)S(1)}, f32[64,1024]{1,0:T(8,128)S(1)}, u32[]{:S(2)}, u32[]{:S(2)}) collective-permute-start(f32[64,1024]{1,0:T(8,128)S(1)} %get-tuple-element.18.refs_0_), channel_id=1, source_target_pairs={{0,4},{12,8},{1,5},{13,9},{2,6},{14,10},{3,7},{15,11},{16,20},{28,... | collective-permute-start | bytes 786440 | tf_op jit(solution)/shard_map/ppermute | solution.py:189
  8.9 18.5 %collective-permute-start.2 = (f32[64,1024]{1,0:T(8,128)S(1)}, f32[64,1024]{1,0:T(8,128)S(1)}, u32[]{:S(2)}, u32[]{:S(2)}) collective-permute-start(f32[64,1024]{1,0:T(8,128)S(1)} %get-tuple-element.19), channel_id=1, source_target_pairs={{0,8},{12,4},{1,9},{13,5},{2,10},{14,6},{3,11},{15,7},{16,24},{28,... | collective-permute-start | bytes 786440 | tf_op jit(solution)/shard_map/ppermute | solution.py:191
  11.2 16.2 %collective-permute-start.1 = (f32[64,1024]{1,0:T(8,128)S(1)}, f32[64,1024]{1,0:T(8,128)S(1)}, u32[]{:S(2)}, u32[]{:S(2)}) collective-permute-start(f32[64,1024]{1,0:T(8,128)S(1)} %get-tuple-element.19), channel_id=1, source_target_pairs={{4,8},{8,4},{5,9},{9,5},{6,10},{10,6},{7,11},{11,7},{20,24},{24,20... | collective-permute-start | bytes 786440 | tf_op jit(solution)/shard_map/ppermute | solution.py:183
  22.3 9.8 %collective-permute-start.3 = (f32[64,1024]{1,0:T(8,128)S(1)}, f32[64,1024]{1,0:T(8,128)S(1)}, u32[]{:S(2)}, u32[]{:S(2)}) collective-permute-start(f32[64,1024]{1,0:T(8,128)S(1)} %get-tuple-element.22.refs_0_), channel_id=1, source_target_pairs={{0,4},{12,8},{1,5},{13,9},{2,6},{14,10},{3,7},{15,11},{16,20},{28,... | collective-permute-start | bytes 786440 | tf_op jit(solution)/shard_map/ppermute | solution.py:189
  25.4 10.9 %collective-permute-start.5 = (f32[64,1024]{1,0:T(8,128)S(1)}, f32[64,1024]{1,0:T(8,128)S(1)}, u32[]{:S(2)}, u32[]{:S(2)}) collective-permute-start(f32[64,1024]{1,0:T(8,128)S(1)} %get-tuple-element.23), channel_id=1, source_target_pairs={{0,8},{12,4},{1,9},{13,5},{2,10},{14,6},{3,11},{15,7},{16,24},{28,... | collective-permute-start | bytes 786440 | tf_op jit(solution)/shard_map/ppermute | solution.py:191
  26.7 9.6 %collective-permute-start.4 = (f32[64,1024]{1,0:T(8,128)S(1)}, f32[64,1024]{1,0:T(8,128)S(1)}, u32[]{:S(2)}, u32[]{:S(2)}) collective-permute-start(f32[64,1024]{1,0:T(8,128)S(1)} %get-tuple-element.23), channel_id=1, source_target_pairs={{4,8},{8,4},{5,9},{9,5},{6,10},{10,6},{7,11},{11,7},{20,24},{24,20... | collective-permute-start | bytes 786440 | tf_op jit(solution)/shard_map/ppermute | solution.py:183
  27.8 14.6 %collective-permute-start.10 = (bf16[8,64,128]{2,1,0:T(8,128)(2,1)S(1)}, bf16[8,64,128]{2,1,0:T(8,128)(2,1)S(1)}, u32[]{:S(2)}, u32[]{:S(2)}) collective-permute-start(bf16[8,64,128]{2,1,0:T(8,128)(2,1)S(1)} %get-tuple-element.26.refs_0_), channel_id=1, source_target_pairs={{0,3},{1,2},{2,1},{3,0},{4,7},{5,6},{6,5},{7,4},{8,11},{9,10},{10,... | collective-permute-start | bytes 393224 | tf_op jit(solution)/shard_map/ppermute | solution.py:394
  28.2 14.2 %collective-permute-start.9 = (bf16[8,64,128]{2,1,0:T(8,128)(2,1)S(1)}, bf16[8,64,128]{2,1,0:T(8,128)(2,1)S(1)}, u32[]{:S(2)}, u32[]{:S(2)}) collective-permute-start(bf16[8,64,128]{2,1,0:T(8,128)(2,1)S(1)} %get-tuple-element.26.refs_0_), channel_id=1, source_target_pairs={{0,2},{1,3},{2,0},{3,1},{4,6},{5,7},{6,4},{7,5},{8,10},{9,11},{10,... | collective-permute-start | bytes 393224 | tf_op jit(solution)/shard_map/ppermute | solution.py:394
  32.1 10.4 %collective-permute-start.8 = (bf16[8,64,128]{2,1,0:T(8,128)(2,1)S(1)}, bf16[8,64,128]{2,1,0:T(8,128)(2,1)S(1)}, u32[]{:S(2)}, u32[]{:S(2)}) collective-permute-start(bf16[8,64,128]{2,1,0:T(8,128)(2,1)S(1)} %get-tuple-element.26.refs_0_), channel_id=1, source_target_pairs={{0,1},{1,0},{2,3},{3,2},{4,5},{5,4},{6,7},{7,6},{8,9},{9,8},{10,11... | collective-permute-start | bytes 393224 | tf_op jit(solution)/shard_map/ppermute | solution.py:394
  37.2 1.3 %collective-permute-start.6 = (f32[64,128]{1,0:T(8,128)S(1)}, f32[64,128]{1,0:T(8,128)S(1)}, u32[]{:S(2)}, u32[]{:S(2)}) collective-permute-start(f32[64,128]{1,0:T(8,128)S(1)} %get-tuple-element.24), channel_id=1, source_target_pairs={{0,1},{1,0},{2,3},{3,2},{4,5},{5,4},{6,7},{7,6},{8,9},{9,8},{10,11... | collective-permute-start | bytes 98312 | tf_op jit(solution)/shard_map/ppermute | solution.py:394
  38.5 3.9 %collective-permute-start.7 = (f32[64,128]{1,0:T(8,128)S(1)}, f32[64,128]{1,0:T(8,128)S(1)}, u32[]{:S(2)}, u32[]{:S(2)}) collective-permute-start(f32[64,128]{1,0:T(8,128)S(1)} %add.6.own_ref), channel_id=1, source_target_pairs={{0,2},{1,3},{2,0},{3,1},{4,6},{5,7},{6,4},{7,5},{8,10},{9,11},{10,... | collective-permute-start | bytes 98312 | tf_op jit(solution)/shard_map/ppermute | solution.py:394
  46.9 7.8 %collective-permute-start.12 = (f32[4,64]{1,0:T(4,128)S(1)}, f32[4,64]{1,0:T(4,128)S(1)}, u32[]{:S(2)}, u32[]{:S(2)}) collective-permute-start(f32[4,64]{1,0:T(4,128)S(1)} %score.1), channel_id=1, source_target_pairs={{8,0},{4,12},{9,1},{5,13},{10,2},{6,14},{11,3},{7,15},{24,16},{20,... | collective-permute-start | bytes 3080 | tf_op jit(solution)/shard_map/ppermute | solution.py:419
  48.2 7.9 %collective-permute-start.11 = (f32[4,64]{1,0:T(4,128)S(1)}, f32[4,64]{1,0:T(4,128)S(1)}, u32[]{:S(2)}, u32[]{:S(2)}) collective-permute-start(f32[4,64]{1,0:T(4,128)S(1)} %score.1), channel_id=1, source_target_pairs={{4,0},{8,12},{5,1},{9,13},{6,2},{10,14},{7,3},{11,15},{20,16},{24,... | collective-permute-start | bytes 3080 | tf_op jit(solution)/shard_map/ppermute | solution.py:418
  56.1 2.9 %collective-permute-start.13 = (f32[4,64]{1,0:T(4,128)S(1)}, f32[4,64]{1,0:T(4,128)S(1)}, u32[]{:S(2)}, u32[]{:S(2)}) collective-permute-start(f32[4,64]{1,0:T(4,128)S(1)} %add.7), channel_id=1, source_target_pairs={{0,4},{12,8},{1,5},{13,9},{2,6},{14,10},{3,7},{15,11},{16,20},{28,... | collective-permute-start | bytes 3080 | tf_op jit(solution)/shard_map/ppermute | solution.py:420

commit v12 on v11

--- a/solution.py
+++ b/solution.py
@@ -270,36 +270,49 @@
     return out
 
 
-def damped_inverses(matrices):
-    size = matrices[0].shape[0]
-    rows = lax.broadcasted_iota(jnp.int32, (size, size), 0)
-    cols = lax.broadcasted_iota(jnp.int32, (size, size), 1)
+def halves(value):
+    high = value.astype(jnp.bfloat16)
+    return high, (value - high.astype(jnp.float32)).astype(jnp.bfloat16)
+
+
+def stacked(value):
+    once = jnp.concatenate(halves(value), axis=1)
+    return jnp.concatenate([once, once], axis=0)
+
+
+def product(left, right):
+    lanes = right.shape[1]
+    both = nn(jnp.concatenate(halves(left), axis=1), stacked(right))
+    return both[:, :lanes] + both[:, lanes:]
+
+
+def damped_inverses(pair):
+    size, both = pair.shape
+    left = lax.broadcasted_iota(jnp.int32, pair.shape, 1) < size
+    whole = jnp.concatenate([jnp.where(left, pair, 0.0), jnp.where(left, 0.0, pair)], axis=0)
+    rows = lax.broadcasted_iota(jnp.int32, whole.shape, 0)
+    cols = lax.broadcasted_iota(jnp.int32, whole.shape, 1)
     diagonal = rows == cols
+    on_diagonal = jnp.where(diagonal, whole, 0.0)
+    unit = jnp.where(
+        rows < size, jnp.sum(on_diagonal[:size]) / size, jnp.sum(on_diagonal[size:]) / size
+    )
     eye = jnp.where(diagonal, 1.0, 0.0)
-    units = [jnp.sum(jnp.where(diagonal, matrix, 0.0)) / size for matrix in matrices]
-    damped = [matrix / unit + 0.1 * eye for matrix, unit in zip(matrices, units)]
+    matrix = whole / unit + 0.1 * eye
     low, high = 0.1, size + 0.1
     start = 2.0 / (low + high)
     steps = scales(7, high / low)
-    y = [matrix * start for matrix in damped]
-    x = [(2.0 * start * steps[0]) * eye - (start * steps[0]) * v for v in y]
-    y = [steps[0] * (2.0 * v - nn(v, v, HIGHEST)) for v in y]
+    y = matrix * start
+    x = (2.0 * start * steps[0]) * eye - (start * steps[0]) * y
+    y = steps[0] * (2.0 * y - product(y, y))
     for scale in steps[1:-1]:
-        both = [nn(jnp.concatenate(pair, axis=0), pair[1], HIGHEST) for pair in zip(x, y)]
-        x = [scale * (2.0 * u - product[:size]) for u, product in zip(x, both)]
-        y = [scale * (2.0 * v - product[size:]) for v, product in zip(y, both)]
-    x = [steps[-1] * (2.0 * u - nn(u, v, HIGHEST)) for u, v in zip(x, y)]
-    rest = [eye - nn(matrix, u, HIGHEST) for matrix, u in zip(damped, x)]
-    x = [u + nn(u, r, HIGHEST) for u, r in zip(x, rest)]
-    return [u / unit for u, unit in zip(x, units)]
-
-
-def split(value):
-    high = value.astype(jnp.bfloat16)
-    rest = value - high.astype(jnp.float32)
-    middle = rest.astype(jnp.bfloat16)
-    low = (rest - middle.astype(jnp.float32)).astype(jnp.bfloat16)
-    return high, middle, low
+        turn = product(jnp.concatenate([x, y], axis=0), y)
+        x = scale * (2.0 * x - turn[:both])
+        y = scale * (2.0 * y - turn[both:])
+    x = steps[-1] * (2.0 * x - product(x, y))
+    x = x + product(x, eye - product(matrix, x))
+    x = x + product(x, eye - nn(matrix, x, HIGHEST))
+    return x / unit
 
 
 def score_kernel(tokens, place_ref, own_ref, other_ref, sample_ref, *refs):
@@ -309,24 +322,18 @@
         held[place_ref[0] ^ k] = piece[...]
     pair = (own_ref[...] + other_ref[...]) / tokens
     size, both = pair.shape
-    left, right = damped_inverses([pair[:, :size], pair[:, size:]])
+    inverses = damped_inverses(pair)
     samples = [sample_ref[s] for s in range(sample_ref.shape[0])]
     seqs = len(samples)
     blocks = held.shape[1]
     pairs = parts * blocks
-    first = jnp.concatenate(split(left), axis=0)
+    first = jnp.concatenate(halves(inverses[:size, :size]), axis=0)
     none = jnp.zeros_like(first)
     first = jnp.concatenate(
         [jnp.concatenate([first, none], axis=1), jnp.concatenate([none, first], axis=1)], axis=0
     )
-    none = jnp.zeros_like(right)
-    twice = jnp.concatenate(
-        [jnp.concatenate([right, none], axis=1), jnp.concatenate([none, right], axis=1)], axis=0
-    )
-    high, middle, _ = split(twice)
-    once = jnp.concatenate([high, middle], axis=1)
-    second = jnp.concatenate([once, once], axis=0)
-
+    right = inverses[size:]
+    second = stacked(jnp.concatenate([pltpu.roll(right, size, 1), right], axis=0))
     for part in range(parts // 2):
         for block in range(0, blocks, 2):
             rows = jnp.concatenate(
@@ -340,9 +347,8 @@
             )
             result = nt(first, rows)
             for k in range(2):
-                three = result[3 * size * k : 3 * size * (k + 1)]
-                value = three[:size] + three[size : 2 * size] + three[2 * size :]
-                high, middle, _ = split(value)
+                two = result[both * k : both * (k + 1)]
+                high, middle = halves(two[:size] + two[size:])
                 pair = (2 * part + k) * blocks + block
                 lanes = slice(pair * both, (pair + 2) * both)
                 half[0, :, lanes] = high
@@ -415,10 +421,13 @@
         other = swap(cov, "dp", bit)
         bit *= 2
     scores = score(place, cov, other, sample, query_pieces, tokens)
-    outer = lax.ppermute(scores, "tensor", [(1, 0), (2, 3)])
-    outer = outer + lax.ppermute(scores, "tensor", [(2, 0), (1, 3)])
-    back = lax.ppermute(outer, "tensor", [(0, 1), (3, 2)])
-    return jnp.where((column == 1) | (column == 2), back, outer)
+    owner = (column == 1) | (column == 2)
+    pieces = [
+        across(scores),
+        lax.ppermute(scores, "tensor", [(1, 0), (2, 3)]),
+        lax.ppermute(scores, "tensor", [(2, 0), (1, 3)]),
+    ]
+    return jnp.where(owner, scores, 0.0) + pieces[0] + pieces[1] + pieces[2]
 
 
 def damp(matrix):

time: 59.9 us -> 57.2 us (0.955)
  the two profiles are of different devices: /device:TPU:0 before, /device:TPU:12 now
where the time goes in v12:
time: 57.2 us; the launch traced here: 56.9 us
  Pallas kernels  19.4 us (34%)
  starting transfers between devices  19.2 us (34%)
  waiting for transfers between devices  17.6 us (31%)
  other arithmetic  0.59 us (1%)
    pallas_call x1, Pallas kernels, project_out(): pl.pallas_call(project_out_kernel, in_specs=[smem(), hbm(), vmem(), hbm()...  10.4 us
    ppermute x3, starting transfers between devices, across(): return lax.ppermute(value, 'tensor', [(1, 2), (2, 1)])  8.2 us
    ppermute x3, waiting for transfers between devices, across(): return lax.ppermute(value, 'tensor', [(1, 2), (2, 1)])  5.7 us
    ppermute x2, waiting for transfers between devices, to_owner(): lax.ppermute(far, 'tensor', [(0, 2), (3, 1)])  4.15 us
    ppermute x2, waiting for transfers between devices, to_owner(): lax.ppermute(near, 'tensor', [(0, 1), (3, 2)])  4.08 us
    pallas_call x1, Pallas kernels, project_in(): pl.pallas_call(project_in_kernel, in_specs=[smem(), hbm(), hbm(), hbm()],...  3.89 us
    pallas_call x1, Pallas kernels, score(): pl.pallas_call(functools.partial(score_kernel, tokens), in_specs=[smem()]...  3.74 us
    ppermute x5, waiting for transfers between devices, swap(): lax.ppermute(value, axis, [(i, i ^ bit) for i in range(lax.axis_size(axis...  3.63 us
  transfers between devices with their start and end apart: 14, of which 6 were waited for; matrix products, arithmetic and copies ran while one was open for 0% of the time, Pallas kernels for 21%

profile of v12, /device:TPU:12, one launch (start us, length us, event | category | flops | bytes accessed | tf_op | source)
XLA Modules:
  0.0 56.9 jit_solution(13347515286881664995)
XLA Ops:
  0.0 0.0 copy-start
  0.0 3.9 %project_in.1 = (f32[64,1024]{1,0:T(8,128)S(1)}, f32[64,1024]{1,0:T(8,128)S(1)}, bf16[2,256,3584]{2,1,0:T(8,128)(2,1)S(1)}) custom-call(s32[1]{0:T(128)} %bitcast.1.side_ref, bf16[4,256,2048]{2,1,0:T(8,128)(2,1)} %rows_hbm.2, bf16[2,64,2048]{2,1,0:T(8,128)(2,1)} %proj_hbm.1, bf16[2,4,256,7168]{3,2,1,0:T(8,128)(2,1)} %rows_hbm.3), custom_call_target="tpu_custom_call" | custom-call | tf_op jit(solution)/shard_map/project_in/pallas_call | solution.py:91
  3.9 1.3 %collective-permute-start = (f32[64,1024]{1,0:T(8,128)S(1)}, f32[64,1024]{1,0:T(8,128)S(1)}, u32[]{:S(2)}, u32[]{:S(2)}) collective-permute-start(f32[64,1024]{1,0:T(8,128)S(1)} %get-tuple-element.18.refs_0_), channel_id=1, source_target_pairs={{0,4},{12,8},{1,5},{13,9},{2,6},{14,10},{3,7},{15,11},{16,20},{28,... | collective-permute-start | bytes 786440 | tf_op jit(solution)/shard_map/ppermute | solution.py:189
  5.2 1.3 %collective-permute-start.2 = (f32[64,1024]{1,0:T(8,128)S(1)}, f32[64,1024]{1,0:T(8,128)S(1)}, u32[]{:S(2)}, u32[]{:S(2)}) collective-permute-start(f32[64,1024]{1,0:T(8,128)S(1)} %get-tuple-element.19), channel_id=1, source_target_pairs={{0,8},{12,4},{1,9},{13,5},{2,10},{14,6},{3,11},{15,7},{16,24},{28,... | collective-permute-start | bytes 786440 | tf_op jit(solution)/shard_map/ppermute | solution.py:191
  6.5 3.5 %collective-permute-start.1 = (f32[64,1024]{1,0:T(8,128)S(1)}, f32[64,1024]{1,0:T(8,128)S(1)}, u32[]{:S(2)}, u32[]{:S(2)}) collective-permute-start(f32[64,1024]{1,0:T(8,128)S(1)} %get-tuple-element.19), channel_id=1, source_target_pairs={{4,8},{8,4},{5,9},{9,5},{6,10},{10,6},{7,11},{11,7},{20,24},{24,20... | collective-permute-start | bytes 786440 | tf_op jit(solution)/shard_map/ppermute | solution.py:183
  10.0 0.0 copy-done
  10.0 10.4 %project_out.1 = (f32[64,1024]{1,0:T(8,128)S(1)}, f32[64,1024]{1,0:T(8,128)S(1)}, bf16[8,64,128]{2,1,0:T(8,128)(2,1)S(1)}) custom-call(s32[1]{0:T(128)} %bitcast.1.side_ref, bf16[2,4,256,7168]{3,2,1,0:T(8,128)(2,1)} %rows_hbm.3, bf16[2,64,7168]{2,1,0:T(8,128)(2,1)S(1)} %copy-done, bf16[16,2,64,64]{3,2,1,0:T(8,128)(2,1)} %queries_hbm.1, ...), custom_call_target="tpu_custom_call" | custom-call | tf_op jit(solution)/shard_map/project_out/pallas_call | solution.py:161
  20.4 1.3 %collective-permute-start.3 = (f32[64,1024]{1,0:T(8,128)S(1)}, f32[64,1024]{1,0:T(8,128)S(1)}, u32[]{:S(2)}, u32[]{:S(2)}) collective-permute-start(f32[64,1024]{1,0:T(8,128)S(1)} %get-tuple-element.22.refs_0_), channel_id=1, source_target_pairs={{0,4},{12,8},{1,5},{13,9},{2,6},{14,10},{3,7},{15,11},{16,20},{28,... | collective-permute-start | bytes 786440 | tf_op jit(solution)/shard_map/ppermute | solution.py:189
  21.7 1.3 %collective-permute-start.5 = (f32[64,1024]{1,0:T(8,128)S(1)}, f32[64,1024]{1,0:T(8,128)S(1)}, u32[]{:S(2)}, u32[]{:S(2)}) collective-permute-start(f32[64,1024]{1,0:T(8,128)S(1)} %get-tuple-element.23), channel_id=1, source_target_pairs={{0,8},{12,4},{1,9},{13,5},{2,10},{14,6},{3,11},{15,7},{16,24},{28,... | collective-permute-start | bytes 786440 | tf_op jit(solution)/shard_map/ppermute | solution.py:191
  23.0 0.0 collective-permute-done.refs_1_
  23.0 2.4 %collective-permute-start.4 = (f32[64,1024]{1,0:T(8,128)S(1)}, f32[64,1024]{1,0:T(8,128)S(1)}, u32[]{:S(2)}, u32[]{:S(2)}) collective-permute-start(f32[64,1024]{1,0:T(8,128)S(1)} %get-tuple-element.23), channel_id=1, source_target_pairs={{4,8},{8,4},{5,9},{9,5},{6,10},{10,6},{7,11},{11,7},{20,24},{24,20... | collective-permute-start | bytes 786440 | tf_op jit(solution)/shard_map/ppermute | solution.py:183
  25.4 0.0 collective-permute-done.2.refs_3_
  25.4 0.0 collective-permute-done.1.refs_2_
  25.4 0.4 cov_in.1
  25.8 0.4 collective-permute-start.10
  26.3 1.2 %collective-permute-start.9 = (bf16[8,64,128]{2,1,0:T(8,128)(2,1)S(1)}, bf16[8,64,128]{2,1,0:T(8,128)(2,1)S(1)}, u32[]{:S(2)}, u32[]{:S(2)}) collective-permute-start(bf16[8,64,128]{2,1,0:T(8,128)(2,1)S(1)} %get-tuple-element.26.refs_0_), channel_id=1, source_target_pairs={{0,2},{1,3},{2,0},{3,1},{4,6},{5,7},{6,4},{7,5},{8,10},{9,11},{10,... | collective-permute-start | bytes 393224 | tf_op jit(solution)/shard_map/ppermute | solution.py:400
  27.5 4.1 %collective-permute-done.3.refs_1_ = f32[64,1024]{1,0:T(8,128)S(1)} collective-permute-done((f32[64,1024]{1,0:T(8,128)S(1)}, f32[64,1024]{1,0:T(8,128)S(1)}, u32[]{:S(2)}, u32[]{:S(2)}) %collective-permute-start.3) | collective-permute-done | bytes 262176 | tf_op jit(solution)/shard_map/ppermute | solution.py:189
  31.5 0.0 collective-permute-start.8
  31.5 4.1 %collective-permute-done.5.refs_3_ = f32[64,1024]{1,0:T(8,128)S(1)} collective-permute-done((f32[64,1024]{1,0:T(8,128)S(1)}, f32[64,1024]{1,0:T(8,128)S(1)}, u32[]{:S(2)}, u32[]{:S(2)}) %collective-permute-start.5) | collective-permute-done | bytes 262176 | tf_op jit(solution)/shard_map/ppermute | solution.py:191
  35.7 2.6 %collective-permute-done.4.refs_2_ = f32[64,1024]{1,0:T(8,128)S(1)} collective-permute-done((f32[64,1024]{1,0:T(8,128)S(1)}, f32[64,1024]{1,0:T(8,128)S(1)}, u32[]{:S(2)}, u32[]{:S(2)}) %collective-permute-start.4) | collective-permute-done | bytes 262176 | tf_op jit(solution)/shard_map/ppermute | solution.py:183
  38.3 1.0 %cov_out.1 = (f32[64,128]{1,0:T(8,128)S(1)}, f32[4,64,128]{2,1,0:T(8,128)S(1)}) custom-call(f32[64,1024]{1,0:T(8,128)S(1)} %get-tuple-element.20.x_ref, f32[64,128]{1,0:T(8,128)S(1)} %get-tuple-element.21.cov_ref, f32[64,1024]{1,0:T(8,128)S(1)} %get-tuple-element.22.refs_0_, f32[64,1024]{1,0:T(8,128)S(1)} %collective-permute-done.3.refs_1_, ...), custom_call_target="tpu_custom_call" | custom-call | tf_op jit(solution)/shard_map/cov_out/pallas_call | solution.py:251
  39.3 0.1 collective-permute-start.6
  39.3 1.2 %collective-permute-done.6 = f32[64,128]{1,0:T(8,128)S(1)} collective-permute-done((f32[64,128]{1,0:T(8,128)S(1)}, f32[64,128]{1,0:T(8,128)S(1)}, u32[]{:S(2)}, u32[]{:S(2)}) %collective-permute-start.6) | collective-permute-done | bytes 32800 | tf_op jit(solution)/shard_map/ppermute | solution.py:400
  40.5 1.5 %collective-permute-start.7 = (f32[64,128]{1,0:T(8,128)S(1)}, f32[64,128]{1,0:T(8,128)S(1)}, u32[]{:S(2)}, u32[]{:S(2)}) collective-permute-start(f32[64,128]{1,0:T(8,128)S(1)} %add.12.own_ref), channel_id=1, source_target_pairs={{0,2},{1,3},{2,0},{3,1},{4,6},{5,7},{6,4},{7,5},{8,10},{9,11},{10,... | collective-permute-start | bytes 98312 | tf_op jit(solution)/shard_map/ppermute | solution.py:400
  42.0 2.4 %collective-permute-done.7.other_ref = f32[64,128]{1,0:T(8,128)S(1)} collective-permute-done((f32[64,128]{1,0:T(8,128)S(1)}, f32[64,128]{1,0:T(8,128)S(1)}, u32[]{:S(2)}, u32[]{:S(2)}) %collective-permute-start.7) | collective-permute-done | bytes 32800 | tf_op jit(solution)/shard_map/ppermute | solution.py:400
  44.5 0.0 collective-permute-done.10.refs_3_
  44.5 0.0 collective-permute-done.9.refs_2_
  44.5 0.0 collective-permute-done.8.refs_1_
  44.5 3.7 %score.1 = f32[4,64]{1,0:T(4,128)S(1)} custom-call(s32[1]{0:T(128)} %bitcast.place_ref, f32[64,128]{1,0:T(8,128)S(1)} %add.12.own_ref, f32[64,128]{1,0:T(8,128)S(1)} %collective-permute-done.7.other_ref, f32[4,64,128]{2,1,0:T(8,128)S(1)} %get-tuple-element.25.sample_ref, bf16[8,64,128]{2,1,0:T(8,128)(2,1)S(1)} %get-tuple-element.26.refs_0_, ...), custom_call_target="tpu_custom_call" | custom-call | tf_op jit(solution)/shard_map/score/pallas_call | solution.py:385
  48.2 1.3 %collective-permute-start.13 = (f32[4,64]{1,0:T(4,128)S(1)}, f32[4,64]{1,0:T(4,128)S(1)}, u32[]{:S(2)}, u32[]{:S(2)}) collective-permute-start(f32[4,64]{1,0:T(4,128)S(1)} %score.1), channel_id=1, source_target_pairs={{8,0},{4,12},{9,1},{5,13},{10,2},{6,14},{11,3},{7,15},{24,16},{20,... | collective-permute-start | bytes 3080 | tf_op jit(solution)/shard_map/ppermute | solution.py:428
  49.5 1.3 %collective-permute-start.12 = (f32[4,64]{1,0:T(4,128)S(1)}, f32[4,64]{1,0:T(4,128)S(1)}, u32[]{:S(2)}, u32[]{:S(2)}) collective-permute-start(f32[4,64]{1,0:T(4,128)S(1)} %score.1), channel_id=1, source_target_pairs={{4,0},{8,12},{5,1},{9,13},{6,2},{10,14},{7,3},{11,15},{20,16},{24,... | collective-permute-start | bytes 3080 | tf_op jit(solution)/shard_map/ppermute | solution.py:427
  50.8 2.4 %collective-permute-start.11 = (f32[4,64]{1,0:T(4,128)S(1)}, f32[4,64]{1,0:T(4,128)S(1)}, u32[]{:S(2)}, u32[]{:S(2)}) collective-permute-start(f32[4,64]{1,0:T(4,128)S(1)} %score.1), channel_id=1, source_target_pairs={{4,8},{8,4},{5,9},{9,5},{6,10},{10,6},{7,11},{11,7},{20,24},{24,20... | collective-permute-start | bytes 3080 | tf_op jit(solution)/shard_map/ppermute | solution.py:183
  53.2 0.0 collective-permute-done.13
  53.2 0.0 collective-permute-done.12
  53.2 3.1 %collective-permute-done.11 = f32[4,64]{1,0:T(4,128)S(1)} collective-permute-done((f32[4,64]{1,0:T(4,128)S(1)}, f32[4,64]{1,0:T(4,128)S(1)}, u32[]{:S(2)}, u32[]{:S(2)}) %collective-permute-start.11) | collective-permute-done | bytes 1056 | tf_op jit(solution)/shard_map/ppermute | solution.py:183
  56.3 0.6 %add_add_fusion = f32[4,64]{1,0:T(4,128)} fusion(f32[4,64]{1,0:T(4,128)S(1)} %collective-permute-done.13, f32[4,64]{1,0:T(4,128)S(1)} %collective-permute-done.12, f32[4,64]{1,0:T(4,128)S(1)} %collective-permute-done.11, f32[4,64]{1,0:T(4,128)S(1)} %score.1, pred[]{:T(512)S(6)} %or.3), kind=kLoop, calls=%fused_computation | loop fusion | flops 1024 | bytes 5121 | tf_op jit(solution)/shard_map/add | solution.py:430
  (1 shorter events, 0.0 us)
Async XLA Ops:
  0.0 10.0 %copy-start = (bf16[2,64,7168]{2,1,0:T(8,128)(2,1)S(1)}, bf16[2,64,7168]{2,1,0:T(8,128)(2,1)}, u32[]{:S(2)}) copy-start(bf16[2,64,7168]{2,1,0:T(8,128)(2,1)} %proj_ref.1) | copy-start | bytes 5505028
  3.9 19.1 %collective-permute-start = (f32[64,1024]{1,0:T(8,128)S(1)}, f32[64,1024]{1,0:T(8,128)S(1)}, u32[]{:S(2)}, u32[]{:S(2)}) collective-permute-start(f32[64,1024]{1,0:T(8,128)S(1)} %get-tuple-element.18.refs_0_), channel_id=1, source_target_pairs={{0,4},{12,8},{1,5},{13,9},{2,6},{14,10},{3,7},{15,11},{16,20},{28,... | collective-permute-start | bytes 786440 | tf_op jit(solution)/shard_map/ppermute | solution.py:189
  5.2 20.2 %collective-permute-start.2 = (f32[64,1024]{1,0:T(8,128)S(1)}, f32[64,1024]{1,0:T(8,128)S(1)}, u32[]{:S(2)}, u32[]{:S(2)}) collective-permute-start(f32[64,1024]{1,0:T(8,128)S(1)} %get-tuple-element.19), channel_id=1, source_target_pairs={{0,8},{12,4},{1,9},{13,5},{2,10},{14,6},{3,11},{15,7},{16,24},{28,... | collective-permute-start | bytes 786440 | tf_op jit(solution)/shard_map/ppermute | solution.py:191
  6.5 18.9 %collective-permute-start.1 = (f32[64,1024]{1,0:T(8,128)S(1)}, f32[64,1024]{1,0:T(8,128)S(1)}, u32[]{:S(2)}, u32[]{:S(2)}) collective-permute-start(f32[64,1024]{1,0:T(8,128)S(1)} %get-tuple-element.19), channel_id=1, source_target_pairs={{4,8},{8,4},{5,9},{9,5},{6,10},{10,6},{7,11},{11,7},{20,24},{24,20... | collective-permute-start | bytes 786440 | tf_op jit(solution)/shard_map/ppermute | solution.py:183
  20.4 11.1 %collective-permute-start.3 = (f32[64,1024]{1,0:T(8,128)S(1)}, f32[64,1024]{1,0:T(8,128)S(1)}, u32[]{:S(2)}, u32[]{:S(2)}) collective-permute-start(f32[64,1024]{1,0:T(8,128)S(1)} %get-tuple-element.22.refs_0_), channel_id=1, source_target_pairs={{0,4},{12,8},{1,5},{13,9},{2,6},{14,10},{3,7},{15,11},{16,20},{28,... | collective-permute-start | bytes 786440 | tf_op jit(solution)/shard_map/ppermute | solution.py:189
  21.7 14.0 %collective-permute-start.5 = (f32[64,1024]{1,0:T(8,128)S(1)}, f32[64,1024]{1,0:T(8,128)S(1)}, u32[]{:S(2)}, u32[]{:S(2)}) collective-permute-start(f32[64,1024]{1,0:T(8,128)S(1)} %get-tuple-element.23), channel_id=1, source_target_pairs={{0,8},{12,4},{1,9},{13,5},{2,10},{14,6},{3,11},{15,7},{16,24},{28,... | collective-permute-start | bytes 786440 | tf_op jit(solution)/shard_map/ppermute | solution.py:191
  23.0 15.3 %collective-permute-start.4 = (f32[64,1024]{1,0:T(8,128)S(1)}, f32[64,1024]{1,0:T(8,128)S(1)}, u32[]{:S(2)}, u32[]{:S(2)}) collective-permute-start(f32[64,1024]{1,0:T(8,128)S(1)} %get-tuple-element.23), channel_id=1, source_target_pairs={{4,8},{8,4},{5,9},{9,5},{6,10},{10,6},{7,11},{11,7},{20,24},{24,20... | collective-permute-start | bytes 786440 | tf_op jit(solution)/shard_map/ppermute | solution.py:183
  25.8 18.6 %collective-permute-start.10 = (bf16[8,64,128]{2,1,0:T(8,128)(2,1)S(1)}, bf16[8,64,128]{2,1,0:T(8,128)(2,1)S(1)}, u32[]{:S(2)}, u32[]{:S(2)}) collective-permute-start(bf16[8,64,128]{2,1,0:T(8,128)(2,1)S(1)} %get-tuple-element.26.refs_0_), channel_id=1, source_target_pairs={{0,3},{1,2},{2,1},{3,0},{4,7},{5,6},{6,5},{7,4},{8,11},{9,10},{10,... | collective-permute-start | bytes 393224 | tf_op jit(solution)/shard_map/ppermute | solution.py:400
  26.3 18.2 %collective-permute-start.9 = (bf16[8,64,128]{2,1,0:T(8,128)(2,1)S(1)}, bf16[8,64,128]{2,1,0:T(8,128)(2,1)S(1)}, u32[]{:S(2)}, u32[]{:S(2)}) collective-permute-start(bf16[8,64,128]{2,1,0:T(8,128)(2,1)S(1)} %get-tuple-element.26.refs_0_), channel_id=1, source_target_pairs={{0,2},{1,3},{2,0},{3,1},{4,6},{5,7},{6,4},{7,5},{8,10},{9,11},{10,... | collective-permute-start | bytes 393224 | tf_op jit(solution)/shard_map/ppermute | solution.py:400
  31.5 12.9 %collective-permute-start.8 = (bf16[8,64,128]{2,1,0:T(8,128)(2,1)S(1)}, bf16[8,64,128]{2,1,0:T(8,128)(2,1)S(1)}, u32[]{:S(2)}, u32[]{:S(2)}) collective-permute-start(bf16[8,64,128]{2,1,0:T(8,128)(2,1)S(1)} %get-tuple-element.26.refs_0_), channel_id=1, source_target_pairs={{0,1},{1,0},{2,3},{3,2},{4,5},{5,4},{6,7},{7,6},{8,9},{9,8},{10,11... | collective-permute-start | bytes 393224 | tf_op jit(solution)/shard_map/ppermute | solution.py:400
  39.3 1.3 %collective-permute-start.6 = (f32[64,128]{1,0:T(8,128)S(1)}, f32[64,128]{1,0:T(8,128)S(1)}, u32[]{:S(2)}, u32[]{:S(2)}) collective-permute-start(f32[64,128]{1,0:T(8,128)S(1)} %get-tuple-element.24), channel_id=1, source_target_pairs={{0,1},{1,0},{2,3},{3,2},{4,5},{5,4},{6,7},{7,6},{8,9},{9,8},{10,11... | collective-permute-start | bytes 98312 | tf_op jit(solution)/shard_map/ppermute | solution.py:400
  40.5 3.9 %collective-permute-start.7 = (f32[64,128]{1,0:T(8,128)S(1)}, f32[64,128]{1,0:T(8,128)S(1)}, u32[]{:S(2)}, u32[]{:S(2)}) collective-permute-start(f32[64,128]{1,0:T(8,128)S(1)} %add.12.own_ref), channel_id=1, source_target_pairs={{0,2},{1,3},{2,0},{3,1},{4,6},{5,7},{6,4},{7,5},{8,10},{9,11},{10,... | collective-permute-start | bytes 98312 | tf_op jit(solution)/shard_map/ppermute | solution.py:400
  48.2 5.0 %collective-permute-start.13 = (f32[4,64]{1,0:T(4,128)S(1)}, f32[4,64]{1,0:T(4,128)S(1)}, u32[]{:S(2)}, u32[]{:S(2)}) collective-permute-start(f32[4,64]{1,0:T(4,128)S(1)} %score.1), channel_id=1, source_target_pairs={{8,0},{4,12},{9,1},{5,13},{10,2},{6,14},{11,3},{7,15},{24,16},{20,... | collective-permute-start | bytes 3080 | tf_op jit(solution)/shard_map/ppermute | solution.py:428
  49.5 3.7 %collective-permute-start.12 = (f32[4,64]{1,0:T(4,128)S(1)}, f32[4,64]{1,0:T(4,128)S(1)}, u32[]{:S(2)}, u32[]{:S(2)}) collective-permute-start(f32[4,64]{1,0:T(4,128)S(1)} %score.1), channel_id=1, source_target_pairs={{4,0},{8,12},{5,1},{9,13},{6,2},{10,14},{7,3},{11,15},{20,16},{24,... | collective-permute-start | bytes 3080 | tf_op jit(solution)/shard_map/ppermute | solution.py:427
  50.8 5.5 %collective-permute-start.11 = (f32[4,64]{1,0:T(4,128)S(1)}, f32[4,64]{1,0:T(4,128)S(1)}, u32[]{:S(2)}, u32[]{:S(2)}) collective-permute-start(f32[4,64]{1,0:T(4,128)S(1)} %score.1), channel_id=1, source_target_pairs={{4,8},{8,4},{5,9},{9,5},{6,10},{10,6},{7,11},{11,7},{20,24},{24,20... | collective-permute-start | bytes 3080 | tf_op jit(solution)/shard_map/ppermute | solution.py:183

commit v13 on v12

--- a/solution.py
+++ b/solution.py
@@ -48,7 +48,7 @@
 
 
 def project_in_kernel(
-    side_ref, rows_hbm, proj_hbm, grads_hbm, near, far, early, rows, proj, acc, sems, proj_sem, early_sem
+    parity_ref, rows_hbm, proj_hbm, grads_hbm, first, second, early, rows, proj, acc, sems, proj_sem, early_sem
 ):
     seqs, length, width = rows.shape
     rank = proj.shape[1]
@@ -79,12 +79,12 @@
             acc[0, :, tokens] = part[:rank]
             acc[1, :, tokens] = part[rank:]
 
-    far[...] = acc[1 - side_ref[0]]
-    near[...] = acc[side_ref[0]]
+    first[...] = acc[parity_ref[0]]
+    second[...] = acc[1 - parity_ref[0]]
     early_copy.wait()
 
 
-def project_in(side, rows, proj, grads):
+def project_in(parity, rows, proj, grads):
     seqs, length, _ = rows.shape
     early = (2, length, grads.shape[3] // 2)
     rank = proj.shape[1]
@@ -107,11 +107,11 @@
         ],
         compiler_params=params(16),
         name="project_in",
-    )(side, in_hbm(rows), in_hbm(proj), in_hbm(grads))
-
-
-def project_out_kernel(side_ref, rows_hbm, proj_ref, queries_hbm, early, *refs):
-    (near, far, packed), (rows, held, acc, sems, sem) = refs[:3], refs[3:]
+    )(parity, in_hbm(rows), in_hbm(proj), in_hbm(grads))
+
+
+def project_out_kernel(parity_ref, side_ref, rows_hbm, proj_ref, queries_hbm, early, *refs):
+    (first, second, packed), (rows, held, acc, sems, sem) = refs[:3], refs[3:]
     _, seqs, length, width = rows.shape
     parts = sems.shape[2]
     piece = width // parts
@@ -144,8 +144,8 @@
                 if part > 0:
                     value = value + acc[layer, :, tokens]
                 acc[layer, :, tokens] = value
-    far[...] = acc[1 - side_ref[0]]
-    near[...] = acc[side_ref[0]]
+    first[...] = acc[parity_ref[0]]
+    second[...] = acc[1 - parity_ref[0]]
     copy.wait()
     blocks = held.shape[0] // 2
     for k in range(blocks):
@@ -153,14 +153,14 @@
         packed[k] = jnp.concatenate(pair, axis=1).astype(held.dtype)
 
 
-def project_out(side, rows, proj, queries, early):
+def project_out(parity, side, rows, proj, queries, early):
     _, seqs, length, width = rows.shape
     rank = proj.shape[1]
     count = queries.shape[0]
     parts = 4 if width % 512 == 0 else 2
     return pl.pallas_call(
         project_out_kernel,
-        in_specs=[smem(), hbm(), vmem(), hbm(), vmem()],
+        in_specs=[smem(), smem(), hbm(), vmem(), hbm(), vmem()],
         out_specs=[vmem()] * 3,
         out_shape=[
             jax.ShapeDtypeStruct((rank, seqs * length), jnp.float32),
@@ -176,19 +176,15 @@
         ],
         compiler_params=params(40),
         name="project_out",
-    )(side, in_hbm(rows), proj, in_hbm(queries), early)
-
-
-def across(value):
-    return lax.ppermute(value, "tensor", [(1, 2), (2, 1)])
-
-
-def to_owner(near, far):
+    )(parity, side, in_hbm(rows), proj, in_hbm(queries), early)
+
+
+def to_owner(first, second):
     return [
-        near,
-        lax.ppermute(near, "tensor", [(0, 1), (3, 2)]),
-        across(far),
-        lax.ppermute(far, "tensor", [(0, 2), (3, 1)]),
+        second,
+        lax.ppermute(first, "tensor", [(3, 2), (2, 1)]),
+        lax.ppermute(first, "tensor", [(0, 1), (1, 2)]),
+        lax.ppermute(second, "tensor", [(0, 2), (3, 1)]),
     ]
 
 
@@ -407,10 +403,11 @@
     column = lax.axis_index("tensor").astype(jnp.int32)
     side = (column >= 2).astype(jnp.int32).reshape(1)
     place = lax.axis_index("dp").astype(jnp.int32).reshape(1)
-    x_near, x_far, early = project_in(side, acts, proj_in, grads)
-    x_pieces = to_owner(x_near, x_far)
-    near, far, packed = project_out(side, grads, proj_out, queries, early)
-    pieces = to_owner(near, far)
+    parity = (column & 1).reshape(1)
+    x_first, x_second, early = project_in(parity, acts, proj_in, grads)
+    x_pieces = to_owner(x_first, x_second)
+    first, second, packed = project_out(parity, side, grads, proj_out, queries, early)
+    pieces = to_owner(first, second)
     packed, x, cov = cov_in(packed, x_pieces)
     query_pieces = [packed] + [swap(packed, "dp", bits) for bits in range(1, parts)]
     cov, sample = cov_out(x, cov, pieces, seqs)
@@ -423,9 +420,9 @@
     scores = score(place, cov, other, sample, query_pieces, tokens)
     owner = (column == 1) | (column == 2)
     pieces = [
-        across(scores),
-        lax.ppermute(scores, "tensor", [(1, 0), (2, 3)]),
-        lax.ppermute(scores, "tensor", [(2, 0), (1, 3)]),
+        lax.ppermute(scores, "tensor", [(2, 1), (1, 0)]),
+        lax.ppermute(scores, "tensor", [(1, 2), (2, 3)]),
+        lax.ppermute(scores, "tensor", [(1, 3), (2, 0)]),
     ]
     return jnp.where(owner, scores, 0.0) + pieces[0] + pieces[1] + pieces[2]
 

time: 57.2 us -> 63.4 us (1.11)
  the two profiles are of different devices: /device:TPU:12 before, /device:TPU:0 now
where the time goes in v13:
time: 63.4 us; the launch traced here: 63.1 us
  starting transfers between devices  21.5 us (34%)
  Pallas kernels  19.4 us (31%)
  waiting for transfers between devices  17.7 us (28%)
  local copies, waits for them, and re-layouts  3.8 us (6%)
    ppermute x2, starting transfers between devices, to_owner(): lax.ppermute(second, 'tensor', [(0, 2), (3, 1)])  11.1 us
    pallas_call x1, Pallas kernels, project_out(): pl.pallas_call(project_out_kernel, in_specs=[smem(), smem(), hbm(), vmem(...  10.3 us
    ppermute x1, waiting for transfers between devices, local_owned(): lax.ppermute(scores, 'tensor', [(2, 1), (1, 0)])  4.4 us
    pallas_call x1, Pallas kernels, project_in(): pl.pallas_call(project_in_kernel, in_specs=[smem(), hbm(), hbm(), hbm()],...  3.89 us
    ppermute x2, waiting for transfers between devices, to_owner(): lax.ppermute(first, 'tensor', [(0, 1), (1, 2)])  3.86 us
    unnamed x6, local copies, waits for them, and re-layouts  3.8 us
    pallas_call x1, Pallas kernels, score(): pl.pallas_call(functools.partial(score_kernel, tokens), in_specs=[smem()]...  3.75 us
    ppermute x5, waiting for transfers between devices, swap(): lax.ppermute(value, axis, [(i, i ^ bit) for i in range(lax.axis_size(axis...  3.62 us
  transfers between devices with their start and end apart: 14, of which 6 were waited for; matrix products, arithmetic and copies ran while one was open for 0% of the time, Pallas kernels for 19%

profile of v13, /device:TPU:0, one launch (start us, length us, event | category | flops | bytes accessed | tf_op | source)
XLA Modules:
  0.0 63.1 jit_solution(16216735343410878931)
XLA Ops:
  0.0 0.0 copy-start.2
  0.0 3.9 %project_in.1 = (f32[64,1024]{1,0:T(8,128)S(1)}, f32[64,1024]{1,0:T(8,128)S(1)}, bf16[2,256,3584]{2,1,0:T(8,128)(2,1)S(1)}) custom-call(s32[1]{0:T(128)} %bitcast.1.parity_ref, bf16[4,256,2048]{2,1,0:T(8,128)(2,1)} %rows_hbm.2, bf16[2,64,2048]{2,1,0:T(8,128)(2,1)} %proj_hbm.1, bf16[2,4,256,7168]{3,2,1,0:T(8,128)(2,1)} %rows_hbm.3), custom_call_target="tpu_custom_call" | custom-call | tf_op jit(solution)/shard_map/project_in/pallas_call | solution.py:91
  3.9 0.0 copy-start
  3.9 1.8 %copy-done = bf16[2,256,3584]{2,1,0:T(8,128)(2,1)} copy-done((bf16[2,256,3584]{2,1,0:T(8,128)(2,1)}, bf16[2,256,3584]{2,1,0:T(8,128)(2,1)S(1)}, u32[]{:S(2)}) %copy-start) | copy-done | bytes 3670040
  5.7 5.9 %collective-permute-start.2 = (f32[64,1024]{1,0:T(8,128)S(1)}, f32[64,1024]{1,0:T(8,128)S(1)}, u32[]{:S(2)}, u32[]{:S(2)}) collective-permute-start(f32[64,1024]{1,0:T(8,128)S(1)} %get-tuple-element.18.refs_0_), channel_id=1, source_target_pairs={{0,8},{12,4},{1,9},{13,5},{2,10},{14,6},{3,11},{15,7},{16,24},{28,... | collective-permute-start | bytes 786440 | tf_op jit(solution)/shard_map/ppermute | solution.py:187
  11.6 1.3 %collective-permute-start.1 = (f32[64,1024]{1,0:T(8,128)S(1)}, f32[64,1024]{1,0:T(8,128)S(1)}, u32[]{:S(2)}, u32[]{:S(2)}) collective-permute-start(f32[64,1024]{1,0:T(8,128)S(1)} %get-tuple-element.19), channel_id=1, source_target_pairs={{0,4},{4,8},{1,5},{5,9},{2,6},{6,10},{3,7},{7,11},{16,20},{20,24},... | collective-permute-start | bytes 786440 | tf_op jit(solution)/shard_map/ppermute | solution.py:186
  12.9 0.7 %collective-permute-start = (f32[64,1024]{1,0:T(8,128)S(1)}, f32[64,1024]{1,0:T(8,128)S(1)}, u32[]{:S(2)}, u32[]{:S(2)}) collective-permute-start(f32[64,1024]{1,0:T(8,128)S(1)} %get-tuple-element.19), channel_id=1, source_target_pairs={{12,8},{8,4},{13,9},{9,5},{14,10},{10,6},{15,11},{11,7},{28,24},{2... | collective-permute-start | bytes 786440 | tf_op jit(solution)/shard_map/ppermute | solution.py:185
  13.6 0.0 copy-done.2
  13.6 0.0 copy-start.1
  13.7 2.0 %copy-done.1 = bf16[2,256,3584]{2,1,0:T(8,128)(2,1)S(1)} copy-done((bf16[2,256,3584]{2,1,0:T(8,128)(2,1)S(1)}, bf16[2,256,3584]{2,1,0:T(8,128)(2,1)}, u32[]{:S(2)}) %copy-start.1) | copy-done | bytes 3670040
  15.7 10.3 %project_out.1 = (f32[64,1024]{1,0:T(8,128)S(1)}, f32[64,1024]{1,0:T(8,128)S(1)}, bf16[8,64,128]{2,1,0:T(8,128)(2,1)S(1)}) custom-call(s32[1]{0:T(128)} %bitcast.1.parity_ref, s32[1]{0:T(128)} %bitcast.2.side_ref, bf16[2,4,256,7168]{3,2,1,0:T(8,128)(2,1)} %rows_hbm.3, bf16[2,64,7168]{2,1,0:T(8,128)(2,1)S(1)} %copy-done.2, ...), custom_call_target="tpu_custom_call" | custom-call | tf_op jit(solution)/shard_map/project_out/pallas_call | solution.py:161
  26.0 5.2 %collective-permute-start.5 = (f32[64,1024]{1,0:T(8,128)S(1)}, f32[64,1024]{1,0:T(8,128)S(1)}, u32[]{:S(2)}, u32[]{:S(2)}) collective-permute-start(f32[64,1024]{1,0:T(8,128)S(1)} %get-tuple-element.22.refs_0_), channel_id=1, source_target_pairs={{0,8},{12,4},{1,9},{13,5},{2,10},{14,6},{3,11},{15,7},{16,24},{28,... | collective-permute-start | bytes 786440 | tf_op jit(solution)/shard_map/ppermute | solution.py:187
  31.2 1.3 %collective-permute-start.4 = (f32[64,1024]{1,0:T(8,128)S(1)}, f32[64,1024]{1,0:T(8,128)S(1)}, u32[]{:S(2)}, u32[]{:S(2)}) collective-permute-start(f32[64,1024]{1,0:T(8,128)S(1)} %get-tuple-element.23), channel_id=1, source_target_pairs={{0,4},{4,8},{1,5},{5,9},{2,6},{6,10},{3,7},{7,11},{16,20},{20,24},... | collective-permute-start | bytes 786440 | tf_op jit(solution)/shard_map/ppermute | solution.py:186
  32.5 0.0 collective-permute-done.2.refs_3_
  32.5 0.7 %collective-permute-start.3 = (f32[64,1024]{1,0:T(8,128)S(1)}, f32[64,1024]{1,0:T(8,128)S(1)}, u32[]{:S(2)}, u32[]{:S(2)}) collective-permute-start(f32[64,1024]{1,0:T(8,128)S(1)} %get-tuple-element.23), channel_id=1, source_target_pairs={{12,8},{8,4},{13,9},{9,5},{14,10},{10,6},{15,11},{11,7},{28,24},{2... | collective-permute-start | bytes 786440 | tf_op jit(solution)/shard_map/ppermute | solution.py:185
  33.2 0.0 collective-permute-done.1.refs_2_
  33.2 0.0 collective-permute-done.refs_1_
  33.2 0.4 cov_in.1
  33.6 0.2 collective-permute-start.10
  33.8 1.5 %collective-permute-start.9 = (bf16[8,64,128]{2,1,0:T(8,128)(2,1)S(1)}, bf16[8,64,128]{2,1,0:T(8,128)(2,1)S(1)}, u32[]{:S(2)}, u32[]{:S(2)}) collective-permute-start(bf16[8,64,128]{2,1,0:T(8,128)(2,1)S(1)} %get-tuple-element.26.refs_0_), channel_id=1, source_target_pairs={{0,2},{1,3},{2,0},{3,1},{4,6},{5,7},{6,4},{7,5},{8,10},{9,11},{10,... | collective-permute-start | bytes 393224 | tf_op jit(solution)/shard_map/ppermute | solution.py:396
  35.3 2.7 %collective-permute-done.5.refs_3_ = f32[64,1024]{1,0:T(8,128)S(1)} collective-permute-done((f32[64,1024]{1,0:T(8,128)S(1)}, f32[64,1024]{1,0:T(8,128)S(1)}, u32[]{:S(2)}, u32[]{:S(2)}) %collective-permute-start.5) | collective-permute-done | bytes 262176 | tf_op jit(solution)/shard_map/ppermute | solution.py:187
  38.0 0.0 collective-permute-start.8
  38.0 3.9 %collective-permute-done.4.refs_2_ = f32[64,1024]{1,0:T(8,128)S(1)} collective-permute-done((f32[64,1024]{1,0:T(8,128)S(1)}, f32[64,1024]{1,0:T(8,128)S(1)}, u32[]{:S(2)}, u32[]{:S(2)}) %collective-permute-start.4) | collective-permute-done | bytes 262176 | tf_op jit(solution)/shard_map/ppermute | solution.py:186
  41.8 0.0 collective-permute-done.3.refs_1_
  41.8 1.0 %cov_out.1 = (f32[64,128]{1,0:T(8,128)S(1)}, f32[4,64,128]{2,1,0:T(8,128)S(1)}) custom-call(f32[64,1024]{1,0:T(8,128)S(1)} %get-tuple-element.20.x_ref, f32[64,128]{1,0:T(8,128)S(1)} %get-tuple-element.21.cov_ref, f32[64,1024]{1,0:T(8,128)S(1)} %get-tuple-element.22.refs_0_, f32[64,1024]{1,0:T(8,128)S(1)} %collective-permute-done.3.refs_1_, ...), custom_call_target="tpu_custom_call" | custom-call | tf_op jit(solution)/shard_map/cov_out/pallas_call | solution.py:247
  42.8 0.1 collective-permute-start.6
  42.9 1.2 %collective-permute-done.6 = f32[64,128]{1,0:T(8,128)S(1)} collective-permute-done((f32[64,128]{1,0:T(8,128)S(1)}, f32[64,128]{1,0:T(8,128)S(1)}, u32[]{:S(2)}, u32[]{:S(2)}) %collective-permute-start.6) | collective-permute-done | bytes 32800 | tf_op jit(solution)/shard_map/ppermute | solution.py:396
  44.1 1.5 %collective-permute-start.7 = (f32[64,128]{1,0:T(8,128)S(1)}, f32[64,128]{1,0:T(8,128)S(1)}, u32[]{:S(2)}, u32[]{:S(2)}) collective-permute-start(f32[64,128]{1,0:T(8,128)S(1)} %add.12.own_ref), channel_id=1, source_target_pairs={{0,2},{1,3},{2,0},{3,1},{4,6},{5,7},{6,4},{7,5},{8,10},{9,11},{10,... | collective-permute-start | bytes 98312 | tf_op jit(solution)/shard_map/ppermute | solution.py:396
  45.6 2.4 %collective-permute-done.7.other_ref = f32[64,128]{1,0:T(8,128)S(1)} collective-permute-done((f32[64,128]{1,0:T(8,128)S(1)}, f32[64,128]{1,0:T(8,128)S(1)}, u32[]{:S(2)}, u32[]{:S(2)}) %collective-permute-start.7) | collective-permute-done | bytes 32800 | tf_op jit(solution)/shard_map/ppermute | solution.py:396
  48.0 0.0 collective-permute-done.10.refs_3_
  48.0 0.0 collective-permute-done.9.refs_2_
  48.0 0.0 collective-permute-done.8.refs_1_
  48.0 3.7 %score.1 = f32[4,64]{1,0:T(4,128)S(1)} custom-call(s32[1]{0:T(128)} %bitcast.place_ref, f32[64,128]{1,0:T(8,128)S(1)} %add.12.own_ref, f32[64,128]{1,0:T(8,128)S(1)} %collective-permute-done.7.other_ref, f32[4,64,128]{2,1,0:T(8,128)S(1)} %get-tuple-element.25.sample_ref, bf16[8,64,128]{2,1,0:T(8,128)(2,1)S(1)} %get-tuple-element.26.refs_0_, ...), custom_call_target="tpu_custom_call" | custom-call | tf_op jit(solution)/shard_map/score/pallas_call | solution.py:381
  51.8 1.3 %collective-permute-start.13 = (f32[4,64]{1,0:T(4,128)S(1)}, f32[4,64]{1,0:T(4,128)S(1)}, u32[]{:S(2)}, u32[]{:S(2)}) collective-permute-start(f32[4,64]{1,0:T(4,128)S(1)} %score.1), channel_id=1, source_target_pairs={{4,12},{8,0},{5,13},{9,1},{6,14},{10,2},{7,15},{11,3},{20,28},{24,... | collective-permute-start | bytes 3080 | tf_op jit(solution)/shard_map/ppermute | solution.py:425
  53.1 0.7 %collective-permute-start.12 = (f32[4,64]{1,0:T(4,128)S(1)}, f32[4,64]{1,0:T(4,128)S(1)}, u32[]{:S(2)}, u32[]{:S(2)}) collective-permute-start(f32[4,64]{1,0:T(4,128)S(1)} %score.1), channel_id=1, source_target_pairs={{4,8},{8,12},{5,9},{9,13},{6,10},{10,14},{7,11},{11,15},{20,24},{2... | collective-permute-start | bytes 3080 | tf_op jit(solution)/shard_map/ppermute | solution.py:424
  53.7 1.3 %collective-permute-start.11 = (f32[4,64]{1,0:T(4,128)S(1)}, f32[4,64]{1,0:T(4,128)S(1)}, u32[]{:S(2)}, u32[]{:S(2)}) collective-permute-start(f32[4,64]{1,0:T(4,128)S(1)} %score.1), channel_id=1, source_target_pairs={{8,4},{4,0},{9,5},{5,1},{10,6},{6,2},{11,7},{7,3},{24,20},{20,16},... | collective-permute-start | bytes 3080 | tf_op jit(solution)/shard_map/ppermute | solution.py:423
  55.1 3.1 %collective-permute-done.13 = f32[4,64]{1,0:T(4,128)S(1)} collective-permute-done((f32[4,64]{1,0:T(4,128)S(1)}, f32[4,64]{1,0:T(4,128)S(1)}, u32[]{:S(2)}, u32[]{:S(2)}) %collective-permute-start.13) | collective-permute-done | bytes 1056 | tf_op jit(solution)/shard_map/ppermute | solution.py:425
  58.2 0.0 collective-permute-done.12
  58.2 4.4 %collective-permute-done.11 = f32[4,64]{1,0:T(4,128)S(1)} collective-permute-done((f32[4,64]{1,0:T(4,128)S(1)}, f32[4,64]{1,0:T(4,128)S(1)}, u32[]{:S(2)}, u32[]{:S(2)}) %collective-permute-start.11) | collective-permute-done | bytes 1056 | tf_op jit(solution)/shard_map/ppermute | solution.py:423
  62.6 0.6 add_add_fusion
  (1 shorter events, 0.0 us)
Async XLA Ops:
  0.0 13.6 %copy-start.2 = (bf16[2,64,7168]{2,1,0:T(8,128)(2,1)S(1)}, bf16[2,64,7168]{2,1,0:T(8,128)(2,1)}, u32[]{:S(2)}) copy-start(bf16[2,64,7168]{2,1,0:T(8,128)(2,1)} %proj_ref.1) | copy-start | bytes 5505028
  3.9 1.8 %copy-start = (bf16[2,256,3584]{2,1,0:T(8,128)(2,1)}, bf16[2,256,3584]{2,1,0:T(8,128)(2,1)S(1)}, u32[]{:S(2)}) copy-start(bf16[2,256,3584]{2,1,0:T(8,128)(2,1)S(1)} %get-tuple-element.16.early) | copy-start | bytes 11010052
  5.7 26.8 %collective-permute-start.2 = (f32[64,1024]{1,0:T(8,128)S(1)}, f32[64,1024]{1,0:T(8,128)S(1)}, u32[]{:S(2)}, u32[]{:S(2)}) collective-permute-start(f32[64,1024]{1,0:T(8,128)S(1)} %get-tuple-element.18.refs_0_), channel_id=1, source_target_pairs={{0,8},{12,4},{1,9},{13,5},{2,10},{14,6},{3,11},{15,7},{16,24},{28,... | collective-permute-start | bytes 786440 | tf_op jit(solution)/shard_map/ppermute | solution.py:187
  11.6 21.6 %collective-permute-start.1 = (f32[64,1024]{1,0:T(8,128)S(1)}, f32[64,1024]{1,0:T(8,128)S(1)}, u32[]{:S(2)}, u32[]{:S(2)}) collective-permute-start(f32[64,1024]{1,0:T(8,128)S(1)} %get-tuple-element.19), channel_id=1, source_target_pairs={{0,4},{4,8},{1,5},{5,9},{2,6},{6,10},{3,7},{7,11},{16,20},{20,24},... | collective-permute-start | bytes 786440 | tf_op jit(solution)/shard_map/ppermute | solution.py:186
  12.9 20.3 %collective-permute-start = (f32[64,1024]{1,0:T(8,128)S(1)}, f32[64,1024]{1,0:T(8,128)S(1)}, u32[]{:S(2)}, u32[]{:S(2)}) collective-permute-start(f32[64,1024]{1,0:T(8,128)S(1)} %get-tuple-element.19), channel_id=1, source_target_pairs={{12,8},{8,4},{13,9},{9,5},{14,10},{10,6},{15,11},{11,7},{28,24},{2... | collective-permute-start | bytes 786440 | tf_op jit(solution)/shard_map/ppermute | solution.py:185
  13.6 2.0 %copy-start.1 = (bf16[2,256,3584]{2,1,0:T(8,128)(2,1)S(1)}, bf16[2,256,3584]{2,1,0:T(8,128)(2,1)}, u32[]{:S(2)}) copy-start(bf16[2,256,3584]{2,1,0:T(8,128)(2,1)} %copy-done) | copy-start | bytes 11010052
  26.0 11.9 %collective-permute-start.5 = (f32[64,1024]{1,0:T(8,128)S(1)}, f32[64,1024]{1,0:T(8,128)S(1)}, u32[]{:S(2)}, u32[]{:S(2)}) collective-permute-start(f32[64,1024]{1,0:T(8,128)S(1)} %get-tuple-element.22.refs_0_), channel_id=1, source_target_pairs={{0,8},{12,4},{1,9},{13,5},{2,10},{14,6},{3,11},{15,7},{16,24},{28,... | collective-permute-start | bytes 786440 | tf_op jit(solution)/shard_map/ppermute | solution.py:187
  31.2 10.6 %collective-permute-start.4 = (f32[64,1024]{1,0:T(8,128)S(1)}, f32[64,1024]{1,0:T(8,128)S(1)}, u32[]{:S(2)}, u32[]{:S(2)}) collective-permute-start(f32[64,1024]{1,0:T(8,128)S(1)} %get-tuple-element.23), channel_id=1, source_target_pairs={{0,4},{4,8},{1,5},{5,9},{2,6},{6,10},{3,7},{7,11},{16,20},{20,24},... | collective-permute-start | bytes 786440 | tf_op jit(solution)/shard_map/ppermute | solution.py:186
  32.5 9.3 %collective-permute-start.3 = (f32[64,1024]{1,0:T(8,128)S(1)}, f32[64,1024]{1,0:T(8,128)S(1)}, u32[]{:S(2)}, u32[]{:S(2)}) collective-permute-start(f32[64,1024]{1,0:T(8,128)S(1)} %get-tuple-element.23), channel_id=1, source_target_pairs={{12,8},{8,4},{13,9},{9,5},{14,10},{10,6},{15,11},{11,7},{28,24},{2... | collective-permute-start | bytes 786440 | tf_op jit(solution)/shard_map/ppermute | solution.py:185
  33.6 14.4 %collective-permute-start.10 = (bf16[8,64,128]{2,1,0:T(8,128)(2,1)S(1)}, bf16[8,64,128]{2,1,0:T(8,128)(2,1)S(1)}, u32[]{:S(2)}, u32[]{:S(2)}) collective-permute-start(bf16[8,64,128]{2,1,0:T(8,128)(2,1)S(1)} %get-tuple-element.26.refs_0_), channel_id=1, source_target_pairs={{0,3},{1,2},{2,1},{3,0},{4,7},{5,6},{6,5},{7,4},{8,11},{9,10},{10,... | collective-permute-start | bytes 393224 | tf_op jit(solution)/shard_map/ppermute | solution.py:396
  33.8 14.2 %collective-permute-start.9 = (bf16[8,64,128]{2,1,0:T(8,128)(2,1)S(1)}, bf16[8,64,128]{2,1,0:T(8,128)(2,1)S(1)}, u32[]{:S(2)}, u32[]{:S(2)}) collective-permute-start(bf16[8,64,128]{2,1,0:T(8,128)(2,1)S(1)} %get-tuple-element.26.refs_0_), channel_id=1, source_target_pairs={{0,2},{1,3},{2,0},{3,1},{4,6},{5,7},{6,4},{7,5},{8,10},{9,11},{10,... | collective-permute-start | bytes 393224 | tf_op jit(solution)/shard_map/ppermute | solution.py:396
  38.0 10.0 %collective-permute-start.8 = (bf16[8,64,128]{2,1,0:T(8,128)(2,1)S(1)}, bf16[8,64,128]{2,1,0:T(8,128)(2,1)S(1)}, u32[]{:S(2)}, u32[]{:S(2)}) collective-permute-start(bf16[8,64,128]{2,1,0:T(8,128)(2,1)S(1)} %get-tuple-element.26.refs_0_), channel_id=1, source_target_pairs={{0,1},{1,0},{2,3},{3,2},{4,5},{5,4},{6,7},{7,6},{8,9},{9,8},{10,11... | collective-permute-start | bytes 393224 | tf_op jit(solution)/shard_map/ppermute | solution.py:396
  42.8 1.3 %collective-permute-start.6 = (f32[64,128]{1,0:T(8,128)S(1)}, f32[64,128]{1,0:T(8,128)S(1)}, u32[]{:S(2)}, u32[]{:S(2)}) collective-permute-start(f32[64,128]{1,0:T(8,128)S(1)} %get-tuple-element.24), channel_id=1, source_target_pairs={{0,1},{1,0},{2,3},{3,2},{4,5},{5,4},{6,7},{7,6},{8,9},{9,8},{10,11... | collective-permute-start | bytes 98312 | tf_op jit(solution)/shard_map/ppermute | solution.py:396
  44.1 3.9 %collective-permute-start.7 = (f32[64,128]{1,0:T(8,128)S(1)}, f32[64,128]{1,0:T(8,128)S(1)}, u32[]{:S(2)}, u32[]{:S(2)}) collective-permute-start(f32[64,128]{1,0:T(8,128)S(1)} %add.12.own_ref), channel_id=1, source_target_pairs={{0,2},{1,3},{2,0},{3,1},{4,6},{5,7},{6,4},{7,5},{8,10},{9,11},{10,... | collective-permute-start | bytes 98312 | tf_op jit(solution)/shard_map/ppermute | solution.py:396
  51.8 6.4 %collective-permute-start.13 = (f32[4,64]{1,0:T(4,128)S(1)}, f32[4,64]{1,0:T(4,128)S(1)}, u32[]{:S(2)}, u32[]{:S(2)}) collective-permute-start(f32[4,64]{1,0:T(4,128)S(1)} %score.1), channel_id=1, source_target_pairs={{4,12},{8,0},{5,13},{9,1},{6,14},{10,2},{7,15},{11,3},{20,28},{24,... | collective-permute-start | bytes 3080 | tf_op jit(solution)/shard_map/ppermute | solution.py:425
  53.1 5.1 %collective-permute-start.12 = (f32[4,64]{1,0:T(4,128)S(1)}, f32[4,64]{1,0:T(4,128)S(1)}, u32[]{:S(2)}, u32[]{:S(2)}) collective-permute-start(f32[4,64]{1,0:T(4,128)S(1)} %score.1), channel_id=1, source_target_pairs={{4,8},{8,12},{5,9},{9,13},{6,10},{10,14},{7,11},{11,15},{20,24},{2... | collective-permute-start | bytes 3080 | tf_op jit(solution)/shard_map/ppermute | solution.py:424
  53.7 8.8 %collective-permute-start.11 = (f32[4,64]{1,0:T(4,128)S(1)}, f32[4,64]{1,0:T(4,128)S(1)}, u32[]{:S(2)}, u32[]{:S(2)}) collective-permute-start(f32[4,64]{1,0:T(4,128)S(1)} %score.1), channel_id=1, source_target_pairs={{8,4},{4,0},{9,5},{5,1},{10,6},{6,2},{11,7},{7,3},{24,20},{20,16},... | collective-permute-start | bytes 3080 | tf_op jit(solution)/shard_map/ppermute | solution.py:423

commit v14 on v12

--- a/solution.py
+++ b/solution.py
@@ -48,7 +48,7 @@
 
 
 def project_in_kernel(
-    side_ref, rows_hbm, proj_hbm, grads_hbm, near, far, early, rows, proj, acc, sems, proj_sem, early_sem
+    side_ref, rows_hbm, proj_hbm, grads_hbm, near, far, again, early, rows, proj, acc, sems, proj_sem, early_sem
 ):
     seqs, length, width = rows.shape
     rank = proj.shape[1]
@@ -80,6 +80,7 @@
             acc[1, :, tokens] = part[rank:]
 
     far[...] = acc[1 - side_ref[0]]
+    again[...] = acc[1 - side_ref[0]]
     near[...] = acc[side_ref[0]]
     early_copy.wait()
 
@@ -91,8 +92,9 @@
     return pl.pallas_call(
         project_in_kernel,
         in_specs=[smem(), hbm(), hbm(), hbm()],
-        out_specs=[vmem()] * 3,
+        out_specs=[vmem()] * 4,
         out_shape=[
+            jax.ShapeDtypeStruct((rank, seqs * length), jnp.float32),
             jax.ShapeDtypeStruct((rank, seqs * length), jnp.float32),
             jax.ShapeDtypeStruct((rank, seqs * length), jnp.float32),
             jax.ShapeDtypeStruct(early, grads.dtype),
@@ -111,7 +113,7 @@
 
 
 def project_out_kernel(side_ref, rows_hbm, proj_ref, queries_hbm, early, *refs):
-    (near, far, packed), (rows, held, acc, sems, sem) = refs[:3], refs[3:]
+    (near, far, again, packed), (rows, held, acc, sems, sem) = refs[:4], refs[4:]
     _, seqs, length, width = rows.shape
     parts = sems.shape[2]
     piece = width // parts
@@ -145,6 +147,7 @@
                     value = value + acc[layer, :, tokens]
                 acc[layer, :, tokens] = value
     far[...] = acc[1 - side_ref[0]]
+    again[...] = acc[1 - side_ref[0]]
     near[...] = acc[side_ref[0]]
     copy.wait()
     blocks = held.shape[0] // 2
@@ -161,8 +164,9 @@
     return pl.pallas_call(
         project_out_kernel,
         in_specs=[smem(), hbm(), vmem(), hbm(), vmem()],
-        out_specs=[vmem()] * 3,
+        out_specs=[vmem()] * 4,
         out_shape=[
+            jax.ShapeDtypeStruct((rank, seqs * length), jnp.float32),
             jax.ShapeDtypeStruct((rank, seqs * length), jnp.float32),
             jax.ShapeDtypeStruct((rank, seqs * length), jnp.float32),
             jax.ShapeDtypeStruct((count // 2, rank, 2 * rank), queries.dtype),
@@ -183,12 +187,12 @@
     return lax.ppermute(value, "tensor", [(1, 2), (2, 1)])
 
 
-def to_owner(near, far):
+def to_owner(near, far, again):
     return [
         near,
         lax.ppermute(near, "tensor", [(0, 1), (3, 2)]),
-        across(far),
         lax.ppermute(far, "tensor", [(0, 2), (3, 1)]),
+        across(again),
     ]
 
 
@@ -400,6 +404,12 @@
     return lax.ppermute(value, axis, [(i, i ^ bit) for i in range(lax.axis_size(axis))])
 
 
+def owners_swap(value, bits):
+    parts = lax.axis_size("dp")
+    places = [(t * parts + k, t * parts + (k ^ bits)) for t in (1, 2) for k in range(parts)]
+    return lax.ppermute(value, ("tensor", "dp"), places)
+
+
 def local_owned(acts, grads, proj_in, proj_out, queries):
     seqs, length, _ = acts.shape
     parts = lax.axis_size("dp")
@@ -407,12 +417,12 @@
     column = lax.axis_index("tensor").astype(jnp.int32)
     side = (column >= 2).astype(jnp.int32).reshape(1)
     place = lax.axis_index("dp").astype(jnp.int32).reshape(1)
-    x_near, x_far, early = project_in(side, acts, proj_in, grads)
-    x_pieces = to_owner(x_near, x_far)
-    near, far, packed = project_out(side, grads, proj_out, queries, early)
-    pieces = to_owner(near, far)
+    x_near, x_far, x_again, early = project_in(side, acts, proj_in, grads)
+    x_pieces = to_owner(x_near, x_far, x_again)
+    near, far, again, packed = project_out(side, grads, proj_out, queries, early)
+    pieces = to_owner(near, far, again)
     packed, x, cov = cov_in(packed, x_pieces)
-    query_pieces = [packed] + [swap(packed, "dp", bits) for bits in range(1, parts)]
+    query_pieces = [packed] + [owners_swap(packed, bits) for bits in range(1, parts)]
     cov, sample = cov_out(x, cov, pieces, seqs)
     other = jnp.zeros_like(cov)
     bit = 1

time: 57.2 us -> 55.8 us (0.976)
  the two profiles are of different devices: /device:TPU:12 before, /device:TPU:8 now
where the time goes in v14:
time: 55.8 us; the launch traced here: 55.4 us
  starting transfers between devices  25.1 us (45%)
  Pallas kernels  19.4 us (35%)
  waiting for transfers between devices  10.1 us (18%)
  other arithmetic  0.59 us (1%)
    pallas_call x1, Pallas kernels, project_out(): pl.pallas_call(project_out_kernel, in_specs=[smem(), hbm(), vmem(), hbm()...  10.4 us
    ppermute x3, starting transfers between devices, across(): return lax.ppermute(value, 'tensor', [(1, 2), (2, 1)])  8.32 us
    ppermute x3, starting transfers between devices, owners_swap(): return lax.ppermute(value, ('tensor', 'dp'), places)  7.24 us
    ppermute x3, waiting for transfers between devices, across(): return lax.ppermute(value, 'tensor', [(1, 2), (2, 1)])  5.16 us
    pallas_call x1, Pallas kernels, project_in(): pl.pallas_call(project_in_kernel, in_specs=[smem(), hbm(), hbm(), hbm()],...  3.91 us
    pallas_call x1, Pallas kernels, score(): pl.pallas_call(functools.partial(score_kernel, tokens), in_specs=[smem()]...  3.75 us
    ppermute x2, waiting for transfers between devices, swap(): lax.ppermute(value, axis, [(i, i ^ bit) for i in range(lax.axis_size(axis...  3.62 us
    ppermute x2, starting transfers between devices, to_owner(): lax.ppermute(far, 'tensor', [(0, 2), (3, 1)])  2.58 us
  transfers between devices with their start and end apart: 14, of which 5 were waited for; matrix products, arithmetic and copies ran while one was open for 0% of the time, Pallas kernels for 21%

profile of v14, /device:TPU:8, one launch (start us, length us, event | category | flops | bytes accessed | tf_op | source)
XLA Modules:
  0.0 55.4 jit_solution(11075447739886439007)
XLA Ops:
  0.0 0.0 copy-start
  0.0 3.9 %project_in.1 = (f32[64,1024]{1,0:T(8,128)S(1)}, f32[64,1024]{1,0:T(8,128)S(1)}, f32[64,1024]{1,0:T(8,128)S(1)}, bf16[2,256,3584]{2,1,0:T(8,128)(2,1)S(1)}) custom-call(s32[1]{0:T(128)} %bitcast.1.side_ref, bf16[4,256,2048]{2,1,0:T(8,128)(2,1)} %rows_hbm.2, bf16[2,64,2048]{2,1,0:T(8,128)(2,1)} %proj_hbm.1, bf16[2,4,256,7168]{3,2,1,0:T(8,128)(2,1)} %rows_hbm.3), custom_call_target="tpu_custom_call" | custom-call | tf_op jit(solution)/shard_map/project_in/pallas_call | solution.py:92
  3.9 1.3 %collective-permute-start.1 = (f32[64,1024]{1,0:T(8,128)S(1)}, f32[64,1024]{1,0:T(8,128)S(1)}, u32[]{:S(2)}, u32[]{:S(2)}) collective-permute-start(f32[64,1024]{1,0:T(8,128)S(1)} %get-tuple-element.21), channel_id=1, source_target_pairs={{0,8},{12,4},{1,9},{13,5},{2,10},{14,6},{3,11},{15,7},{16,24},{28,... | collective-permute-start | bytes 786440 | tf_op jit(solution)/shard_map/ppermute | solution.py:194
  5.2 3.5 %collective-permute-start.2 = (f32[64,1024]{1,0:T(8,128)S(1)}, f32[64,1024]{1,0:T(8,128)S(1)}, u32[]{:S(2)}, u32[]{:S(2)}) collective-permute-start(f32[64,1024]{1,0:T(8,128)S(1)} %get-tuple-element.22), channel_id=1, source_target_pairs={{4,8},{8,4},{5,9},{9,5},{6,10},{10,6},{7,11},{11,7},{20,24},{24,20... | collective-permute-start | bytes 786440 | tf_op jit(solution)/shard_map/ppermute | solution.py:187
  8.7 1.3 %collective-permute-start = (f32[64,1024]{1,0:T(8,128)S(1)}, f32[64,1024]{1,0:T(8,128)S(1)}, u32[]{:S(2)}, u32[]{:S(2)}) collective-permute-start(f32[64,1024]{1,0:T(8,128)S(1)} %get-tuple-element.20.refs_0_), channel_id=1, source_target_pairs={{0,4},{12,8},{1,5},{13,9},{2,6},{14,10},{3,7},{15,11},{16,20},{28,... | collective-permute-start | bytes 786440 | tf_op jit(solution)/shard_map/ppermute | solution.py:193
  10.0 0.0 copy-done
  10.0 10.4 %project_out.1 = (f32[64,1024]{1,0:T(8,128)S(1)}, f32[64,1024]{1,0:T(8,128)S(1)}, f32[64,1024]{1,0:T(8,128)S(1)}, bf16[8,64,128]{2,1,0:T(8,128)(2,1)S(1)}) custom-call(s32[1]{0:T(128)} %bitcast.1.side_ref, bf16[2,4,256,7168]{3,2,1,0:T(8,128)(2,1)} %rows_hbm.3, bf16[2,64,7168]{2,1,0:T(8,128)(2,1)S(1)} %copy-done, bf16[16,2,64,64]{3,2,1,0:T(8,128)(2,1)} %queries_hbm.1, ...), custom_call_target="tpu_custom_call" | custom-call | tf_op jit(solution)/shard_map/project_out/pallas_call | solution.py:164
  20.4 1.3 %collective-permute-start.4 = (f32[64,1024]{1,0:T(8,128)S(1)}, f32[64,1024]{1,0:T(8,128)S(1)}, u32[]{:S(2)}, u32[]{:S(2)}) collective-permute-start(f32[64,1024]{1,0:T(8,128)S(1)} %get-tuple-element.26), channel_id=1, source_target_pairs={{0,8},{12,4},{1,9},{13,5},{2,10},{14,6},{3,11},{15,7},{16,24},{28,... | collective-permute-start | bytes 786440 | tf_op jit(solution)/shard_map/ppermute | solution.py:194
  21.7 2.4 %collective-permute-start.5 = (f32[64,1024]{1,0:T(8,128)S(1)}, f32[64,1024]{1,0:T(8,128)S(1)}, u32[]{:S(2)}, u32[]{:S(2)}) collective-permute-start(f32[64,1024]{1,0:T(8,128)S(1)} %get-tuple-element.27), channel_id=1, source_target_pairs={{4,8},{8,4},{5,9},{9,5},{6,10},{10,6},{7,11},{11,7},{20,24},{24,20... | collective-permute-start | bytes 786440 | tf_op jit(solution)/shard_map/ppermute | solution.py:187
  24.1 0.0 collective-permute-done.1.refs_2_
  24.1 1.3 %collective-permute-start.3 = (f32[64,1024]{1,0:T(8,128)S(1)}, f32[64,1024]{1,0:T(8,128)S(1)}, u32[]{:S(2)}, u32[]{:S(2)}) collective-permute-start(f32[64,1024]{1,0:T(8,128)S(1)} %get-tuple-element.25.refs_0_), channel_id=1, source_target_pairs={{0,4},{12,8},{1,5},{13,9},{2,6},{14,10},{3,7},{15,11},{16,20},{28,... | collective-permute-start | bytes 786440 | tf_op jit(solution)/shard_map/ppermute | solution.py:193
  25.4 0.0 collective-permute-done.2.refs_3_
  25.4 0.0 collective-permute-done.refs_1_
  25.4 0.4 cov_in.1
  25.8 2.3 %collective-permute-start.10 = (bf16[8,64,128]{2,1,0:T(8,128)(2,1)S(1)}, bf16[8,64,128]{2,1,0:T(8,128)(2,1)S(1)}, u32[]{:S(2)}, u32[]{:S(2)}) collective-permute-start(bf16[8,64,128]{2,1,0:T(8,128)(2,1)S(1)} %get-tuple-element.30.refs_0_), channel_id=1, source_target_pairs={{4,7},{5,6},{6,5},{7,4},{8,11},{9,10},{10,9},{11,8},{20,23},{21,22... | collective-permute-start | bytes 393224 | tf_op jit(solution)/shard_map/ppermute | solution.py:410
  28.1 3.0 %collective-permute-start.9 = (bf16[8,64,128]{2,1,0:T(8,128)(2,1)S(1)}, bf16[8,64,128]{2,1,0:T(8,128)(2,1)S(1)}, u32[]{:S(2)}, u32[]{:S(2)}) collective-permute-start(bf16[8,64,128]{2,1,0:T(8,128)(2,1)S(1)} %get-tuple-element.30.refs_0_), channel_id=1, source_target_pairs={{4,6},{5,7},{6,4},{7,5},{8,10},{9,11},{10,8},{11,9},{20,22},{21,23... | collective-permute-start | bytes 393224 | tf_op jit(solution)/shard_map/ppermute | solution.py:410
  31.2 1.3 %collective-permute-done.4.refs_2_ = f32[64,1024]{1,0:T(8,128)S(1)} collective-permute-done((f32[64,1024]{1,0:T(8,128)S(1)}, f32[64,1024]{1,0:T(8,128)S(1)}, u32[]{:S(2)}, u32[]{:S(2)}) %collective-permute-start.4) | collective-permute-done | bytes 262176 | tf_op jit(solution)/shard_map/ppermute | solution.py:194
  32.5 1.9 %collective-permute-start.8 = (bf16[8,64,128]{2,1,0:T(8,128)(2,1)S(1)}, bf16[8,64,128]{2,1,0:T(8,128)(2,1)S(1)}, u32[]{:S(2)}, u32[]{:S(2)}) collective-permute-start(bf16[8,64,128]{2,1,0:T(8,128)(2,1)S(1)} %get-tuple-element.30.refs_0_), channel_id=1, source_target_pairs={{4,5},{5,4},{6,7},{7,6},{8,9},{9,8},{10,11},{11,10},{20,21},{21,20... | collective-permute-start | bytes 393224 | tf_op jit(solution)/shard_map/ppermute | solution.py:410
  34.4 2.2 %collective-permute-done.5.refs_3_ = f32[64,1024]{1,0:T(8,128)S(1)} collective-permute-done((f32[64,1024]{1,0:T(8,128)S(1)}, f32[64,1024]{1,0:T(8,128)S(1)}, u32[]{:S(2)}, u32[]{:S(2)}) %collective-permute-start.5) | collective-permute-done | bytes 262176 | tf_op jit(solution)/shard_map/ppermute | solution.py:187
  36.6 0.0 collective-permute-done.3.refs_1_
  36.6 1.0 %cov_out.1 = (f32[64,128]{1,0:T(8,128)S(1)}, f32[4,64,128]{2,1,0:T(8,128)S(1)}) custom-call(f32[64,1024]{1,0:T(8,128)S(1)} %get-tuple-element.23.x_ref, f32[64,128]{1,0:T(8,128)S(1)} %get-tuple-element.24.cov_ref, f32[64,1024]{1,0:T(8,128)S(1)} %get-tuple-element.25.refs_0_, f32[64,1024]{1,0:T(8,128)S(1)} %collective-permute-done.3.refs_1_, ...), custom_call_target="tpu_custom_call" | custom-call | tf_op jit(solution)/shard_map/cov_out/pallas_call | solution.py:255
  37.6 0.1 collective-permute-start.6
  37.7 1.2 %collective-permute-done.6 = f32[64,128]{1,0:T(8,128)S(1)} collective-permute-done((f32[64,128]{1,0:T(8,128)S(1)}, f32[64,128]{1,0:T(8,128)S(1)}, u32[]{:S(2)}, u32[]{:S(2)}) %collective-permute-start.6) | collective-permute-done | bytes 32800 | tf_op jit(solution)/shard_map/ppermute | solution.py:404
  38.9 1.5 %collective-permute-start.7 = (f32[64,128]{1,0:T(8,128)S(1)}, f32[64,128]{1,0:T(8,128)S(1)}, u32[]{:S(2)}, u32[]{:S(2)}) collective-permute-start(f32[64,128]{1,0:T(8,128)S(1)} %add.12.own_ref), channel_id=1, source_target_pairs={{0,2},{1,3},{2,0},{3,1},{4,6},{5,7},{6,4},{7,5},{8,10},{9,11},{10,... | collective-permute-start | bytes 98312 | tf_op jit(solution)/shard_map/ppermute | solution.py:404
  40.4 2.4 %collective-permute-done.7.other_ref = f32[64,128]{1,0:T(8,128)S(1)} collective-permute-done((f32[64,128]{1,0:T(8,128)S(1)}, f32[64,128]{1,0:T(8,128)S(1)}, u32[]{:S(2)}, u32[]{:S(2)}) %collective-permute-start.7) | collective-permute-done | bytes 32800 | tf_op jit(solution)/shard_map/ppermute | solution.py:404
  42.8 0.0 collective-permute-done.10.refs_3_
  42.8 0.0 collective-permute-done.9.refs_2_
  42.8 0.0 collective-permute-done.8.refs_1_
  42.8 3.7 %score.1 = f32[4,64]{1,0:T(4,128)S(1)} custom-call(s32[1]{0:T(128)} %bitcast.place_ref, f32[64,128]{1,0:T(8,128)S(1)} %add.12.own_ref, f32[64,128]{1,0:T(8,128)S(1)} %collective-permute-done.7.other_ref, f32[4,64,128]{2,1,0:T(8,128)S(1)} %get-tuple-element.29.sample_ref, bf16[8,64,128]{2,1,0:T(8,128)(2,1)S(1)} %get-tuple-element.30.refs_0_, ...), custom_call_target="tpu_custom_call" | custom-call | tf_op jit(solution)/shard_map/score/pallas_call | solution.py:389
  46.6 1.5 %collective-permute-start.13 = (f32[4,64]{1,0:T(4,128)S(1)}, f32[4,64]{1,0:T(4,128)S(1)}, u32[]{:S(2)}, u32[]{:S(2)}) collective-permute-start(f32[4,64]{1,0:T(4,128)S(1)} %score.1), channel_id=1, source_target_pairs={{8,0},{4,12},{9,1},{5,13},{10,2},{6,14},{11,3},{7,15},{24,16},{20,... | collective-permute-start | bytes 3080 | tf_op jit(solution)/shard_map/ppermute | solution.py:438
  48.1 1.3 %collective-permute-start.12 = (f32[4,64]{1,0:T(4,128)S(1)}, f32[4,64]{1,0:T(4,128)S(1)}, u32[]{:S(2)}, u32[]{:S(2)}) collective-permute-start(f32[4,64]{1,0:T(4,128)S(1)} %score.1), channel_id=1, source_target_pairs={{4,0},{8,12},{5,1},{9,13},{6,2},{10,14},{7,3},{11,15},{20,16},{24,... | collective-permute-start | bytes 3080 | tf_op jit(solution)/shard_map/ppermute | solution.py:437
  49.4 2.5 %collective-permute-start.11 = (f32[4,64]{1,0:T(4,128)S(1)}, f32[4,64]{1,0:T(4,128)S(1)}, u32[]{:S(2)}, u32[]{:S(2)}) collective-permute-start(f32[4,64]{1,0:T(4,128)S(1)} %score.1), channel_id=1, source_target_pairs={{4,8},{8,4},{5,9},{9,5},{6,10},{10,6},{7,11},{11,7},{20,24},{24,20... | collective-permute-start | bytes 3080 | tf_op jit(solution)/shard_map/ppermute | solution.py:187
  51.9 0.0 collective-permute-done.13
  51.9 0.0 collective-permute-done.12
  51.9 3.0 %collective-permute-done.11 = f32[4,64]{1,0:T(4,128)S(1)} collective-permute-done((f32[4,64]{1,0:T(4,128)S(1)}, f32[4,64]{1,0:T(4,128)S(1)}, u32[]{:S(2)}, u32[]{:S(2)}) %collective-permute-start.11) | collective-permute-done | bytes 1056 | tf_op jit(solution)/shard_map/ppermute | solution.py:187
  54.9 0.6 %add_add_fusion = f32[4,64]{1,0:T(4,128)} fusion(f32[4,64]{1,0:T(4,128)S(1)} %collective-permute-done.13, f32[4,64]{1,0:T(4,128)S(1)} %collective-permute-done.12, f32[4,64]{1,0:T(4,128)S(1)} %collective-permute-done.11, f32[4,64]{1,0:T(4,128)S(1)} %score.1, pred[]{:T(512)S(6)} %or.3), kind=kLoop, calls=%fused_computation | loop fusion | flops 1024 | bytes 5121 | tf_op jit(solution)/shard_map/add | solution.py:440
  (1 shorter events, 0.0 us)
Async XLA Ops:
  0.0 10.0 %copy-start = (bf16[2,64,7168]{2,1,0:T(8,128)(2,1)S(1)}, bf16[2,64,7168]{2,1,0:T(8,128)(2,1)}, u32[]{:S(2)}) copy-start(bf16[2,64,7168]{2,1,0:T(8,128)(2,1)} %proj_ref.1) | copy-start | bytes 5505028
  3.9 20.2 %collective-permute-start.1 = (f32[64,1024]{1,0:T(8,128)S(1)}, f32[64,1024]{1,0:T(8,128)S(1)}, u32[]{:S(2)}, u32[]{:S(2)}) collective-permute-start(f32[64,1024]{1,0:T(8,128)S(1)} %get-tuple-element.21), channel_id=1, source_target_pairs={{0,8},{12,4},{1,9},{13,5},{2,10},{14,6},{3,11},{15,7},{16,24},{28,... | collective-permute-start | bytes 786440 | tf_op jit(solution)/shard_map/ppermute | solution.py:194
  5.2 20.2 %collective-permute-start.2 = (f32[64,1024]{1,0:T(8,128)S(1)}, f32[64,1024]{1,0:T(8,128)S(1)}, u32[]{:S(2)}, u32[]{:S(2)}) collective-permute-start(f32[64,1024]{1,0:T(8,128)S(1)} %get-tuple-element.22), channel_id=1, source_target_pairs={{4,8},{8,4},{5,9},{9,5},{6,10},{10,6},{7,11},{11,7},{20,24},{24,20... | collective-permute-start | bytes 786440 | tf_op jit(solution)/shard_map/ppermute | solution.py:187
  8.7 16.7 %collective-permute-start = (f32[64,1024]{1,0:T(8,128)S(1)}, f32[64,1024]{1,0:T(8,128)S(1)}, u32[]{:S(2)}, u32[]{:S(2)}) collective-permute-start(f32[64,1024]{1,0:T(8,128)S(1)} %get-tuple-element.20.refs_0_), channel_id=1, source_target_pairs={{0,4},{12,8},{1,5},{13,9},{2,6},{14,10},{3,7},{15,11},{16,20},{28,... | collective-permute-start | bytes 786440 | tf_op jit(solution)/shard_map/ppermute | solution.py:193
  20.4 12.1 %collective-permute-start.4 = (f32[64,1024]{1,0:T(8,128)S(1)}, f32[64,1024]{1,0:T(8,128)S(1)}, u32[]{:S(2)}, u32[]{:S(2)}) collective-permute-start(f32[64,1024]{1,0:T(8,128)S(1)} %get-tuple-element.26), channel_id=1, source_target_pairs={{0,8},{12,4},{1,9},{13,5},{2,10},{14,6},{3,11},{15,7},{16,24},{28,... | collective-permute-start | bytes 786440 | tf_op jit(solution)/shard_map/ppermute | solution.py:194
  21.7 14.9 %collective-permute-start.5 = (f32[64,1024]{1,0:T(8,128)S(1)}, f32[64,1024]{1,0:T(8,128)S(1)}, u32[]{:S(2)}, u32[]{:S(2)}) collective-permute-start(f32[64,1024]{1,0:T(8,128)S(1)} %get-tuple-element.27), channel_id=1, source_target_pairs={{4,8},{8,4},{5,9},{9,5},{6,10},{10,6},{7,11},{11,7},{20,24},{24,20... | collective-permute-start | bytes 786440 | tf_op jit(solution)/shard_map/ppermute | solution.py:187
  24.1 12.5 %collective-permute-start.3 = (f32[64,1024]{1,0:T(8,128)S(1)}, f32[64,1024]{1,0:T(8,128)S(1)}, u32[]{:S(2)}, u32[]{:S(2)}) collective-permute-start(f32[64,1024]{1,0:T(8,128)S(1)} %get-tuple-element.25.refs_0_), channel_id=1, source_target_pairs={{0,4},{12,8},{1,5},{13,9},{2,6},{14,10},{3,7},{15,11},{16,20},{28,... | collective-permute-start | bytes 786440 | tf_op jit(solution)/shard_map/ppermute | solution.py:193
  25.8 17.0 %collective-permute-start.10 = (bf16[8,64,128]{2,1,0:T(8,128)(2,1)S(1)}, bf16[8,64,128]{2,1,0:T(8,128)(2,1)S(1)}, u32[]{:S(2)}, u32[]{:S(2)}) collective-permute-start(bf16[8,64,128]{2,1,0:T(8,128)(2,1)S(1)} %get-tuple-element.30.refs_0_), channel_id=1, source_target_pairs={{4,7},{5,6},{6,5},{7,4},{8,11},{9,10},{10,9},{11,8},{20,23},{21,22... | collective-permute-start | bytes 393224 | tf_op jit(solution)/shard_map/ppermute | solution.py:410
  28.1 14.7 %collective-permute-start.9 = (bf16[8,64,128]{2,1,0:T(8,128)(2,1)S(1)}, bf16[8,64,128]{2,1,0:T(8,128)(2,1)S(1)}, u32[]{:S(2)}, u32[]{:S(2)}) collective-permute-start(bf16[8,64,128]{2,1,0:T(8,128)(2,1)S(1)} %get-tuple-element.30.refs_0_), channel_id=1, source_target_pairs={{4,6},{5,7},{6,4},{7,5},{8,10},{9,11},{10,8},{11,9},{20,22},{21,23... | collective-permute-start | bytes 393224 | tf_op jit(solution)/shard_map/ppermute | solution.py:410
  32.5 10.3 %collective-permute-start.8 = (bf16[8,64,128]{2,1,0:T(8,128)(2,1)S(1)}, bf16[8,64,128]{2,1,0:T(8,128)(2,1)S(1)}, u32[]{:S(2)}, u32[]{:S(2)}) collective-permute-start(bf16[8,64,128]{2,1,0:T(8,128)(2,1)S(1)} %get-tuple-element.30.refs_0_), channel_id=1, source_target_pairs={{4,5},{5,4},{6,7},{7,6},{8,9},{9,8},{10,11},{11,10},{20,21},{21,20... | collective-permute-start | bytes 393224 | tf_op jit(solution)/shard_map/ppermute | solution.py:410
  37.6 1.3 %collective-permute-start.6 = (f32[64,128]{1,0:T(8,128)S(1)}, f32[64,128]{1,0:T(8,128)S(1)}, u32[]{:S(2)}, u32[]{:S(2)}) collective-permute-start(f32[64,128]{1,0:T(8,128)S(1)} %get-tuple-element.28), channel_id=1, source_target_pairs={{0,1},{1,0},{2,3},{3,2},{4,5},{5,4},{6,7},{7,6},{8,9},{9,8},{10,11... | collective-permute-start | bytes 98312 | tf_op jit(solution)/shard_map/ppermute | solution.py:404
  38.9 3.9 %collective-permute-start.7 = (f32[64,128]{1,0:T(8,128)S(1)}, f32[64,128]{1,0:T(8,128)S(1)}, u32[]{:S(2)}, u32[]{:S(2)}) collective-permute-start(f32[64,128]{1,0:T(8,128)S(1)} %add.12.own_ref), channel_id=1, source_target_pairs={{0,2},{1,3},{2,0},{3,1},{4,6},{5,7},{6,4},{7,5},{8,10},{9,11},{10,... | collective-permute-start | bytes 98312 | tf_op jit(solution)/shard_map/ppermute | solution.py:404
  46.6 5.3 %collective-permute-start.13 = (f32[4,64]{1,0:T(4,128)S(1)}, f32[4,64]{1,0:T(4,128)S(1)}, u32[]{:S(2)}, u32[]{:S(2)}) collective-permute-start(f32[4,64]{1,0:T(4,128)S(1)} %score.1), channel_id=1, source_target_pairs={{8,0},{4,12},{9,1},{5,13},{10,2},{6,14},{11,3},{7,15},{24,16},{20,... | collective-permute-start | bytes 3080 | tf_op jit(solution)/shard_map/ppermute | solution.py:438
  48.1 3.8 %collective-permute-start.12 = (f32[4,64]{1,0:T(4,128)S(1)}, f32[4,64]{1,0:T(4,128)S(1)}, u32[]{:S(2)}, u32[]{:S(2)}) collective-permute-start(f32[4,64]{1,0:T(4,128)S(1)} %score.1), channel_id=1, source_target_pairs={{4,0},{8,12},{5,1},{9,13},{6,2},{10,14},{7,3},{11,15},{20,16},{24,... | collective-permute-start | bytes 3080 | tf_op jit(solution)/shard_map/ppermute | solution.py:437
  49.4 5.5 %collective-permute-start.11 = (f32[4,64]{1,0:T(4,128)S(1)}, f32[4,64]{1,0:T(4,128)S(1)}, u32[]{:S(2)}, u32[]{:S(2)}) collective-permute-start(f32[4,64]{1,0:T(4,128)S(1)} %score.1), channel_id=1, source_target_pairs={{4,8},{8,4},{5,9},{9,5},{6,10},{10,6},{7,11},{11,7},{20,24},{24,20... | collective-permute-start | bytes 3080 | tf_op jit(solution)/shard_map/ppermute | solution.py:187

commit v15 on v14

--- a/solution.py
+++ b/solution.py
@@ -404,6 +404,11 @@
     return lax.ppermute(value, axis, [(i, i ^ bit) for i in range(lax.axis_size(axis))])
 
 
+def shift(value, axis, by):
+    size = lax.axis_size(axis)
+    return lax.ppermute(value, axis, [(i, (i + by) % size) for i in range(size)])
+
+
 def owners_swap(value, bits):
     parts = lax.axis_size("dp")
     places = [(t * parts + k, t * parts + (k ^ bits)) for t in (1, 2) for k in range(parts)]
@@ -431,13 +436,11 @@
         other = swap(cov, "dp", bit)
         bit *= 2
     scores = score(place, cov, other, sample, query_pieces, tokens)
+    above = shift(scores, "tensor", -1)
+    opposite = shift(scores, "tensor", 2)
+    below = shift(scores, "tensor", 1)
     owner = (column == 1) | (column == 2)
-    pieces = [
-        across(scores),
-        lax.ppermute(scores, "tensor", [(1, 0), (2, 3)]),
-        lax.ppermute(scores, "tensor", [(2, 0), (1, 3)]),
-    ]
-    return jnp.where(owner, scores, 0.0) + pieces[0] + pieces[1] + pieces[2]
+    return jnp.where(owner, scores, opposite) + jnp.where(column >= 2, below, above)
 
 
 def damp(matrix):

time: 55.8 us -> 55 us (0.986)
  the two profiles are of different devices: /device:TPU:8 before, /device:TPU:0 now
where the time goes in v15:
time: 55 us; the launch traced here: 54.7 us
  starting transfers between devices  23.6 us (43%)
  Pallas kernels  19.4 us (35%)
  waiting for transfers between devices  10.8 us (20%)
  other arithmetic  0.59 us (1%)
    pallas_call x1, Pallas kernels, project_out(): pl.pallas_call(project_out_kernel, in_specs=[smem(), hbm(), vmem(), hbm()...  10.4 us
    ppermute x2, starting transfers between devices, to_owner(): lax.ppermute(far, 'tensor', [(0, 2), (3, 1)])  7.26 us
    ppermute x2, starting transfers between devices, to_owner(): lax.ppermute(near, 'tensor', [(0, 1), (3, 2)])  6.04 us
    ppermute x3, starting transfers between devices, shift(): lax.ppermute(value, axis, [(i, (i + by) % size) for i in range(size)])  5.43 us
    pallas_call x1, Pallas kernels, project_in(): pl.pallas_call(project_in_kernel, in_specs=[smem(), hbm(), hbm(), hbm()],...  3.91 us
    pallas_call x1, Pallas kernels, score(): pl.pallas_call(functools.partial(score_kernel, tokens), in_specs=[smem()]...  3.75 us
    ppermute x2, waiting for transfers between devices, swap(): lax.ppermute(value, axis, [(i, i ^ bit) for i in range(lax.axis_size(axis...  3.61 us
    ppermute x2, waiting for transfers between devices, to_owner(): lax.ppermute(near, 'tensor', [(0, 1), (3, 2)])  3.47 us
  transfers between devices with their start and end apart: 14, of which 6 were waited for; matrix products, arithmetic and copies ran while one was open for 0% of the time, Pallas kernels for 22%

profile of v15, /device:TPU:0, one launch (start us, length us, event | category | flops | bytes accessed | tf_op | source)
XLA Modules:
  0.0 54.7 jit_solution(18075397741229741277)
XLA Ops:
  0.0 0.0 copy-start
  0.0 3.9 %project_in.1 = (f32[64,1024]{1,0:T(8,128)S(1)}, f32[64,1024]{1,0:T(8,128)S(1)}, f32[64,1024]{1,0:T(8,128)S(1)}, bf16[2,256,3584]{2,1,0:T(8,128)(2,1)S(1)}) custom-call(s32[1]{0:T(128)} %bitcast.1.side_ref, bf16[4,256,2048]{2,1,0:T(8,128)(2,1)} %rows_hbm.2, bf16[2,64,2048]{2,1,0:T(8,128)(2,1)} %proj_hbm.1, bf16[2,4,256,7168]{3,2,1,0:T(8,128)(2,1)} %rows_hbm.3), custom_call_target="tpu_custom_call" | custom-call | tf_op jit(solution)/shard_map/project_in/pallas_call | solution.py:92
  3.9 6.0 %collective-permute-start.1 = (f32[64,1024]{1,0:T(8,128)S(1)}, f32[64,1024]{1,0:T(8,128)S(1)}, u32[]{:S(2)}, u32[]{:S(2)}) collective-permute-start(f32[64,1024]{1,0:T(8,128)S(1)} %get-tuple-element.21), channel_id=1, source_target_pairs={{0,8},{12,4},{1,9},{13,5},{2,10},{14,6},{3,11},{15,7},{16,24},{28,... | collective-permute-start | bytes 786440 | tf_op jit(solution)/shard_map/ppermute | solution.py:194
  9.9 0.7 %collective-permute-start.2 = (f32[64,1024]{1,0:T(8,128)S(1)}, f32[64,1024]{1,0:T(8,128)S(1)}, u32[]{:S(2)}, u32[]{:S(2)}) collective-permute-start(f32[64,1024]{1,0:T(8,128)S(1)} %get-tuple-element.22), channel_id=1, source_target_pairs={{4,8},{8,4},{5,9},{9,5},{6,10},{10,6},{7,11},{11,7},{20,24},{24,20... | collective-permute-start | bytes 786440 | tf_op jit(solution)/shard_map/ppermute | solution.py:187
  10.6 3.1 %collective-permute-start = (f32[64,1024]{1,0:T(8,128)S(1)}, f32[64,1024]{1,0:T(8,128)S(1)}, u32[]{:S(2)}, u32[]{:S(2)}) collective-permute-start(f32[64,1024]{1,0:T(8,128)S(1)} %get-tuple-element.20.refs_0_), channel_id=1, source_target_pairs={{0,4},{12,8},{1,5},{13,9},{2,6},{14,10},{3,7},{15,11},{16,20},{28,... | collective-permute-start | bytes 786440 | tf_op jit(solution)/shard_map/ppermute | solution.py:193
  13.7 0.0 copy-done
  13.7 10.4 %project_out.1 = (f32[64,1024]{1,0:T(8,128)S(1)}, f32[64,1024]{1,0:T(8,128)S(1)}, f32[64,1024]{1,0:T(8,128)S(1)}, bf16[8,64,128]{2,1,0:T(8,128)(2,1)S(1)}) custom-call(s32[1]{0:T(128)} %bitcast.1.side_ref, bf16[2,4,256,7168]{3,2,1,0:T(8,128)(2,1)} %rows_hbm.3, bf16[2,64,7168]{2,1,0:T(8,128)(2,1)S(1)} %copy-done, bf16[16,2,64,64]{3,2,1,0:T(8,128)(2,1)} %queries_hbm.1, ...), custom_call_target="tpu_custom_call" | custom-call | tf_op jit(solution)/shard_map/project_out/pallas_call | solution.py:164
  24.1 1.3 %collective-permute-start.4 = (f32[64,1024]{1,0:T(8,128)S(1)}, f32[64,1024]{1,0:T(8,128)S(1)}, u32[]{:S(2)}, u32[]{:S(2)}) collective-permute-start(f32[64,1024]{1,0:T(8,128)S(1)} %get-tuple-element.26), channel_id=1, source_target_pairs={{0,8},{12,4},{1,9},{13,5},{2,10},{14,6},{3,11},{15,7},{16,24},{28,... | collective-permute-start | bytes 786440 | tf_op jit(solution)/shard_map/ppermute | solution.py:194
  25.4 0.7 %collective-permute-start.5 = (f32[64,1024]{1,0:T(8,128)S(1)}, f32[64,1024]{1,0:T(8,128)S(1)}, u32[]{:S(2)}, u32[]{:S(2)}) collective-permute-start(f32[64,1024]{1,0:T(8,128)S(1)} %get-tuple-element.27), channel_id=1, source_target_pairs={{4,8},{8,4},{5,9},{9,5},{6,10},{10,6},{7,11},{11,7},{20,24},{24,20... | collective-permute-start | bytes 786440 | tf_op jit(solution)/shard_map/ppermute | solution.py:187
  26.1 0.0 collective-permute-done.1.refs_2_
  26.1 3.0 %collective-permute-start.3 = (f32[64,1024]{1,0:T(8,128)S(1)}, f32[64,1024]{1,0:T(8,128)S(1)}, u32[]{:S(2)}, u32[]{:S(2)}) collective-permute-start(f32[64,1024]{1,0:T(8,128)S(1)} %get-tuple-element.25.refs_0_), channel_id=1, source_target_pairs={{0,4},{12,8},{1,5},{13,9},{2,6},{14,10},{3,7},{15,11},{16,20},{28,... | collective-permute-start | bytes 786440 | tf_op jit(solution)/shard_map/ppermute | solution.py:193
  29.1 0.0 collective-permute-done.2.refs_3_
  29.1 0.0 collective-permute-done.refs_1_
  29.1 0.4 cov_in.1
  29.5 0.7 %collective-permute-start.10 = (bf16[8,64,128]{2,1,0:T(8,128)(2,1)S(1)}, bf16[8,64,128]{2,1,0:T(8,128)(2,1)S(1)}, u32[]{:S(2)}, u32[]{:S(2)}) collective-permute-start(bf16[8,64,128]{2,1,0:T(8,128)(2,1)S(1)} %get-tuple-element.30.refs_0_), channel_id=1, source_target_pairs={{4,7},{5,6},{6,5},{7,4},{8,11},{9,10},{10,9},{11,8},{20,23},{21,22... | collective-permute-start | bytes 393224 | tf_op jit(solution)/shard_map/ppermute | solution.py:415
  30.2 0.7 %collective-permute-start.9 = (bf16[8,64,128]{2,1,0:T(8,128)(2,1)S(1)}, bf16[8,64,128]{2,1,0:T(8,128)(2,1)S(1)}, u32[]{:S(2)}, u32[]{:S(2)}) collective-permute-start(bf16[8,64,128]{2,1,0:T(8,128)(2,1)S(1)} %get-tuple-element.30.refs_0_), channel_id=1, source_target_pairs={{4,6},{5,7},{6,4},{7,5},{8,10},{9,11},{10,8},{11,9},{20,22},{21,23... | collective-permute-start | bytes 393224 | tf_op jit(solution)/shard_map/ppermute | solution.py:415
  30.9 1.3 %collective-permute-done.4.refs_2_ = f32[64,1024]{1,0:T(8,128)S(1)} collective-permute-done((f32[64,1024]{1,0:T(8,128)S(1)}, f32[64,1024]{1,0:T(8,128)S(1)}, u32[]{:S(2)}, u32[]{:S(2)}) %collective-permute-start.4) | collective-permute-done | bytes 262176 | tf_op jit(solution)/shard_map/ppermute | solution.py:194
  32.2 0.7 %collective-permute-start.8 = (bf16[8,64,128]{2,1,0:T(8,128)(2,1)S(1)}, bf16[8,64,128]{2,1,0:T(8,128)(2,1)S(1)}, u32[]{:S(2)}, u32[]{:S(2)}) collective-permute-start(bf16[8,64,128]{2,1,0:T(8,128)(2,1)S(1)} %get-tuple-element.30.refs_0_), channel_id=1, source_target_pairs={{4,5},{5,4},{6,7},{7,6},{8,9},{9,8},{10,11},{11,10},{20,21},{21,20... | collective-permute-start | bytes 393224 | tf_op jit(solution)/shard_map/ppermute | solution.py:415
  32.8 0.0 collective-permute-done.5.refs_3_
  32.8 3.5 %collective-permute-done.3.refs_1_ = f32[64,1024]{1,0:T(8,128)S(1)} collective-permute-done((f32[64,1024]{1,0:T(8,128)S(1)}, f32[64,1024]{1,0:T(8,128)S(1)}, u32[]{:S(2)}, u32[]{:S(2)}) %collective-permute-start.3) | collective-permute-done | bytes 262176 | tf_op jit(solution)/shard_map/ppermute | solution.py:193
  36.3 1.0 %cov_out.1 = (f32[64,128]{1,0:T(8,128)S(1)}, f32[4,64,128]{2,1,0:T(8,128)S(1)}) custom-call(f32[64,1024]{1,0:T(8,128)S(1)} %get-tuple-element.23.x_ref, f32[64,128]{1,0:T(8,128)S(1)} %get-tuple-element.24.cov_ref, f32[64,1024]{1,0:T(8,128)S(1)} %get-tuple-element.25.refs_0_, f32[64,1024]{1,0:T(8,128)S(1)} %collective-permute-done.3.refs_1_, ...), custom_call_target="tpu_custom_call" | custom-call | tf_op jit(solution)/shard_map/cov_out/pallas_call | solution.py:255
  37.3 0.1 collective-permute-start.6
  37.4 1.2 %collective-permute-done.6 = f32[64,128]{1,0:T(8,128)S(1)} collective-permute-done((f32[64,128]{1,0:T(8,128)S(1)}, f32[64,128]{1,0:T(8,128)S(1)}, u32[]{:S(2)}, u32[]{:S(2)}) %collective-permute-start.6) | collective-permute-done | bytes 32800 | tf_op jit(solution)/shard_map/ppermute | solution.py:404
  38.6 1.5 %collective-permute-start.7 = (f32[64,128]{1,0:T(8,128)S(1)}, f32[64,128]{1,0:T(8,128)S(1)}, u32[]{:S(2)}, u32[]{:S(2)}) collective-permute-start(f32[64,128]{1,0:T(8,128)S(1)} %add.6.own_ref), channel_id=1, source_target_pairs={{0,2},{1,3},{2,0},{3,1},{4,6},{5,7},{6,4},{7,5},{8,10},{9,11},{10,... | collective-permute-start | bytes 98312 | tf_op jit(solution)/shard_map/ppermute | solution.py:404
  40.1 2.4 %collective-permute-done.7.other_ref = f32[64,128]{1,0:T(8,128)S(1)} collective-permute-done((f32[64,128]{1,0:T(8,128)S(1)}, f32[64,128]{1,0:T(8,128)S(1)}, u32[]{:S(2)}, u32[]{:S(2)}) %collective-permute-start.7) | collective-permute-done | bytes 32800 | tf_op jit(solution)/shard_map/ppermute | solution.py:404
  42.5 0.0 collective-permute-done.10.refs_3_
  42.5 0.0 collective-permute-done.9.refs_2_
  42.5 0.0 collective-permute-done.8.refs_1_
  42.5 3.7 %score.1 = f32[4,64]{1,0:T(4,128)S(1)} custom-call(s32[1]{0:T(128)} %bitcast.place_ref, f32[64,128]{1,0:T(8,128)S(1)} %add.6.own_ref, f32[64,128]{1,0:T(8,128)S(1)} %collective-permute-done.7.other_ref, f32[4,64,128]{2,1,0:T(8,128)S(1)} %get-tuple-element.29.sample_ref, bf16[8,64,128]{2,1,0:T(8,128)(2,1)S(1)} %get-tuple-element.30.refs_0_, ...), custom_call_target="tpu_custom_call" | custom-call | tf_op jit(solution)/shard_map/score/pallas_call | solution.py:389
  46.2 2.4 %collective-permute-start.13 = (f32[4,64]{1,0:T(4,128)S(1)}, f32[4,64]{1,0:T(4,128)S(1)}, u32[]{:S(2)}, u32[]{:S(2)}) collective-permute-start(f32[4,64]{1,0:T(4,128)S(1)} %score.1), channel_id=1, source_target_pairs={{0,12},{4,0},{8,4},{12,8},{1,13},{5,1},{9,5},{13,9},{2,14},{6,2},{... | collective-permute-start | bytes 3080 | tf_op jit(solution)/shard_map/ppermute | solution.py:409
  48.6 1.0 %collective-permute-start.12 = (f32[4,64]{1,0:T(4,128)S(1)}, f32[4,64]{1,0:T(4,128)S(1)}, u32[]{:S(2)}, u32[]{:S(2)}) collective-permute-start(f32[4,64]{1,0:T(4,128)S(1)} %score.1), channel_id=1, source_target_pairs={{0,4},{4,8},{8,12},{12,0},{1,5},{5,9},{9,13},{13,1},{2,6},{6,10},{... | collective-permute-start | bytes 3080 | tf_op jit(solution)/shard_map/ppermute | solution.py:409
  49.6 2.1 %collective-permute-start.11 = (f32[4,64]{1,0:T(4,128)S(1)}, f32[4,64]{1,0:T(4,128)S(1)}, u32[]{:S(2)}, u32[]{:S(2)}) collective-permute-start(f32[4,64]{1,0:T(4,128)S(1)} %score.1), channel_id=1, source_target_pairs={{0,8},{4,12},{8,0},{12,4},{1,9},{5,13},{9,1},{13,5},{2,10},{6,14},... | collective-permute-start | bytes 3080 | tf_op jit(solution)/shard_map/ppermute | solution.py:409
  51.7 0.0 collective-permute-done.13
  51.7 2.3 %collective-permute-done.12 = f32[4,64]{1,0:T(4,128)S(1)} collective-permute-done((f32[4,64]{1,0:T(4,128)S(1)}, f32[4,64]{1,0:T(4,128)S(1)}, u32[]{:S(2)}, u32[]{:S(2)}) %collective-permute-start.12) | collective-permute-done | bytes 1056 | tf_op jit(solution)/shard_map/ppermute | solution.py:409
  54.0 0.1 collective-permute-done.11
  54.1 0.6 %select_add_fusion = f32[4,64]{1,0:T(4,128)} fusion(f32[4,64]{1,0:T(4,128)S(1)} %collective-permute-done.12, f32[4,64]{1,0:T(4,128)S(1)} %collective-permute-done.13, f32[4,64]{1,0:T(4,128)S(1)} %score.1, f32[4,64]{1,0:T(4,128)S(1)} %collective-permute-done.11, pred[]{:T(512)S(6)} %ge.4, pred[]{:T(512)S(6)} %or.3), kind=kLoop, calls=%fused_computation | loop fusion | flops 768 | bytes 5122 | tf_op jit(solution)/shard_map/add | solution.py:443
  (1 shorter events, 0.0 us)
Async XLA Ops:
  0.0 13.7 %copy-start = (bf16[2,64,7168]{2,1,0:T(8,128)(2,1)S(1)}, bf16[2,64,7168]{2,1,0:T(8,128)(2,1)}, u32[]{:S(2)}) copy-start(bf16[2,64,7168]{2,1,0:T(8,128)(2,1)} %proj_ref.1) | copy-start | bytes 5505028
  3.9 22.2 %collective-permute-start.1 = (f32[64,1024]{1,0:T(8,128)S(1)}, f32[64,1024]{1,0:T(8,128)S(1)}, u32[]{:S(2)}, u32[]{:S(2)}) collective-permute-start(f32[64,1024]{1,0:T(8,128)S(1)} %get-tuple-element.21), channel_id=1, source_target_pairs={{0,8},{12,4},{1,9},{13,5},{2,10},{14,6},{3,11},{15,7},{16,24},{28,... | collective-permute-start | bytes 786440 | tf_op jit(solution)/shard_map/ppermute | solution.py:194
  9.9 19.2 %collective-permute-start.2 = (f32[64,1024]{1,0:T(8,128)S(1)}, f32[64,1024]{1,0:T(8,128)S(1)}, u32[]{:S(2)}, u32[]{:S(2)}) collective-permute-start(f32[64,1024]{1,0:T(8,128)S(1)} %get-tuple-element.22), channel_id=1, source_target_pairs={{4,8},{8,4},{5,9},{9,5},{6,10},{10,6},{7,11},{11,7},{20,24},{24,20... | collective-permute-start | bytes 786440 | tf_op jit(solution)/shard_map/ppermute | solution.py:187
  10.6 18.5 %collective-permute-start = (f32[64,1024]{1,0:T(8,128)S(1)}, f32[64,1024]{1,0:T(8,128)S(1)}, u32[]{:S(2)}, u32[]{:S(2)}) collective-permute-start(f32[64,1024]{1,0:T(8,128)S(1)} %get-tuple-element.20.refs_0_), channel_id=1, source_target_pairs={{0,4},{12,8},{1,5},{13,9},{2,6},{14,10},{3,7},{15,11},{16,20},{28,... | collective-permute-start | bytes 786440 | tf_op jit(solution)/shard_map/ppermute | solution.py:193
  24.1 8.1 %collective-permute-start.4 = (f32[64,1024]{1,0:T(8,128)S(1)}, f32[64,1024]{1,0:T(8,128)S(1)}, u32[]{:S(2)}, u32[]{:S(2)}) collective-permute-start(f32[64,1024]{1,0:T(8,128)S(1)} %get-tuple-element.26), channel_id=1, source_target_pairs={{0,8},{12,4},{1,9},{13,5},{2,10},{14,6},{3,11},{15,7},{16,24},{28,... | collective-permute-start | bytes 786440 | tf_op jit(solution)/shard_map/ppermute | solution.py:194
  25.4 7.4 %collective-permute-start.5 = (f32[64,1024]{1,0:T(8,128)S(1)}, f32[64,1024]{1,0:T(8,128)S(1)}, u32[]{:S(2)}, u32[]{:S(2)}) collective-permute-start(f32[64,1024]{1,0:T(8,128)S(1)} %get-tuple-element.27), channel_id=1, source_target_pairs={{4,8},{8,4},{5,9},{9,5},{6,10},{10,6},{7,11},{11,7},{20,24},{24,20... | collective-permute-start | bytes 786440 | tf_op jit(solution)/shard_map/ppermute | solution.py:187
  26.1 10.2 %collective-permute-start.3 = (f32[64,1024]{1,0:T(8,128)S(1)}, f32[64,1024]{1,0:T(8,128)S(1)}, u32[]{:S(2)}, u32[]{:S(2)}) collective-permute-start(f32[64,1024]{1,0:T(8,128)S(1)} %get-tuple-element.25.refs_0_), channel_id=1, source_target_pairs={{0,4},{12,8},{1,5},{13,9},{2,6},{14,10},{3,7},{15,11},{16,20},{28,... | collective-permute-start | bytes 786440 | tf_op jit(solution)/shard_map/ppermute | solution.py:193
  29.5 13.0 %collective-permute-start.10 = (bf16[8,64,128]{2,1,0:T(8,128)(2,1)S(1)}, bf16[8,64,128]{2,1,0:T(8,128)(2,1)S(1)}, u32[]{:S(2)}, u32[]{:S(2)}) collective-permute-start(bf16[8,64,128]{2,1,0:T(8,128)(2,1)S(1)} %get-tuple-element.30.refs_0_), channel_id=1, source_target_pairs={{4,7},{5,6},{6,5},{7,4},{8,11},{9,10},{10,9},{11,8},{20,23},{21,22... | collective-permute-start | bytes 393224 | tf_op jit(solution)/shard_map/ppermute | solution.py:415
  30.2 12.3 %collective-permute-start.9 = (bf16[8,64,128]{2,1,0:T(8,128)(2,1)S(1)}, bf16[8,64,128]{2,1,0:T(8,128)(2,1)S(1)}, u32[]{:S(2)}, u32[]{:S(2)}) collective-permute-start(bf16[8,64,128]{2,1,0:T(8,128)(2,1)S(1)} %get-tuple-element.30.refs_0_), channel_id=1, source_target_pairs={{4,6},{5,7},{6,4},{7,5},{8,10},{9,11},{10,8},{11,9},{20,22},{21,23... | collective-permute-start | bytes 393224 | tf_op jit(solution)/shard_map/ppermute | solution.py:415
  32.2 10.3 %collective-permute-start.8 = (bf16[8,64,128]{2,1,0:T(8,128)(2,1)S(1)}, bf16[8,64,128]{2,1,0:T(8,128)(2,1)S(1)}, u32[]{:S(2)}, u32[]{:S(2)}) collective-permute-start(bf16[8,64,128]{2,1,0:T(8,128)(2,1)S(1)} %get-tuple-element.30.refs_0_), channel_id=1, source_target_pairs={{4,5},{5,4},{6,7},{7,6},{8,9},{9,8},{10,11},{11,10},{20,21},{21,20... | collective-permute-start | bytes 393224 | tf_op jit(solution)/shard_map/ppermute | solution.py:415
  37.3 1.3 %collective-permute-start.6 = (f32[64,128]{1,0:T(8,128)S(1)}, f32[64,128]{1,0:T(8,128)S(1)}, u32[]{:S(2)}, u32[]{:S(2)}) collective-permute-start(f32[64,128]{1,0:T(8,128)S(1)} %get-tuple-element.28), channel_id=1, source_target_pairs={{0,1},{1,0},{2,3},{3,2},{4,5},{5,4},{6,7},{7,6},{8,9},{9,8},{10,11... | collective-permute-start | bytes 98312 | tf_op jit(solution)/shard_map/ppermute | solution.py:404
  38.6 3.9 %collective-permute-start.7 = (f32[64,128]{1,0:T(8,128)S(1)}, f32[64,128]{1,0:T(8,128)S(1)}, u32[]{:S(2)}, u32[]{:S(2)}) collective-permute-start(f32[64,128]{1,0:T(8,128)S(1)} %add.6.own_ref), channel_id=1, source_target_pairs={{0,2},{1,3},{2,0},{3,1},{4,6},{5,7},{6,4},{7,5},{8,10},{9,11},{10,... | collective-permute-start | bytes 98312 | tf_op jit(solution)/shard_map/ppermute | solution.py:404
  46.2 5.4 %collective-permute-start.13 = (f32[4,64]{1,0:T(4,128)S(1)}, f32[4,64]{1,0:T(4,128)S(1)}, u32[]{:S(2)}, u32[]{:S(2)}) collective-permute-start(f32[4,64]{1,0:T(4,128)S(1)} %score.1), channel_id=1, source_target_pairs={{0,12},{4,0},{8,4},{12,8},{1,13},{5,1},{9,5},{13,9},{2,14},{6,2},{... | collective-permute-start | bytes 3080 | tf_op jit(solution)/shard_map/ppermute | solution.py:409
  48.6 5.4 %collective-permute-start.12 = (f32[4,64]{1,0:T(4,128)S(1)}, f32[4,64]{1,0:T(4,128)S(1)}, u32[]{:S(2)}, u32[]{:S(2)}) collective-permute-start(f32[4,64]{1,0:T(4,128)S(1)} %score.1), channel_id=1, source_target_pairs={{0,4},{4,8},{8,12},{12,0},{1,5},{5,9},{9,13},{13,1},{2,6},{6,10},{... | collective-permute-start | bytes 3080 | tf_op jit(solution)/shard_map/ppermute | solution.py:409
  49.6 4.5 %collective-permute-start.11 = (f32[4,64]{1,0:T(4,128)S(1)}, f32[4,64]{1,0:T(4,128)S(1)}, u32[]{:S(2)}, u32[]{:S(2)}) collective-permute-start(f32[4,64]{1,0:T(4,128)S(1)} %score.1), channel_id=1, source_target_pairs={{0,8},{4,12},{8,0},{12,4},{1,9},{5,13},{9,1},{13,5},{2,10},{6,14},... | collective-permute-start | bytes 3080 | tf_op jit(solution)/shard_map/ppermute | solution.py:409

commit v16 on v15

--- a/solution.py
+++ b/solution.py
@@ -319,12 +319,13 @@
     return x / unit
 
 
-def score_kernel(tokens, place_ref, own_ref, other_ref, sample_ref, *refs):
-    pieces, (out, held, half) = refs[:-3], refs[-3:]
+def score_kernel(tokens, place_ref, sample_ref, *refs):
+    (out, held, half) = refs[-3:]
     parts = held.shape[0]
+    covs, pieces = refs[:parts], refs[parts : 2 * parts]
     for k, piece in enumerate(pieces):
         held[place_ref[0] ^ k] = piece[...]
-    pair = (own_ref[...] + other_ref[...]) / tokens
+    pair = total(covs) / tokens
     size, both = pair.shape
     inverses = damped_inverses(pair)
     samples = [sample_ref[s] for s in range(sample_ref.shape[0])]
@@ -381,14 +382,14 @@
             ]
 
 
-def score(place, own, other, sample, pieces, tokens):
+def score(place, covs, sample, pieces, tokens):
     blocks, rank, both = pieces[0].shape
     parts = len(pieces)
     pairs = parts * blocks
     seqs = sample.shape[0]
     return pl.pallas_call(
         functools.partial(score_kernel, tokens),
-        in_specs=[smem()] + [vmem()] * (3 + len(pieces)),
+        in_specs=[smem(), vmem()] + [vmem()] * (len(covs) + len(pieces)),
         out_specs=vmem(),
         out_shape=jax.ShapeDtypeStruct((seqs, 2 * pairs), jnp.float32),
         scratch_shapes=[
@@ -397,7 +398,7 @@
         ],
         compiler_params=params(16),
         name="score",
-    )(place, own, other, sample, *pieces)
+    )(place, sample, *covs, *pieces)
 
 
 def swap(value, axis, bit):
@@ -429,18 +430,13 @@
     packed, x, cov = cov_in(packed, x_pieces)
     query_pieces = [packed] + [owners_swap(packed, bits) for bits in range(1, parts)]
     cov, sample = cov_out(x, cov, pieces, seqs)
-    other = jnp.zeros_like(cov)
-    bit = 1
-    while bit < parts:
-        cov = cov if bit == 1 else cov + other
-        other = swap(cov, "dp", bit)
-        bit *= 2
-    scores = score(place, cov, other, sample, query_pieces, tokens)
+    covs = [cov] + [swap(cov, "dp", bits) for bits in range(1, parts)]
+    scores = score(place, covs, sample, query_pieces, tokens)
+    owner = (column == 1) | (column == 2)
+    below = shift(scores, "tensor", 1)
     above = shift(scores, "tensor", -1)
     opposite = shift(scores, "tensor", 2)
-    below = shift(scores, "tensor", 1)
-    owner = (column == 1) | (column == 2)
-    return jnp.where(owner, scores, opposite) + jnp.where(column >= 2, below, above)
+    return jnp.where(column >= 2, below, above) + jnp.where(owner, scores, opposite)
 
 
 def damp(matrix):

time: 55 us -> 58.1 us (1.056)
  waiting for transfers between devices: 10.8 us -> 13.3 us
  starting transfers between devices: 23.6 us -> 24.3 us
    ppermute x3, waiting for transfers between devices: 2.42 us -> 5.38 us  [shift(): lax.ppermute(value, axis, [(i, (i + by) % size) for i in range(size)])]
    ppermute x2 -> x3, waiting for transfers between devices: 3.61 us -> 3.15 us  [swap(): lax.ppermute(value, axis, [(i, i ^ bit) for i in range(lax.axis_size(axis...]
    ppermute x2 -> x3, starting transfers between devices: 1.57 us -> 1.75 us  [swap(): lax.ppermute(value, axis, [(i, i ^ bit) for i in range(lax.axis_size(axis...]
  transfers between devices with their start and end apart: 14 -> 15, of which waited for: 6 -> 7; matrix products, arithmetic and copies ran while one was open for 0% -> 0% of each run, Pallas kernels for 22% -> 20%
where the time goes in v16:
time: 58.1 us; the launch traced here: 57.8 us
  starting transfers between devices  24.3 us (42%)
  Pallas kernels  19.4 us (33%)
  waiting for transfers between devices  13.3 us (23%)
    pallas_call x1, Pallas kernels, project_out(): pl.pallas_call(project_out_kernel, in_specs=[smem(), hbm(), vmem(), hbm()...  10.4 us
    ppermute x2, starting transfers between devices, to_owner(): lax.ppermute(far, 'tensor', [(0, 2), (3, 1)])  7.26 us
    ppermute x2, starting transfers between devices, to_owner(): lax.ppermute(near, 'tensor', [(0, 1), (3, 2)])  6.04 us
    ppermute x3, starting transfers between devices, shift(): lax.ppermute(value, axis, [(i, (i + by) % size) for i in range(size)])  5.92 us
    ppermute x3, waiting for transfers between devices, shift(): lax.ppermute(value, axis, [(i, (i + by) % size) for i in range(size)])  5.38 us
    pallas_call x1, Pallas kernels, project_in(): pl.pallas_call(project_in_kernel, in_specs=[smem(), hbm(), hbm(), hbm()],...  3.91 us
    pallas_call x1, Pallas kernels, score(): pl.pallas_call(functools.partial(score_kernel, tokens), in_specs=[smem(),...  3.75 us
    ppermute x2, waiting for transfers between devices, to_owner(): lax.ppermute(near, 'tensor', [(0, 1), (3, 2)])  3.47 us
  transfers between devices with their start and end apart: 15, of which 7 were waited for; matrix products, arithmetic and copies ran while one was open for 0% of the time, Pallas kernels for 20%

profile of v16, /device:TPU:0, one launch (start us, length us, event | category | flops | bytes accessed | tf_op | source)
XLA Modules:
  0.0 57.8 jit_solution(13254202317742800902)
XLA Ops:
  0.0 0.0 copy-start
  0.0 3.9 %project_in.1 = (f32[64,1024]{1,0:T(8,128)S(1)}, f32[64,1024]{1,0:T(8,128)S(1)}, f32[64,1024]{1,0:T(8,128)S(1)}, bf16[2,256,3584]{2,1,0:T(8,128)(2,1)S(1)}) custom-call(s32[1]{0:T(128)} %bitcast.1.side_ref, bf16[4,256,2048]{2,1,0:T(8,128)(2,1)} %rows_hbm.2, bf16[2,64,2048]{2,1,0:T(8,128)(2,1)} %proj_hbm.1, bf16[2,4,256,7168]{3,2,1,0:T(8,128)(2,1)} %rows_hbm.3), custom_call_target="tpu_custom_call" | custom-call | tf_op jit(solution)/shard_map/project_in/pallas_call | solution.py:92
  3.9 6.0 %collective-permute-start.1 = (f32[64,1024]{1,0:T(8,128)S(1)}, f32[64,1024]{1,0:T(8,128)S(1)}, u32[]{:S(2)}, u32[]{:S(2)}) collective-permute-start(f32[64,1024]{1,0:T(8,128)S(1)} %get-tuple-element.21), channel_id=1, source_target_pairs={{0,8},{12,4},{1,9},{13,5},{2,10},{14,6},{3,11},{15,7},{16,24},{28,... | collective-permute-start | bytes 786440 | tf_op jit(solution)/shard_map/ppermute | solution.py:194
  9.9 0.7 %collective-permute-start.2 = (f32[64,1024]{1,0:T(8,128)S(1)}, f32[64,1024]{1,0:T(8,128)S(1)}, u32[]{:S(2)}, u32[]{:S(2)}) collective-permute-start(f32[64,1024]{1,0:T(8,128)S(1)} %get-tuple-element.22), channel_id=1, source_target_pairs={{4,8},{8,4},{5,9},{9,5},{6,10},{10,6},{7,11},{11,7},{20,24},{24,20... | collective-permute-start | bytes 786440 | tf_op jit(solution)/shard_map/ppermute | solution.py:187
  10.6 3.1 %collective-permute-start = (f32[64,1024]{1,0:T(8,128)S(1)}, f32[64,1024]{1,0:T(8,128)S(1)}, u32[]{:S(2)}, u32[]{:S(2)}) collective-permute-start(f32[64,1024]{1,0:T(8,128)S(1)} %get-tuple-element.20.refs_0_), channel_id=1, source_target_pairs={{0,4},{12,8},{1,5},{13,9},{2,6},{14,10},{3,7},{15,11},{16,20},{28,... | collective-permute-start | bytes 786440 | tf_op jit(solution)/shard_map/ppermute | solution.py:193
  13.7 0.0 copy-done
  13.7 10.4 %project_out.1 = (f32[64,1024]{1,0:T(8,128)S(1)}, f32[64,1024]{1,0:T(8,128)S(1)}, f32[64,1024]{1,0:T(8,128)S(1)}, bf16[8,64,128]{2,1,0:T(8,128)(2,1)S(1)}) custom-call(s32[1]{0:T(128)} %bitcast.1.side_ref, bf16[2,4,256,7168]{3,2,1,0:T(8,128)(2,1)} %rows_hbm.3, bf16[2,64,7168]{2,1,0:T(8,128)(2,1)S(1)} %copy-done, bf16[16,2,64,64]{3,2,1,0:T(8,128)(2,1)} %queries_hbm.1, ...), custom_call_target="tpu_custom_call" | custom-call | tf_op jit(solution)/shard_map/project_out/pallas_call | solution.py:164
  24.1 1.3 %collective-permute-start.4 = (f32[64,1024]{1,0:T(8,128)S(1)}, f32[64,1024]{1,0:T(8,128)S(1)}, u32[]{:S(2)}, u32[]{:S(2)}) collective-permute-start(f32[64,1024]{1,0:T(8,128)S(1)} %get-tuple-element.26), channel_id=1, source_target_pairs={{0,8},{12,4},{1,9},{13,5},{2,10},{14,6},{3,11},{15,7},{16,24},{28,... | collective-permute-start | bytes 786440 | tf_op jit(solution)/shard_map/ppermute | solution.py:194
  25.4 0.7 %collective-permute-start.5 = (f32[64,1024]{1,0:T(8,128)S(1)}, f32[64,1024]{1,0:T(8,128)S(1)}, u32[]{:S(2)}, u32[]{:S(2)}) collective-permute-start(f32[64,1024]{1,0:T(8,128)S(1)} %get-tuple-element.27), channel_id=1, source_target_pairs={{4,8},{8,4},{5,9},{9,5},{6,10},{10,6},{7,11},{11,7},{20,24},{24,20... | collective-permute-start | bytes 786440 | tf_op jit(solution)/shard_map/ppermute | solution.py:187
  26.1 0.0 collective-permute-done.1.refs_2_
  26.1 3.0 %collective-permute-start.3 = (f32[64,1024]{1,0:T(8,128)S(1)}, f32[64,1024]{1,0:T(8,128)S(1)}, u32[]{:S(2)}, u32[]{:S(2)}) collective-permute-start(f32[64,1024]{1,0:T(8,128)S(1)} %get-tuple-element.25.refs_0_), channel_id=1, source_target_pairs={{0,4},{12,8},{1,5},{13,9},{2,6},{14,10},{3,7},{15,11},{16,20},{28,... | collective-permute-start | bytes 786440 | tf_op jit(solution)/shard_map/ppermute | solution.py:193
  29.1 0.0 collective-permute-done.2.refs_3_
  29.1 0.0 collective-permute-done.refs_1_
  29.1 0.4 cov_in.1
  29.5 0.7 %collective-permute-start.11 = (bf16[8,64,128]{2,1,0:T(8,128)(2,1)S(1)}, bf16[8,64,128]{2,1,0:T(8,128)(2,1)S(1)}, u32[]{:S(2)}, u32[]{:S(2)}) collective-permute-start(bf16[8,64,128]{2,1,0:T(8,128)(2,1)S(1)} %get-tuple-element.30.refs_4_), channel_id=1, source_target_pairs={{4,7},{5,6},{6,5},{7,4},{8,11},{9,10},{10,9},{11,8},{20,23},{21,22... | collective-permute-start | bytes 393224 | tf_op jit(solution)/shard_map/ppermute | solution.py:416
  30.2 0.7 %collective-permute-start.10 = (bf16[8,64,128]{2,1,0:T(8,128)(2,1)S(1)}, bf16[8,64,128]{2,1,0:T(8,128)(2,1)S(1)}, u32[]{:S(2)}, u32[]{:S(2)}) collective-permute-start(bf16[8,64,128]{2,1,0:T(8,128)(2,1)S(1)} %get-tuple-element.30.refs_4_), channel_id=1, source_target_pairs={{4,6},{5,7},{6,4},{7,5},{8,10},{9,11},{10,8},{11,9},{20,22},{21,23... | collective-permute-start | bytes 393224 | tf_op jit(solution)/shard_map/ppermute | solution.py:416
  30.9 1.3 %collective-permute-done.4.refs_2_ = f32[64,1024]{1,0:T(8,128)S(1)} collective-permute-done((f32[64,1024]{1,0:T(8,128)S(1)}, f32[64,1024]{1,0:T(8,128)S(1)}, u32[]{:S(2)}, u32[]{:S(2)}) %collective-permute-start.4) | collective-permute-done | bytes 262176 | tf_op jit(solution)/shard_map/ppermute | solution.py:194
  32.2 0.7 %collective-permute-start.9 = (bf16[8,64,128]{2,1,0:T(8,128)(2,1)S(1)}, bf16[8,64,128]{2,1,0:T(8,128)(2,1)S(1)}, u32[]{:S(2)}, u32[]{:S(2)}) collective-permute-start(bf16[8,64,128]{2,1,0:T(8,128)(2,1)S(1)} %get-tuple-element.30.refs_4_), channel_id=1, source_target_pairs={{4,5},{5,4},{6,7},{7,6},{8,9},{9,8},{10,11},{11,10},{20,21},{21,20... | collective-permute-start | bytes 393224 | tf_op jit(solution)/shard_map/ppermute | solution.py:416
  32.8 0.0 collective-permute-done.5.refs_3_
  32.8 3.5 %collective-permute-done.3.refs_1_ = f32[64,1024]{1,0:T(8,128)S(1)} collective-permute-done((f32[64,1024]{1,0:T(8,128)S(1)}, f32[64,1024]{1,0:T(8,128)S(1)}, u32[]{:S(2)}, u32[]{:S(2)}) %collective-permute-start.3) | collective-permute-done | bytes 262176 | tf_op jit(solution)/shard_map/ppermute | solution.py:193
  36.3 1.0 %cov_out.1 = (f32[64,128]{1,0:T(8,128)S(1)}, f32[4,64,128]{2,1,0:T(8,128)S(1)}) custom-call(f32[64,1024]{1,0:T(8,128)S(1)} %get-tuple-element.23.x_ref, f32[64,128]{1,0:T(8,128)S(1)} %get-tuple-element.24.cov_ref, f32[64,1024]{1,0:T(8,128)S(1)} %get-tuple-element.25.refs_0_, f32[64,1024]{1,0:T(8,128)S(1)} %collective-permute-done.3.refs_1_, ...), custom_call_target="tpu_custom_call" | custom-call | tf_op jit(solution)/shard_map/cov_out/pallas_call | solution.py:255
  37.3 0.1 collective-permute-start.8
  37.4 1.6 %collective-permute-start.7 = (f32[64,128]{1,0:T(8,128)S(1)}, f32[64,128]{1,0:T(8,128)S(1)}, u32[]{:S(2)}, u32[]{:S(2)}) collective-permute-start(f32[64,128]{1,0:T(8,128)S(1)} %get-tuple-element.29.refs_0_), channel_id=1, source_target_pairs={{0,2},{1,3},{2,0},{3,1},{4,6},{5,7},{6,4},{7,5},{8,10},{9,11},{10,... | collective-permute-start | bytes 98312 | tf_op jit(solution)/shard_map/ppermute | solution.py:405
  38.9 2.1 %collective-permute-done.8.refs_3_ = f32[64,128]{1,0:T(8,128)S(1)} collective-permute-done((f32[64,128]{1,0:T(8,128)S(1)}, f32[64,128]{1,0:T(8,128)S(1)}, u32[]{:S(2)}, u32[]{:S(2)}) %collective-permute-start.8) | collective-permute-done | bytes 32800 | tf_op jit(solution)/shard_map/ppermute | solution.py:405
  41.0 0.1 collective-permute-start.6
  41.1 0.3 collective-permute-done.7.refs_2_
  41.4 0.8 %collective-permute-done.6.refs_1_ = f32[64,128]{1,0:T(8,128)S(1)} collective-permute-done((f32[64,128]{1,0:T(8,128)S(1)}, f32[64,128]{1,0:T(8,128)S(1)}, u32[]{:S(2)}, u32[]{:S(2)}) %collective-permute-start.6) | collective-permute-done | bytes 32800 | tf_op jit(solution)/shard_map/ppermute | solution.py:405
  42.2 0.0 collective-permute-done.11.refs_7_
  42.2 0.0 collective-permute-done.10.refs_6_
  42.2 0.0 collective-permute-done.9.refs_5_
  42.2 3.7 %score.1 = f32[4,64]{1,0:T(4,128)S(1)} custom-call(s32[1]{0:T(128)} %bitcast.place_ref, f32[4,64,128]{2,1,0:T(8,128)S(1)} %get-tuple-element.28.sample_ref, f32[64,128]{1,0:T(8,128)S(1)} %get-tuple-element.29.refs_0_, f32[64,128]{1,0:T(8,128)S(1)} %collective-permute-done.6.refs_1_, f32[64,128]{1,0:T(8,128)S(1)} %collective-permute-done.7.refs_2_, ...), custom_call_target="tpu_custom_call" | custom-call | tf_op jit(solution)/shard_map/score/pallas_call | solution.py:390
  46.0 3.6 %collective-permute-start.14 = (f32[4,64]{1,0:T(4,128)S(1)}, f32[4,64]{1,0:T(4,128)S(1)}, u32[]{:S(2)}, u32[]{:S(2)}) collective-permute-start(f32[4,64]{1,0:T(4,128)S(1)} %score.1), channel_id=1, source_target_pairs={{0,8},{4,12},{8,0},{12,4},{1,9},{5,13},{9,1},{13,5},{2,10},{6,14},... | collective-permute-start | bytes 3080 | tf_op jit(solution)/shard_map/ppermute | solution.py:410
  49.5 2.3 %collective-permute-start.13 = (f32[4,64]{1,0:T(4,128)S(1)}, f32[4,64]{1,0:T(4,128)S(1)}, u32[]{:S(2)}, u32[]{:S(2)}) collective-permute-start(f32[4,64]{1,0:T(4,128)S(1)} %score.1), channel_id=1, source_target_pairs={{0,12},{4,0},{8,4},{12,8},{1,13},{5,1},{9,5},{13,9},{2,14},{6,2},{... | collective-permute-start | bytes 3080 | tf_op jit(solution)/shard_map/ppermute | solution.py:410
  51.9 0.0 collective-permute-start.12
  51.9 0.0 collective-permute-done.14
  51.9 1.3 %collective-permute-done.13 = f32[4,64]{1,0:T(4,128)S(1)} collective-permute-done((f32[4,64]{1,0:T(4,128)S(1)}, f32[4,64]{1,0:T(4,128)S(1)}, u32[]{:S(2)}, u32[]{:S(2)}) %collective-permute-start.13) | collective-permute-done | bytes 1056 | tf_op jit(solution)/shard_map/ppermute | solution.py:410
  53.2 4.1 %collective-permute-done.12 = f32[4,64]{1,0:T(4,128)S(1)} collective-permute-done((f32[4,64]{1,0:T(4,128)S(1)}, f32[4,64]{1,0:T(4,128)S(1)}, u32[]{:S(2)}, u32[]{:S(2)}) %collective-permute-start.12) | collective-permute-done | bytes 1056 | tf_op jit(solution)/shard_map/ppermute | solution.py:410
  57.3 0.6 %select_add_fusion = f32[4,64]{1,0:T(4,128)} fusion(f32[4,64]{1,0:T(4,128)S(1)} %score.1, f32[4,64]{1,0:T(4,128)S(1)} %collective-permute-done.14, f32[4,64]{1,0:T(4,128)S(1)} %collective-permute-done.12, f32[4,64]{1,0:T(4,128)S(1)} %collective-permute-done.13, pred[]{:T(512)S(6)} %or.3, pred[]{:T(512)S(6)} %ge.4), kind=kLoop, calls=%fused_computation | loop fusion | flops 768 | bytes 5122 | tf_op jit(solution)/shard_map/add | solution.py:439
Async XLA Ops:
  0.0 13.7 %copy-start = (bf16[2,64,7168]{2,1,0:T(8,128)(2,1)S(1)}, bf16[2,64,7168]{2,1,0:T(8,128)(2,1)}, u32[]{:S(2)}) copy-start(bf16[2,64,7168]{2,1,0:T(8,128)(2,1)} %proj_ref.1) | copy-start | bytes 5505028
  3.9 22.2 %collective-permute-start.1 = (f32[64,1024]{1,0:T(8,128)S(1)}, f32[64,1024]{1,0:T(8,128)S(1)}, u32[]{:S(2)}, u32[]{:S(2)}) collective-permute-start(f32[64,1024]{1,0:T(8,128)S(1)} %get-tuple-element.21), channel_id=1, source_target_pairs={{0,8},{12,4},{1,9},{13,5},{2,10},{14,6},{3,11},{15,7},{16,24},{28,... | collective-permute-start | bytes 786440 | tf_op jit(solution)/shard_map/ppermute | solution.py:194
  9.9 19.2 %collective-permute-start.2 = (f32[64,1024]{1,0:T(8,128)S(1)}, f32[64,1024]{1,0:T(8,128)S(1)}, u32[]{:S(2)}, u32[]{:S(2)}) collective-permute-start(f32[64,1024]{1,0:T(8,128)S(1)} %get-tuple-element.22), channel_id=1, source_target_pairs={{4,8},{8,4},{5,9},{9,5},{6,10},{10,6},{7,11},{11,7},{20,24},{24,20... | collective-permute-start | bytes 786440 | tf_op jit(solution)/shard_map/ppermute | solution.py:187
  10.6 18.5 %collective-permute-start = (f32[64,1024]{1,0:T(8,128)S(1)}, f32[64,1024]{1,0:T(8,128)S(1)}, u32[]{:S(2)}, u32[]{:S(2)}) collective-permute-start(f32[64,1024]{1,0:T(8,128)S(1)} %get-tuple-element.20.refs_0_), channel_id=1, source_target_pairs={{0,4},{12,8},{1,5},{13,9},{2,6},{14,10},{3,7},{15,11},{16,20},{28,... | collective-permute-start | bytes 786440 | tf_op jit(solution)/shard_map/ppermute | solution.py:193
  24.1 8.1 %collective-permute-start.4 = (f32[64,1024]{1,0:T(8,128)S(1)}, f32[64,1024]{1,0:T(8,128)S(1)}, u32[]{:S(2)}, u32[]{:S(2)}) collective-permute-start(f32[64,1024]{1,0:T(8,128)S(1)} %get-tuple-element.26), channel_id=1, source_target_pairs={{0,8},{12,4},{1,9},{13,5},{2,10},{14,6},{3,11},{15,7},{16,24},{28,... | collective-permute-start | bytes 786440 | tf_op jit(solution)/shard_map/ppermute | solution.py:194
  25.4 7.4 %collective-permute-start.5 = (f32[64,1024]{1,0:T(8,128)S(1)}, f32[64,1024]{1,0:T(8,128)S(1)}, u32[]{:S(2)}, u32[]{:S(2)}) collective-permute-start(f32[64,1024]{1,0:T(8,128)S(1)} %get-tuple-element.27), channel_id=1, source_target_pairs={{4,8},{8,4},{5,9},{9,5},{6,10},{10,6},{7,11},{11,7},{20,24},{24,20... | collective-permute-start | bytes 786440 | tf_op jit(solution)/shard_map/ppermute | solution.py:187
  26.1 10.2 %collective-permute-start.3 = (f32[64,1024]{1,0:T(8,128)S(1)}, f32[64,1024]{1,0:T(8,128)S(1)}, u32[]{:S(2)}, u32[]{:S(2)}) collective-permute-start(f32[64,1024]{1,0:T(8,128)S(1)} %get-tuple-element.25.refs_0_), channel_id=1, source_target_pairs={{0,4},{12,8},{1,5},{13,9},{2,6},{14,10},{3,7},{15,11},{16,20},{28,... | collective-permute-start | bytes 786440 | tf_op jit(solution)/shard_map/ppermute | solution.py:193
  29.5 12.7 %collective-permute-start.11 = (bf16[8,64,128]{2,1,0:T(8,128)(2,1)S(1)}, bf16[8,64,128]{2,1,0:T(8,128)(2,1)S(1)}, u32[]{:S(2)}, u32[]{:S(2)}) collective-permute-start(bf16[8,64,128]{2,1,0:T(8,128)(2,1)S(1)} %get-tuple-element.30.refs_4_), channel_id=1, source_target_pairs={{4,7},{5,6},{6,5},{7,4},{8,11},{9,10},{10,9},{11,8},{20,23},{21,22... | collective-permute-start | bytes 393224 | tf_op jit(solution)/shard_map/ppermute | solution.py:416
  30.2 12.0 %collective-permute-start.10 = (bf16[8,64,128]{2,1,0:T(8,128)(2,1)S(1)}, bf16[8,64,128]{2,1,0:T(8,128)(2,1)S(1)}, u32[]{:S(2)}, u32[]{:S(2)}) collective-permute-start(bf16[8,64,128]{2,1,0:T(8,128)(2,1)S(1)} %get-tuple-element.30.refs_4_), channel_id=1, source_target_pairs={{4,6},{5,7},{6,4},{7,5},{8,10},{9,11},{10,8},{11,9},{20,22},{21,23... | collective-permute-start | bytes 393224 | tf_op jit(solution)/shard_map/ppermute | solution.py:416
  32.2 10.0 %collective-permute-start.9 = (bf16[8,64,128]{2,1,0:T(8,128)(2,1)S(1)}, bf16[8,64,128]{2,1,0:T(8,128)(2,1)S(1)}, u32[]{:S(2)}, u32[]{:S(2)}) collective-permute-start(bf16[8,64,128]{2,1,0:T(8,128)(2,1)S(1)} %get-tuple-element.30.refs_4_), channel_id=1, source_target_pairs={{4,5},{5,4},{6,7},{7,6},{8,9},{9,8},{10,11},{11,10},{20,21},{21,20... | collective-permute-start | bytes 393224 | tf_op jit(solution)/shard_map/ppermute | solution.py:416
  37.3 3.7 %collective-permute-start.8 = (f32[64,128]{1,0:T(8,128)S(1)}, f32[64,128]{1,0:T(8,128)S(1)}, u32[]{:S(2)}, u32[]{:S(2)}) collective-permute-start(f32[64,128]{1,0:T(8,128)S(1)} %get-tuple-element.29.refs_0_), channel_id=1, source_target_pairs={{0,3},{1,2},{2,1},{3,0},{4,7},{5,6},{6,5},{7,4},{8,11},{9,10},{10,... | collective-permute-start | bytes 98312 | tf_op jit(solution)/shard_map/ppermute | solution.py:405
  37.4 4.0 %collective-permute-start.7 = (f32[64,128]{1,0:T(8,128)S(1)}, f32[64,128]{1,0:T(8,128)S(1)}, u32[]{:S(2)}, u32[]{:S(2)}) collective-permute-start(f32[64,128]{1,0:T(8,128)S(1)} %get-tuple-element.29.refs_0_), channel_id=1, source_target_pairs={{0,2},{1,3},{2,0},{3,1},{4,6},{5,7},{6,4},{7,5},{8,10},{9,11},{10,... | collective-permute-start | bytes 98312 | tf_op jit(solution)/shard_map/ppermute | solution.py:405
  41.0 1.2 %collective-permute-start.6 = (f32[64,128]{1,0:T(8,128)S(1)}, f32[64,128]{1,0:T(8,128)S(1)}, u32[]{:S(2)}, u32[]{:S(2)}) collective-permute-start(f32[64,128]{1,0:T(8,128)S(1)} %get-tuple-element.29.refs_0_), channel_id=1, source_target_pairs={{0,1},{1,0},{2,3},{3,2},{4,5},{5,4},{6,7},{7,6},{8,9},{9,8},{10,11... | collective-permute-start | bytes 98312 | tf_op jit(solution)/shard_map/ppermute | solution.py:405
  46.0 5.9 %collective-permute-start.14 = (f32[4,64]{1,0:T(4,128)S(1)}, f32[4,64]{1,0:T(4,128)S(1)}, u32[]{:S(2)}, u32[]{:S(2)}) collective-permute-start(f32[4,64]{1,0:T(4,128)S(1)} %score.1), channel_id=1, source_target_pairs={{0,8},{4,12},{8,0},{12,4},{1,9},{5,13},{9,1},{13,5},{2,10},{6,14},... | collective-permute-start | bytes 3080 | tf_op jit(solution)/shard_map/ppermute | solution.py:410
  49.5 3.7 %collective-permute-start.13 = (f32[4,64]{1,0:T(4,128)S(1)}, f32[4,64]{1,0:T(4,128)S(1)}, u32[]{:S(2)}, u32[]{:S(2)}) collective-permute-start(f32[4,64]{1,0:T(4,128)S(1)} %score.1), channel_id=1, source_target_pairs={{0,12},{4,0},{8,4},{12,8},{1,13},{5,1},{9,5},{13,9},{2,14},{6,2},{... | collective-permute-start | bytes 3080 | tf_op jit(solution)/shard_map/ppermute | solution.py:410
  51.9 5.4 %collective-permute-start.12 = (f32[4,64]{1,0:T(4,128)S(1)}, f32[4,64]{1,0:T(4,128)S(1)}, u32[]{:S(2)}, u32[]{:S(2)}) collective-permute-start(f32[4,64]{1,0:T(4,128)S(1)} %score.1), channel_id=1, source_target_pairs={{0,4},{4,8},{8,12},{12,0},{1,5},{5,9},{9,13},{13,1},{2,6},{6,10},{... | collective-permute-start | bytes 3080 | tf_op jit(solution)/shard_map/ppermute | solution.py:410

commit v17 on v14

--- a/solution.py
+++ b/solution.py
@@ -432,12 +432,8 @@
         bit *= 2
     scores = score(place, cov, other, sample, query_pieces, tokens)
     owner = (column == 1) | (column == 2)
-    pieces = [
-        across(scores),
-        lax.ppermute(scores, "tensor", [(1, 0), (2, 3)]),
-        lax.ppermute(scores, "tensor", [(2, 0), (1, 3)]),
-    ]
-    return jnp.where(owner, scores, 0.0) + pieces[0] + pieces[1] + pieces[2]
+    one, two, three = (swap(scores, "tensor", bits) for bits in (1, 2, 3))
+    return jnp.where(~owner, one, scores) + jnp.where(~owner, two, three)
 
 
 def damp(matrix):

time: 55.8 us -> 55.5 us (level)
  the two profiles are of different devices: /device:TPU:8 before, /device:TPU:0 now
where the time goes in v17:
time: 55.5 us; the launch traced here: 55.2 us
  starting transfers between devices  23.1 us (42%)
  Pallas kernels  19.4 us (35%)
  waiting for transfers between devices  12 us (22%)
  other arithmetic  0.59 us (1%)
    pallas_call x1, Pallas kernels, project_out(): pl.pallas_call(project_out_kernel, in_specs=[smem(), hbm(), vmem(), hbm()...  10.4 us
    ppermute x2, starting transfers between devices, to_owner(): lax.ppermute(far, 'tensor', [(0, 2), (3, 1)])  7.26 us
    ppermute x5, waiting for transfers between devices, swap(): lax.ppermute(value, axis, [(i, i ^ bit) for i in range(lax.axis_size(axis...  7.19 us
    ppermute x5, starting transfers between devices, swap(): lax.ppermute(value, axis, [(i, i ^ bit) for i in range(lax.axis_size(axis...  6.4 us
    ppermute x2, starting transfers between devices, to_owner(): lax.ppermute(near, 'tensor', [(0, 1), (3, 2)])  6.04 us
    pallas_call x1, Pallas kernels, project_in(): pl.pallas_call(project_in_kernel, in_specs=[smem(), hbm(), hbm(), hbm()],...  3.91 us
    pallas_call x1, Pallas kernels, score(): pl.pallas_call(functools.partial(score_kernel, tokens), in_specs=[smem()]...  3.75 us
    ppermute x2, waiting for transfers between devices, to_owner(): lax.ppermute(near, 'tensor', [(0, 1), (3, 2)])  3.47 us
  transfers between devices with their start and end apart: 14, of which 7 were waited for; matrix products, arithmetic and copies ran while one was open for 0% of the time, Pallas kernels for 21%

profile of v17, /device:TPU:0, one launch (start us, length us, event | category | flops | bytes accessed | tf_op | source)
XLA Modules:
  0.0 55.2 jit_solution(17856601968359498462)
XLA Ops:
  0.0 0.0 copy-start
  0.0 3.9 %project_in.1 = (f32[64,1024]{1,0:T(8,128)S(1)}, f32[64,1024]{1,0:T(8,128)S(1)}, f32[64,1024]{1,0:T(8,128)S(1)}, bf16[2,256,3584]{2,1,0:T(8,128)(2,1)S(1)}) custom-call(s32[1]{0:T(128)} %bitcast.1.side_ref, bf16[4,256,2048]{2,1,0:T(8,128)(2,1)} %rows_hbm.2, bf16[2,64,2048]{2,1,0:T(8,128)(2,1)} %proj_hbm.1, bf16[2,4,256,7168]{3,2,1,0:T(8,128)(2,1)} %rows_hbm.3), custom_call_target="tpu_custom_call" | custom-call | tf_op jit(solution)/shard_map/project_in/pallas_call | solution.py:92
  3.9 6.0 %collective-permute-start.1 = (f32[64,1024]{1,0:T(8,128)S(1)}, f32[64,1024]{1,0:T(8,128)S(1)}, u32[]{:S(2)}, u32[]{:S(2)}) collective-permute-start(f32[64,1024]{1,0:T(8,128)S(1)} %get-tuple-element.21), channel_id=1, source_target_pairs={{0,8},{12,4},{1,9},{13,5},{2,10},{14,6},{3,11},{15,7},{16,24},{28,... | collective-permute-start | bytes 786440 | tf_op jit(solution)/shard_map/ppermute | solution.py:194
  9.9 0.7 %collective-permute-start.2 = (f32[64,1024]{1,0:T(8,128)S(1)}, f32[64,1024]{1,0:T(8,128)S(1)}, u32[]{:S(2)}, u32[]{:S(2)}) collective-permute-start(f32[64,1024]{1,0:T(8,128)S(1)} %get-tuple-element.22), channel_id=1, source_target_pairs={{4,8},{8,4},{5,9},{9,5},{6,10},{10,6},{7,11},{11,7},{20,24},{24,20... | collective-permute-start | bytes 786440 | tf_op jit(solution)/shard_map/ppermute | solution.py:187
  10.6 3.1 %collective-permute-start = (f32[64,1024]{1,0:T(8,128)S(1)}, f32[64,1024]{1,0:T(8,128)S(1)}, u32[]{:S(2)}, u32[]{:S(2)}) collective-permute-start(f32[64,1024]{1,0:T(8,128)S(1)} %get-tuple-element.20.refs_0_), channel_id=1, source_target_pairs={{0,4},{12,8},{1,5},{13,9},{2,6},{14,10},{3,7},{15,11},{16,20},{28,... | collective-permute-start | bytes 786440 | tf_op jit(solution)/shard_map/ppermute | solution.py:193
  13.7 0.0 copy-done
  13.7 10.4 %project_out.1 = (f32[64,1024]{1,0:T(8,128)S(1)}, f32[64,1024]{1,0:T(8,128)S(1)}, f32[64,1024]{1,0:T(8,128)S(1)}, bf16[8,64,128]{2,1,0:T(8,128)(2,1)S(1)}) custom-call(s32[1]{0:T(128)} %bitcast.1.side_ref, bf16[2,4,256,7168]{3,2,1,0:T(8,128)(2,1)} %rows_hbm.3, bf16[2,64,7168]{2,1,0:T(8,128)(2,1)S(1)} %copy-done, bf16[16,2,64,64]{3,2,1,0:T(8,128)(2,1)} %queries_hbm.1, ...), custom_call_target="tpu_custom_call" | custom-call | tf_op jit(solution)/shard_map/project_out/pallas_call | solution.py:164
  24.1 1.3 %collective-permute-start.4 = (f32[64,1024]{1,0:T(8,128)S(1)}, f32[64,1024]{1,0:T(8,128)S(1)}, u32[]{:S(2)}, u32[]{:S(2)}) collective-permute-start(f32[64,1024]{1,0:T(8,128)S(1)} %get-tuple-element.26), channel_id=1, source_target_pairs={{0,8},{12,4},{1,9},{13,5},{2,10},{14,6},{3,11},{15,7},{16,24},{28,... | collective-permute-start | bytes 786440 | tf_op jit(solution)/shard_map/ppermute | solution.py:194
  25.4 0.7 %collective-permute-start.5 = (f32[64,1024]{1,0:T(8,128)S(1)}, f32[64,1024]{1,0:T(8,128)S(1)}, u32[]{:S(2)}, u32[]{:S(2)}) collective-permute-start(f32[64,1024]{1,0:T(8,128)S(1)} %get-tuple-element.27), channel_id=1, source_target_pairs={{4,8},{8,4},{5,9},{9,5},{6,10},{10,6},{7,11},{11,7},{20,24},{24,20... | collective-permute-start | bytes 786440 | tf_op jit(solution)/shard_map/ppermute | solution.py:187
  26.1 0.0 collective-permute-done.1.refs_2_
  26.1 3.0 %collective-permute-start.3 = (f32[64,1024]{1,0:T(8,128)S(1)}, f32[64,1024]{1,0:T(8,128)S(1)}, u32[]{:S(2)}, u32[]{:S(2)}) collective-permute-start(f32[64,1024]{1,0:T(8,128)S(1)} %get-tuple-element.25.refs_0_), channel_id=1, source_target_pairs={{0,4},{12,8},{1,5},{13,9},{2,6},{14,10},{3,7},{15,11},{16,20},{28,... | collective-permute-start | bytes 786440 | tf_op jit(solution)/shard_map/ppermute | solution.py:193
  29.1 0.0 collective-permute-done.2.refs_3_
  29.1 0.0 collective-permute-done.refs_1_
  29.1 0.4 cov_in.1
  29.5 0.7 %collective-permute-start.10 = (bf16[8,64,128]{2,1,0:T(8,128)(2,1)S(1)}, bf16[8,64,128]{2,1,0:T(8,128)(2,1)S(1)}, u32[]{:S(2)}, u32[]{:S(2)}) collective-permute-start(bf16[8,64,128]{2,1,0:T(8,128)(2,1)S(1)} %get-tuple-element.30.refs_0_), channel_id=1, source_target_pairs={{4,7},{5,6},{6,5},{7,4},{8,11},{9,10},{10,9},{11,8},{20,23},{21,22... | collective-permute-start | bytes 393224 | tf_op jit(solution)/shard_map/ppermute | solution.py:410
  30.2 0.7 %collective-permute-start.9 = (bf16[8,64,128]{2,1,0:T(8,128)(2,1)S(1)}, bf16[8,64,128]{2,1,0:T(8,128)(2,1)S(1)}, u32[]{:S(2)}, u32[]{:S(2)}) collective-permute-start(bf16[8,64,128]{2,1,0:T(8,128)(2,1)S(1)} %get-tuple-element.30.refs_0_), channel_id=1, source_target_pairs={{4,6},{5,7},{6,4},{7,5},{8,10},{9,11},{10,8},{11,9},{20,22},{21,23... | collective-permute-start | bytes 393224 | tf_op jit(solution)/shard_map/ppermute | solution.py:410
  30.9 1.3 %collective-permute-done.4.refs_2_ = f32[64,1024]{1,0:T(8,128)S(1)} collective-permute-done((f32[64,1024]{1,0:T(8,128)S(1)}, f32[64,1024]{1,0:T(8,128)S(1)}, u32[]{:S(2)}, u32[]{:S(2)}) %collective-permute-start.4) | collective-permute-done | bytes 262176 | tf_op jit(solution)/shard_map/ppermute | solution.py:194
  32.2 0.7 %collective-permute-start.8 = (bf16[8,64,128]{2,1,0:T(8,128)(2,1)S(1)}, bf16[8,64,128]{2,1,0:T(8,128)(2,1)S(1)}, u32[]{:S(2)}, u32[]{:S(2)}) collective-permute-start(bf16[8,64,128]{2,1,0:T(8,128)(2,1)S(1)} %get-tuple-element.30.refs_0_), channel_id=1, source_target_pairs={{4,5},{5,4},{6,7},{7,6},{8,9},{9,8},{10,11},{11,10},{20,21},{21,20... | collective-permute-start | bytes 393224 | tf_op jit(solution)/shard_map/ppermute | solution.py:410
  32.8 0.0 collective-permute-done.5.refs_3_
  32.8 3.5 %collective-permute-done.3.refs_1_ = f32[64,1024]{1,0:T(8,128)S(1)} collective-permute-done((f32[64,1024]{1,0:T(8,128)S(1)}, f32[64,1024]{1,0:T(8,128)S(1)}, u32[]{:S(2)}, u32[]{:S(2)}) %collective-permute-start.3) | collective-permute-done | bytes 262176 | tf_op jit(solution)/shard_map/ppermute | solution.py:193
  36.3 1.0 %cov_out.1 = (f32[64,128]{1,0:T(8,128)S(1)}, f32[4,64,128]{2,1,0:T(8,128)S(1)}) custom-call(f32[64,1024]{1,0:T(8,128)S(1)} %get-tuple-element.23.x_ref, f32[64,128]{1,0:T(8,128)S(1)} %get-tuple-element.24.cov_ref, f32[64,1024]{1,0:T(8,128)S(1)} %get-tuple-element.25.refs_0_, f32[64,1024]{1,0:T(8,128)S(1)} %collective-permute-done.3.refs_1_, ...), custom_call_target="tpu_custom_call" | custom-call | tf_op jit(solution)/shard_map/cov_out/pallas_call | solution.py:255
  37.3 0.1 collective-permute-start.6
  37.4 1.2 %collective-permute-done.6 = f32[64,128]{1,0:T(8,128)S(1)} collective-permute-done((f32[64,128]{1,0:T(8,128)S(1)}, f32[64,128]{1,0:T(8,128)S(1)}, u32[]{:S(2)}, u32[]{:S(2)}) %collective-permute-start.6) | collective-permute-done | bytes 32800 | tf_op jit(solution)/shard_map/ppermute | solution.py:404
  38.6 1.5 %collective-permute-start.7 = (f32[64,128]{1,0:T(8,128)S(1)}, f32[64,128]{1,0:T(8,128)S(1)}, u32[]{:S(2)}, u32[]{:S(2)}) collective-permute-start(f32[64,128]{1,0:T(8,128)S(1)} %add.6.own_ref), channel_id=1, source_target_pairs={{0,2},{1,3},{2,0},{3,1},{4,6},{5,7},{6,4},{7,5},{8,10},{9,11},{10,... | collective-permute-start | bytes 98312 | tf_op jit(solution)/shard_map/ppermute | solution.py:404
  40.1 2.4 %collective-permute-done.7.other_ref = f32[64,128]{1,0:T(8,128)S(1)} collective-permute-done((f32[64,128]{1,0:T(8,128)S(1)}, f32[64,128]{1,0:T(8,128)S(1)}, u32[]{:S(2)}, u32[]{:S(2)}) %collective-permute-start.7) | collective-permute-done | bytes 32800 | tf_op jit(solution)/shard_map/ppermute | solution.py:404
  42.5 0.0 collective-permute-done.10.refs_3_
  42.5 0.0 collective-permute-done.9.refs_2_
  42.5 0.0 collective-permute-done.8.refs_1_
  42.5 3.7 %score.1 = f32[4,64]{1,0:T(4,128)S(1)} custom-call(s32[1]{0:T(128)} %bitcast.place_ref, f32[64,128]{1,0:T(8,128)S(1)} %add.6.own_ref, f32[64,128]{1,0:T(8,128)S(1)} %collective-permute-done.7.other_ref, f32[4,64,128]{2,1,0:T(8,128)S(1)} %get-tuple-element.29.sample_ref, bf16[8,64,128]{2,1,0:T(8,128)(2,1)S(1)} %get-tuple-element.30.refs_0_, ...), custom_call_target="tpu_custom_call" | custom-call | tf_op jit(solution)/shard_map/score/pallas_call | solution.py:389
  46.2 2.4 %collective-permute-start.13 = (f32[4,64]{1,0:T(4,128)S(1)}, f32[4,64]{1,0:T(4,128)S(1)}, u32[]{:S(2)}, u32[]{:S(2)}) collective-permute-start(f32[4,64]{1,0:T(4,128)S(1)} %score.1), channel_id=1, source_target_pairs={{0,12},{4,8},{8,4},{12,0},{1,13},{5,9},{9,5},{13,1},{2,14},{6,10},... | collective-permute-start | bytes 3080 | tf_op jit(solution)/shard_map/ppermute | solution.py:404
  48.6 2.4 %collective-permute-start.12 = (f32[4,64]{1,0:T(4,128)S(1)}, f32[4,64]{1,0:T(4,128)S(1)}, u32[]{:S(2)}, u32[]{:S(2)}) collective-permute-start(f32[4,64]{1,0:T(4,128)S(1)} %score.1), channel_id=1, source_target_pairs={{0,8},{4,12},{8,0},{12,4},{1,9},{5,13},{9,1},{13,5},{2,10},{6,14},... | collective-permute-start | bytes 3080 | tf_op jit(solution)/shard_map/ppermute | solution.py:404
  51.1 0.0 collective-permute-start.11
  51.1 0.6 %collective-permute-done.13 = f32[4,64]{1,0:T(4,128)S(1)} collective-permute-done((f32[4,64]{1,0:T(4,128)S(1)}, f32[4,64]{1,0:T(4,128)S(1)}, u32[]{:S(2)}, u32[]{:S(2)}) %collective-permute-start.13) | collective-permute-done | bytes 1056 | tf_op jit(solution)/shard_map/ppermute | solution.py:404
  51.7 1.5 %collective-permute-done.12 = f32[4,64]{1,0:T(4,128)S(1)} collective-permute-done((f32[4,64]{1,0:T(4,128)S(1)}, f32[4,64]{1,0:T(4,128)S(1)}, u32[]{:S(2)}, u32[]{:S(2)}) %collective-permute-start.12) | collective-permute-done | bytes 1056 | tf_op jit(solution)/shard_map/ppermute | solution.py:404
  53.1 1.5 %collective-permute-done.11 = f32[4,64]{1,0:T(4,128)S(1)} collective-permute-done((f32[4,64]{1,0:T(4,128)S(1)}, f32[4,64]{1,0:T(4,128)S(1)}, u32[]{:S(2)}, u32[]{:S(2)}) %collective-permute-start.11) | collective-permute-done | bytes 1056 | tf_op jit(solution)/shard_map/ppermute | solution.py:404
  54.7 0.6 %select_add_fusion = f32[4,64]{1,0:T(4,128)} fusion(f32[4,64]{1,0:T(4,128)S(1)} %collective-permute-done.12, f32[4,64]{1,0:T(4,128)S(1)} %collective-permute-done.13, f32[4,64]{1,0:T(4,128)S(1)} %collective-permute-done.11, f32[4,64]{1,0:T(4,128)S(1)} %score.1, pred[]{:T(512)S(6)} %not.4), kind=kLoop, calls=%fused_computation | loop fusion | flops 768 | bytes 5121 | tf_op jit(solution)/shard_map/add | solution.py:436
  (1 shorter events, 0.0 us)
Async XLA Ops:
  0.0 13.7 %copy-start = (bf16[2,64,7168]{2,1,0:T(8,128)(2,1)S(1)}, bf16[2,64,7168]{2,1,0:T(8,128)(2,1)}, u32[]{:S(2)}) copy-start(bf16[2,64,7168]{2,1,0:T(8,128)(2,1)} %proj_ref.1) | copy-start | bytes 5505028
  3.9 22.2 %collective-permute-start.1 = (f32[64,1024]{1,0:T(8,128)S(1)}, f32[64,1024]{1,0:T(8,128)S(1)}, u32[]{:S(2)}, u32[]{:S(2)}) collective-permute-start(f32[64,1024]{1,0:T(8,128)S(1)} %get-tuple-element.21), channel_id=1, source_target_pairs={{0,8},{12,4},{1,9},{13,5},{2,10},{14,6},{3,11},{15,7},{16,24},{28,... | collective-permute-start | bytes 786440 | tf_op jit(solution)/shard_map/ppermute | solution.py:194
  9.9 19.2 %collective-permute-start.2 = (f32[64,1024]{1,0:T(8,128)S(1)}, f32[64,1024]{1,0:T(8,128)S(1)}, u32[]{:S(2)}, u32[]{:S(2)}) collective-permute-start(f32[64,1024]{1,0:T(8,128)S(1)} %get-tuple-element.22), channel_id=1, source_target_pairs={{4,8},{8,4},{5,9},{9,5},{6,10},{10,6},{7,11},{11,7},{20,24},{24,20... | collective-permute-start | bytes 786440 | tf_op jit(solution)/shard_map/ppermute | solution.py:187
  10.6 18.5 %collective-permute-start = (f32[64,1024]{1,0:T(8,128)S(1)}, f32[64,1024]{1,0:T(8,128)S(1)}, u32[]{:S(2)}, u32[]{:S(2)}) collective-permute-start(f32[64,1024]{1,0:T(8,128)S(1)} %get-tuple-element.20.refs_0_), channel_id=1, source_target_pairs={{0,4},{12,8},{1,5},{13,9},{2,6},{14,10},{3,7},{15,11},{16,20},{28,... | collective-permute-start | bytes 786440 | tf_op jit(solution)/shard_map/ppermute | solution.py:193
  24.1 8.1 %collective-permute-start.4 = (f32[64,1024]{1,0:T(8,128)S(1)}, f32[64,1024]{1,0:T(8,128)S(1)}, u32[]{:S(2)}, u32[]{:S(2)}) collective-permute-start(f32[64,1024]{1,0:T(8,128)S(1)} %get-tuple-element.26), channel_id=1, source_target_pairs={{0,8},{12,4},{1,9},{13,5},{2,10},{14,6},{3,11},{15,7},{16,24},{28,... | collective-permute-start | bytes 786440 | tf_op jit(solution)/shard_map/ppermute | solution.py:194
  25.4 7.4 %collective-permute-start.5 = (f32[64,1024]{1,0:T(8,128)S(1)}, f32[64,1024]{1,0:T(8,128)S(1)}, u32[]{:S(2)}, u32[]{:S(2)}) collective-permute-start(f32[64,1024]{1,0:T(8,128)S(1)} %get-tuple-element.27), channel_id=1, source_target_pairs={{4,8},{8,4},{5,9},{9,5},{6,10},{10,6},{7,11},{11,7},{20,24},{24,20... | collective-permute-start | bytes 786440 | tf_op jit(solution)/shard_map/ppermute | solution.py:187
  26.1 10.2 %collective-permute-start.3 = (f32[64,1024]{1,0:T(8,128)S(1)}, f32[64,1024]{1,0:T(8,128)S(1)}, u32[]{:S(2)}, u32[]{:S(2)}) collective-permute-start(f32[64,1024]{1,0:T(8,128)S(1)} %get-tuple-element.25.refs_0_), channel_id=1, source_target_pairs={{0,4},{12,8},{1,5},{13,9},{2,6},{14,10},{3,7},{15,11},{16,20},{28,... | collective-permute-start | bytes 786440 | tf_op jit(solution)/shard_map/ppermute | solution.py:193
  29.5 13.0 %collective-permute-start.10 = (bf16[8,64,128]{2,1,0:T(8,128)(2,1)S(1)}, bf16[8,64,128]{2,1,0:T(8,128)(2,1)S(1)}, u32[]{:S(2)}, u32[]{:S(2)}) collective-permute-start(bf16[8,64,128]{2,1,0:T(8,128)(2,1)S(1)} %get-tuple-element.30.refs_0_), channel_id=1, source_target_pairs={{4,7},{5,6},{6,5},{7,4},{8,11},{9,10},{10,9},{11,8},{20,23},{21,22... | collective-permute-start | bytes 393224 | tf_op jit(solution)/shard_map/ppermute | solution.py:410
  30.2 12.3 %collective-permute-start.9 = (bf16[8,64,128]{2,1,0:T(8,128)(2,1)S(1)}, bf16[8,64,128]{2,1,0:T(8,128)(2,1)S(1)}, u32[]{:S(2)}, u32[]{:S(2)}) collective-permute-start(bf16[8,64,128]{2,1,0:T(8,128)(2,1)S(1)} %get-tuple-element.30.refs_0_), channel_id=1, source_target_pairs={{4,6},{5,7},{6,4},{7,5},{8,10},{9,11},{10,8},{11,9},{20,22},{21,23... | collective-permute-start | bytes 393224 | tf_op jit(solution)/shard_map/ppermute | solution.py:410
  32.2 10.3 %collective-permute-start.8 = (bf16[8,64,128]{2,1,0:T(8,128)(2,1)S(1)}, bf16[8,64,128]{2,1,0:T(8,128)(2,1)S(1)}, u32[]{:S(2)}, u32[]{:S(2)}) collective-permute-start(bf16[8,64,128]{2,1,0:T(8,128)(2,1)S(1)} %get-tuple-element.30.refs_0_), channel_id=1, source_target_pairs={{4,5},{5,4},{6,7},{7,6},{8,9},{9,8},{10,11},{11,10},{20,21},{21,20... | collective-permute-start | bytes 393224 | tf_op jit(solution)/shard_map/ppermute | solution.py:410
  37.3 1.3 %collective-permute-start.6 = (f32[64,128]{1,0:T(8,128)S(1)}, f32[64,128]{1,0:T(8,128)S(1)}, u32[]{:S(2)}, u32[]{:S(2)}) collective-permute-start(f32[64,128]{1,0:T(8,128)S(1)} %get-tuple-element.28), channel_id=1, source_target_pairs={{0,1},{1,0},{2,3},{3,2},{4,5},{5,4},{6,7},{7,6},{8,9},{9,8},{10,11... | collective-permute-start | bytes 98312 | tf_op jit(solution)/shard_map/ppermute | solution.py:404
  38.6 3.9 %collective-permute-start.7 = (f32[64,128]{1,0:T(8,128)S(1)}, f32[64,128]{1,0:T(8,128)S(1)}, u32[]{:S(2)}, u32[]{:S(2)}) collective-permute-start(f32[64,128]{1,0:T(8,128)S(1)} %add.6.own_ref), channel_id=1, source_target_pairs={{0,2},{1,3},{2,0},{3,1},{4,6},{5,7},{6,4},{7,5},{8,10},{9,11},{10,... | collective-permute-start | bytes 98312 | tf_op jit(solution)/shard_map/ppermute | solution.py:404
  46.2 5.4 %collective-permute-start.13 = (f32[4,64]{1,0:T(4,128)S(1)}, f32[4,64]{1,0:T(4,128)S(1)}, u32[]{:S(2)}, u32[]{:S(2)}) collective-permute-start(f32[4,64]{1,0:T(4,128)S(1)} %score.1), channel_id=1, source_target_pairs={{0,12},{4,8},{8,4},{12,0},{1,13},{5,9},{9,5},{13,1},{2,14},{6,10},... | collective-permute-start | bytes 3080 | tf_op jit(solution)/shard_map/ppermute | solution.py:404
  48.6 4.5 %collective-permute-start.12 = (f32[4,64]{1,0:T(4,128)S(1)}, f32[4,64]{1,0:T(4,128)S(1)}, u32[]{:S(2)}, u32[]{:S(2)}) collective-permute-start(f32[4,64]{1,0:T(4,128)S(1)} %score.1), channel_id=1, source_target_pairs={{0,8},{4,12},{8,0},{12,4},{1,9},{5,13},{9,1},{13,5},{2,10},{6,14},... | collective-permute-start | bytes 3080 | tf_op jit(solution)/shard_map/ppermute | solution.py:404
  51.1 3.6 %collective-permute-start.11 = (f32[4,64]{1,0:T(4,128)S(1)}, f32[4,64]{1,0:T(4,128)S(1)}, u32[]{:S(2)}, u32[]{:S(2)}) collective-permute-start(f32[4,64]{1,0:T(4,128)S(1)} %score.1), channel_id=1, source_target_pairs={{0,4},{4,0},{8,12},{12,8},{1,5},{5,1},{9,13},{13,9},{2,6},{6,2},{1... | collective-permute-start | bytes 3080 | tf_op jit(solution)/shard_map/ppermute | solution.py:404

commit v18 on v17

--- a/solution.py
+++ b/solution.py
@@ -433,7 +433,7 @@
     scores = score(place, cov, other, sample, query_pieces, tokens)
     owner = (column == 1) | (column == 2)
     one, two, three = (swap(scores, "tensor", bits) for bits in (1, 2, 3))
-    return jnp.where(~owner, one, scores) + jnp.where(~owner, two, three)
+    return jnp.where(owner, three, one) + jnp.where(owner, scores, two)
 
 
 def damp(matrix):

time: 55.5 us -> 55.9 us (level)
  starting transfers between devices: 23.1 us -> 24 us
    ppermute x5, starting transfers between devices: 6.4 us -> 7.3 us  [swap(): lax.ppermute(value, axis, [(i, i ^ bit) for i in range(lax.axis_size(axis...]
  transfers between devices with their start and end apart: 14 -> 14, of which waited for: 7 -> 6; matrix products, arithmetic and copies ran while one was open for 0% -> 0% of each run, Pallas kernels for 21% -> 21%
where the time goes in v18:
time: 55.9 us; the launch traced here: 55.6 us
  starting transfers between devices  24 us (43%)
  Pallas kernels  19.4 us (35%)
  waiting for transfers between devices  11.5 us (21%)
  other arithmetic  0.59 us (1%)
    pallas_call x1, Pallas kernels, project_out(): pl.pallas_call(project_out_kernel, in_specs=[smem(), hbm(), vmem(), hbm()...  10.4 us
    ppermute x5, starting transfers between devices, swap(): lax.ppermute(value, axis, [(i, i ^ bit) for i in range(lax.axis_size(axis...  7.3 us
    ppermute x2, starting transfers between devices, to_owner(): lax.ppermute(far, 'tensor', [(0, 2), (3, 1)])  7.26 us
    ppermute x5, waiting for transfers between devices, swap(): lax.ppermute(value, axis, [(i, i ^ bit) for i in range(lax.axis_size(axis...  6.67 us
    ppermute x2, starting transfers between devices, to_owner(): lax.ppermute(near, 'tensor', [(0, 1), (3, 2)])  6.04 us
    pallas_call x1, Pallas kernels, project_in(): pl.pallas_call(project_in_kernel, in_specs=[smem(), hbm(), hbm(), hbm()],...  3.91 us
    pallas_call x1, Pallas kernels, score(): pl.pallas_call(functools.partial(score_kernel, tokens), in_specs=[smem()]...  3.75 us
    ppermute x2, waiting for transfers between devices, to_owner(): lax.ppermute(near, 'tensor', [(0, 1), (3, 2)])  3.47 us
  transfers between devices with their start and end apart: 14, of which 6 were waited for; matrix products, arithmetic and copies ran while one was open for 0% of the time, Pallas kernels for 21%

profile of v18, /device:TPU:0, one launch (start us, length us, event | category | flops | bytes accessed | tf_op | source)
XLA Modules:
  0.0 55.6 jit_solution(11600424834945260269)
XLA Ops:
  0.0 0.0 copy-start
  0.0 3.9 %project_in.1 = (f32[64,1024]{1,0:T(8,128)S(1)}, f32[64,1024]{1,0:T(8,128)S(1)}, f32[64,1024]{1,0:T(8,128)S(1)}, bf16[2,256,3584]{2,1,0:T(8,128)(2,1)S(1)}) custom-call(s32[1]{0:T(128)} %bitcast.1.side_ref, bf16[4,256,2048]{2,1,0:T(8,128)(2,1)} %rows_hbm.2, bf16[2,64,2048]{2,1,0:T(8,128)(2,1)} %proj_hbm.1, bf16[2,4,256,7168]{3,2,1,0:T(8,128)(2,1)} %rows_hbm.3), custom_call_target="tpu_custom_call" | custom-call | tf_op jit(solution)/shard_map/project_in/pallas_call | solution.py:92
  3.9 6.0 %collective-permute-start.1 = (f32[64,1024]{1,0:T(8,128)S(1)}, f32[64,1024]{1,0:T(8,128)S(1)}, u32[]{:S(2)}, u32[]{:S(2)}) collective-permute-start(f32[64,1024]{1,0:T(8,128)S(1)} %get-tuple-element.21), channel_id=1, source_target_pairs={{0,8},{12,4},{1,9},{13,5},{2,10},{14,6},{3,11},{15,7},{16,24},{28,... | collective-permute-start | bytes 786440 | tf_op jit(solution)/shard_map/ppermute | solution.py:194
  9.9 0.7 %collective-permute-start.2 = (f32[64,1024]{1,0:T(8,128)S(1)}, f32[64,1024]{1,0:T(8,128)S(1)}, u32[]{:S(2)}, u32[]{:S(2)}) collective-permute-start(f32[64,1024]{1,0:T(8,128)S(1)} %get-tuple-element.22), channel_id=1, source_target_pairs={{4,8},{8,4},{5,9},{9,5},{6,10},{10,6},{7,11},{11,7},{20,24},{24,20... | collective-permute-start | bytes 786440 | tf_op jit(solution)/shard_map/ppermute | solution.py:187
  10.6 3.1 %collective-permute-start = (f32[64,1024]{1,0:T(8,128)S(1)}, f32[64,1024]{1,0:T(8,128)S(1)}, u32[]{:S(2)}, u32[]{:S(2)}) collective-permute-start(f32[64,1024]{1,0:T(8,128)S(1)} %get-tuple-element.20.refs_0_), channel_id=1, source_target_pairs={{0,4},{12,8},{1,5},{13,9},{2,6},{14,10},{3,7},{15,11},{16,20},{28,... | collective-permute-start | bytes 786440 | tf_op jit(solution)/shard_map/ppermute | solution.py:193
  13.7 0.0 copy-done
  13.7 10.4 %project_out.1 = (f32[64,1024]{1,0:T(8,128)S(1)}, f32[64,1024]{1,0:T(8,128)S(1)}, f32[64,1024]{1,0:T(8,128)S(1)}, bf16[8,64,128]{2,1,0:T(8,128)(2,1)S(1)}) custom-call(s32[1]{0:T(128)} %bitcast.1.side_ref, bf16[2,4,256,7168]{3,2,1,0:T(8,128)(2,1)} %rows_hbm.3, bf16[2,64,7168]{2,1,0:T(8,128)(2,1)S(1)} %copy-done, bf16[16,2,64,64]{3,2,1,0:T(8,128)(2,1)} %queries_hbm.1, ...), custom_call_target="tpu_custom_call" | custom-call | tf_op jit(solution)/shard_map/project_out/pallas_call | solution.py:164
  24.1 1.3 %collective-permute-start.4 = (f32[64,1024]{1,0:T(8,128)S(1)}, f32[64,1024]{1,0:T(8,128)S(1)}, u32[]{:S(2)}, u32[]{:S(2)}) collective-permute-start(f32[64,1024]{1,0:T(8,128)S(1)} %get-tuple-element.26), channel_id=1, source_target_pairs={{0,8},{12,4},{1,9},{13,5},{2,10},{14,6},{3,11},{15,7},{16,24},{28,... | collective-permute-start | bytes 786440 | tf_op jit(solution)/shard_map/ppermute | solution.py:194
  25.4 0.7 %collective-permute-start.5 = (f32[64,1024]{1,0:T(8,128)S(1)}, f32[64,1024]{1,0:T(8,128)S(1)}, u32[]{:S(2)}, u32[]{:S(2)}) collective-permute-start(f32[64,1024]{1,0:T(8,128)S(1)} %get-tuple-element.27), channel_id=1, source_target_pairs={{4,8},{8,4},{5,9},{9,5},{6,10},{10,6},{7,11},{11,7},{20,24},{24,20... | collective-permute-start | bytes 786440 | tf_op jit(solution)/shard_map/ppermute | solution.py:187
  26.1 0.0 collective-permute-done.1.refs_2_
  26.1 3.0 %collective-permute-start.3 = (f32[64,1024]{1,0:T(8,128)S(1)}, f32[64,1024]{1,0:T(8,128)S(1)}, u32[]{:S(2)}, u32[]{:S(2)}) collective-permute-start(f32[64,1024]{1,0:T(8,128)S(1)} %get-tuple-element.25.refs_0_), channel_id=1, source_target_pairs={{0,4},{12,8},{1,5},{13,9},{2,6},{14,10},{3,7},{15,11},{16,20},{28,... | collective-permute-start | bytes 786440 | tf_op jit(solution)/shard_map/ppermute | solution.py:193
  29.1 0.0 collective-permute-done.2.refs_3_
  29.1 0.0 collective-permute-done.refs_1_
  29.1 0.4 cov_in.1
  29.5 0.7 %collective-permute-start.10 = (bf16[8,64,128]{2,1,0:T(8,128)(2,1)S(1)}, bf16[8,64,128]{2,1,0:T(8,128)(2,1)S(1)}, u32[]{:S(2)}, u32[]{:S(2)}) collective-permute-start(bf16[8,64,128]{2,1,0:T(8,128)(2,1)S(1)} %get-tuple-element.30.refs_0_), channel_id=1, source_target_pairs={{4,7},{5,6},{6,5},{7,4},{8,11},{9,10},{10,9},{11,8},{20,23},{21,22... | collective-permute-start | bytes 393224 | tf_op jit(solution)/shard_map/ppermute | solution.py:410
  30.2 0.7 %collective-permute-start.9 = (bf16[8,64,128]{2,1,0:T(8,128)(2,1)S(1)}, bf16[8,64,128]{2,1,0:T(8,128)(2,1)S(1)}, u32[]{:S(2)}, u32[]{:S(2)}) collective-permute-start(bf16[8,64,128]{2,1,0:T(8,128)(2,1)S(1)} %get-tuple-element.30.refs_0_), channel_id=1, source_target_pairs={{4,6},{5,7},{6,4},{7,5},{8,10},{9,11},{10,8},{11,9},{20,22},{21,23... | collective-permute-start | bytes 393224 | tf_op jit(solution)/shard_map/ppermute | solution.py:410
  30.9 1.3 %collective-permute-done.4.refs_2_ = f32[64,1024]{1,0:T(8,128)S(1)} collective-permute-done((f32[64,1024]{1,0:T(8,128)S(1)}, f32[64,1024]{1,0:T(8,128)S(1)}, u32[]{:S(2)}, u32[]{:S(2)}) %collective-permute-start.4) | collective-permute-done | bytes 262176 | tf_op jit(solution)/shard_map/ppermute | solution.py:194
  32.2 0.7 %collective-permute-start.8 = (bf16[8,64,128]{2,1,0:T(8,128)(2,1)S(1)}, bf16[8,64,128]{2,1,0:T(8,128)(2,1)S(1)}, u32[]{:S(2)}, u32[]{:S(2)}) collective-permute-start(bf16[8,64,128]{2,1,0:T(8,128)(2,1)S(1)} %get-tuple-element.30.refs_0_), channel_id=1, source_target_pairs={{4,5},{5,4},{6,7},{7,6},{8,9},{9,8},{10,11},{11,10},{20,21},{21,20... | collective-permute-start | bytes 393224 | tf_op jit(solution)/shard_map/ppermute | solution.py:410
  32.8 0.0 collective-permute-done.5.refs_3_
  32.8 3.5 %collective-permute-done.3.refs_1_ = f32[64,1024]{1,0:T(8,128)S(1)} collective-permute-done((f32[64,1024]{1,0:T(8,128)S(1)}, f32[64,1024]{1,0:T(8,128)S(1)}, u32[]{:S(2)}, u32[]{:S(2)}) %collective-permute-start.3) | collective-permute-done | bytes 262176 | tf_op jit(solution)/shard_map/ppermute | solution.py:193
  36.3 1.0 %cov_out.1 = (f32[64,128]{1,0:T(8,128)S(1)}, f32[4,64,128]{2,1,0:T(8,128)S(1)}) custom-call(f32[64,1024]{1,0:T(8,128)S(1)} %get-tuple-element.23.x_ref, f32[64,128]{1,0:T(8,128)S(1)} %get-tuple-element.24.cov_ref, f32[64,1024]{1,0:T(8,128)S(1)} %get-tuple-element.25.refs_0_, f32[64,1024]{1,0:T(8,128)S(1)} %collective-permute-done.3.refs_1_, ...), custom_call_target="tpu_custom_call" | custom-call | tf_op jit(solution)/shard_map/cov_out/pallas_call | solution.py:255
  37.3 0.1 collective-permute-start.6
  37.4 1.2 %collective-permute-done.6 = f32[64,128]{1,0:T(8,128)S(1)} collective-permute-done((f32[64,128]{1,0:T(8,128)S(1)}, f32[64,128]{1,0:T(8,128)S(1)}, u32[]{:S(2)}, u32[]{:S(2)}) %collective-permute-start.6) | collective-permute-done | bytes 32800 | tf_op jit(solution)/shard_map/ppermute | solution.py:404
  38.6 1.5 %collective-permute-start.7 = (f32[64,128]{1,0:T(8,128)S(1)}, f32[64,128]{1,0:T(8,128)S(1)}, u32[]{:S(2)}, u32[]{:S(2)}) collective-permute-start(f32[64,128]{1,0:T(8,128)S(1)} %add.6.own_ref), channel_id=1, source_target_pairs={{0,2},{1,3},{2,0},{3,1},{4,6},{5,7},{6,4},{7,5},{8,10},{9,11},{10,... | collective-permute-start | bytes 98312 | tf_op jit(solution)/shard_map/ppermute | solution.py:404
  40.1 2.4 %collective-permute-done.7.other_ref = f32[64,128]{1,0:T(8,128)S(1)} collective-permute-done((f32[64,128]{1,0:T(8,128)S(1)}, f32[64,128]{1,0:T(8,128)S(1)}, u32[]{:S(2)}, u32[]{:S(2)}) %collective-permute-start.7) | collective-permute-done | bytes 32800 | tf_op jit(solution)/shard_map/ppermute | solution.py:404
  42.5 0.0 collective-permute-done.10.refs_3_
  42.5 0.0 collective-permute-done.9.refs_2_
  42.5 0.0 collective-permute-done.8.refs_1_
  42.5 3.7 %score.1 = f32[4,64]{1,0:T(4,128)S(1)} custom-call(s32[1]{0:T(128)} %bitcast.place_ref, f32[64,128]{1,0:T(8,128)S(1)} %add.6.own_ref, f32[64,128]{1,0:T(8,128)S(1)} %collective-permute-done.7.other_ref, f32[4,64,128]{2,1,0:T(8,128)S(1)} %get-tuple-element.29.sample_ref, bf16[8,64,128]{2,1,0:T(8,128)(2,1)S(1)} %get-tuple-element.30.refs_0_, ...), custom_call_target="tpu_custom_call" | custom-call | tf_op jit(solution)/shard_map/score/pallas_call | solution.py:389
  46.2 3.4 %collective-permute-start.13 = (f32[4,64]{1,0:T(4,128)S(1)}, f32[4,64]{1,0:T(4,128)S(1)}, u32[]{:S(2)}, u32[]{:S(2)}) collective-permute-start(f32[4,64]{1,0:T(4,128)S(1)} %score.1), channel_id=1, source_target_pairs={{0,8},{4,12},{8,0},{12,4},{1,9},{5,13},{9,1},{13,5},{2,10},{6,14},... | collective-permute-start | bytes 3080 | tf_op jit(solution)/shard_map/ppermute | solution.py:404
  49.6 0.0 collective-permute-start.12
  49.7 2.3 %collective-permute-start.11 = (f32[4,64]{1,0:T(4,128)S(1)}, f32[4,64]{1,0:T(4,128)S(1)}, u32[]{:S(2)}, u32[]{:S(2)}) collective-permute-start(f32[4,64]{1,0:T(4,128)S(1)} %score.1), channel_id=1, source_target_pairs={{0,12},{4,8},{8,4},{12,0},{1,13},{5,9},{9,5},{13,1},{2,14},{6,10},... | collective-permute-start | bytes 3080 | tf_op jit(solution)/shard_map/ppermute | solution.py:404
  52.0 0.0 collective-permute-done.13
  52.0 1.3 %collective-permute-done.12 = f32[4,64]{1,0:T(4,128)S(1)} collective-permute-done((f32[4,64]{1,0:T(4,128)S(1)}, f32[4,64]{1,0:T(4,128)S(1)}, u32[]{:S(2)}, u32[]{:S(2)}) %collective-permute-start.12) | collective-permute-done | bytes 1056 | tf_op jit(solution)/shard_map/ppermute | solution.py:404
  53.2 1.8 %collective-permute-done.11 = f32[4,64]{1,0:T(4,128)S(1)} collective-permute-done((f32[4,64]{1,0:T(4,128)S(1)}, f32[4,64]{1,0:T(4,128)S(1)}, u32[]{:S(2)}, u32[]{:S(2)}) %collective-permute-start.11) | collective-permute-done | bytes 1056 | tf_op jit(solution)/shard_map/ppermute | solution.py:404
  55.0 0.6 %select_add_fusion = f32[4,64]{1,0:T(4,128)} fusion(f32[4,64]{1,0:T(4,128)S(1)} %score.1, f32[4,64]{1,0:T(4,128)S(1)} %collective-permute-done.13, f32[4,64]{1,0:T(4,128)S(1)} %collective-permute-done.11, f32[4,64]{1,0:T(4,128)S(1)} %collective-permute-done.12, pred[]{:T(512)S(6)} %or.3), kind=kLoop, calls=%fused_computation | loop fusion | flops 768 | bytes 5121 | tf_op jit(solution)/shard_map/add | solution.py:436
  (1 shorter events, 0.0 us)
Async XLA Ops:
  0.0 13.7 %copy-start = (bf16[2,64,7168]{2,1,0:T(8,128)(2,1)S(1)}, bf16[2,64,7168]{2,1,0:T(8,128)(2,1)}, u32[]{:S(2)}) copy-start(bf16[2,64,7168]{2,1,0:T(8,128)(2,1)} %proj_ref.1) | copy-start | bytes 5505028
  3.9 22.2 %collective-permute-start.1 = (f32[64,1024]{1,0:T(8,128)S(1)}, f32[64,1024]{1,0:T(8,128)S(1)}, u32[]{:S(2)}, u32[]{:S(2)}) collective-permute-start(f32[64,1024]{1,0:T(8,128)S(1)} %get-tuple-element.21), channel_id=1, source_target_pairs={{0,8},{12,4},{1,9},{13,5},{2,10},{14,6},{3,11},{15,7},{16,24},{28,... | collective-permute-start | bytes 786440 | tf_op jit(solution)/shard_map/ppermute | solution.py:194
  9.9 19.2 %collective-permute-start.2 = (f32[64,1024]{1,0:T(8,128)S(1)}, f32[64,1024]{1,0:T(8,128)S(1)}, u32[]{:S(2)}, u32[]{:S(2)}) collective-permute-start(f32[64,1024]{1,0:T(8,128)S(1)} %get-tuple-element.22), channel_id=1, source_target_pairs={{4,8},{8,4},{5,9},{9,5},{6,10},{10,6},{7,11},{11,7},{20,24},{24,20... | collective-permute-start | bytes 786440 | tf_op jit(solution)/shard_map/ppermute | solution.py:187
  10.6 18.5 %collective-permute-start = (f32[64,1024]{1,0:T(8,128)S(1)}, f32[64,1024]{1,0:T(8,128)S(1)}, u32[]{:S(2)}, u32[]{:S(2)}) collective-permute-start(f32[64,1024]{1,0:T(8,128)S(1)} %get-tuple-element.20.refs_0_), channel_id=1, source_target_pairs={{0,4},{12,8},{1,5},{13,9},{2,6},{14,10},{3,7},{15,11},{16,20},{28,... | collective-permute-start | bytes 786440 | tf_op jit(solution)/shard_map/ppermute | solution.py:193
  24.1 8.1 %collective-permute-start.4 = (f32[64,1024]{1,0:T(8,128)S(1)}, f32[64,1024]{1,0:T(8,128)S(1)}, u32[]{:S(2)}, u32[]{:S(2)}) collective-permute-start(f32[64,1024]{1,0:T(8,128)S(1)} %get-tuple-element.26), channel_id=1, source_target_pairs={{0,8},{12,4},{1,9},{13,5},{2,10},{14,6},{3,11},{15,7},{16,24},{28,... | collective-permute-start | bytes 786440 | tf_op jit(solution)/shard_map/ppermute | solution.py:194
  25.4 7.4 %collective-permute-start.5 = (f32[64,1024]{1,0:T(8,128)S(1)}, f32[64,1024]{1,0:T(8,128)S(1)}, u32[]{:S(2)}, u32[]{:S(2)}) collective-permute-start(f32[64,1024]{1,0:T(8,128)S(1)} %get-tuple-element.27), channel_id=1, source_target_pairs={{4,8},{8,4},{5,9},{9,5},{6,10},{10,6},{7,11},{11,7},{20,24},{24,20... | collective-permute-start | bytes 786440 | tf_op jit(solution)/shard_map/ppermute | solution.py:187
  26.1 10.2 %collective-permute-start.3 = (f32[64,1024]{1,0:T(8,128)S(1)}, f32[64,1024]{1,0:T(8,128)S(1)}, u32[]{:S(2)}, u32[]{:S(2)}) collective-permute-start(f32[64,1024]{1,0:T(8,128)S(1)} %get-tuple-element.25.refs_0_), channel_id=1, source_target_pairs={{0,4},{12,8},{1,5},{13,9},{2,6},{14,10},{3,7},{15,11},{16,20},{28,... | collective-permute-start | bytes 786440 | tf_op jit(solution)/shard_map/ppermute | solution.py:193
  29.5 13.0 %collective-permute-start.10 = (bf16[8,64,128]{2,1,0:T(8,128)(2,1)S(1)}, bf16[8,64,128]{2,1,0:T(8,128)(2,1)S(1)}, u32[]{:S(2)}, u32[]{:S(2)}) collective-permute-start(bf16[8,64,128]{2,1,0:T(8,128)(2,1)S(1)} %get-tuple-element.30.refs_0_), channel_id=1, source_target_pairs={{4,7},{5,6},{6,5},{7,4},{8,11},{9,10},{10,9},{11,8},{20,23},{21,22... | collective-permute-start | bytes 393224 | tf_op jit(solution)/shard_map/ppermute | solution.py:410
  30.2 12.3 %collective-permute-start.9 = (bf16[8,64,128]{2,1,0:T(8,128)(2,1)S(1)}, bf16[8,64,128]{2,1,0:T(8,128)(2,1)S(1)}, u32[]{:S(2)}, u32[]{:S(2)}) collective-permute-start(bf16[8,64,128]{2,1,0:T(8,128)(2,1)S(1)} %get-tuple-element.30.refs_0_), channel_id=1, source_target_pairs={{4,6},{5,7},{6,4},{7,5},{8,10},{9,11},{10,8},{11,9},{20,22},{21,23... | collective-permute-start | bytes 393224 | tf_op jit(solution)/shard_map/ppermute | solution.py:410
  32.2 10.3 %collective-permute-start.8 = (bf16[8,64,128]{2,1,0:T(8,128)(2,1)S(1)}, bf16[8,64,128]{2,1,0:T(8,128)(2,1)S(1)}, u32[]{:S(2)}, u32[]{:S(2)}) collective-permute-start(bf16[8,64,128]{2,1,0:T(8,128)(2,1)S(1)} %get-tuple-element.30.refs_0_), channel_id=1, source_target_pairs={{4,5},{5,4},{6,7},{7,6},{8,9},{9,8},{10,11},{11,10},{20,21},{21,20... | collective-permute-start | bytes 393224 | tf_op jit(solution)/shard_map/ppermute | solution.py:410
  37.3 1.3 %collective-permute-start.6 = (f32[64,128]{1,0:T(8,128)S(1)}, f32[64,128]{1,0:T(8,128)S(1)}, u32[]{:S(2)}, u32[]{:S(2)}) collective-permute-start(f32[64,128]{1,0:T(8,128)S(1)} %get-tuple-element.28), channel_id=1, source_target_pairs={{0,1},{1,0},{2,3},{3,2},{4,5},{5,4},{6,7},{7,6},{8,9},{9,8},{10,11... | collective-permute-start | bytes 98312 | tf_op jit(solution)/shard_map/ppermute | solution.py:404
  38.6 3.9 %collective-permute-start.7 = (f32[64,128]{1,0:T(8,128)S(1)}, f32[64,128]{1,0:T(8,128)S(1)}, u32[]{:S(2)}, u32[]{:S(2)}) collective-permute-start(f32[64,128]{1,0:T(8,128)S(1)} %add.6.own_ref), channel_id=1, source_target_pairs={{0,2},{1,3},{2,0},{3,1},{4,6},{5,7},{6,4},{7,5},{8,10},{9,11},{10,... | collective-permute-start | bytes 98312 | tf_op jit(solution)/shard_map/ppermute | solution.py:404
  46.2 5.7 %collective-permute-start.13 = (f32[4,64]{1,0:T(4,128)S(1)}, f32[4,64]{1,0:T(4,128)S(1)}, u32[]{:S(2)}, u32[]{:S(2)}) collective-permute-start(f32[4,64]{1,0:T(4,128)S(1)} %score.1), channel_id=1, source_target_pairs={{0,8},{4,12},{8,0},{12,4},{1,9},{5,13},{9,1},{13,5},{2,10},{6,14},... | collective-permute-start | bytes 3080 | tf_op jit(solution)/shard_map/ppermute | solution.py:404
  49.6 3.6 %collective-permute-start.12 = (f32[4,64]{1,0:T(4,128)S(1)}, f32[4,64]{1,0:T(4,128)S(1)}, u32[]{:S(2)}, u32[]{:S(2)}) collective-permute-start(f32[4,64]{1,0:T(4,128)S(1)} %score.1), channel_id=1, source_target_pairs={{0,4},{4,0},{8,12},{12,8},{1,5},{5,1},{9,13},{13,9},{2,6},{6,2},{1... | collective-permute-start | bytes 3080 | tf_op jit(solution)/shard_map/ppermute | solution.py:404
  49.7 5.4 %collective-permute-start.11 = (f32[4,64]{1,0:T(4,128)S(1)}, f32[4,64]{1,0:T(4,128)S(1)}, u32[]{:S(2)}, u32[]{:S(2)}) collective-permute-start(f32[4,64]{1,0:T(4,128)S(1)} %score.1), channel_id=1, source_target_pairs={{0,12},{4,8},{8,4},{12,0},{1,13},{5,9},{9,5},{13,1},{2,14},{6,10},... | collective-permute-start | bytes 3080 | tf_op jit(solution)/shard_map/ppermute | solution.py:404

commit v19 on v15

--- a/solution.py
+++ b/solution.py
@@ -190,8 +190,8 @@
 def to_owner(near, far, again):
     return [
         near,
-        lax.ppermute(near, "tensor", [(0, 1), (3, 2)]),
-        lax.ppermute(far, "tensor", [(0, 2), (3, 1)]),
+        lax.ppermute(near, "tensor", [(0, 1), (3, 2), (1, 0), (2, 3)]),
+        lax.ppermute(far, "tensor", [(0, 2), (3, 1), (1, 0), (2, 3)]),
         across(again),
     ]
 

time: 55 us -> 52.7 us (0.958)
  starting transfers between devices: 23.6 us -> 19 us
  waiting for transfers between devices: 10.8 us -> 13.3 us
    ppermute x4, starting transfers between devices: 13.3 us -> 10.9 us  [the longest x2 6.74 us: to_owner(): lax.ppermute(near, 'tensor', [(0, 1), (3, 2), (1, 0), (2, 3)])]
    ppermute x3, starting transfers between devices: 5.43 us -> 3.26 us  [shift(): lax.ppermute(value, axis, [(i, (i + by) % size) for i in range(size)])]
    ppermute x4, waiting for transfers between devices: 4.79 us -> 6.36 us  [the longest x2 3.46 us: to_owner(): lax.ppermute(far, 'tensor', [(0, 2), (3, 1), (1, 0), (2, 3)])]
    ppermute x3, waiting for transfers between devices: 2.42 us -> 3.34 us  [shift(): lax.ppermute(value, axis, [(i, (i + by) % size) for i in range(size)])]
where the time goes in v19:
time: 52.7 us; the launch traced here: 52.5 us
  Pallas kernels  19.4 us (37%)
  starting transfers between devices  19 us (36%)
  waiting for transfers between devices  13.3 us (25%)
  other arithmetic  0.59 us (1%)
    pallas_call x1, Pallas kernels, project_out(): pl.pallas_call(project_out_kernel, in_specs=[smem(), hbm(), vmem(), hbm()...  10.4 us
    ppermute x2, starting transfers between devices, to_owner(): lax.ppermute(near, 'tensor', [(0, 1), (3, 2), (1, 0), (2, 3)])  6.74 us
    ppermute x2, starting transfers between devices, to_owner(): lax.ppermute(far, 'tensor', [(0, 2), (3, 1), (1, 0), (2, 3)])  4.14 us
    pallas_call x1, Pallas kernels, project_in(): pl.pallas_call(project_in_kernel, in_specs=[smem(), hbm(), hbm(), hbm()],...  3.91 us
    pallas_call x1, Pallas kernels, score(): pl.pallas_call(functools.partial(score_kernel, tokens), in_specs=[smem()]...  3.75 us
    ppermute x2, waiting for transfers between devices, swap(): lax.ppermute(value, axis, [(i, i ^ bit) for i in range(lax.axis_size(axis...  3.62 us
    ppermute x2, waiting for transfers between devices, to_owner(): lax.ppermute(far, 'tensor', [(0, 2), (3, 1), (1, 0), (2, 3)])  3.46 us
    ppermute x3, waiting for transfers between devices, shift(): lax.ppermute(value, axis, [(i, (i + by) % size) for i in range(size)])  3.34 us
  transfers between devices with their start and end apart: 14, of which 6 were waited for; matrix products, arithmetic and copies ran while one was open for 0% of the time, Pallas kernels for 22%

profile of v19, /device:TPU:0, one launch (start us, length us, event | category | flops | bytes accessed | tf_op | source)
XLA Modules:
  0.0 52.5 jit_solution(8328148135675893743)
XLA Ops:
  0.0 0.0 copy-start
  0.0 3.9 %project_in.1 = (f32[64,1024]{1,0:T(8,128)S(1)}, f32[64,1024]{1,0:T(8,128)S(1)}, f32[64,1024]{1,0:T(8,128)S(1)}, bf16[2,256,3584]{2,1,0:T(8,128)(2,1)S(1)}) custom-call(s32[1]{0:T(128)} %bitcast.1.side_ref, bf16[4,256,2048]{2,1,0:T(8,128)(2,1)} %rows_hbm.2, bf16[2,64,2048]{2,1,0:T(8,128)(2,1)} %proj_hbm.1, bf16[2,4,256,7168]{3,2,1,0:T(8,128)(2,1)} %rows_hbm.3), custom_call_target="tpu_custom_call" | custom-call | tf_op jit(solution)/shard_map/project_in/pallas_call | solution.py:92
  3.9 4.1 %collective-permute-start.1 = (f32[64,1024]{1,0:T(8,128)S(1)}, f32[64,1024]{1,0:T(8,128)S(1)}, u32[]{:S(2)}, u32[]{:S(2)}) collective-permute-start(f32[64,1024]{1,0:T(8,128)S(1)} %get-tuple-element.21), channel_id=1, source_target_pairs={{0,8},{12,4},{4,0},{8,12},{1,9},{13,5},{5,1},{9,13},{2,10},{14,6},... | collective-permute-start | bytes 786440 | tf_op jit(solution)/shard_map/ppermute | solution.py:194
  8.0 0.7 %collective-permute-start.2 = (f32[64,1024]{1,0:T(8,128)S(1)}, f32[64,1024]{1,0:T(8,128)S(1)}, u32[]{:S(2)}, u32[]{:S(2)}) collective-permute-start(f32[64,1024]{1,0:T(8,128)S(1)} %get-tuple-element.22), channel_id=1, source_target_pairs={{4,8},{8,4},{5,9},{9,5},{6,10},{10,6},{7,11},{11,7},{20,24},{24,20... | collective-permute-start | bytes 786440 | tf_op jit(solution)/shard_map/ppermute | solution.py:187
  8.7 3.4 %collective-permute-start = (f32[64,1024]{1,0:T(8,128)S(1)}, f32[64,1024]{1,0:T(8,128)S(1)}, u32[]{:S(2)}, u32[]{:S(2)}) collective-permute-start(f32[64,1024]{1,0:T(8,128)S(1)} %get-tuple-element.20.refs_0_), channel_id=1, source_target_pairs={{0,4},{12,8},{4,0},{8,12},{1,5},{13,9},{5,1},{9,13},{2,6},{14,10},... | collective-permute-start | bytes 786440 | tf_op jit(solution)/shard_map/ppermute | solution.py:193
  12.1 0.0 copy-done
  12.1 10.4 %project_out.1 = (f32[64,1024]{1,0:T(8,128)S(1)}, f32[64,1024]{1,0:T(8,128)S(1)}, f32[64,1024]{1,0:T(8,128)S(1)}, bf16[8,64,128]{2,1,0:T(8,128)(2,1)S(1)}) custom-call(s32[1]{0:T(128)} %bitcast.1.side_ref, bf16[2,4,256,7168]{3,2,1,0:T(8,128)(2,1)} %rows_hbm.3, bf16[2,64,7168]{2,1,0:T(8,128)(2,1)S(1)} %copy-done, bf16[16,2,64,64]{3,2,1,0:T(8,128)(2,1)} %queries_hbm.1, ...), custom_call_target="tpu_custom_call" | custom-call | tf_op jit(solution)/shard_map/project_out/pallas_call | solution.py:164
  22.5 0.1 collective-permute-start.4
  22.6 0.7 %collective-permute-start.5 = (f32[64,1024]{1,0:T(8,128)S(1)}, f32[64,1024]{1,0:T(8,128)S(1)}, u32[]{:S(2)}, u32[]{:S(2)}) collective-permute-start(f32[64,1024]{1,0:T(8,128)S(1)} %get-tuple-element.27), channel_id=1, source_target_pairs={{4,8},{8,4},{5,9},{9,5},{6,10},{10,6},{7,11},{11,7},{20,24},{24,20... | collective-permute-start | bytes 786440 | tf_op jit(solution)/shard_map/ppermute | solution.py:187
  23.3 0.0 collective-permute-done.1.refs_2_
  23.3 3.3 %collective-permute-start.3 = (f32[64,1024]{1,0:T(8,128)S(1)}, f32[64,1024]{1,0:T(8,128)S(1)}, u32[]{:S(2)}, u32[]{:S(2)}) collective-permute-start(f32[64,1024]{1,0:T(8,128)S(1)} %get-tuple-element.25.refs_0_), channel_id=1, source_target_pairs={{0,4},{12,8},{4,0},{8,12},{1,5},{13,9},{5,1},{9,13},{2,6},{14,10},... | collective-permute-start | bytes 786440 | tf_op jit(solution)/shard_map/ppermute | solution.py:193
  26.6 0.0 collective-permute-done.2.refs_3_
  26.6 0.0 collective-permute-done.refs_1_
  26.6 0.4 cov_in.1
  27.0 0.7 %collective-permute-start.10 = (bf16[8,64,128]{2,1,0:T(8,128)(2,1)S(1)}, bf16[8,64,128]{2,1,0:T(8,128)(2,1)S(1)}, u32[]{:S(2)}, u32[]{:S(2)}) collective-permute-start(bf16[8,64,128]{2,1,0:T(8,128)(2,1)S(1)} %get-tuple-element.30.refs_0_), channel_id=1, source_target_pairs={{4,7},{5,6},{6,5},{7,4},{8,11},{9,10},{10,9},{11,8},{20,23},{21,22... | collective-permute-start | bytes 393224 | tf_op jit(solution)/shard_map/ppermute | solution.py:415
  27.7 0.7 %collective-permute-start.9 = (bf16[8,64,128]{2,1,0:T(8,128)(2,1)S(1)}, bf16[8,64,128]{2,1,0:T(8,128)(2,1)S(1)}, u32[]{:S(2)}, u32[]{:S(2)}) collective-permute-start(bf16[8,64,128]{2,1,0:T(8,128)(2,1)S(1)} %get-tuple-element.30.refs_0_), channel_id=1, source_target_pairs={{4,6},{5,7},{6,4},{7,5},{8,10},{9,11},{10,8},{11,9},{20,22},{21,23... | collective-permute-start | bytes 393224 | tf_op jit(solution)/shard_map/ppermute | solution.py:415
  28.4 3.5 %collective-permute-done.4.refs_2_ = f32[64,1024]{1,0:T(8,128)S(1)} collective-permute-done((f32[64,1024]{1,0:T(8,128)S(1)}, f32[64,1024]{1,0:T(8,128)S(1)}, u32[]{:S(2)}, u32[]{:S(2)}) %collective-permute-start.4) | collective-permute-done | bytes 262176 | tf_op jit(solution)/shard_map/ppermute | solution.py:194
  31.8 0.7 %collective-permute-start.8 = (bf16[8,64,128]{2,1,0:T(8,128)(2,1)S(1)}, bf16[8,64,128]{2,1,0:T(8,128)(2,1)S(1)}, u32[]{:S(2)}, u32[]{:S(2)}) collective-permute-start(bf16[8,64,128]{2,1,0:T(8,128)(2,1)S(1)} %get-tuple-element.30.refs_0_), channel_id=1, source_target_pairs={{4,5},{5,4},{6,7},{7,6},{8,9},{9,8},{10,11},{11,10},{20,21},{21,20... | collective-permute-start | bytes 393224 | tf_op jit(solution)/shard_map/ppermute | solution.py:415
  32.5 0.0 collective-permute-done.5.refs_3_
  32.5 2.9 %collective-permute-done.3.refs_1_ = f32[64,1024]{1,0:T(8,128)S(1)} collective-permute-done((f32[64,1024]{1,0:T(8,128)S(1)}, f32[64,1024]{1,0:T(8,128)S(1)}, u32[]{:S(2)}, u32[]{:S(2)}) %collective-permute-start.3) | collective-permute-done | bytes 262176 | tf_op jit(solution)/shard_map/ppermute | solution.py:193
  35.4 1.0 %cov_out.1 = (f32[64,128]{1,0:T(8,128)S(1)}, f32[4,64,128]{2,1,0:T(8,128)S(1)}) custom-call(f32[64,1024]{1,0:T(8,128)S(1)} %get-tuple-element.23.x_ref, f32[64,128]{1,0:T(8,128)S(1)} %get-tuple-element.24.cov_ref, f32[64,1024]{1,0:T(8,128)S(1)} %get-tuple-element.25.refs_0_, f32[64,1024]{1,0:T(8,128)S(1)} %collective-permute-done.3.refs_1_, ...), custom_call_target="tpu_custom_call" | custom-call | tf_op jit(solution)/shard_map/cov_out/pallas_call | solution.py:255
  36.4 0.1 collective-permute-start.6
  36.5 1.2 %collective-permute-done.6 = f32[64,128]{1,0:T(8,128)S(1)} collective-permute-done((f32[64,128]{1,0:T(8,128)S(1)}, f32[64,128]{1,0:T(8,128)S(1)}, u32[]{:S(2)}, u32[]{:S(2)}) %collective-permute-start.6) | collective-permute-done | bytes 32800 | tf_op jit(solution)/shard_map/ppermute | solution.py:404
  37.7 1.5 %collective-permute-start.7 = (f32[64,128]{1,0:T(8,128)S(1)}, f32[64,128]{1,0:T(8,128)S(1)}, u32[]{:S(2)}, u32[]{:S(2)}) collective-permute-start(f32[64,128]{1,0:T(8,128)S(1)} %add.6.own_ref), channel_id=1, source_target_pairs={{0,2},{1,3},{2,0},{3,1},{4,6},{5,7},{6,4},{7,5},{8,10},{9,11},{10,... | collective-permute-start | bytes 98312 | tf_op jit(solution)/shard_map/ppermute | solution.py:404
  39.2 2.4 %collective-permute-done.7.other_ref = f32[64,128]{1,0:T(8,128)S(1)} collective-permute-done((f32[64,128]{1,0:T(8,128)S(1)}, f32[64,128]{1,0:T(8,128)S(1)}, u32[]{:S(2)}, u32[]{:S(2)}) %collective-permute-start.7) | collective-permute-done | bytes 32800 | tf_op jit(solution)/shard_map/ppermute | solution.py:404
  41.6 0.0 collective-permute-done.10.refs_3_
  41.6 0.0 collective-permute-done.9.refs_2_
  41.6 0.0 collective-permute-done.8.refs_1_
  41.6 3.7 %score.1 = f32[4,64]{1,0:T(4,128)S(1)} custom-call(s32[1]{0:T(128)} %bitcast.place_ref, f32[64,128]{1,0:T(8,128)S(1)} %add.6.own_ref, f32[64,128]{1,0:T(8,128)S(1)} %collective-permute-done.7.other_ref, f32[4,64,128]{2,1,0:T(8,128)S(1)} %get-tuple-element.29.sample_ref, bf16[8,64,128]{2,1,0:T(8,128)(2,1)S(1)} %get-tuple-element.30.refs_0_, ...), custom_call_target="tpu_custom_call" | custom-call | tf_op jit(solution)/shard_map/score/pallas_call | solution.py:389
  45.3 1.2 %collective-permute-start.13 = (f32[4,64]{1,0:T(4,128)S(1)}, f32[4,64]{1,0:T(4,128)S(1)}, u32[]{:S(2)}, u32[]{:S(2)}) collective-permute-start(f32[4,64]{1,0:T(4,128)S(1)} %score.1), channel_id=1, source_target_pairs={{0,12},{4,0},{8,4},{12,8},{1,13},{5,1},{9,5},{13,9},{2,14},{6,2},{... | collective-permute-start | bytes 3080 | tf_op jit(solution)/shard_map/ppermute | solution.py:409
  46.6 0.8 %collective-permute-start.12 = (f32[4,64]{1,0:T(4,128)S(1)}, f32[4,64]{1,0:T(4,128)S(1)}, u32[]{:S(2)}, u32[]{:S(2)}) collective-permute-start(f32[4,64]{1,0:T(4,128)S(1)} %score.1), channel_id=1, source_target_pairs={{0,4},{4,8},{8,12},{12,0},{1,5},{5,9},{9,13},{13,1},{2,6},{6,10},{... | collective-permute-start | bytes 3080 | tf_op jit(solution)/shard_map/ppermute | solution.py:409
  47.4 1.2 %collective-permute-start.11 = (f32[4,64]{1,0:T(4,128)S(1)}, f32[4,64]{1,0:T(4,128)S(1)}, u32[]{:S(2)}, u32[]{:S(2)}) collective-permute-start(f32[4,64]{1,0:T(4,128)S(1)} %score.1), channel_id=1, source_target_pairs={{0,8},{4,12},{8,0},{12,4},{1,9},{5,13},{9,1},{13,5},{2,10},{6,14},... | collective-permute-start | bytes 3080 | tf_op jit(solution)/shard_map/ppermute | solution.py:409
  48.6 0.4 collective-permute-done.13
  49.0 3.0 %collective-permute-done.12 = f32[4,64]{1,0:T(4,128)S(1)} collective-permute-done((f32[4,64]{1,0:T(4,128)S(1)}, f32[4,64]{1,0:T(4,128)S(1)}, u32[]{:S(2)}, u32[]{:S(2)}) %collective-permute-start.12) | collective-permute-done | bytes 1056 | tf_op jit(solution)/shard_map/ppermute | solution.py:409
  51.9 0.0 collective-permute-done.11
  51.9 0.6 %select_add_fusion = f32[4,64]{1,0:T(4,128)} fusion(f32[4,64]{1,0:T(4,128)S(1)} %collective-permute-done.12, f32[4,64]{1,0:T(4,128)S(1)} %collective-permute-done.13, f32[4,64]{1,0:T(4,128)S(1)} %score.1, f32[4,64]{1,0:T(4,128)S(1)} %collective-permute-done.11, pred[]{:T(512)S(6)} %ge.4, pred[]{:T(512)S(6)} %or.3), kind=kLoop, calls=%fused_computation | loop fusion | flops 768 | bytes 5122 | tf_op jit(solution)/shard_map/add | solution.py:443
  (1 shorter events, 0.0 us)
Async XLA Ops:
  0.0 12.1 %copy-start = (bf16[2,64,7168]{2,1,0:T(8,128)(2,1)S(1)}, bf16[2,64,7168]{2,1,0:T(8,128)(2,1)}, u32[]{:S(2)}) copy-start(bf16[2,64,7168]{2,1,0:T(8,128)(2,1)} %proj_ref.1) | copy-start | bytes 5505028
  3.9 19.4 %collective-permute-start.1 = (f32[64,1024]{1,0:T(8,128)S(1)}, f32[64,1024]{1,0:T(8,128)S(1)}, u32[]{:S(2)}, u32[]{:S(2)}) collective-permute-start(f32[64,1024]{1,0:T(8,128)S(1)} %get-tuple-element.21), channel_id=1, source_target_pairs={{0,8},{12,4},{4,0},{8,12},{1,9},{13,5},{5,1},{9,13},{2,10},{14,6},... | collective-permute-start | bytes 786440 | tf_op jit(solution)/shard_map/ppermute | solution.py:194
  8.0 18.6 %collective-permute-start.2 = (f32[64,1024]{1,0:T(8,128)S(1)}, f32[64,1024]{1,0:T(8,128)S(1)}, u32[]{:S(2)}, u32[]{:S(2)}) collective-permute-start(f32[64,1024]{1,0:T(8,128)S(1)} %get-tuple-element.22), channel_id=1, source_target_pairs={{4,8},{8,4},{5,9},{9,5},{6,10},{10,6},{7,11},{11,7},{20,24},{24,20... | collective-permute-start | bytes 786440 | tf_op jit(solution)/shard_map/ppermute | solution.py:187
  8.7 17.9 %collective-permute-start = (f32[64,1024]{1,0:T(8,128)S(1)}, f32[64,1024]{1,0:T(8,128)S(1)}, u32[]{:S(2)}, u32[]{:S(2)}) collective-permute-start(f32[64,1024]{1,0:T(8,128)S(1)} %get-tuple-element.20.refs_0_), channel_id=1, source_target_pairs={{0,4},{12,8},{4,0},{8,12},{1,5},{13,9},{5,1},{9,13},{2,6},{14,10},... | collective-permute-start | bytes 786440 | tf_op jit(solution)/shard_map/ppermute | solution.py:193
  22.5 9.3 %collective-permute-start.4 = (f32[64,1024]{1,0:T(8,128)S(1)}, f32[64,1024]{1,0:T(8,128)S(1)}, u32[]{:S(2)}, u32[]{:S(2)}) collective-permute-start(f32[64,1024]{1,0:T(8,128)S(1)} %get-tuple-element.26), channel_id=1, source_target_pairs={{0,8},{12,4},{4,0},{8,12},{1,9},{13,5},{5,1},{9,13},{2,10},{14,6},... | collective-permute-start | bytes 786440 | tf_op jit(solution)/shard_map/ppermute | solution.py:194
  22.6 9.9 %collective-permute-start.5 = (f32[64,1024]{1,0:T(8,128)S(1)}, f32[64,1024]{1,0:T(8,128)S(1)}, u32[]{:S(2)}, u32[]{:S(2)}) collective-permute-start(f32[64,1024]{1,0:T(8,128)S(1)} %get-tuple-element.27), channel_id=1, source_target_pairs={{4,8},{8,4},{5,9},{9,5},{6,10},{10,6},{7,11},{11,7},{20,24},{24,20... | collective-permute-start | bytes 786440 | tf_op jit(solution)/shard_map/ppermute | solution.py:187
  23.3 12.1 %collective-permute-start.3 = (f32[64,1024]{1,0:T(8,128)S(1)}, f32[64,1024]{1,0:T(8,128)S(1)}, u32[]{:S(2)}, u32[]{:S(2)}) collective-permute-start(f32[64,1024]{1,0:T(8,128)S(1)} %get-tuple-element.25.refs_0_), channel_id=1, source_target_pairs={{0,4},{12,8},{4,0},{8,12},{1,5},{13,9},{5,1},{9,13},{2,6},{14,10},... | collective-permute-start | bytes 786440 | tf_op jit(solution)/shard_map/ppermute | solution.py:193
  27.0 14.6 %collective-permute-start.10 = (bf16[8,64,128]{2,1,0:T(8,128)(2,1)S(1)}, bf16[8,64,128]{2,1,0:T(8,128)(2,1)S(1)}, u32[]{:S(2)}, u32[]{:S(2)}) collective-permute-start(bf16[8,64,128]{2,1,0:T(8,128)(2,1)S(1)} %get-tuple-element.30.refs_0_), channel_id=1, source_target_pairs={{4,7},{5,6},{6,5},{7,4},{8,11},{9,10},{10,9},{11,8},{20,23},{21,22... | collective-permute-start | bytes 393224 | tf_op jit(solution)/shard_map/ppermute | solution.py:415
  27.7 13.9 %collective-permute-start.9 = (bf16[8,64,128]{2,1,0:T(8,128)(2,1)S(1)}, bf16[8,64,128]{2,1,0:T(8,128)(2,1)S(1)}, u32[]{:S(2)}, u32[]{:S(2)}) collective-permute-start(bf16[8,64,128]{2,1,0:T(8,128)(2,1)S(1)} %get-tuple-element.30.refs_0_), channel_id=1, source_target_pairs={{4,6},{5,7},{6,4},{7,5},{8,10},{9,11},{10,8},{11,9},{20,22},{21,23... | collective-permute-start | bytes 393224 | tf_op jit(solution)/shard_map/ppermute | solution.py:415
  31.8 9.8 %collective-permute-start.8 = (bf16[8,64,128]{2,1,0:T(8,128)(2,1)S(1)}, bf16[8,64,128]{2,1,0:T(8,128)(2,1)S(1)}, u32[]{:S(2)}, u32[]{:S(2)}) collective-permute-start(bf16[8,64,128]{2,1,0:T(8,128)(2,1)S(1)} %get-tuple-element.30.refs_0_), channel_id=1, source_target_pairs={{4,5},{5,4},{6,7},{7,6},{8,9},{9,8},{10,11},{11,10},{20,21},{21,20... | collective-permute-start | bytes 393224 | tf_op jit(solution)/shard_map/ppermute | solution.py:415
  36.4 1.3 %collective-permute-start.6 = (f32[64,128]{1,0:T(8,128)S(1)}, f32[64,128]{1,0:T(8,128)S(1)}, u32[]{:S(2)}, u32[]{:S(2)}) collective-permute-start(f32[64,128]{1,0:T(8,128)S(1)} %get-tuple-element.28), channel_id=1, source_target_pairs={{0,1},{1,0},{2,3},{3,2},{4,5},{5,4},{6,7},{7,6},{8,9},{9,8},{10,11... | collective-permute-start | bytes 98312 | tf_op jit(solution)/shard_map/ppermute | solution.py:404
  37.7 3.9 %collective-permute-start.7 = (f32[64,128]{1,0:T(8,128)S(1)}, f32[64,128]{1,0:T(8,128)S(1)}, u32[]{:S(2)}, u32[]{:S(2)}) collective-permute-start(f32[64,128]{1,0:T(8,128)S(1)} %add.6.own_ref), channel_id=1, source_target_pairs={{0,2},{1,3},{2,0},{3,1},{4,6},{5,7},{6,4},{7,5},{8,10},{9,11},{10,... | collective-permute-start | bytes 98312 | tf_op jit(solution)/shard_map/ppermute | solution.py:404
  45.3 3.6 %collective-permute-start.13 = (f32[4,64]{1,0:T(4,128)S(1)}, f32[4,64]{1,0:T(4,128)S(1)}, u32[]{:S(2)}, u32[]{:S(2)}) collective-permute-start(f32[4,64]{1,0:T(4,128)S(1)} %score.1), channel_id=1, source_target_pairs={{0,12},{4,0},{8,4},{12,8},{1,13},{5,1},{9,5},{13,9},{2,14},{6,2},{... | collective-permute-start | bytes 3080 | tf_op jit(solution)/shard_map/ppermute | solution.py:409
  46.6 5.4 %collective-permute-start.12 = (f32[4,64]{1,0:T(4,128)S(1)}, f32[4,64]{1,0:T(4,128)S(1)}, u32[]{:S(2)}, u32[]{:S(2)}) collective-permute-start(f32[4,64]{1,0:T(4,128)S(1)} %score.1), channel_id=1, source_target_pairs={{0,4},{4,8},{8,12},{12,0},{1,5},{5,9},{9,13},{13,1},{2,6},{6,10},{... | collective-permute-start | bytes 3080 | tf_op jit(solution)/shard_map/ppermute | solution.py:409
  47.4 4.5 %collective-permute-start.11 = (f32[4,64]{1,0:T(4,128)S(1)}, f32[4,64]{1,0:T(4,128)S(1)}, u32[]{:S(2)}, u32[]{:S(2)}) collective-permute-start(f32[4,64]{1,0:T(4,128)S(1)} %score.1), channel_id=1, source_target_pairs={{0,8},{4,12},{8,0},{12,4},{1,9},{5,13},{9,1},{13,5},{2,10},{6,14},... | collective-permute-start | bytes 3080 | tf_op jit(solution)/shard_map/ppermute | solution.py:409

commit v20 on v19

--- a/solution.py
+++ b/solution.py
@@ -409,12 +409,6 @@
     return lax.ppermute(value, axis, [(i, (i + by) % size) for i in range(size)])
 
 
-def owners_swap(value, bits):
-    parts = lax.axis_size("dp")
-    places = [(t * parts + k, t * parts + (k ^ bits)) for t in (1, 2) for k in range(parts)]
-    return lax.ppermute(value, ("tensor", "dp"), places)
-
-
 def local_owned(acts, grads, proj_in, proj_out, queries):
     seqs, length, _ = acts.shape
     parts = lax.axis_size("dp")
@@ -427,7 +421,7 @@
     near, far, again, packed = project_out(side, grads, proj_out, queries, early)
     pieces = to_owner(near, far, again)
     packed, x, cov = cov_in(packed, x_pieces)
-    query_pieces = [packed] + [owners_swap(packed, bits) for bits in range(1, parts)]
+    query_pieces = [packed] + [swap(packed, "dp", bits) for bits in range(1, parts)]
     cov, sample = cov_out(x, cov, pieces, seqs)
     other = jnp.zeros_like(cov)
     bit = 1

time: 52.7 us -> 52.7 us (level)
    ppermute x3 -> x0, starting transfers between devices: 2 us -> none  [owners_swap(): return lax.ppermute(value, ('tensor', 'dp'), places)]
    ppermute x2 -> x5, starting transfers between devices: 1.56 us -> 3.19 us  [swap(): lax.ppermute(value, axis, [(i, i ^ bit) for i in range(lax.axis_size(axis...]
    ppermute x2, waiting for transfers between devices: 2.9 us -> 3.57 us  [to_owner(): lax.ppermute(near, 'tensor', [(0, 1), (3, 2), (1, 0), (2, 3)])]
    ppermute x2 -> x5, waiting for transfers between devices: 3.62 us -> 3.63 us  [swap(): lax.ppermute(value, axis, [(i, i ^ bit) for i in range(lax.axis_size(axis...]
where the time goes in v20:
time: 52.7 us; the launch traced here: 52.5 us
  Pallas kernels  19.4 us (37%)
  starting transfers between devices  18.7 us (35%)
  waiting for transfers between devices  13.7 us (26%)
  other arithmetic  0.59 us (1%)
    pallas_call x1, Pallas kernels, project_out(): pl.pallas_call(project_out_kernel, in_specs=[smem(), hbm(), vmem(), hbm()...  10.4 us
    ppermute x2, starting transfers between devices, to_owner(): lax.ppermute(near, 'tensor', [(0, 1), (3, 2), (1, 0), (2, 3)])  6.74 us
    ppermute x2, starting transfers between devices, to_owner(): lax.ppermute(far, 'tensor', [(0, 2), (3, 1), (1, 0), (2, 3)])  4.14 us
    pallas_call x1, Pallas kernels, project_in(): pl.pallas_call(project_in_kernel, in_specs=[smem(), hbm(), hbm(), hbm()],...  3.91 us
    pallas_call x1, Pallas kernels, score(): pl.pallas_call(functools.partial(score_kernel, tokens), in_specs=[smem()]...  3.75 us
    ppermute x5, waiting for transfers between devices, swap(): lax.ppermute(value, axis, [(i, i ^ bit) for i in range(lax.axis_size(axis...  3.63 us
    ppermute x2, waiting for transfers between devices, to_owner(): lax.ppermute(near, 'tensor', [(0, 1), (3, 2), (1, 0), (2, 3)])  3.57 us
    ppermute x3, waiting for transfers between devices, shift(): lax.ppermute(value, axis, [(i, (i + by) % size) for i in range(size)])  3.34 us
  transfers between devices with their start and end apart: 14, of which 6 were waited for; matrix products, arithmetic and copies ran while one was open for 0% of the time, Pallas kernels for 22%

profile of v20, /device:TPU:0, one launch (start us, length us, event | category | flops | bytes accessed | tf_op | source)
XLA Modules:
  0.0 52.5 jit_solution(3648769192926833862)
XLA Ops:
  0.0 0.0 copy-start
  0.0 3.9 %project_in.1 = (f32[64,1024]{1,0:T(8,128)S(1)}, f32[64,1024]{1,0:T(8,128)S(1)}, f32[64,1024]{1,0:T(8,128)S(1)}, bf16[2,256,3584]{2,1,0:T(8,128)(2,1)S(1)}) custom-call(s32[1]{0:T(128)} %bitcast.1.side_ref, bf16[4,256,2048]{2,1,0:T(8,128)(2,1)} %rows_hbm.2, bf16[2,64,2048]{2,1,0:T(8,128)(2,1)} %proj_hbm.1, bf16[2,4,256,7168]{3,2,1,0:T(8,128)(2,1)} %rows_hbm.3), custom_call_target="tpu_custom_call" | custom-call | tf_op jit(solution)/shard_map/project_in/pallas_call | solution.py:92
  3.9 4.1 %collective-permute-start.1 = (f32[64,1024]{1,0:T(8,128)S(1)}, f32[64,1024]{1,0:T(8,128)S(1)}, u32[]{:S(2)}, u32[]{:S(2)}) collective-permute-start(f32[64,1024]{1,0:T(8,128)S(1)} %get-tuple-element.21), channel_id=1, source_target_pairs={{0,8},{12,4},{4,0},{8,12},{1,9},{13,5},{5,1},{9,13},{2,10},{14,6},... | collective-permute-start | bytes 786440 | tf_op jit(solution)/shard_map/ppermute | solution.py:194
  8.0 0.7 %collective-permute-start.2 = (f32[64,1024]{1,0:T(8,128)S(1)}, f32[64,1024]{1,0:T(8,128)S(1)}, u32[]{:S(2)}, u32[]{:S(2)}) collective-permute-start(f32[64,1024]{1,0:T(8,128)S(1)} %get-tuple-element.22), channel_id=1, source_target_pairs={{4,8},{8,4},{5,9},{9,5},{6,10},{10,6},{7,11},{11,7},{20,24},{24,20... | collective-permute-start | bytes 786440 | tf_op jit(solution)/shard_map/ppermute | solution.py:187
  8.7 3.4 %collective-permute-start = (f32[64,1024]{1,0:T(8,128)S(1)}, f32[64,1024]{1,0:T(8,128)S(1)}, u32[]{:S(2)}, u32[]{:S(2)}) collective-permute-start(f32[64,1024]{1,0:T(8,128)S(1)} %get-tuple-element.20.refs_0_), channel_id=1, source_target_pairs={{0,4},{12,8},{4,0},{8,12},{1,5},{13,9},{5,1},{9,13},{2,6},{14,10},... | collective-permute-start | bytes 786440 | tf_op jit(solution)/shard_map/ppermute | solution.py:193
  12.1 0.0 copy-done
  12.1 10.4 %project_out.1 = (f32[64,1024]{1,0:T(8,128)S(1)}, f32[64,1024]{1,0:T(8,128)S(1)}, f32[64,1024]{1,0:T(8,128)S(1)}, bf16[8,64,128]{2,1,0:T(8,128)(2,1)S(1)}) custom-call(s32[1]{0:T(128)} %bitcast.1.side_ref, bf16[2,4,256,7168]{3,2,1,0:T(8,128)(2,1)} %rows_hbm.3, bf16[2,64,7168]{2,1,0:T(8,128)(2,1)S(1)} %copy-done, bf16[16,2,64,64]{3,2,1,0:T(8,128)(2,1)} %queries_hbm.1, ...), custom_call_target="tpu_custom_call" | custom-call | tf_op jit(solution)/shard_map/project_out/pallas_call | solution.py:164
  22.5 0.1 collective-permute-start.4
  22.6 0.7 %collective-permute-start.5 = (f32[64,1024]{1,0:T(8,128)S(1)}, f32[64,1024]{1,0:T(8,128)S(1)}, u32[]{:S(2)}, u32[]{:S(2)}) collective-permute-start(f32[64,1024]{1,0:T(8,128)S(1)} %get-tuple-element.27), channel_id=1, source_target_pairs={{4,8},{8,4},{5,9},{9,5},{6,10},{10,6},{7,11},{11,7},{20,24},{24,20... | collective-permute-start | bytes 786440 | tf_op jit(solution)/shard_map/ppermute | solution.py:187
  23.3 0.0 collective-permute-done.1.refs_2_
  23.3 3.3 %collective-permute-start.3 = (f32[64,1024]{1,0:T(8,128)S(1)}, f32[64,1024]{1,0:T(8,128)S(1)}, u32[]{:S(2)}, u32[]{:S(2)}) collective-permute-start(f32[64,1024]{1,0:T(8,128)S(1)} %get-tuple-element.25.refs_0_), channel_id=1, source_target_pairs={{0,4},{12,8},{4,0},{8,12},{1,5},{13,9},{5,1},{9,13},{2,6},{14,10},... | collective-permute-start | bytes 786440 | tf_op jit(solution)/shard_map/ppermute | solution.py:193
  26.6 0.0 collective-permute-done.2.refs_3_
  26.6 0.0 collective-permute-done.refs_1_
  26.6 0.4 cov_in.1
  27.0 0.1 collective-permute-start.10
  27.1 1.6 %collective-permute-start.9 = (bf16[8,64,128]{2,1,0:T(8,128)(2,1)S(1)}, bf16[8,64,128]{2,1,0:T(8,128)(2,1)S(1)}, u32[]{:S(2)}, u32[]{:S(2)}) collective-permute-start(bf16[8,64,128]{2,1,0:T(8,128)(2,1)S(1)} %get-tuple-element.30.refs_0_), channel_id=1, source_target_pairs={{0,2},{1,3},{2,0},{3,1},{4,6},{5,7},{6,4},{7,5},{8,10},{9,11},{10,... | collective-permute-start | bytes 393224 | tf_op jit(solution)/shard_map/ppermute | solution.py:404
  28.7 3.2 %collective-permute-done.4.refs_2_ = f32[64,1024]{1,0:T(8,128)S(1)} collective-permute-done((f32[64,1024]{1,0:T(8,128)S(1)}, f32[64,1024]{1,0:T(8,128)S(1)}, u32[]{:S(2)}, u32[]{:S(2)}) %collective-permute-start.4) | collective-permute-done | bytes 262176 | tf_op jit(solution)/shard_map/ppermute | solution.py:194
  31.8 0.0 collective-permute-start.8
  31.8 0.0 collective-permute-done.5.refs_3_
  31.8 3.6 %collective-permute-done.3.refs_1_ = f32[64,1024]{1,0:T(8,128)S(1)} collective-permute-done((f32[64,1024]{1,0:T(8,128)S(1)}, f32[64,1024]{1,0:T(8,128)S(1)}, u32[]{:S(2)}, u32[]{:S(2)}) %collective-permute-start.3) | collective-permute-done | bytes 262176 | tf_op jit(solution)/shard_map/ppermute | solution.py:193
  35.4 1.0 %cov_out.1 = (f32[64,128]{1,0:T(8,128)S(1)}, f32[4,64,128]{2,1,0:T(8,128)S(1)}) custom-call(f32[64,1024]{1,0:T(8,128)S(1)} %get-tuple-element.23.x_ref, f32[64,128]{1,0:T(8,128)S(1)} %get-tuple-element.24.cov_ref, f32[64,1024]{1,0:T(8,128)S(1)} %get-tuple-element.25.refs_0_, f32[64,1024]{1,0:T(8,128)S(1)} %collective-permute-done.3.refs_1_, ...), custom_call_target="tpu_custom_call" | custom-call | tf_op jit(solution)/shard_map/cov_out/pallas_call | solution.py:255
  36.4 0.1 collective-permute-start.6
  36.5 1.2 %collective-permute-done.6 = f32[64,128]{1,0:T(8,128)S(1)} collective-permute-done((f32[64,128]{1,0:T(8,128)S(1)}, f32[64,128]{1,0:T(8,128)S(1)}, u32[]{:S(2)}, u32[]{:S(2)}) %collective-permute-start.6) | collective-permute-done | bytes 32800 | tf_op jit(solution)/shard_map/ppermute | solution.py:404
  37.7 1.5 %collective-permute-start.7 = (f32[64,128]{1,0:T(8,128)S(1)}, f32[64,128]{1,0:T(8,128)S(1)}, u32[]{:S(2)}, u32[]{:S(2)}) collective-permute-start(f32[64,128]{1,0:T(8,128)S(1)} %add.6.own_ref), channel_id=1, source_target_pairs={{0,2},{1,3},{2,0},{3,1},{4,6},{5,7},{6,4},{7,5},{8,10},{9,11},{10,... | collective-permute-start | bytes 98312 | tf_op jit(solution)/shard_map/ppermute | solution.py:404
  39.2 2.4 %collective-permute-done.7.other_ref = f32[64,128]{1,0:T(8,128)S(1)} collective-permute-done((f32[64,128]{1,0:T(8,128)S(1)}, f32[64,128]{1,0:T(8,128)S(1)}, u32[]{:S(2)}, u32[]{:S(2)}) %collective-permute-start.7) | collective-permute-done | bytes 32800 | tf_op jit(solution)/shard_map/ppermute | solution.py:404
  41.6 0.0 collective-permute-done.10.refs_3_
  41.6 0.0 collective-permute-done.9.refs_2_
  41.6 0.0 collective-permute-done.8.refs_1_
  41.6 3.7 %score.1 = f32[4,64]{1,0:T(4,128)S(1)} custom-call(s32[1]{0:T(128)} %bitcast.place_ref, f32[64,128]{1,0:T(8,128)S(1)} %add.6.own_ref, f32[64,128]{1,0:T(8,128)S(1)} %collective-permute-done.7.other_ref, f32[4,64,128]{2,1,0:T(8,128)S(1)} %get-tuple-element.29.sample_ref, bf16[8,64,128]{2,1,0:T(8,128)(2,1)S(1)} %get-tuple-element.30.refs_0_, ...), custom_call_target="tpu_custom_call" | custom-call | tf_op jit(solution)/shard_map/score/pallas_call | solution.py:389
  45.3 1.2 %collective-permute-start.13 = (f32[4,64]{1,0:T(4,128)S(1)}, f32[4,64]{1,0:T(4,128)S(1)}, u32[]{:S(2)}, u32[]{:S(2)}) collective-permute-start(f32[4,64]{1,0:T(4,128)S(1)} %score.1), channel_id=1, source_target_pairs={{0,12},{4,0},{8,4},{12,8},{1,13},{5,1},{9,5},{13,9},{2,14},{6,2},{... | collective-permute-start | bytes 3080 | tf_op jit(solution)/shard_map/ppermute | solution.py:409
  46.6 0.8 %collective-permute-start.12 = (f32[4,64]{1,0:T(4,128)S(1)}, f32[4,64]{1,0:T(4,128)S(1)}, u32[]{:S(2)}, u32[]{:S(2)}) collective-permute-start(f32[4,64]{1,0:T(4,128)S(1)} %score.1), channel_id=1, source_target_pairs={{0,4},{4,8},{8,12},{12,0},{1,5},{5,9},{9,13},{13,1},{2,6},{6,10},{... | collective-permute-start | bytes 3080 | tf_op jit(solution)/shard_map/ppermute | solution.py:409
  47.4 1.2 %collective-permute-start.11 = (f32[4,64]{1,0:T(4,128)S(1)}, f32[4,64]{1,0:T(4,128)S(1)}, u32[]{:S(2)}, u32[]{:S(2)}) collective-permute-start(f32[4,64]{1,0:T(4,128)S(1)} %score.1), channel_id=1, source_target_pairs={{0,8},{4,12},{8,0},{12,4},{1,9},{5,13},{9,1},{13,5},{2,10},{6,14},... | collective-permute-start | bytes 3080 | tf_op jit(solution)/shard_map/ppermute | solution.py:409
  48.6 0.4 collective-permute-done.13
  49.0 3.0 %collective-permute-done.12 = f32[4,64]{1,0:T(4,128)S(1)} collective-permute-done((f32[4,64]{1,0:T(4,128)S(1)}, f32[4,64]{1,0:T(4,128)S(1)}, u32[]{:S(2)}, u32[]{:S(2)}) %collective-permute-start.12) | collective-permute-done | bytes 1056 | tf_op jit(solution)/shard_map/ppermute | solution.py:409
  51.9 0.0 collective-permute-done.11
  51.9 0.6 %select_add_fusion = f32[4,64]{1,0:T(4,128)} fusion(f32[4,64]{1,0:T(4,128)S(1)} %collective-permute-done.12, f32[4,64]{1,0:T(4,128)S(1)} %collective-permute-done.13, f32[4,64]{1,0:T(4,128)S(1)} %score.1, f32[4,64]{1,0:T(4,128)S(1)} %collective-permute-done.11, pred[]{:T(512)S(6)} %ge.4, pred[]{:T(512)S(6)} %or.3), kind=kLoop, calls=%fused_computation | loop fusion | flops 768 | bytes 5122 | tf_op jit(solution)/shard_map/add | solution.py:437
  (1 shorter events, 0.0 us)
Async XLA Ops:
  0.0 12.1 %copy-start = (bf16[2,64,7168]{2,1,0:T(8,128)(2,1)S(1)}, bf16[2,64,7168]{2,1,0:T(8,128)(2,1)}, u32[]{:S(2)}) copy-start(bf16[2,64,7168]{2,1,0:T(8,128)(2,1)} %proj_ref.1) | copy-start | bytes 5505028
  3.9 19.4 %collective-permute-start.1 = (f32[64,1024]{1,0:T(8,128)S(1)}, f32[64,1024]{1,0:T(8,128)S(1)}, u32[]{:S(2)}, u32[]{:S(2)}) collective-permute-start(f32[64,1024]{1,0:T(8,128)S(1)} %get-tuple-element.21), channel_id=1, source_target_pairs={{0,8},{12,4},{4,0},{8,12},{1,9},{13,5},{5,1},{9,13},{2,10},{14,6},... | collective-permute-start | bytes 786440 | tf_op jit(solution)/shard_map/ppermute | solution.py:194
  8.0 18.6 %collective-permute-start.2 = (f32[64,1024]{1,0:T(8,128)S(1)}, f32[64,1024]{1,0:T(8,128)S(1)}, u32[]{:S(2)}, u32[]{:S(2)}) collective-permute-start(f32[64,1024]{1,0:T(8,128)S(1)} %get-tuple-element.22), channel_id=1, source_target_pairs={{4,8},{8,4},{5,9},{9,5},{6,10},{10,6},{7,11},{11,7},{20,24},{24,20... | collective-permute-start | bytes 786440 | tf_op jit(solution)/shard_map/ppermute | solution.py:187
  8.7 17.9 %collective-permute-start = (f32[64,1024]{1,0:T(8,128)S(1)}, f32[64,1024]{1,0:T(8,128)S(1)}, u32[]{:S(2)}, u32[]{:S(2)}) collective-permute-start(f32[64,1024]{1,0:T(8,128)S(1)} %get-tuple-element.20.refs_0_), channel_id=1, source_target_pairs={{0,4},{12,8},{4,0},{8,12},{1,5},{13,9},{5,1},{9,13},{2,6},{14,10},... | collective-permute-start | bytes 786440 | tf_op jit(solution)/shard_map/ppermute | solution.py:193
  22.5 9.3 %collective-permute-start.4 = (f32[64,1024]{1,0:T(8,128)S(1)}, f32[64,1024]{1,0:T(8,128)S(1)}, u32[]{:S(2)}, u32[]{:S(2)}) collective-permute-start(f32[64,1024]{1,0:T(8,128)S(1)} %get-tuple-element.26), channel_id=1, source_target_pairs={{0,8},{12,4},{4,0},{8,12},{1,9},{13,5},{5,1},{9,13},{2,10},{14,6},... | collective-permute-start | bytes 786440 | tf_op jit(solution)/shard_map/ppermute | solution.py:194
  22.6 9.2 %collective-permute-start.5 = (f32[64,1024]{1,0:T(8,128)S(1)}, f32[64,1024]{1,0:T(8,128)S(1)}, u32[]{:S(2)}, u32[]{:S(2)}) collective-permute-start(f32[64,1024]{1,0:T(8,128)S(1)} %get-tuple-element.27), channel_id=1, source_target_pairs={{4,8},{8,4},{5,9},{9,5},{6,10},{10,6},{7,11},{11,7},{20,24},{24,20... | collective-permute-start | bytes 786440 | tf_op jit(solution)/shard_map/ppermute | solution.py:187
  23.3 12.1 %collective-permute-start.3 = (f32[64,1024]{1,0:T(8,128)S(1)}, f32[64,1024]{1,0:T(8,128)S(1)}, u32[]{:S(2)}, u32[]{:S(2)}) collective-permute-start(f32[64,1024]{1,0:T(8,128)S(1)} %get-tuple-element.25.refs_0_), channel_id=1, source_target_pairs={{0,4},{12,8},{4,0},{8,12},{1,5},{13,9},{5,1},{9,13},{2,6},{14,10},... | collective-permute-start | bytes 786440 | tf_op jit(solution)/shard_map/ppermute | solution.py:193
  27.0 14.6 %collective-permute-start.10 = (bf16[8,64,128]{2,1,0:T(8,128)(2,1)S(1)}, bf16[8,64,128]{2,1,0:T(8,128)(2,1)S(1)}, u32[]{:S(2)}, u32[]{:S(2)}) collective-permute-start(bf16[8,64,128]{2,1,0:T(8,128)(2,1)S(1)} %get-tuple-element.30.refs_0_), channel_id=1, source_target_pairs={{0,3},{1,2},{2,1},{3,0},{4,7},{5,6},{6,5},{7,4},{8,11},{9,10},{10,... | collective-permute-start | bytes 393224 | tf_op jit(solution)/shard_map/ppermute | solution.py:404
  27.1 14.5 %collective-permute-start.9 = (bf16[8,64,128]{2,1,0:T(8,128)(2,1)S(1)}, bf16[8,64,128]{2,1,0:T(8,128)(2,1)S(1)}, u32[]{:S(2)}, u32[]{:S(2)}) collective-permute-start(bf16[8,64,128]{2,1,0:T(8,128)(2,1)S(1)} %get-tuple-element.30.refs_0_), channel_id=1, source_target_pairs={{0,2},{1,3},{2,0},{3,1},{4,6},{5,7},{6,4},{7,5},{8,10},{9,11},{10,... | collective-permute-start | bytes 393224 | tf_op jit(solution)/shard_map/ppermute | solution.py:404
  31.8 9.8 %collective-permute-start.8 = (bf16[8,64,128]{2,1,0:T(8,128)(2,1)S(1)}, bf16[8,64,128]{2,1,0:T(8,128)(2,1)S(1)}, u32[]{:S(2)}, u32[]{:S(2)}) collective-permute-start(bf16[8,64,128]{2,1,0:T(8,128)(2,1)S(1)} %get-tuple-element.30.refs_0_), channel_id=1, source_target_pairs={{0,1},{1,0},{2,3},{3,2},{4,5},{5,4},{6,7},{7,6},{8,9},{9,8},{10,11... | collective-permute-start | bytes 393224 | tf_op jit(solution)/shard_map/ppermute | solution.py:404
  36.4 1.3 %collective-permute-start.6 = (f32[64,128]{1,0:T(8,128)S(1)}, f32[64,128]{1,0:T(8,128)S(1)}, u32[]{:S(2)}, u32[]{:S(2)}) collective-permute-start(f32[64,128]{1,0:T(8,128)S(1)} %get-tuple-element.28), channel_id=1, source_target_pairs={{0,1},{1,0},{2,3},{3,2},{4,5},{5,4},{6,7},{7,6},{8,9},{9,8},{10,11... | collective-permute-start | bytes 98312 | tf_op jit(solution)/shard_map/ppermute | solution.py:404
  37.7 3.9 %collective-permute-start.7 = (f32[64,128]{1,0:T(8,128)S(1)}, f32[64,128]{1,0:T(8,128)S(1)}, u32[]{:S(2)}, u32[]{:S(2)}) collective-permute-start(f32[64,128]{1,0:T(8,128)S(1)} %add.6.own_ref), channel_id=1, source_target_pairs={{0,2},{1,3},{2,0},{3,1},{4,6},{5,7},{6,4},{7,5},{8,10},{9,11},{10,... | collective-permute-start | bytes 98312 | tf_op jit(solution)/shard_map/ppermute | solution.py:404
  45.3 3.6 %collective-permute-start.13 = (f32[4,64]{1,0:T(4,128)S(1)}, f32[4,64]{1,0:T(4,128)S(1)}, u32[]{:S(2)}, u32[]{:S(2)}) collective-permute-start(f32[4,64]{1,0:T(4,128)S(1)} %score.1), channel_id=1, source_target_pairs={{0,12},{4,0},{8,4},{12,8},{1,13},{5,1},{9,5},{13,9},{2,14},{6,2},{... | collective-permute-start | bytes 3080 | tf_op jit(solution)/shard_map/ppermute | solution.py:409
  46.6 5.4 %collective-permute-start.12 = (f32[4,64]{1,0:T(4,128)S(1)}, f32[4,64]{1,0:T(4,128)S(1)}, u32[]{:S(2)}, u32[]{:S(2)}) collective-permute-start(f32[4,64]{1,0:T(4,128)S(1)} %score.1), channel_id=1, source_target_pairs={{0,4},{4,8},{8,12},{12,0},{1,5},{5,9},{9,13},{13,1},{2,6},{6,10},{... | collective-permute-start | bytes 3080 | tf_op jit(solution)/shard_map/ppermute | solution.py:409
  47.4 4.5 %collective-permute-start.11 = (f32[4,64]{1,0:T(4,128)S(1)}, f32[4,64]{1,0:T(4,128)S(1)}, u32[]{:S(2)}, u32[]{:S(2)}) collective-permute-start(f32[4,64]{1,0:T(4,128)S(1)} %score.1), channel_id=1, source_target_pairs={{0,8},{4,12},{8,0},{12,4},{1,9},{5,13},{9,1},{13,5},{2,10},{6,14},... | collective-permute-start | bytes 3080 | tf_op jit(solution)/shard_map/ppermute | solution.py:409
